TPU v7x, 32 devices: a whole 2x2x4 slice. The times are simulated.
32 devices in a mesh: tx: 2 (over x), ty: 4 (over y, core), mem: 4 (over z).
Axes of the slice: x: 2, y: 2, z: 4, core: 2. Of those that a mesh axis runs over, the one named last changes fastest.
Arguments:
- alpha: float32 [16, 128, 2560], P('tx', 'ty', 'mem'), may hold values from -6 to 6
- lv_sqrt: float32 [32, 32], replicated, may hold values from -1 to 1
- ens_pert: bfloat16 [80, 32, 64, 512], P('mem', None, 'tx', 'ty'), may hold values from -0.625 to 0.625
- bg_sigma: float32 [32, 64, 512], P(None, 'tx', 'ty'), may hold values from 0.1 to 1
- static_ctrl: float32 [32, 64, 512], P(None, 'tx', 'ty'), may hold values from -6 to 6
- obs_owner: int32 [262144, 1], P(('tx', 'ty', 'mem')), may hold values from 0 to 7; in each aligned block of 8192 rows (0 to 8191, 8192 to 16383, ...) at most 2048 rows name the same one
- obs_column: int32 [262144], P(('tx', 'ty', 'mem')), may hold values from 0 to 3966, as said below
- obs_level: int32 [262144], P(('tx', 'ty', 'mem')), may hold values from 0 to 30
- obs_frac: float32 [3, 262144], P(None, ('tx', 'ty', 'mem')), may hold values from 0 to 1
- innovation: float32 [262144], P(('tx', 'ty', 'mem')), may hold values from -6 to 6
- obs_rinv: float32 [262144], P(('tx', 'ty', 'mem')), may hold values from 0.5 to 8
- obs_count: int32 [32], P(('tx', 'ty', 'mem')), may hold values from 4096 to 8192, as said below
Outputs:
- grad_alpha: float32 [16, 128, 2560], P('tx', 'ty', 'mem')
- grad_static: float32 [32, 64, 512], P(None, 'tx', 'ty')
- departures: float32 [262144], P(('tx', 'ty', 'mem'))
Inputs may be any that keep to these rules, and one draw needn't show every extreme that they name: `obs_owner`: tile number (tx index) * 4 + (ty index). Among one device's 8192 rows no tile is named more than 2048 times, a bound that some block reaches. `obs_column`: i * 128 + j with i < 31 and j < 127. `obs_count`: the live slots of a device are its first ones; some device has all 8192 live and some half of them.
All inputs are finite; a program needn't handle non-finite values.
Results may differ from a plain program's by a relative error of at most 0.0003.
Values sent between devices are 32-bit elements; how exact they have to be, the bound alone decides.
No kernel may reach another device: no remote copies, remote signals or barrier semaphores. Data moves between devices by JAX's collectives and lax.ppermute only.
A program may use at most 128 MiB of HBM per device.

v0:
```python
import functools

import jax
import jax.numpy as jnp
import numpy as np
from jax import lax
from jax.experimental import pallas as pl
from jax.experimental.pallas import tpu as pltpu
from jax.sharding import PartitionSpec as P

RATIO = 4
NSTEP = 4
NU = 0.2
VMEM = pl.BlockSpec(memory_space=pltpu.VMEM)
SMEM = pl.BlockSpec(memory_space=pltpu.SMEM)
ROOM = pltpu.CompilerParams(vmem_limit_bytes=48 << 20)
BLOCK = 256
LANES = 128
WINDOW = 12
HALF = jnp.bfloat16


def split_two(value):
    high = value.astype(HALF)
    return high, (value - high.astype(jnp.float32)).astype(HALF)


def dot_nt(a, b):
    return lax.dot_general(a, b, (((1,), (1,)), ((), ())), preferred_element_type=jnp.float32)


def dot_nn(a, b):
    return jnp.dot(a, b, preferred_element_type=jnp.float32)


def iota(shape, dim):
    return lax.broadcasted_iota(jnp.int32, shape, dim)


def pack_kernel(
    tiles, levels, plane, capacity,
    count_ref, owner_ref, column_ref, level_ref, frac_ref, innov_ref, rinv_ref,
    out_ref, target_ref,
    carry, total, gathered,
):
    blocks = owner_ref.shape[0] * LANES // BLOCK
    keys = tiles * levels
    deep = capacity // BLOCK
    slot_rows = tiles * deep
    group = 4
    count = count_ref[0]

    def row_of(ref, j):
        pair = ref[pl.ds(2 * j, 2), :]
        return jnp.concatenate([pair[0:1], pair[1:2]], 1)

    def onehot(j):
        live = iota((1, BLOCK), 1) + j * BLOCK < count
        key = jnp.where(live, row_of(owner_ref, j) * levels + row_of(level_ref, j), -1)
        return live, iota((keys, BLOCK), 0) == key

    ones = jnp.ones((BLOCK, LANES), HALF)
    total[...] = jnp.zeros_like(total)

    def count_block(j, unused):
        live, mask = onehot(j)
        total[...] += dot_nn(jnp.where(mask, 1.0, 0.0).astype(HALF), ones)
        return unused

    lax.fori_loop(0, blocks, count_block, 0)
    high = jnp.floor(total[...] * (1.0 / LANES))
    low = total[...] - high * LANES
    row_key, col_key = iota((keys, keys), 0), iota((keys, keys), 1)
    before = jnp.where((col_key < row_key) & (col_key // levels == row_key // levels), 1.0, 0.0).astype(HALF)
    start = dot_nn(before, high.astype(HALF)) * LANES + dot_nn(before, low.astype(HALF))
    carry[...] = start + ((iota((keys, LANES), 0) // levels) * capacity).astype(jnp.float32)

    earlier = jnp.where(iota((BLOCK, BLOCK), 0) < iota((BLOCK, BLOCK), 1), 1.0, 0.0).astype(HALF)
    prefix = jnp.concatenate([earlier, ones], 1)
    gathered[...] = jnp.zeros_like(gathered)

    def place(j):
        live, mask = onehot(j)
        ranks = dot_nn(jnp.where(mask, 1.0, 0.0).astype(HALF), prefix)
        now = carry[...]
        here = ranks[:, :BLOCK] + jnp.concatenate([now] * (BLOCK // LANES), 1)
        carry[...] = now + ranks[:, BLOCK:]
        slot = jnp.sum(jnp.where(mask, here, 0.0), 0, keepdims=True)
        target = jnp.where(live, slot.astype(jnp.int32), -1)
        target_ref[pl.ds(2 * j, 2), :] = jnp.concatenate([target[:, :LANES], target[:, LANES:]], 0)
        rows = jnp.where(iota((slot_rows, BLOCK), 0) == (target >> 8), 1.0, 0.0).astype(HALF)
        lanes = jnp.where(iota((BLOCK, BLOCK), 0) == (target & (BLOCK - 1)), 1.0, 0.0).astype(HALF)
        column = row_of(column_ref, j)
        frac = frac_ref[:, pl.ds(pl.multiple_of(j * BLOCK, BLOCK), BLOCK)]
        terms = []
        for value in (frac[0:1], frac[1:2], frac[2:3], row_of(innov_ref, j), row_of(rinv_ref, j)):
            terms.extend(split_two(jnp.broadcast_to(value, (16, BLOCK))))
        for value in (row_of(level_ref, j), column >> 7, column & (LANES - 1)):
            terms.append(jnp.broadcast_to(value.astype(jnp.float32), (16, BLOCK)).astype(HALF))
        spread = [rows * jnp.concatenate([term] * (slot_rows // 16), 0) for term in terms]
        return jnp.concatenate(spread, 0), lanes

    def scatter_group(g, unused):
        placed = [place(g * group + i) for i in range(group)]
        left = jnp.concatenate([a for a, b in placed], 1)
        right = jnp.concatenate([b for a, b in placed], 1)
        gathered[...] += dot_nt(left, right)
        return unused

    lax.fori_loop(0, blocks // group, scatter_group, 0)

    def part(index, tile):
        begin = index * slot_rows + tile * deep
        return gathered[begin:begin + deep, :]

    for tile in range(tiles):
        for p in range(5):
            out_ref[tile, p * deep:(p + 1) * deep, :] = part(2 * p, tile) + part(2 * p + 1, tile)
        base = part(10, tile) * plane + part(11, tile) * LANES + part(12, tile)
        out_ref[tile, 5 * deep:6 * deep, :] = base


def pack(tiles, levels, plane, capacity, count, owner, column, level, frac, innov, rinv):
    slots = owner.shape[0]
    rows = slots // LANES
    deep = capacity // BLOCK
    vmem = pl.BlockSpec(memory_space=pltpu.VMEM)
    return pl.pallas_call(
        functools.partial(pack_kernel, tiles, levels, plane, capacity),
        out_shape=(
            jax.ShapeDtypeStruct((tiles, 6 * deep, BLOCK), jnp.float32),
            jax.ShapeDtypeStruct((rows, LANES), jnp.int32),
        ),
        in_specs=[pl.BlockSpec(memory_space=pltpu.SMEM)] + [vmem] * 6,
        out_specs=(vmem, vmem),
        scratch_shapes=[
            pltpu.VMEM((tiles * levels, LANES), jnp.float32),
            pltpu.VMEM((tiles * levels, LANES), jnp.float32),
            pltpu.VMEM((13 * tiles * deep, BLOCK), jnp.float32),
        ],
        compiler_params=pltpu.CompilerParams(vmem_limit_bytes=40 << 20),
        cost_estimate=pl.CostEstimate(flops=8 << 30, bytes_accessed=1 << 20, transcendentals=0),
        name="pack",
    )(count, *[a.reshape(rows, LANES) for a in (owner, column, level)], frac,
      *[a.reshape(rows, LANES) for a in (innov, rinv)])


def stencil_kernel(
    ahead_ref, behind_ref, first_ref, windows_ref, parts_refs, sigma_ref, static_ref, incoming_ref,
    dep_ref, adj_refs,
    field_t, row_hi, row_lo, adjoint,
):
    levels, fine_x, fine_y = sigma_ref.shape
    sources, packed_rows, block = incoming_ref.shape
    deep = packed_rows // 6
    plane = fine_x * fine_y
    chunk = LANES // fine_x
    share = levels // len(parts_refs)
    span = WINDOW // chunk
    width = WINDOW * fine_x
    adjoint[...] = jnp.zeros_like(adjoint)
    dep_ref[...] = jnp.zeros_like(dep_ref)
    field_t[:, levels * fine_x:] = jnp.zeros((2 * fine_y, width), HALF)
    for slot, part in enumerate(parts_refs):
        start = behind_ref[slot] * share
        static = sigma_ref[pl.ds(start, share)] * static_ref[pl.ds(start, share)]
        turned = (part[...] + static).reshape(share * fine_x, fine_y).T
        high, low = split_two(turned)
        where = pl.ds(pl.multiple_of(start * fine_x, LANES), share * fine_x)
        field_t[:fine_y, where] = high
        field_t[fine_y:, where] = low

    def one_block(q, unused):
        source, at = q // deep, q % deep

        def row(p):
            return incoming_ref[source, pl.ds(p * deep + at, 1), :]

        windows = windows_ref[q]

        @pl.when(windows > 0)
        def _():
            rinv, base = row(4), row(5)
            level = jnp.floor(base * (1.0 / plane))
            rest = base - level * plane
            across = jnp.floor(rest * (1.0 / fine_y))
            along = rest - across * fine_y
            frac_x, frac_y, frac_l = row(0), row(1), row(2)
            first = first_ref[q]
            rows_x = iota((fine_x, block), 0).astype(jnp.float32)
            pick_x = jnp.where(rows_x == across, 1.0 - frac_x, 0.0) + jnp.where(rows_x == across + 1.0, frac_x, 0.0)

            def at_window(w):
                return pl.ds(pl.multiple_of((first + w * span) * LANES, LANES), width)

            def forward(w, acc):
                bottom = ((first + w * span) * chunk).astype(jnp.float32)
                offset = level - bottom
                picks = []
                for g in range(WINDOW):
                    pick_l = jnp.where(offset == float(g), 1.0 - frac_l, 0.0) + jnp.where(offset == float(g - 1), frac_l, 0.0)
                    picks.append(pick_x * pick_l)
                high, low = split_two(jnp.concatenate(picks, 0))
                where = at_window(w)
                row_hi[where, :] = high
                row_lo[where, :] = low
                both = field_t[:, where]
                twice = dot_nn(both, high)
                return acc + (twice[:fine_y] + twice[fine_y:]) + dot_nn(both[:fine_y], low)

            picked = lax.fori_loop(0, windows, forward, jnp.zeros((fine_y, block), jnp.float32))
            rows_y = iota((fine_y, block), 0).astype(jnp.float32)
            pick_y = jnp.where(rows_y == along, 1.0 - frac_y, 0.0) + jnp.where(rows_y == along + 1.0, frac_y, 0.0)
            departure = jnp.sum(picked * pick_y, 0, keepdims=True) - row(3)
            dep_ref[source, pl.ds(at, 1), :] = departure
            high, low = split_two(pick_y * (rinv * departure))
            both = jnp.concatenate([high, low], 0)

            def backward(w, unused):
                where = at_window(w)
                adjoint[where, :] += dot_nt(row_hi[where, :], both)
                adjoint[where, :fine_y] += dot_nt(row_lo[where, :], high)
                return unused

            lax.fori_loop(0, windows, backward, 0)

        return unused

    lax.fori_loop(0, sources * deep, one_block, 0)
    for slot, adj_ref in enumerate(adj_refs):
        rows = pl.ds(pl.multiple_of(ahead_ref[slot] * share * fine_x, LANES), share * fine_x)
        both = adjoint[rows, :]
        adj_ref[...] = (both[:, :fine_y] + both[:, fine_y:]).reshape(share, fine_x, fine_y)


def stencil(parts, incoming, bg_sigma, static_ctrl, ahead, behind):
    levels, fine_x, fine_y = bg_sigma.shape
    sources, packed_rows, block = incoming.shape
    deep, groups = packed_rows // 6, len(parts)
    rows = levels * fine_x + WINDOW * fine_x
    chunk = LANES // fine_x
    level = (incoming[:, 5 * deep:] * (1.0 / (fine_x * fine_y))).astype(jnp.int32)
    used = incoming[:, 4 * deep:5 * deep] > 0.0
    lowest = jnp.min(jnp.where(used, level, levels), 2).reshape(-1)
    highest = jnp.max(jnp.where(used, level, -1), 2).reshape(-1)
    first = lowest // chunk
    windows = jnp.where(highest >= 0, ((highest + 1) // chunk - first) // (WINDOW // chunk) + 1, 0)

    def kernel(*refs):
        parts_end = 4 + groups
        stencil_kernel(
            *refs[:4], refs[4:parts_end], *refs[parts_end:parts_end + 4],
            refs[parts_end + 4:parts_end + 4 + groups], *refs[parts_end + 4 + groups:]
        )

    results = pl.pallas_call(
        kernel,
        out_shape=(jax.ShapeDtypeStruct((sources, deep, block), jnp.float32),)
        + tuple(jax.ShapeDtypeStruct(part.shape, jnp.float32) for part in parts),
        in_specs=[SMEM] * 4 + [VMEM] * (groups + 3),
        out_specs=(VMEM,) * (1 + groups),
        scratch_shapes=[
            pltpu.VMEM((2 * fine_y, rows), HALF),
            pltpu.VMEM((rows, block), HALF),
            pltpu.VMEM((rows, block), HALF),
            pltpu.VMEM((rows, 2 * fine_y), jnp.float32),
        ],
        compiler_params=ROOM,
        cost_estimate=pl.CostEstimate(flops=16 << 30, bytes_accessed=1 << 20, transcendentals=0),
        name="stencil",
    )(ahead, behind, first, windows, *parts, bg_sigma, static_ctrl, incoming)
    return results[0], results[1:]


def unpack_kernel(target_ref, table_ref, out_ref):
    rows = target_ref.shape[0]
    target = target_ref[...]
    wanted, lane = target >> 7, target & (LANES - 1)

    def one_row(r, found):
        pair = table_ref[pl.ds(r, 1), :]
        for h in range(BLOCK // LANES):
            line = jnp.broadcast_to(pair[:, h * LANES:(h + 1) * LANES], (rows, LANES))
            value = jnp.take_along_axis(line, lane, axis=1, mode="promise_in_bounds")
            found = jnp.where(wanted == r * (BLOCK // LANES) + h, value, found)
        return found

    out_ref[...] = lax.fori_loop(0, table_ref.shape[0], one_row, jnp.zeros((rows, LANES), jnp.float32))


def unpack(target, table):
    vmem = pl.BlockSpec(memory_space=pltpu.VMEM)
    return pl.pallas_call(
        unpack_kernel,
        out_shape=jax.ShapeDtypeStruct(target.shape, jnp.float32),
        in_specs=[vmem, vmem],
        out_specs=vmem,
        cost_estimate=pl.CostEstimate(flops=16 << 20, bytes_accessed=1 << 18, transcendentals=0),
        name="unpack",
    )(target, table).reshape(-1)


REACH = NSTEP
EDGE = 8
PAD = 2 * EDGE
SCALE = NU**NSTEP


def interpolation(shape, fine_dim, coarse_dim, shift):
    fine, coarse = iota(shape, fine_dim), iota(shape, coarse_dim) - shift
    frac = (fine % RATIO).astype(jnp.float32) * (1.0 / RATIO)
    low = jnp.where(coarse == fine // RATIO, 1.0 - frac, 0.0)
    return (low + jnp.where(coarse == fine // RATIO + 1, frac, 0.0)).astype(HALF)


def interpolation_rows(fine_x, depth, copies, transposed):
    long, short = EDGE * fine_x, EDGE * depth
    shape = (short, long) if transposed else (long, copies * short)
    fine, coarse = iota(shape, 1 if transposed else 0), iota(shape, 0 if transposed else 1)
    for copy in range(1, copies):
        coarse = jnp.where(coarse >= short, coarse - short, coarse)
    place, target = fine % fine_x, coarse // EDGE
    frac = (place % RATIO).astype(jnp.float32) * (1.0 / RATIO)
    low = jnp.where(target == place // RATIO, 1.0 - frac, 0.0)
    weight = low + jnp.where(target == place // RATIO + 1, frac, 0.0)
    return jnp.where(fine // fine_x == coarse % EDGE, weight, 0.0).astype(HALF)


def neighbours(field):
    width = field.shape[1]
    return pltpu.roll(field, 1, 1) + pltpu.roll(field, width - 1, 1)


def ensemble_kernel(
    coarse_x, coarse_y, offsets,
    order_ref, alpha_ref, above_ref, below_ref,
    left_ref, left_above_ref, left_below_ref, right_ref, right_above_ref, right_below_ref,
    mix_ref, pert_hbm, out_refs, pert_ref, sem, ext, coarse,
):
    members, levels, fine_x, fine_y = pert_ref.shape
    channels = alpha_ref.shape[2]
    fetch = pltpu.make_async_copy(pert_hbm, pert_ref, sem)
    fetch.start()
    ext[:, :EDGE, :] = jnp.zeros((ext.shape[0], EDGE, channels), jnp.float32)
    ext[:, EDGE + coarse_y:, :] = jnp.zeros((ext.shape[0], EDGE, channels), jnp.float32)
    above, below = offsets
    groups = (
        (0, REACH, above, above_ref, left_above_ref, right_above_ref),
        (REACH, coarse_x, 0, alpha_ref, left_ref, right_ref),
        (REACH + coarse_x, REACH + 1, below, below_ref, left_below_ref, right_below_ref),
    )
    for begin, count, offset, middle, left, right in groups:
        ext[begin:begin + count, EDGE:EDGE + coarse_y, :] = middle[offset:offset + count]
        for i in range(count):
            at = offset + i
            ext[begin + i, EDGE - REACH:EDGE, :] = left[at * REACH:(at + 1) * REACH, :]
            ext[begin + i, EDGE + coarse_y:EDGE + coarse_y + REACH + 1, :] = right[
                at * (REACH + 1):(at + 1) * (REACH + 1), :
            ]
    spread_y = interpolation((fine_y, coarse_y + PAD), 0, 1, EDGE)
    spread_y = jnp.concatenate([spread_y.astype(jnp.float32)] * 2, 1).astype(HALF)
    high, low = split_two(mix_ref[...])
    mix = jnp.concatenate([high, high, low], 1)

    def one_group(g, unused):
        lanes = pl.ds(pl.multiple_of(g * LANES, LANES), LANES)
        field = ext[:, :, lanes]
        for step in range(NSTEP):
            inner = field[1:-1]
            field = inner + field[2:] + field[:-2] + neighbours(inner)
        high, low = split_two(field * SCALE)
        for c in range(coarse_x + 1):
            wide = dot_nn(spread_y, jnp.concatenate([high[c], low[c]], 0))
            wide_high, wide_low = split_two(wide)
            coarse[c, lanes, :] = dot_nt(mix, jnp.concatenate([wide_high, wide_low, wide_high], 1))
        return unused

    lax.fori_loop(0, channels // LANES, one_group, 0)
    fetch.wait()
    depth = coarse_x + 2
    spread_x = interpolation_rows(fine_x, depth, 2, False)
    share = levels // len(out_refs)

    for slot, out_ref in enumerate(out_refs):
        for sub in range(share // EDGE):
            first = pl.multiple_of(order_ref[slot] * share + sub * EDGE, EDGE)

            def stacked(k):
                rows = pl.ds(pl.multiple_of(k * levels + first, EDGE), EDGE)
                parts = [coarse[c, rows, :] for c in range(coarse_x + 1)]
                return jnp.concatenate(parts + [jnp.zeros((EDGE, fine_y), jnp.float32)], 0)

            def perturbation(k):
                return pert_ref[k, pl.ds(first, EDGE)].reshape(EDGE * fine_x, fine_y).astype(jnp.float32)

            def pair(p, total):
                high, low = split_two(jnp.concatenate([stacked(2 * p), stacked(2 * p + 1)], 1))
                fine = dot_nn(spread_x, jnp.concatenate([high, low], 0))
                return total + fine[:, :fine_y] * perturbation(2 * p) + fine[:, fine_y:] * perturbation(2 * p + 1)

            total = lax.fori_loop(0, members // 2, pair, jnp.zeros((EDGE * fine_x, fine_y), jnp.float32))
            out_ref[sub * EDGE:(sub + 1) * EDGE] = total.reshape(EDGE, fine_x, fine_y)


def backward_kernel(
    coarse_x, coarse_y, joined,
    order_ref, parts_refs, mix_ref, sigma_ref, static_ref, pert_ref,
    grad_ref, center_ref, middle_refs, left_refs, right_refs,
    adjoint, coarse,
):
    members, levels, fine_x, fine_y = pert_ref.shape
    channels = members * levels
    share = levels // len(parts_refs)
    for slot, part in enumerate(parts_refs):
        first = order_ref[slot] * share
        adjoint[pl.ds(first, share)] = part[...]
    grad_ref[...] = static_ref[...] + sigma_ref[...] * adjoint[...]
    depth = coarse_x + 2
    fold_x = interpolation_rows(fine_x, depth, 1, True)

    for group in range(levels // EDGE):
        field = adjoint[group * EDGE:(group + 1) * EDGE].reshape(EDGE * fine_x, fine_y)

        def member(k, unused):
            scaled = pert_ref[k, group * EDGE:(group + 1) * EDGE].reshape(EDGE * fine_x, fine_y).astype(jnp.float32)
            high, low = split_two(scaled * field)
            both = dot_nn(fold_x, jnp.concatenate([high, low], 1))
            rows = pl.ds(pl.multiple_of(k * levels + group * EDGE, EDGE), EDGE)
            for c in range(coarse_x + 1):
                piece = both[c * EDGE:(c + 1) * EDGE]
                coarse[c, rows, :] = piece[:, :fine_y] + piece[:, fine_y:]
            return unused

        lax.fori_loop(0, members, member, 0)

    fold_y = interpolation((coarse_y + PAD, fine_y), 1, 0, EDGE)
    fold_y = jnp.concatenate([fold_y, fold_y], 1)
    high, low = split_two(mix_ref[...])
    mix = jnp.concatenate([high, high, low], 0)

    def one_group(g, unused):
        lanes = pl.ds(pl.multiple_of(g * LANES, LANES), LANES)
        rows = []
        for c in range(coarse_x + 1):
            high, low = split_two(coarse[c, lanes, :])
            narrow = dot_nt(fold_y, jnp.concatenate([high, low], 1))
            high, low = split_two(narrow)
            rows.append(dot_nn(jnp.concatenate([high, low, high], 1), mix)[None])
        field = jnp.concatenate(rows, 0) * SCALE
        empty = jnp.zeros((1,) + field.shape[1:], jnp.float32)
        for step in range(NSTEP):
            own = field + neighbours(field)
            field = jnp.concatenate([field, empty, empty], 0) + jnp.concatenate([empty, own, empty], 0) + jnp.concatenate(
                [empty, empty, field], 0
            )
        inside = field[REACH:REACH + coarse_x]
        up, down = field[:REACH], field[REACH + coarse_x:]
        if joined:
            none = jnp.zeros((coarse_x - REACH - 1,) + field.shape[1:], jnp.float32)
            outside = [jnp.concatenate([down, none], 0) + jnp.concatenate([none, empty, up], 0)]
        else:
            outside = [up, down]
        center_ref[:, :, lanes] = inside[:, EDGE:EDGE + coarse_y]
        for ref, value in zip(middle_refs, outside):
            ref[:, :, lanes] = value[:, EDGE:EDGE + coarse_y]
        for left, right, value in zip(left_refs, right_refs, [inside] + outside):
            for i in range(value.shape[0]):
                left[i * REACH:(i + 1) * REACH, lanes] = value[i, EDGE - REACH:EDGE]
                right[i * (REACH + 1):(i + 1) * (REACH + 1), lanes] = value[
                    i, EDGE + coarse_y:EDGE + coarse_y + REACH + 1
                ]
        return unused

    lax.fori_loop(0, channels // LANES, one_group, 0)


def fold_kernel(places, alpha_ref, center_ref, *refs):
    part_refs, out_ref = refs[:-1], refs[-1]
    out_ref[...] = alpha_ref[...] + center_ref[...]
    for (row, count, column, width), ref in zip(places, part_refs):
        if width == out_ref.shape[1]:
            out_ref[row:row + count] += ref[...]
        else:
            for i in range(count):
                out_ref[row + i, column:column + width, :] += ref[i * width:(i + 1) * width, :]


def shifted(value, by_x, by_y):
    count_x, count_y = lax.axis_size("tx"), lax.axis_size("ty")
    pairs = [
        (x * count_y + y, (x + by_x) % count_x * count_y + (y + by_y) % count_y)
        for x in range(count_x)
        for y in range(count_y)
    ]
    return lax.ppermute(value, ("tx", "ty"), pairs)


def ensemble(alpha, mix, ens_pert, order):
    coarse_x, coarse_y, channels = alpha.shape
    members, levels, fine_x, fine_y = ens_pert.shape
    joined = lax.axis_size("tx") == 2
    ends = alpha[:, coarse_y - REACH:]
    starts = alpha[:, :REACH + 1]

    def flat(strip):
        return strip.reshape(-1, channels)

    if joined:
        other = shifted(alpha, 1, 0)
        above = below = other
        left_above = left_below = shifted(flat(ends), 1, 1)
        right_above = right_below = shifted(flat(starts), 1, -1)
        offsets = (coarse_x - REACH, 0)
    else:
        last = slice(coarse_x - REACH, coarse_x)
        first = slice(0, REACH + 1)
        above, below = shifted(alpha[last], 1, 0), shifted(alpha[first], -1, 0)
        left_above, left_below = shifted(flat(ends[last]), 1, 1), shifted(flat(ends[first]), -1, 1)
        right_above, right_below = shifted(flat(starts[last]), 1, -1), shifted(flat(starts[first]), -1, -1)
        offsets = (0, 0)
    left, right = shifted(flat(ends), 0, 1), shifted(flat(starts), 0, -1)
    groups = order.shape[0]

    def kernel(*refs):
        ensemble_kernel(coarse_x, coarse_y, offsets, *refs[:12], refs[12:12 + groups], *refs[12 + groups:])

    return pl.pallas_call(
        kernel,
        out_shape=tuple(jax.ShapeDtypeStruct((levels // groups, fine_x, fine_y), jnp.float32) for _ in range(groups)),
        in_specs=[SMEM] + [VMEM] * 10 + [pl.BlockSpec(memory_space=pl.ANY)],
        out_specs=(VMEM,) * groups,
        scratch_shapes=[
            pltpu.VMEM(ens_pert.shape, ens_pert.dtype),
            pltpu.SemaphoreType.DMA,
            pltpu.VMEM((coarse_x + 2 * REACH + 1, coarse_y + PAD, channels), jnp.float32),
            pltpu.VMEM((coarse_x + 1, channels, fine_y), jnp.float32),
        ],
        compiler_params=ROOM,
        cost_estimate=pl.CostEstimate(flops=8 << 30, bytes_accessed=8 << 20, transcendentals=0),
        name="ensemble",
    )(order, alpha, above, below, left, left_above, left_below, right, right_above, right_below, mix, ens_pert)


def backward(alpha, adjoint_parts, mix, bg_sigma, static_ctrl, ens_pert, order):
    coarse_x, coarse_y, channels = alpha.shape
    members, levels, fine_x, fine_y = ens_pert.shape
    joined = lax.axis_size("tx") == 2
    groups = len(adjoint_parts)
    outside = [coarse_x] if joined else [REACH, REACH + 1]
    strips = [coarse_x] + outside
    shapes = [bg_sigma.shape, alpha.shape]
    shapes += [(rows, coarse_y, channels) for rows in outside]
    shapes += [(rows * REACH, channels) for rows in strips]
    shapes += [(rows * (REACH + 1), channels) for rows in strips]
    n_in, n_mid, n_strip = 5 + groups, len(outside), len(strips)

    def kernel(*refs):
        order_ref, parts, rest = refs[0], refs[1:1 + groups], refs[1 + groups:n_in]
        outs = refs[n_in:n_in + len(shapes)]
        middle = outs[2:2 + n_mid]
        left = outs[2 + n_mid:2 + n_mid + n_strip]
        right = outs[2 + n_mid + n_strip:]
        backward_kernel(
            coarse_x, coarse_y, joined, order_ref, parts, *rest,
            outs[0], outs[1], middle, left, right, *refs[n_in + len(shapes):]
        )

    results = pl.pallas_call(
        kernel,
        out_shape=tuple(jax.ShapeDtypeStruct(shape, jnp.float32) for shape in shapes),
        in_specs=[SMEM] + [VMEM] * (groups + 4),
        out_specs=(VMEM,) * len(shapes),
        scratch_shapes=[
            pltpu.VMEM(bg_sigma.shape, jnp.float32),
            pltpu.VMEM((coarse_x + 1, channels, fine_y), jnp.float32),
        ],
        compiler_params=ROOM,
        cost_estimate=pl.CostEstimate(flops=8 << 30, bytes_accessed=8 << 20, transcendentals=0),
        name="backward",
    )(order, *adjoint_parts, mix, bg_sigma, static_ctrl, ens_pert)
    grad_static, center = results[:2]
    middle = results[2:2 + n_mid]
    left, right = results[2 + n_mid:2 + n_mid + n_strip], results[2 + n_mid + n_strip:]
    last, wide = coarse_y - REACH, REACH + 1
    moves = [(1, 0, coarse_x)] if joined else [(-1, coarse_x - REACH, REACH), (1, 0, REACH + 1)]
    places, parts = [], []
    for (by, row, count), value, to_left, to_right in zip(moves, middle, left[1:], right[1:]):
        parts += [shifted(value, by, 0), shifted(to_left, by, -1), shifted(to_right, by, 1)]
        places += [(row, count, 0, coarse_y), (row, count, last, REACH), (row, count, 0, wide)]
    parts += [shifted(left[0], 0, -1), shifted(right[0], 0, 1)]
    places += [(0, coarse_x, last, REACH), (0, coarse_x, 0, wide)]
    grad_alpha = pl.pallas_call(
        functools.partial(fold_kernel, places),
        out_shape=jax.ShapeDtypeStruct(alpha.shape, jnp.float32),
        in_specs=[VMEM] * (2 + len(parts)),
        out_specs=VMEM,
        compiler_params=ROOM,
        cost_estimate=pl.CostEstimate(flops=1 << 20, bytes_accessed=2 << 20, transcendentals=0),
        name="fold",
    )(alpha, center, *parts)
    return grad_alpha, grad_static


def shared_sum(parts):
    count = len(parts)
    total = parts[0]
    for d in range(1, count):
        total = total + lax.ppermute(parts[d], "mem", [(i, (i + d) % count) for i in range(count)])
    return [total] + [lax.ppermute(total, "mem", [(i, (i + d) % count) for i in range(count)]) for d in range(1, count)]


def per_device(
    alpha,
    lv_sqrt,
    ens_pert,
    bg_sigma,
    static_ctrl,
    obs_owner,
    obs_column,
    obs_level,
    obs_frac,
    innovation,
    obs_rinv,
    obs_count,
):
    levels, fine_x, fine_y = bg_sigma.shape
    tiles = lax.axis_size("tx") * lax.axis_size("ty")
    capacity = 2 * obs_owner.shape[0] // tiles
    groups, me = lax.axis_size("mem"), lax.axis_index("mem")
    ahead = jnp.stack([(me + d) % groups for d in range(groups)]).astype(jnp.int32)
    behind = jnp.stack([(me - d) % groups for d in range(groups)]).astype(jnp.int32)
    copies = LANES // levels
    same = np.kron(np.eye(copies, dtype=np.float32), np.ones((levels, levels), np.float32))
    mix = jnp.tile(lv_sqrt, (copies, copies)) * same
    partial = ensemble(alpha, mix, ens_pert, ahead)
    outgoing, target = pack(
        tiles, levels, fine_x * fine_y, capacity,
        obs_count, obs_owner[:, 0], obs_column, obs_level, obs_frac, innovation, obs_rinv,
    )
    incoming = lax.all_to_all(outgoing, ("tx", "ty"), split_axis=0, concat_axis=0, tiled=True)
    departure, adjoint = stencil(shared_sum(partial), incoming, bg_sigma, static_ctrl, ahead, behind)
    returned = lax.all_to_all(departure, ("tx", "ty"), split_axis=0, concat_axis=0, tiled=True)
    departures = unpack(target, returned.reshape(-1, BLOCK))
    grad_alpha, grad_static = backward(alpha, shared_sum(adjoint), mix, bg_sigma, static_ctrl, ens_pert, behind)
    return (grad_alpha, grad_static, departures)


def solution(mesh):
    placed = (
        P("tx", "ty", "mem"),
        P(),
        P("mem", None, "tx", "ty"),
        P(None, "tx", "ty"),
        P(None, "tx", "ty"),
        P(("tx", "ty", "mem"), None),
        P(("tx", "ty", "mem")),
        P(("tx", "ty", "mem")),
        P(None, ("tx", "ty", "mem")),
        P(("tx", "ty", "mem")),
        P(("tx", "ty", "mem")),
        P(("tx", "ty", "mem")),
    )
    return jax.shard_map(
        per_device,
        mesh=mesh,
        in_specs=placed,
        out_specs=(P("tx", "ty", "mem"), P(None, "tx", "ty"), P(("tx", "ty", "mem"))),
        check_vma=False,
    )
```

profile of v0, /device:TPU:0, one launch (start us, length us, event | category | flops | bytes accessed | tf_op | source)
XLA Modules:
  0.0 197.3 jit_solution(1242350347667468876)
XLA Ops:
  1.6 2.4 %collective-permute-start.2 = (f32[32,640]{1,0:T(8,128)S(1)}, f32[32,640]{1,0:T(8,128)S(1)}, u32[]{:S(2)}, u32[]{:S(2)}) collective-permute-start(f32[32,640]{1,0:T(8,128)S(1)} %reshape.46), channel_id=1, source_target_pairs={{0,20},{4,24},{8,28},{12,16},{16,4},{20,8},{24,12},{28,0},{1,21},{... | collective-permute-start | bytes 245768 | tf_op jit(solution)/shard_map/ppermute | solution.py:495
  6.9 2.0 %collective-permute-start = (f32[8,32,640]{2,1,0:T(8,128)}, f32[8,32,640]{2,1,0:T(8,128)S(1)}, u32[]{:S(2)}, u32[]{:S(2)}) collective-permute-start(f32[8,32,640]{2,1,0:T(8,128)} %alpha_ref.1), channel_id=1, source_target_pairs={{0,16},{4,20},{8,24},{12,28},{16,0},{20,4},{24,8},{28,12},{1,17},{... | collective-permute-start | bytes 1966088 | tf_op jit(solution)/shard_map/ppermute | solution.py:495
  14.3 14.8 %pack.1 = (f32[8,48,256]{2,1,0:T(8,128)}, s32[64,128]{1,0:T(8,128)S(1)}) custom-call(s32[1]{0:T(128)S(6)} %copy.16.count_ref, s32[64,128]{1,0:T(8,128)S(1)} %bitcast.14, s32[64,128]{1,0:T(8,128)S(1)} %bitcast.15, s32[64,128]{1,0:T(8,128)S(1)} %bitcast.16, f32[3,8192]{1,0:T(4,128)S(1)} %copy-done.5, f32[64,128]{1,0:T(8,128)S(1)} %bitcast.17, ...), custom_call_target="tpu_custom_call" | custom-call | flops 8589934592 | bytes 1048576 | tf_op jit(solution)/shard_map/pack/pallas_call | solution.py:128
  29.7 3.5 %all-to-all-start = ((f32[8,48,256]{2,1,0:T(8,128)}), f32[8,48,256]{2,1,0:T(8,128)S(1)}, u32[]{:S(2)}, u32[]{:S(2)}) async-start(f32[8,48,256]{2,1,0:T(8,128)} %get-tuple-element.21), calls=%async_computation | async-start | bytes 786432 | tf_op jit(solution)/shard_map/all_to_all | solution.py:640
  33.7 6.9 %all-to-all-done.refs_10_ = f32[8,48,256]{2,1,0:T(8,128)S(1)} async-done(((f32[8,48,256]{2,1,0:T(8,128)}), f32[8,48,256]{2,1,0:T(8,128)S(1)}, u32[]{:S(2)}, u32[]{:S(2)}) %all-to-all-start) | async-done | bytes 393248 | tf_op jit(solution)/shard_map/all_to_all | solution.py:640
  45.7 18.0 %ensemble.1 = (f32[8,32,128]{2,1,0:T(8,128)S(1)}, f32[8,32,128]{2,1,0:T(8,128)S(1)}, f32[8,32,128]{2,1,0:T(8,128)S(1)}, f32[8,32,128]{2,1,0:T(8,128)S(1)}) custom-call(s32[4]{0:T(128)S(1)} %pad_add_fusion.1.refs_0_, f32[8,32,640]{2,1,0:T(8,128)S(1)} %copy-done, f32[8,32,640]{2,1,0:T(8,128)S(1)} %collective-permute-done.refs_2_.refs_3_, ...), custom_call_target="tpu_custom_call" | custom-call | flops 8589934592 | bytes 8388608 | tf_op jit(solution)/shard_map/ensemble/pallas_call | solution.py:527
  65.3 2.6 %collective-permute-start.6 = (f32[8,32,128]{2,1,0:T(8,128)S(1)}, f32[8,32,128]{2,1,0:T(8,128)S(1)}, u32[]{:S(2)}, u32[]{:S(2)}) collective-permute-start(f32[8,32,128]{2,1,0:T(8,128)S(1)} %get-tuple-element.24), channel_id=1, source_target_pairs={{0,2},{1,3},{2,0},{3,1},{4,6},{5,7},{6,4},{7,5},{8,10},{9,11},{10,... | collective-permute-start | bytes 393224 | tf_op jit(solution)/shard_map/ppermute | solution.py:608
  69.3 2.7 %collective-permute-done.5 = f32[8,32,128]{2,1,0:T(8,128)S(1)} collective-permute-done((f32[8,32,128]{2,1,0:T(8,128)S(1)}, f32[8,32,128]{2,1,0:T(8,128)S(1)}, u32[]{:S(2)}, u32[]{:S(2)}) %collective-permute-start.5) | collective-permute-done | bytes 131104 | tf_op jit(solution)/shard_map/ppermute | solution.py:608
  72.0 4.4 %collective-permute-done.6 = f32[8,32,128]{2,1,0:T(8,128)S(1)} collective-permute-done((f32[8,32,128]{2,1,0:T(8,128)S(1)}, f32[8,32,128]{2,1,0:T(8,128)S(1)}, u32[]{:S(2)}, u32[]{:S(2)}) %collective-permute-start.6) | collective-permute-done | bytes 131104 | tf_op jit(solution)/shard_map/ppermute | solution.py:608
  76.4 4.4 %collective-permute-start.10 = (f32[8,32,128]{2,1,0:T(8,128)S(1)}, f32[8,32,128]{2,1,0:T(8,128)S(1)}, u32[]{:S(2)}, u32[]{:S(2)}) collective-permute-start(f32[8,32,128]{2,1,0:T(8,128)S(1)} %add_add_fusion.1.refs_4_), channel_id=1, source_target_pairs={{0,3},{1,0},{2,1},{3,2},{4,7},{5,4},{6,5},{7,6},{8,11},{9,8},{10,9... | collective-permute-start | bytes 393224 | tf_op jit(solution)/shard_map/ppermute | solution.py:609
  81.5 3.3 %collective-permute-done.10.refs_7_ = f32[8,32,128]{2,1,0:T(8,128)S(1)} collective-permute-done((f32[8,32,128]{2,1,0:T(8,128)S(1)}, f32[8,32,128]{2,1,0:T(8,128)S(1)}, u32[]{:S(2)}, u32[]{:S(2)}) %collective-permute-start.10) | collective-permute-done | bytes 131104 | tf_op jit(solution)/shard_map/ppermute | solution.py:609
  84.8 8.3 %collective-permute-done.9.refs_6_ = f32[8,32,128]{2,1,0:T(8,128)S(1)} collective-permute-done((f32[8,32,128]{2,1,0:T(8,128)S(1)}, f32[8,32,128]{2,1,0:T(8,128)S(1)}, u32[]{:S(2)}, u32[]{:S(2)}) %collective-permute-start.9) | collective-permute-done | bytes 131104 | tf_op jit(solution)/shard_map/ppermute | solution.py:609
  93.1 21.3 %stencil.1 = (f32[8,8,256]{2,1,0:T(8,128)S(1)}, f32[8,32,128]{2,1,0:T(8,128)S(1)}, f32[8,32,128]{2,1,0:T(8,128)S(1)}, f32[8,32,128]{2,1,0:T(8,128)S(1)}, f32[8,32,128]{2,1,0:T(8,128)S(1)}) custom-call(s32[4]{0:T(128)S(1)} %pad_add_fusion.1.refs_0_, s32[4]{0:T(128)S(1)} %pad_add_fusion.refs_1_.refs_0_, s32[64]{0:T(128)S(1)} %get-tuple-element.42.refs_2_, ...), custom_call_target="tpu_custom_call" | custom-call | flops 17179869184 | bytes 1048576 | tf_op jit(solution)/shard_map/stencil/pallas_call | solution.py:256
  114.4 2.5 %collective-permute-start.11 = (f32[8,32,128]{2,1,0:T(8,128)S(1)}, f32[8,32,128]{2,1,0:T(8,128)S(1)}, u32[]{:S(2)}, u32[]{:S(2)}) collective-permute-start(f32[8,32,128]{2,1,0:T(8,128)S(1)} %get-tuple-element.27), channel_id=1, source_target_pairs={{0,1},{1,2},{2,3},{3,0},{4,5},{5,6},{6,7},{7,4},{8,9},{9,10},{10,1... | collective-permute-start | bytes 393224 | tf_op jit(solution)/shard_map/ppermute | solution.py:608
  116.8 3.5 %collective-permute-start.12 = (f32[8,32,128]{2,1,0:T(8,128)S(1)}, f32[8,32,128]{2,1,0:T(8,128)S(1)}, u32[]{:S(2)}, u32[]{:S(2)}) collective-permute-start(f32[8,32,128]{2,1,0:T(8,128)S(1)} %get-tuple-element.28), channel_id=1, source_target_pairs={{0,2},{1,3},{2,0},{3,1},{4,6},{5,7},{6,4},{7,5},{8,10},{9,11},{10,... | collective-permute-start | bytes 393224 | tf_op jit(solution)/shard_map/ppermute | solution.py:608
  120.4 2.8 %collective-permute-start.13 = (f32[8,32,128]{2,1,0:T(8,128)S(1)}, f32[8,32,128]{2,1,0:T(8,128)S(1)}, u32[]{:S(2)}, u32[]{:S(2)}) collective-permute-start(f32[8,32,128]{2,1,0:T(8,128)S(1)} %get-tuple-element.29), channel_id=1, source_target_pairs={{0,3},{1,0},{2,1},{3,2},{4,7},{5,4},{6,5},{7,6},{8,11},{9,8},{10,9... | collective-permute-start | bytes 393224 | tf_op jit(solution)/shard_map/ppermute | solution.py:608
  123.3 2.4 %collective-permute-done.13 = f32[8,32,128]{2,1,0:T(8,128)S(1)} collective-permute-done((f32[8,32,128]{2,1,0:T(8,128)S(1)}, f32[8,32,128]{2,1,0:T(8,128)S(1)}, u32[]{:S(2)}, u32[]{:S(2)}) %collective-permute-start.13) | collective-permute-done | bytes 131104 | tf_op jit(solution)/shard_map/ppermute | solution.py:608
  125.8 4.9 %collective-permute-start.16 = (f32[8,32,128]{2,1,0:T(8,128)S(1)}, f32[8,32,128]{2,1,0:T(8,128)S(1)}, u32[]{:S(2)}, u32[]{:S(2)}) collective-permute-start(f32[8,32,128]{2,1,0:T(8,128)S(1)} %add_add_fusion.refs_1_), channel_id=1, source_target_pairs={{0,3},{1,0},{2,1},{3,2},{4,7},{5,4},{6,5},{7,6},{8,11},{9,8},{10,9... | collective-permute-start | bytes 393224 | tf_op jit(solution)/shard_map/ppermute | solution.py:609
  133.2 5.1 %collective-permute-done.15.refs_3_ = f32[8,32,128]{2,1,0:T(8,128)S(1)} collective-permute-done((f32[8,32,128]{2,1,0:T(8,128)S(1)}, f32[8,32,128]{2,1,0:T(8,128)S(1)}, u32[]{:S(2)}, u32[]{:S(2)}) %collective-permute-start.15) | collective-permute-done | bytes 131104 | tf_op jit(solution)/shard_map/ppermute | solution.py:609
  138.4 20.2 %backward.1 = (f32[32,32,128]{2,1,0:T(8,128)}, f32[8,32,640]{2,1,0:T(8,128)S(1)}, f32[8,32,640]{2,1,0:T(8,128)S(1)}, f32[32,640]{1,0:T(8,128)}, f32[32,640]{1,0:...) custom-call(s32[4]{0:T(128)S(1)} %pad_add_fusion.refs_1_.refs_0_, f32[8,32,128]{2,1,0:T(8,128)S(1)} %add_add_fusion.refs_1_, ...), custom_call_target="tpu_custom_call" | custom-call | flops 8589934592 | bytes 8388608 | tf_op jit(solution)/shard_map/backward/pallas_call | solution.py:568
  158.6 6.8 %collective-permute-start.17 = (f32[8,32,640]{2,1,0:T(8,128)S(1)}, f32[8,32,640]{2,1,0:T(8,128)S(1)}, u32[]{:S(2)}, u32[]{:S(2)}) collective-permute-start(f32[8,32,640]{2,1,0:T(8,128)S(1)} %get-tuple-element.31), channel_id=1, source_target_pairs={{0,16},{4,20},{8,24},{12,28},{16,0},{20,4},{24,8},{28,12},{1,17},{... | collective-permute-start | bytes 1966088 | tf_op jit(solution)/shard_map/ppermute | solution.py:495
  165.3 2.2 %collective-permute-start.19 = (f32[40,640]{1,0:T(8,128)}, f32[40,640]{1,0:T(8,128)S(1)}, u32[]{:S(2)}, u32[]{:S(2)}) collective-permute-start(f32[40,640]{1,0:T(8,128)} %get-tuple-element.33), channel_id=1, source_target_pairs={{0,20},{4,24},{8,28},{12,16},{16,4},{20,8},{24,12},{28,0},{1,21},{... | collective-permute-start | bytes 307208 | tf_op jit(solution)/shard_map/ppermute | solution.py:495
  169.3 18.4 %all_to_all.10 = f32[8,8,256]{2,1,0:T(8,128)} all-to-all(f32[8,8,256]{2,1,0:T(8,128)S(1)} %get-tuple-element.38), channel_id=1, replica_groups=mesh['tx'=2,'ty'=4,'mem'=4] {'tx','ty'}, dimensions={0} | all-to-all | bytes 131072 | tf_op jit(solution)/shard_map/all_to_all | solution.py:642
  187.7 8.5 %unpack.1 = f32[64,128]{1,0:T(8,128)} custom-call(s32[64,128]{1,0:T(8,128)} %copy-done.1, f32[64,256]{1,0:T(8,128)} %bitcast.19), custom_call_target="tpu_custom_call" | custom-call | flops 16777216 | bytes 262144 | tf_op jit(solution)/shard_map/unpack/pallas_call | solution.py:293
  (84 shorter events, 23.9 us)
Async XLA Ops:
  1.6 39.5 %collective-permute-start.2 = (f32[32,640]{1,0:T(8,128)S(1)}, f32[32,640]{1,0:T(8,128)S(1)}, u32[]{:S(2)}, u32[]{:S(2)}) collective-permute-start(f32[32,640]{1,0:T(8,128)S(1)} %reshape.46), channel_id=1, source_target_pairs={{0,20},{4,24},{8,28},{12,16},{16,4},{20,8},{24,12},{28,0},{1,21},{... | collective-permute-start | bytes 245768 | tf_op jit(solution)/shard_map/ppermute | solution.py:495
  4.0 37.7 %collective-permute-start.1 = (f32[32,640]{1,0:T(8,128)S(1)}, f32[32,640]{1,0:T(8,128)S(1)}, u32[]{:S(2)}, u32[]{:S(2)}) collective-permute-start(f32[32,640]{1,0:T(8,128)S(1)} %reshape.46), channel_id=1, source_target_pairs={{0,4},{4,8},{8,12},{12,0},{16,20},{20,24},{24,28},{28,16},{1,5},{5... | collective-permute-start | bytes 245768 | tf_op jit(solution)/shard_map/ppermute | solution.py:495
  6.6 35.8 %collective-permute-start.4 = (f32[40,640]{1,0:T(8,128)S(1)}, f32[40,640]{1,0:T(8,128)S(1)}, u32[]{:S(2)}, u32[]{:S(2)}) collective-permute-start(f32[40,640]{1,0:T(8,128)S(1)} %reshape.47), channel_id=1, source_target_pairs={{0,28},{4,16},{8,20},{12,24},{16,12},{20,0},{24,4},{28,8},{1,29},{... | collective-permute-start | bytes 307208 | tf_op jit(solution)/shard_map/ppermute | solution.py:495
  6.9 35.5 %collective-permute-start.3 = (f32[40,640]{1,0:T(8,128)S(1)}, f32[40,640]{1,0:T(8,128)S(1)}, u32[]{:S(2)}, u32[]{:S(2)}) collective-permute-start(f32[40,640]{1,0:T(8,128)S(1)} %reshape.47), channel_id=1, source_target_pairs={{0,12},{4,0},{8,4},{12,8},{16,28},{20,16},{24,20},{28,24},{1,13},{... | collective-permute-start | bytes 307208 | tf_op jit(solution)/shard_map/ppermute | solution.py:495
  6.9 36.1 %collective-permute-start = (f32[8,32,640]{2,1,0:T(8,128)}, f32[8,32,640]{2,1,0:T(8,128)S(1)}, u32[]{:S(2)}, u32[]{:S(2)}) collective-permute-start(f32[8,32,640]{2,1,0:T(8,128)} %alpha_ref.1), channel_id=1, source_target_pairs={{0,16},{4,20},{8,24},{12,28},{16,0},{20,4},{24,8},{28,12},{1,17},{... | collective-permute-start | bytes 1966088 | tf_op jit(solution)/shard_map/ppermute | solution.py:495
  29.7 10.9 %all-to-all-start = ((f32[8,48,256]{2,1,0:T(8,128)}), f32[8,48,256]{2,1,0:T(8,128)S(1)}, u32[]{:S(2)}, u32[]{:S(2)}) async-start(f32[8,48,256]{2,1,0:T(8,128)} %get-tuple-element.21), calls=%async_computation | async-start | bytes 786432 | tf_op jit(solution)/shard_map/all_to_all | solution.py:640
  41.1 52.0 %copy-start.2 = (f32[32,32,128]{2,1,0:T(8,128)S(1)}, f32[32,32,128]{2,1,0:T(8,128)}, u32[]{:S(2)}) copy-start(f32[32,32,128]{2,1,0:T(8,128)} %refs_6_.1) | copy-start | bytes 1572868
  63.7 8.3 %collective-permute-start.5 = (f32[8,32,128]{2,1,0:T(8,128)S(1)}, f32[8,32,128]{2,1,0:T(8,128)S(1)}, u32[]{:S(2)}, u32[]{:S(2)}) collective-permute-start(f32[8,32,128]{2,1,0:T(8,128)S(1)} %get-tuple-element.23), channel_id=1, source_target_pairs={{0,1},{1,2},{2,3},{3,0},{4,5},{5,6},{6,7},{7,4},{8,9},{9,10},{10,1... | collective-permute-start | bytes 393224 | tf_op jit(solution)/shard_map/ppermute | solution.py:608
  65.3 11.1 %collective-permute-start.6 = (f32[8,32,128]{2,1,0:T(8,128)S(1)}, f32[8,32,128]{2,1,0:T(8,128)S(1)}, u32[]{:S(2)}, u32[]{:S(2)}) collective-permute-start(f32[8,32,128]{2,1,0:T(8,128)S(1)} %get-tuple-element.24), channel_id=1, source_target_pairs={{0,2},{1,3},{2,0},{3,1},{4,6},{5,7},{6,4},{7,5},{8,10},{9,11},{10,... | collective-permute-start | bytes 393224 | tf_op jit(solution)/shard_map/ppermute | solution.py:608
  67.9 8.5 %collective-permute-start.7 = (f32[8,32,128]{2,1,0:T(8,128)S(1)}, f32[8,32,128]{2,1,0:T(8,128)S(1)}, u32[]{:S(2)}, u32[]{:S(2)}) collective-permute-start(f32[8,32,128]{2,1,0:T(8,128)S(1)} %get-tuple-element.25), channel_id=1, source_target_pairs={{0,3},{1,0},{2,1},{3,2},{4,7},{5,4},{6,5},{7,6},{8,11},{9,8},{10,9... | collective-permute-start | bytes 393224 | tf_op jit(solution)/shard_map/ppermute | solution.py:608
  76.4 8.3 %collective-permute-start.10 = (f32[8,32,128]{2,1,0:T(8,128)S(1)}, f32[8,32,128]{2,1,0:T(8,128)S(1)}, u32[]{:S(2)}, u32[]{:S(2)}) collective-permute-start(f32[8,32,128]{2,1,0:T(8,128)S(1)} %add_add_fusion.1.refs_4_), channel_id=1, source_target_pairs={{0,3},{1,0},{2,1},{3,2},{4,7},{5,4},{6,5},{7,6},{8,11},{9,8},{10,9... | collective-permute-start | bytes 393224 | tf_op jit(solution)/shard_map/ppermute | solution.py:609
  80.8 12.2 %collective-permute-start.9 = (f32[8,32,128]{2,1,0:T(8,128)S(1)}, f32[8,32,128]{2,1,0:T(8,128)S(1)}, u32[]{:S(2)}, u32[]{:S(2)}) collective-permute-start(f32[8,32,128]{2,1,0:T(8,128)S(1)} %add_add_fusion.1.refs_4_), channel_id=1, source_target_pairs={{0,2},{1,3},{2,0},{3,1},{4,6},{5,7},{6,4},{7,5},{8,10},{9,11},{10,... | collective-permute-start | bytes 393224 | tf_op jit(solution)/shard_map/ppermute | solution.py:609
  81.2 11.8 %collective-permute-start.8 = (f32[8,32,128]{2,1,0:T(8,128)S(1)}, f32[8,32,128]{2,1,0:T(8,128)S(1)}, u32[]{:S(2)}, u32[]{:S(2)}) collective-permute-start(f32[8,32,128]{2,1,0:T(8,128)S(1)} %add_add_fusion.1.refs_4_), channel_id=1, source_target_pairs={{0,1},{1,2},{2,3},{3,0},{4,5},{5,6},{6,7},{7,4},{8,9},{9,10},{10,1... | collective-permute-start | bytes 393224 | tf_op jit(solution)/shard_map/ppermute | solution.py:609
  114.4 8.8 %collective-permute-start.11 = (f32[8,32,128]{2,1,0:T(8,128)S(1)}, f32[8,32,128]{2,1,0:T(8,128)S(1)}, u32[]{:S(2)}, u32[]{:S(2)}) collective-permute-start(f32[8,32,128]{2,1,0:T(8,128)S(1)} %get-tuple-element.27), channel_id=1, source_target_pairs={{0,1},{1,2},{2,3},{3,0},{4,5},{5,6},{6,7},{7,4},{8,9},{9,10},{10,1... | collective-permute-start | bytes 393224 | tf_op jit(solution)/shard_map/ppermute | solution.py:608
  116.8 6.5 %collective-permute-start.12 = (f32[8,32,128]{2,1,0:T(8,128)S(1)}, f32[8,32,128]{2,1,0:T(8,128)S(1)}, u32[]{:S(2)}, u32[]{:S(2)}) collective-permute-start(f32[8,32,128]{2,1,0:T(8,128)S(1)} %get-tuple-element.28), channel_id=1, source_target_pairs={{0,2},{1,3},{2,0},{3,1},{4,6},{5,7},{6,4},{7,5},{8,10},{9,11},{10,... | collective-permute-start | bytes 393224 | tf_op jit(solution)/shard_map/ppermute | solution.py:608
  120.4 5.4 %collective-permute-start.13 = (f32[8,32,128]{2,1,0:T(8,128)S(1)}, f32[8,32,128]{2,1,0:T(8,128)S(1)}, u32[]{:S(2)}, u32[]{:S(2)}) collective-permute-start(f32[8,32,128]{2,1,0:T(8,128)S(1)} %get-tuple-element.29), channel_id=1, source_target_pairs={{0,3},{1,0},{2,1},{3,2},{4,7},{5,4},{6,5},{7,6},{8,11},{9,8},{10,9... | collective-permute-start | bytes 393224 | tf_op jit(solution)/shard_map/ppermute | solution.py:608
  125.8 7.4 %collective-permute-start.16 = (f32[8,32,128]{2,1,0:T(8,128)S(1)}, f32[8,32,128]{2,1,0:T(8,128)S(1)}, u32[]{:S(2)}, u32[]{:S(2)}) collective-permute-start(f32[8,32,128]{2,1,0:T(8,128)S(1)} %add_add_fusion.refs_1_), channel_id=1, source_target_pairs={{0,3},{1,0},{2,1},{3,2},{4,7},{5,4},{6,5},{7,6},{8,11},{9,8},{10,9... | collective-permute-start | bytes 393224 | tf_op jit(solution)/shard_map/ppermute | solution.py:609
  130.7 7.7 %collective-permute-start.15 = (f32[8,32,128]{2,1,0:T(8,128)S(1)}, f32[8,32,128]{2,1,0:T(8,128)S(1)}, u32[]{:S(2)}, u32[]{:S(2)}) collective-permute-start(f32[8,32,128]{2,1,0:T(8,128)S(1)} %add_add_fusion.refs_1_), channel_id=1, source_target_pairs={{0,2},{1,3},{2,0},{3,1},{4,6},{5,7},{6,4},{7,5},{8,10},{9,11},{10,... | collective-permute-start | bytes 393224 | tf_op jit(solution)/shard_map/ppermute | solution.py:609
  130.7 7.7 %collective-permute-start.14 = (f32[8,32,128]{2,1,0:T(8,128)S(1)}, f32[8,32,128]{2,1,0:T(8,128)S(1)}, u32[]{:S(2)}, u32[]{:S(2)}) collective-permute-start(f32[8,32,128]{2,1,0:T(8,128)S(1)} %add_add_fusion.refs_1_), channel_id=1, source_target_pairs={{0,1},{1,2},{2,3},{3,0},{4,5},{5,6},{6,7},{7,4},{8,9},{9,10},{10,1... | collective-permute-start | bytes 393224 | tf_op jit(solution)/shard_map/ppermute | solution.py:609
  158.6 37.7 %collective-permute-start.17 = (f32[8,32,640]{2,1,0:T(8,128)S(1)}, f32[8,32,640]{2,1,0:T(8,128)S(1)}, u32[]{:S(2)}, u32[]{:S(2)}) collective-permute-start(f32[8,32,640]{2,1,0:T(8,128)S(1)} %get-tuple-element.31), channel_id=1, source_target_pairs={{0,16},{4,20},{8,24},{12,28},{16,0},{20,4},{24,8},{28,12},{1,17},{... | collective-permute-start | bytes 1966088 | tf_op jit(solution)/shard_map/ppermute | solution.py:495
  165.3 30.9 %collective-permute-start.19 = (f32[40,640]{1,0:T(8,128)}, f32[40,640]{1,0:T(8,128)S(1)}, u32[]{:S(2)}, u32[]{:S(2)}) collective-permute-start(f32[40,640]{1,0:T(8,128)} %get-tuple-element.33), channel_id=1, source_target_pairs={{0,20},{4,24},{8,28},{12,16},{16,4},{20,8},{24,12},{28,0},{1,21},{... | collective-permute-start | bytes 307208 | tf_op jit(solution)/shard_map/ppermute | solution.py:495
  167.6 28.7 %collective-permute-start.21 = (f32[40,640]{1,0:T(8,128)}, f32[40,640]{1,0:T(8,128)S(1)}, u32[]{:S(2)}, u32[]{:S(2)}) collective-permute-start(f32[40,640]{1,0:T(8,128)} %get-tuple-element.35), channel_id=1, source_target_pairs={{0,4},{4,8},{8,12},{12,0},{16,20},{20,24},{24,28},{28,16},{1,5},{5... | collective-permute-start | bytes 307208 | tf_op jit(solution)/shard_map/ppermute | solution.py:495
  168.5 27.7 %collective-permute-start.18 = (f32[32,640]{1,0:T(8,128)}, f32[32,640]{1,0:T(8,128)S(1)}, u32[]{:S(2)}, u32[]{:S(2)}) collective-permute-start(f32[32,640]{1,0:T(8,128)} %get-tuple-element.32), channel_id=1, source_target_pairs={{0,28},{4,16},{8,20},{12,24},{16,12},{20,0},{24,4},{28,8},{1,29},{... | collective-permute-start | bytes 245768 | tf_op jit(solution)/shard_map/ppermute | solution.py:495
  169.1 27.2 %collective-permute-start.20 = (f32[32,640]{1,0:T(8,128)}, f32[32,640]{1,0:T(8,128)S(1)}, u32[]{:S(2)}, u32[]{:S(2)}) collective-permute-start(f32[32,640]{1,0:T(8,128)} %get-tuple-element.34), channel_id=1, source_target_pairs={{0,12},{4,0},{8,4},{12,8},{16,28},{20,16},{24,20},{28,24},{1,13},{... | collective-permute-start | bytes 245768 | tf_op jit(solution)/shard_map/ppermute | solution.py:495
  (18 other events, 173.7 us)
where the time goes:
time: 199 us; the launch traced here: 197 us
  Pallas kernels  83.8 us (42%)
  starting transfers between devices  45.5 us (23%)
  waiting for transfers between devices  35.1 us (18%)
  blocking collectives  18.4 us (9%)
  local copies, waits for them, and re-layouts  12.2 us (6%)
    pallas_call x1, Pallas kernels, stencil(): pl.pallas_call(kernel, out_shape=(jax.ShapeDtypeStruct((sources, deep, bl...  21.3 us
    pallas_call x1, Pallas kernels, backward(): pl.pallas_call(kernel, out_shape=tuple((jax.ShapeDtypeStruct(shape, jnp.f...  20.2 us
    ppermute x6, waiting for transfers between devices, shared_sum(): lax.ppermute(total, 'mem', [(i, (i + d) % count) for i in range(count)])  18.6 us
    all_to_all x1, blocking collectives, per_device(): lax.all_to_all(departure, ('tx', 'ty'), split_axis=0, concat_axis=0, tile...  18.4 us
    pallas_call x1, Pallas kernels, ensemble(): pl.pallas_call(kernel, out_shape=tuple((jax.ShapeDtypeStruct((levels // g...  18 us
    ppermute x10, starting transfers between devices, shifted(): return lax.ppermute(value, ('tx', 'ty'), pairs)  17.1 us
    pallas_call x1, Pallas kernels, pack(): pl.pallas_call(functools.partial(pack_kernel, tiles, levels, plane, capac...  14.8 us
    ppermute x6, starting transfers between devices, shared_sum(): lax.ppermute(parts[d], 'mem', [(i, (i + d) % count) for i in range(count)])  14.4 us
  transfers between devices with their start and end apart: 23, of which 9 were waited for; matrix products, arithmetic and copies ran while one was open for 1% of the time, Pallas kernels for 12%

commit v1 on v0

--- a/solution.py
+++ b/solution.py
@@ -1,8 +1,8 @@
 import functools
+import math
 
 import jax
 import jax.numpy as jnp
-import numpy as np
 from jax import lax
 from jax.experimental import pallas as pl
 from jax.experimental.pallas import tpu as pltpu
@@ -13,10 +13,16 @@
 NU = 0.2
 VMEM = pl.BlockSpec(memory_space=pltpu.VMEM)
 SMEM = pl.BlockSpec(memory_space=pltpu.SMEM)
-ROOM = pltpu.CompilerParams(vmem_limit_bytes=48 << 20)
+HBM = pl.BlockSpec(memory_space=pltpu.HBM)
+
+
+def room(mebibytes):
+    return pltpu.CompilerParams(vmem_limit_bytes=mebibytes << 20)
+
 BLOCK = 256
 LANES = 128
-WINDOW = 12
+NARROW = 8
+WIDE = 16
 HALF = jnp.bfloat16
 
 
@@ -39,11 +45,14 @@
 
 def pack_kernel(
     tiles, levels, plane, capacity,
-    count_ref, owner_ref, column_ref, level_ref, frac_ref, innov_ref, rinv_ref,
-    out_ref, target_ref,
-    carry, total, gathered,
+    count_ref, *refs,
 ):
-    blocks = owner_ref.shape[0] * LANES // BLOCK
+    sources, (out_ref, target_ref, carry, total, gathered, *held), sems = refs[:6], refs[6:-1], refs[-1]
+    copies = [pltpu.make_async_copy(source, here, sems.at[i]) for i, (source, here) in enumerate(zip(sources, held))]
+    for copy in copies:
+        copy.start()
+    owner_ref, level_ref, column_ref, frac_ref, innov_ref, rinv_ref = held
+    blocks = target_ref.shape[0] * LANES // BLOCK
     keys = tiles * levels
     deep = capacity // BLOCK
     slot_rows = tiles * deep
@@ -61,13 +70,18 @@
 
     ones = jnp.ones((BLOCK, LANES), HALF)
     total[...] = jnp.zeros_like(total)
-
-    def count_block(j, unused):
-        live, mask = onehot(j)
-        total[...] += dot_nn(jnp.where(mask, 1.0, 0.0).astype(HALF), ones)
+    for copy in copies[:2]:
+        copy.wait()
+
+    def count_group(g, unused):
+        masks = [onehot(g * group + i)[1] for i in range(group)]
+        counted = jnp.concatenate([jnp.where(mask, 1.0, 0.0).astype(HALF) for mask in masks], 1)
+        total[...] += dot_nn(counted, jnp.concatenate([ones] * group, 0))
         return unused
 
-    lax.fori_loop(0, blocks, count_block, 0)
+    lax.fori_loop(0, blocks // group, count_group, 0)
+    for copy in copies[2:]:
+        copy.wait()
     high = jnp.floor(total[...] * (1.0 / LANES))
     low = total[...] - high * LANES
     row_key, col_key = iota((keys, keys), 0), iota((keys, keys), 1)
@@ -124,6 +138,8 @@
     slots = owner.shape[0]
     rows = slots // LANES
     deep = capacity // BLOCK
+    values = [value.reshape(rows, LANES) for value in (owner, level, column)]
+    values += [frac, innov.reshape(rows, LANES), rinv.reshape(rows, LANES)]
     vmem = pl.BlockSpec(memory_space=pltpu.VMEM)
     return pl.pallas_call(
         functools.partial(pack_kernel, tiles, levels, plane, capacity),
@@ -131,125 +147,183 @@
             jax.ShapeDtypeStruct((tiles, 6 * deep, BLOCK), jnp.float32),
             jax.ShapeDtypeStruct((rows, LANES), jnp.int32),
         ),
-        in_specs=[pl.BlockSpec(memory_space=pltpu.SMEM)] + [vmem] * 6,
+        in_specs=[SMEM] + [HBM] * 6,
         out_specs=(vmem, vmem),
         scratch_shapes=[
             pltpu.VMEM((tiles * levels, LANES), jnp.float32),
             pltpu.VMEM((tiles * levels, LANES), jnp.float32),
             pltpu.VMEM((13 * tiles * deep, BLOCK), jnp.float32),
-        ],
-        compiler_params=pltpu.CompilerParams(vmem_limit_bytes=40 << 20),
+        ]
+        + [pltpu.VMEM(value.shape, value.dtype) for value in values]
+        + [pltpu.SemaphoreType.DMA((len(values),))],
+        compiler_params=room(16),
         cost_estimate=pl.CostEstimate(flops=8 << 30, bytes_accessed=1 << 20, transcendentals=0),
         name="pack",
-    )(count, *[a.reshape(rows, LANES) for a in (owner, column, level)], frac,
-      *[a.reshape(rows, LANES) for a in (innov, rinv)])
+    )(count, *values)
 
 
 def stencil_kernel(
-    ahead_ref, behind_ref, first_ref, windows_ref, parts_refs, sigma_ref, static_ref, incoming_ref,
+    me_ref, parts_refs, sigma_ref, static_ref, incoming_ref,
     dep_ref, adj_refs,
-    field_t, row_hi, row_lo, adjoint,
+    field, field_t, adjoint, spans, spans_ref, sem,
 ):
     levels, fine_x, fine_y = sigma_ref.shape
     sources, packed_rows, block = incoming_ref.shape
     deep = packed_rows // 6
     plane = fine_x * fine_y
     chunk = LANES // fine_x
-    share = levels // len(parts_refs)
-    span = WINDOW // chunk
-    width = WINDOW * fine_x
+    groups = len(parts_refs)
+    share = levels // groups
+    rows = levels * fine_x
+    me = me_ref[0]
+    halves = block // LANES
+    column = iota((sources * deep, LANES), 1)
+    found = jnp.zeros((sources * deep, LANES), jnp.int32)
+    for half in range(halves):
+        lanes = slice(half * LANES, (half + 1) * LANES)
+        used = incoming_ref[:, 4 * deep:5 * deep, lanes].reshape(sources * deep, LANES) > 0.0
+        level = jnp.floor(incoming_ref[:, 5 * deep:, lanes].reshape(sources * deep, LANES) * (1.0 / plane))
+        lowest = jnp.min(jnp.where(used, level, float(levels)), 1, keepdims=True).astype(jnp.int32)
+        highest = jnp.max(jnp.where(used, level, -1.0), 1, keepdims=True).astype(jnp.int32)
+        found = jnp.where((column == 2 * half) & (highest >= 0), lowest, found)
+        found = jnp.where((column == 2 * half + 1) & (highest >= 0), highest + 2 - lowest, found)
+    spans[...] = found
+    fetch = pltpu.make_async_copy(spans, spans_ref, sem)
+    fetch.start()
     adjoint[...] = jnp.zeros_like(adjoint)
     dep_ref[...] = jnp.zeros_like(dep_ref)
-    field_t[:, levels * fine_x:] = jnp.zeros((2 * fine_y, width), HALF)
+    field[rows:, :] = jnp.zeros((field.shape[0] - rows, fine_y), jnp.float32)
     for slot, part in enumerate(parts_refs):
-        start = behind_ref[slot] * share
+        start = lax.rem(me + groups - slot, groups) * share
         static = sigma_ref[pl.ds(start, share)] * static_ref[pl.ds(start, share)]
-        turned = (part[...] + static).reshape(share * fine_x, fine_y).T
-        high, low = split_two(turned)
         where = pl.ds(pl.multiple_of(start * fine_x, LANES), share * fine_x)
-        field_t[:fine_y, where] = high
-        field_t[fine_y:, where] = low
-
-    def one_block(q, unused):
-        source, at = q // deep, q % deep
-
+        field[where, :] = (part[...] + static).reshape(share * fine_x, fine_y)
+    for shift in range(chunk):
+        field_t[shift, :, rows:] = jnp.zeros((2 * fine_y, field_t.shape[2] - rows), HALF)
+        for g in range(rows // LANES):
+            begin = shift * fine_x + g * LANES
+            high, low = split_two(field[begin:begin + LANES, :].T)
+            field_t[shift, :fine_y, g * LANES:(g + 1) * LANES] = high
+            field_t[shift, fine_y:, g * LANES:(g + 1) * LANES] = low
+
+    fetch.wait()
+
+    def block_of(source, at, half):
         def row(p):
-            return incoming_ref[source, pl.ds(p * deep + at, 1), :]
-
-        windows = windows_ref[q]
-
-        @pl.when(windows > 0)
+            return incoming_ref[source, pl.ds(p * deep + at, 1), :][:, half * LANES:(half + 1) * LANES]
+
+        base = row(5)
+        level = jnp.floor(base * (1.0 / plane))
+        rest = base - level * plane
+        across = jnp.floor(rest * (1.0 / fine_y))
+        along = rest - across * fine_y
+        frac_x, frac_y, frac_l = row(0), row(1), row(2)
+        rows_x = iota((fine_x, LANES), 0).astype(jnp.float32)
+        pick_x = jnp.where(rows_x == across, 1.0 - frac_x, 0.0) + jnp.where(rows_x == across + 1.0, frac_x, 0.0)
+        rows_y = iota((fine_y, LANES), 0).astype(jnp.float32)
+        pick_y = jnp.where(rows_y == along, 1.0 - frac_y, 0.0) + jnp.where(rows_y == along + 1.0, frac_y, 0.0)
+
+        def weights(bottom, reach):
+            offset = level - bottom.astype(jnp.float32)
+            picks = []
+            for g in range(reach):
+                pick_l = jnp.where(offset == float(g), 1.0 - frac_l, 0.0) + jnp.where(offset == float(g - 1), frac_l, 0.0)
+                picks.append(pick_x * pick_l)
+            return jnp.concatenate(split_two(jnp.concatenate(picks, 0)), 1)
+
+        def finish(picked):
+            departure = jnp.sum(picked * pick_y, 0, keepdims=True) - row(3)
+            turned = jnp.concatenate(split_two((pick_y * (row(4) * departure)).T), 1)
+            return departure, jnp.concatenate([turned, turned], 0)
+
+        return weights, finish
+
+    def look(bottom, pick):
+        lanes = pl.ds(pl.multiple_of((bottom // chunk) * LANES, LANES), pick.shape[0])
+        seen = dot_nn(field_t[lax.rem(bottom, chunk), :, lanes], pick)
+        return seen[:fine_y, :LANES] + (seen[:fine_y, LANES:] + seen[fine_y:, :LANES])
+
+    def spread(pick, term):
+        both = dot_nn(pick, term)
+        return both[:, :fine_y] + both[:, fine_y:]
+
+    def rows_at(bottom, reach):
+        return pl.ds(pl.multiple_of(bottom * fine_x, fine_x), reach * fine_x)
+
+    def together(blocks, bottoms, reach):
+        parts = [block_of(*block) for block in blocks]
+        picks = [weights(bottom, reach) for (weights, finish), bottom in zip(parts, bottoms)]
+        seen = [look(bottom, pick) for bottom, pick in zip(bottoms, picks)]
+        done = [finish(value) for (weights, finish), value in zip(parts, seen)]
+        adds = [spread(pick, term) for pick, (departure, term) in zip(picks, done)]
+        keep(blocks, [departure for departure, term in done])
+        for bottom, add in zip(bottoms, adds):
+            adjoint[rows_at(bottom, reach), :] += add
+
+    def keep(blocks, departures):
+        for i in range(0, len(blocks), halves):
+            source, at, half = blocks[i]
+            dep_ref[source, pl.ds(at, 1), :] = jnp.concatenate(departures[i:i + halves], 1)
+
+    def alone(block, first, needed):
+        weights, finish = block_of(*block)
+        windows = (needed + WIDE - 1) // WIDE
+
+        def forward(w, total):
+            bottom = first + w * WIDE
+            return total + look(bottom, weights(bottom, WIDE))
+
+        departure, term = finish(lax.fori_loop(0, windows, forward, jnp.zeros((fine_y, LANES), jnp.float32)))
+
+        def backward(w, unused):
+            bottom = first + w * WIDE
+            adjoint[rows_at(bottom, WIDE), :] += spread(weights(bottom, WIDE), term)
+            return unused
+
+        lax.fori_loop(0, windows, backward, 0)
+        return departure
+
+    step = 2 if deep % 2 == 0 else 1
+
+    def one_step(i, unused):
+        source, at = i // (deep // step), lax.rem(i, deep // step) * step
+        blocks = [(source, at + r, half) for r in range(step) for half in range(halves)]
+        numbers = [(source * deep + at + r, half) for r in range(step) for half in range(halves)]
+        bottoms = [spans_ref[row, 2 * half] for row, half in numbers]
+        needs = [spans_ref[row, 2 * half + 1] for row, half in numbers]
+        most = functools.reduce(jnp.maximum, needs)
+
+        @pl.when((most > 0) & (most <= NARROW))
         def _():
-            rinv, base = row(4), row(5)
-            level = jnp.floor(base * (1.0 / plane))
-            rest = base - level * plane
-            across = jnp.floor(rest * (1.0 / fine_y))
-            along = rest - across * fine_y
-            frac_x, frac_y, frac_l = row(0), row(1), row(2)
-            first = first_ref[q]
-            rows_x = iota((fine_x, block), 0).astype(jnp.float32)
-            pick_x = jnp.where(rows_x == across, 1.0 - frac_x, 0.0) + jnp.where(rows_x == across + 1.0, frac_x, 0.0)
-
-            def at_window(w):
-                return pl.ds(pl.multiple_of((first + w * span) * LANES, LANES), width)
-
-            def forward(w, acc):
-                bottom = ((first + w * span) * chunk).astype(jnp.float32)
-                offset = level - bottom
-                picks = []
-                for g in range(WINDOW):
-                    pick_l = jnp.where(offset == float(g), 1.0 - frac_l, 0.0) + jnp.where(offset == float(g - 1), frac_l, 0.0)
-                    picks.append(pick_x * pick_l)
-                high, low = split_two(jnp.concatenate(picks, 0))
-                where = at_window(w)
-                row_hi[where, :] = high
-                row_lo[where, :] = low
-                both = field_t[:, where]
-                twice = dot_nn(both, high)
-                return acc + (twice[:fine_y] + twice[fine_y:]) + dot_nn(both[:fine_y], low)
-
-            picked = lax.fori_loop(0, windows, forward, jnp.zeros((fine_y, block), jnp.float32))
-            rows_y = iota((fine_y, block), 0).astype(jnp.float32)
-            pick_y = jnp.where(rows_y == along, 1.0 - frac_y, 0.0) + jnp.where(rows_y == along + 1.0, frac_y, 0.0)
-            departure = jnp.sum(picked * pick_y, 0, keepdims=True) - row(3)
-            dep_ref[source, pl.ds(at, 1), :] = departure
-            high, low = split_two(pick_y * (rinv * departure))
-            both = jnp.concatenate([high, low], 0)
-
-            def backward(w, unused):
-                where = at_window(w)
-                adjoint[where, :] += dot_nt(row_hi[where, :], both)
-                adjoint[where, :fine_y] += dot_nt(row_lo[where, :], high)
-                return unused
-
-            lax.fori_loop(0, windows, backward, 0)
+            together(blocks, bottoms, NARROW)
+
+        @pl.when((most > NARROW) & (most <= WIDE))
+        def _():
+            together(blocks, bottoms, WIDE)
+
+        @pl.when(most > WIDE)
+        def _():
+            keep(blocks, [alone(*each) for each in zip(blocks, bottoms, needs)])
 
         return unused
 
-    lax.fori_loop(0, sources * deep, one_block, 0)
+    lax.fori_loop(0, sources * deep // step, one_step, 0)
     for slot, adj_ref in enumerate(adj_refs):
-        rows = pl.ds(pl.multiple_of(ahead_ref[slot] * share * fine_x, LANES), share * fine_x)
-        both = adjoint[rows, :]
-        adj_ref[...] = (both[:, :fine_y] + both[:, fine_y:]).reshape(share, fine_x, fine_y)
-
-
-def stencil(parts, incoming, bg_sigma, static_ctrl, ahead, behind):
+        start = lax.rem(me + slot, groups) * share * fine_x
+        adj_ref[...] = adjoint[pl.ds(pl.multiple_of(start, LANES), share * fine_x), :].reshape(share, fine_x, fine_y)
+
+
+def stencil(parts, incoming, bg_sigma, static_ctrl, me):
     levels, fine_x, fine_y = bg_sigma.shape
     sources, packed_rows, block = incoming.shape
     deep, groups = packed_rows // 6, len(parts)
-    rows = levels * fine_x + WINDOW * fine_x
-    chunk = LANES // fine_x
-    level = (incoming[:, 5 * deep:] * (1.0 / (fine_x * fine_y))).astype(jnp.int32)
-    used = incoming[:, 4 * deep:5 * deep] > 0.0
-    lowest = jnp.min(jnp.where(used, level, levels), 2).reshape(-1)
-    highest = jnp.max(jnp.where(used, level, -1), 2).reshape(-1)
-    first = lowest // chunk
-    windows = jnp.where(highest >= 0, ((highest + 1) // chunk - first) // (WINDOW // chunk) + 1, 0)
+    rows = levels * fine_x
+    padded = rows + WIDE * fine_x
 
     def kernel(*refs):
-        parts_end = 4 + groups
+        parts_end = 1 + groups
         stencil_kernel(
-            *refs[:4], refs[4:parts_end], *refs[parts_end:parts_end + 4],
+            refs[0], refs[1:parts_end], *refs[parts_end:parts_end + 4],
             refs[parts_end + 4:parts_end + 4 + groups], *refs[parts_end + 4 + groups:]
         )
 
@@ -257,35 +331,42 @@
         kernel,
         out_shape=(jax.ShapeDtypeStruct((sources, deep, block), jnp.float32),)
         + tuple(jax.ShapeDtypeStruct(part.shape, jnp.float32) for part in parts),
-        in_specs=[SMEM] * 4 + [VMEM] * (groups + 3),
+        in_specs=[SMEM] + [VMEM] * (groups + 3),
         out_specs=(VMEM,) * (1 + groups),
         scratch_shapes=[
-            pltpu.VMEM((2 * fine_y, rows), HALF),
-            pltpu.VMEM((rows, block), HALF),
-            pltpu.VMEM((rows, block), HALF),
-            pltpu.VMEM((rows, 2 * fine_y), jnp.float32),
+            pltpu.VMEM((padded, fine_y), jnp.float32),
+            pltpu.VMEM((LANES // fine_x, 2 * fine_y, padded), HALF),
+            pltpu.VMEM((padded, fine_y), jnp.float32),
+            pltpu.VMEM((sources * deep, LANES), jnp.int32),
+            pltpu.SMEM((sources * deep, LANES), jnp.int32),
+            pltpu.SemaphoreType.DMA,
         ],
-        compiler_params=ROOM,
+        compiler_params=room(20),
         cost_estimate=pl.CostEstimate(flops=16 << 30, bytes_accessed=1 << 20, transcendentals=0),
         name="stencil",
-    )(ahead, behind, first, windows, *parts, bg_sigma, static_ctrl, incoming)
+    )(me, *parts, bg_sigma, static_ctrl, incoming)
     return results[0], results[1:]
 
 
 def unpack_kernel(target_ref, table_ref, out_ref):
-    rows = target_ref.shape[0]
-    target = target_ref[...]
-    wanted, lane = target >> 7, target & (LANES - 1)
-
-    def one_row(r, found):
-        pair = table_ref[pl.ds(r, 1), :]
-        for h in range(BLOCK // LANES):
-            line = jnp.broadcast_to(pair[:, h * LANES:(h + 1) * LANES], (rows, LANES))
-            value = jnp.take_along_axis(line, lane, axis=1, mode="promise_in_bounds")
-            found = jnp.where(wanted == r * (BLOCK // LANES) + h, value, found)
-        return found
-
-    out_ref[...] = lax.fori_loop(0, table_ref.shape[0], one_row, jnp.zeros((rows, LANES), jnp.float32))
+    slot_rows = table_ref.shape[0]
+    high, low = split_two(table_ref[...])
+    both = jnp.concatenate([high.astype(jnp.float32), low.astype(jnp.float32)], 0)
+    turned = both.T.astype(HALF)
+    group = 4
+
+    def some_blocks(g, unused):
+        for i in range(group):
+            pair = target_ref[pl.ds(2 * (g * group + i), 2), :]
+            target = jnp.concatenate([pair[0:1], pair[1:2]], 1)
+            rows = jnp.where(iota((slot_rows, BLOCK), 0) == (target >> 8), 1.0, 0.0).astype(HALF)
+            lines = dot_nn(turned, jnp.concatenate([rows, rows], 0))
+            lane = iota((BLOCK, BLOCK), 0) == (target & (BLOCK - 1))
+            found = jnp.sum(jnp.where(lane, lines, 0.0), 0, keepdims=True)
+            out_ref[pl.ds(2 * (g * group + i), 2), :] = jnp.concatenate([found[:, :LANES], found[:, LANES:]], 0)
+        return unused
+
+    lax.fori_loop(0, target_ref.shape[0] // (2 * group), some_blocks, 0)
 
 
 def unpack(target, table):
@@ -295,7 +376,8 @@
         out_shape=jax.ShapeDtypeStruct(target.shape, jnp.float32),
         in_specs=[vmem, vmem],
         out_specs=vmem,
-        cost_estimate=pl.CostEstimate(flops=16 << 20, bytes_accessed=1 << 18, transcendentals=0),
+        compiler_params=room(8),
+        cost_estimate=pl.CostEstimate(flops=2 << 30, bytes_accessed=1 << 18, transcendentals=0),
         name="unpack",
     )(target, table).reshape(-1)
 
@@ -326,6 +408,17 @@
     return jnp.where(fine // fine_x == coarse % EDGE, weight, 0.0).astype(HALF)
 
 
+def mixing(mix_ref):
+    levels = mix_ref.shape[0]
+    tile = jnp.where(iota((LANES, levels), 0) % levels == iota((LANES, levels), 1), 1.0, 0.0).astype(HALF)
+    same = iota((LANES, LANES), 0) // levels == iota((LANES, LANES), 1) // levels
+    terms = []
+    for term in split_two(mix_ref[...]):
+        tiled = dot_nt(dot_nn(tile, term).astype(HALF), tile)
+        terms.append(jnp.where(same, tiled, 0.0).astype(HALF))
+    return terms
+
+
 def neighbours(field):
     width = field.shape[1]
     return pltpu.roll(field, 1, 1) + pltpu.roll(field, width - 1, 1)
@@ -333,7 +426,7 @@
 
 def ensemble_kernel(
     coarse_x, coarse_y, offsets,
-    order_ref, alpha_ref, above_ref, below_ref,
+    me_ref, alpha_ref, above_ref, below_ref,
     left_ref, left_above_ref, left_below_ref, right_ref, right_above_ref, right_below_ref,
     mix_ref, pert_hbm, out_refs, pert_ref, sem, ext, coarse,
 ):
@@ -359,7 +452,7 @@
             ]
     spread_y = interpolation((fine_y, coarse_y + PAD), 0, 1, EDGE)
     spread_y = jnp.concatenate([spread_y.astype(jnp.float32)] * 2, 1).astype(HALF)
-    high, low = split_two(mix_ref[...])
+    high, low = mixing(mix_ref)
     mix = jnp.concatenate([high, high, low], 1)
 
     def one_group(g, unused):
@@ -380,10 +473,11 @@
     depth = coarse_x + 2
     spread_x = interpolation_rows(fine_x, depth, 2, False)
     share = levels // len(out_refs)
+    unroll = math.gcd(members // 2, 5)
 
     for slot, out_ref in enumerate(out_refs):
         for sub in range(share // EDGE):
-            first = pl.multiple_of(order_ref[slot] * share + sub * EDGE, EDGE)
+            first = pl.multiple_of(lax.rem(me_ref[0] + slot, len(out_refs)) * share + sub * EDGE, EDGE)
 
             def stacked(k):
                 rows = pl.ds(pl.multiple_of(k * levels + first, EDGE), EDGE)
@@ -393,49 +487,63 @@
             def perturbation(k):
                 return pert_ref[k, pl.ds(first, EDGE)].reshape(EDGE * fine_x, fine_y).astype(jnp.float32)
 
-            def pair(p, total):
-                high, low = split_two(jnp.concatenate([stacked(2 * p), stacked(2 * p + 1)], 1))
-                fine = dot_nn(spread_x, jnp.concatenate([high, low], 0))
-                return total + fine[:, :fine_y] * perturbation(2 * p) + fine[:, fine_y:] * perturbation(2 * p + 1)
-
-            total = lax.fori_loop(0, members // 2, pair, jnp.zeros((EDGE * fine_x, fine_y), jnp.float32))
+            def pairs(p, total):
+                for i in range(unroll):
+                    k = 2 * (unroll * p + i)
+                    high, low = split_two(jnp.concatenate([stacked(k), stacked(k + 1)], 1))
+                    fine = dot_nn(spread_x, jnp.concatenate([high, low], 0))
+                    total = total + (fine[:, :fine_y] * perturbation(k) + fine[:, fine_y:] * perturbation(k + 1))
+                return total
+
+            total = lax.fori_loop(
+                0, members // (2 * unroll), pairs, jnp.zeros((EDGE * fine_x, fine_y), jnp.float32)
+            )
             out_ref[sub * EDGE:(sub + 1) * EDGE] = total.reshape(EDGE, fine_x, fine_y)
 
 
 def backward_kernel(
     coarse_x, coarse_y, joined,
-    order_ref, parts_refs, mix_ref, sigma_ref, static_ref, pert_ref,
+    me_ref, parts_refs, mix_ref, sigma_ref, static_ref, pert_hbm,
     grad_ref, center_ref, middle_refs, left_refs, right_refs,
-    adjoint, coarse,
+    adjoint, coarse, pert_ref, sems,
 ):
     members, levels, fine_x, fine_y = pert_ref.shape
     channels = members * levels
+    unroll = members // sems.shape[0]
+    copies = []
+    for p in range(sems.shape[0]):
+        some = pl.ds(p * unroll, unroll)
+        copies.append(pltpu.make_async_copy(pert_hbm.at[some], pert_ref.at[some], sems.at[p]))
+        copies[p].start()
     share = levels // len(parts_refs)
     for slot, part in enumerate(parts_refs):
-        first = order_ref[slot] * share
+        first = lax.rem(me_ref[0] + len(parts_refs) - slot, len(parts_refs)) * share
         adjoint[pl.ds(first, share)] = part[...]
     grad_ref[...] = static_ref[...] + sigma_ref[...] * adjoint[...]
     depth = coarse_x + 2
     fold_x = interpolation_rows(fine_x, depth, 1, True)
 
-    for group in range(levels // EDGE):
-        field = adjoint[group * EDGE:(group + 1) * EDGE].reshape(EDGE * fine_x, fine_y)
-
-        def member(k, unused):
-            scaled = pert_ref[k, group * EDGE:(group + 1) * EDGE].reshape(EDGE * fine_x, fine_y).astype(jnp.float32)
-            high, low = split_two(scaled * field)
-            both = dot_nn(fold_x, jnp.concatenate([high, low], 1))
-            rows = pl.ds(pl.multiple_of(k * levels + group * EDGE, EDGE), EDGE)
-            for c in range(coarse_x + 1):
-                piece = both[c * EDGE:(c + 1) * EDGE]
-                coarse[c, rows, :] = piece[:, :fine_y] + piece[:, fine_y:]
+    for p, copy in enumerate(copies):
+        copy.wait()
+
+        def one_level_group(group, unused):
+            some = pl.ds(group * EDGE, EDGE)
+            field = adjoint[some].reshape(EDGE * fine_x, fine_y)
+            for k in range(p * unroll, (p + 1) * unroll):
+                scaled = pert_ref[k, some].reshape(EDGE * fine_x, fine_y).astype(jnp.float32)
+                high, low = split_two(scaled * field)
+                both = dot_nn(fold_x, jnp.concatenate([high, low], 1))
+                rows = pl.ds(pl.multiple_of(k * levels + group * EDGE, EDGE), EDGE)
+                for c in range(coarse_x + 1):
+                    piece = both[c * EDGE:(c + 1) * EDGE]
+                    coarse[c, rows, :] = piece[:, :fine_y] + piece[:, fine_y:]
             return unused
 
-        lax.fori_loop(0, members, member, 0)
+        lax.fori_loop(0, levels // EDGE, one_level_group, 0)
 
     fold_y = interpolation((coarse_y + PAD, fine_y), 1, 0, EDGE)
     fold_y = jnp.concatenate([fold_y, fold_y], 1)
-    high, low = split_two(mix_ref[...])
+    high, low = mixing(mix_ref)
     mix = jnp.concatenate([high, high, low], 0)
 
     def one_group(g, unused):
@@ -495,7 +603,7 @@
     return lax.ppermute(value, ("tx", "ty"), pairs)
 
 
-def ensemble(alpha, mix, ens_pert, order):
+def ensemble(alpha, mix, ens_pert, me, beside):
     coarse_x, coarse_y, channels = alpha.shape
     members, levels, fine_x, fine_y = ens_pert.shape
     joined = lax.axis_size("tx") == 2
@@ -519,15 +627,16 @@
         right_above, right_below = shifted(flat(starts[last]), 1, -1), shifted(flat(starts[first]), -1, -1)
         offsets = (0, 0)
     left, right = shifted(flat(ends), 0, 1), shifted(flat(starts), 0, -1)
-    groups = order.shape[0]
+    left, beside = lax.optimization_barrier((left, beside))
+    groups = lax.axis_size("mem")
 
     def kernel(*refs):
         ensemble_kernel(coarse_x, coarse_y, offsets, *refs[:12], refs[12:12 + groups], *refs[12 + groups:])
 
-    return pl.pallas_call(
+    parts = pl.pallas_call(
         kernel,
         out_shape=tuple(jax.ShapeDtypeStruct((levels // groups, fine_x, fine_y), jnp.float32) for _ in range(groups)),
-        in_specs=[SMEM] + [VMEM] * 10 + [pl.BlockSpec(memory_space=pl.ANY)],
+        in_specs=[SMEM] + [VMEM] * 10 + [HBM],
         out_specs=(VMEM,) * groups,
         scratch_shapes=[
             pltpu.VMEM(ens_pert.shape, ens_pert.dtype),
@@ -535,13 +644,14 @@
             pltpu.VMEM((coarse_x + 2 * REACH + 1, coarse_y + PAD, channels), jnp.float32),
             pltpu.VMEM((coarse_x + 1, channels, fine_y), jnp.float32),
         ],
-        compiler_params=ROOM,
+        compiler_params=room(50),
         cost_estimate=pl.CostEstimate(flops=8 << 30, bytes_accessed=8 << 20, transcendentals=0),
         name="ensemble",
-    )(order, alpha, above, below, left, left_above, left_below, right, right_above, right_below, mix, ens_pert)
-
-
-def backward(alpha, adjoint_parts, mix, bg_sigma, static_ctrl, ens_pert, order):
+    )(me, alpha, above, below, left, left_above, left_below, right, right_above, right_below, mix, ens_pert)
+    return parts, beside
+
+
+def backward(alpha, adjoint_parts, mix, bg_sigma, static_ctrl, ens_pert, me):
     coarse_x, coarse_y, channels = alpha.shape
     members, levels, fine_x, fine_y = ens_pert.shape
     joined = lax.axis_size("tx") == 2
@@ -555,29 +665,31 @@
     n_in, n_mid, n_strip = 5 + groups, len(outside), len(strips)
 
     def kernel(*refs):
-        order_ref, parts, rest = refs[0], refs[1:1 + groups], refs[1 + groups:n_in]
+        me_ref, parts, rest = refs[0], refs[1:1 + groups], refs[1 + groups:n_in]
         outs = refs[n_in:n_in + len(shapes)]
         middle = outs[2:2 + n_mid]
         left = outs[2 + n_mid:2 + n_mid + n_strip]
         right = outs[2 + n_mid + n_strip:]
         backward_kernel(
-            coarse_x, coarse_y, joined, order_ref, parts, *rest,
+            coarse_x, coarse_y, joined, me_ref, parts, *rest,
             outs[0], outs[1], middle, left, right, *refs[n_in + len(shapes):]
         )
 
     results = pl.pallas_call(
         kernel,
         out_shape=tuple(jax.ShapeDtypeStruct(shape, jnp.float32) for shape in shapes),
-        in_specs=[SMEM] + [VMEM] * (groups + 4),
+        in_specs=[SMEM] + [VMEM] * (groups + 3) + [HBM],
         out_specs=(VMEM,) * len(shapes),
         scratch_shapes=[
             pltpu.VMEM(bg_sigma.shape, jnp.float32),
             pltpu.VMEM((coarse_x + 1, channels, fine_y), jnp.float32),
+            pltpu.VMEM(ens_pert.shape, ens_pert.dtype),
+            pltpu.SemaphoreType.DMA((members // math.gcd(members, 5),)),
         ],
-        compiler_params=ROOM,
+        compiler_params=room(50),
         cost_estimate=pl.CostEstimate(flops=8 << 30, bytes_accessed=8 << 20, transcendentals=0),
         name="backward",
-    )(order, *adjoint_parts, mix, bg_sigma, static_ctrl, ens_pert)
+    )(me, *adjoint_parts, mix, bg_sigma, static_ctrl, ens_pert)
     grad_static, center = results[:2]
     middle = results[2:2 + n_mid]
     left, right = results[2 + n_mid:2 + n_mid + n_strip], results[2 + n_mid + n_strip:]
@@ -594,19 +706,24 @@
         out_shape=jax.ShapeDtypeStruct(alpha.shape, jnp.float32),
         in_specs=[VMEM] * (2 + len(parts)),
         out_specs=VMEM,
-        compiler_params=ROOM,
+        compiler_params=room(8),
         cost_estimate=pl.CostEstimate(flops=1 << 20, bytes_accessed=2 << 20, transcendentals=0),
         name="fold",
     )(alpha, center, *parts)
     return grad_alpha, grad_static
 
 
-def shared_sum(parts):
+def owned_sum(parts):
     count = len(parts)
     total = parts[0]
     for d in range(1, count):
         total = total + lax.ppermute(parts[d], "mem", [(i, (i + d) % count) for i in range(count)])
-    return [total] + [lax.ppermute(total, "mem", [(i, (i + d) % count) for i in range(count)]) for d in range(1, count)]
+    return total
+
+
+def gathered(own):
+    count = lax.axis_size("mem")
+    return [own] + [lax.ppermute(own, "mem", [(i, (i + d) % count) for i in range(count)]) for d in range(1, count)]
 
 
 def per_device(
@@ -626,22 +743,20 @@
     levels, fine_x, fine_y = bg_sigma.shape
     tiles = lax.axis_size("tx") * lax.axis_size("ty")
     capacity = 2 * obs_owner.shape[0] // tiles
-    groups, me = lax.axis_size("mem"), lax.axis_index("mem")
-    ahead = jnp.stack([(me + d) % groups for d in range(groups)]).astype(jnp.int32)
-    behind = jnp.stack([(me - d) % groups for d in range(groups)]).astype(jnp.int32)
-    copies = LANES // levels
-    same = np.kron(np.eye(copies, dtype=np.float32), np.ones((levels, levels), np.float32))
-    mix = jnp.tile(lv_sqrt, (copies, copies)) * same
-    partial = ensemble(alpha, mix, ens_pert, ahead)
+    me = lax.axis_index("mem").astype(jnp.int32).reshape(1)
     outgoing, target = pack(
         tiles, levels, fine_x * fine_y, capacity,
         obs_count, obs_owner[:, 0], obs_column, obs_level, obs_frac, innovation, obs_rinv,
     )
+    partial, outgoing = ensemble(alpha, lv_sqrt, ens_pert, me, outgoing)
+    increment, outgoing = lax.optimization_barrier((owned_sum(partial), outgoing))
     incoming = lax.all_to_all(outgoing, ("tx", "ty"), split_axis=0, concat_axis=0, tiled=True)
-    departure, adjoint = stencil(shared_sum(partial), incoming, bg_sigma, static_ctrl, ahead, behind)
+    departure, adjoint = stencil(gathered(increment), incoming, bg_sigma, static_ctrl, me)
+    total, departure = lax.optimization_barrier((owned_sum(adjoint), departure))
     returned = lax.all_to_all(departure, ("tx", "ty"), split_axis=0, concat_axis=0, tiled=True)
     departures = unpack(target, returned.reshape(-1, BLOCK))
-    grad_alpha, grad_static = backward(alpha, shared_sum(adjoint), mix, bg_sigma, static_ctrl, ens_pert, behind)
+    parts, departures = lax.optimization_barrier((gathered(total), departures))
+    grad_alpha, grad_static = backward(alpha, parts, lv_sqrt, bg_sigma, static_ctrl, ens_pert, me)
     return (grad_alpha, grad_static, departures)
 
 

time: 199 us -> 153 us (0.77)
  Pallas kernels: 83.8 us -> 53.5 us
  blocking collectives: 18.4 us -> 0 us
  waiting for transfers between devices: 35.1 us -> 50.1 us
  local copies, waits for them, and re-layouts: 12.2 us -> 6.62 us
  starting transfers between devices: 45.5 us -> 40.5 us
    all_to_all x1 -> x0, blocking collectives: 18.4 us -> none  [per_device(): lax.all_to_all(departure, ('tx', 'ty'), split_axis=0, concat_axis=0, tile...]
    ppermute x10, waiting for transfers between devices: 0.03 us -> 14.1 us  [shifted(): return lax.ppermute(value, ('tx', 'ty'), pairs)]
    pallas_call x1, Pallas kernels: 20.2 us -> 9.89 us  [backward(): pl.pallas_call(kernel, out_shape=tuple((jax.ShapeDtypeStruct(shape, jnp.f...]
    ppermute x12, waiting for transfers between devices: 28.2 us -> 35.9 us  [the longest x6 21 us: gathered(): lax.ppermute(own, 'mem', [(i, (i + d) % count) for i in range(count)])]
    all_to_all x1, waiting for transfers between devices: 6.86 us -> 0.01 us  [per_device(): lax.all_to_all(outgoing, ('tx', 'ty'), split_axis=0, concat_axis=0, tiled...]
    pallas_call x1, Pallas kernels: 21.3 us -> 14.4 us  [stencil(): pl.pallas_call(kernel, out_shape=(jax.ShapeDtypeStruct((sources, deep, bl...]
    ppermute x10, starting transfers between devices: 17.1 us -> 11.4 us  [shifted(): return lax.ppermute(value, ('tx', 'ty'), pairs)]
    pallas_call x1, Pallas kernels: 8.52 us -> 3.11 us  [unpack(): pl.pallas_call(unpack_kernel, out_shape=jax.ShapeDtypeStruct(target.shape...]
  transfers between devices with their start and end apart: 23 -> 24, of which waited for: 9 -> 9; matrix products, arithmetic and copies ran while one was open for 1% -> 1% of each run, Pallas kernels for 12% -> 10%
where the time goes in v1:
time: 153 us; the launch traced here: 152 us
  Pallas kernels  53.5 us (35%)
  waiting for transfers between devices  50.1 us (33%)
  starting transfers between devices  40.5 us (26%)
  local copies, waits for them, and re-layouts  6.62 us (4%)
    ppermute x6, waiting for transfers between devices, gathered(): lax.ppermute(own, 'mem', [(i, (i + d) % count) for i in range(count)])  21 us
    ppermute x6, waiting for transfers between devices, owned_sum(): lax.ppermute(parts[d], 'mem', [(i, (i + d) % count) for i in range(count)])  14.8 us
    pallas_call x1, Pallas kernels, stencil(): pl.pallas_call(kernel, out_shape=(jax.ShapeDtypeStruct((sources, deep, bl...  14.4 us
    ppermute x10, waiting for transfers between devices, shifted(): return lax.ppermute(value, ('tx', 'ty'), pairs)  14.1 us
    pallas_call x1, Pallas kernels, ensemble(): pl.pallas_call(kernel, out_shape=tuple((jax.ShapeDtypeStruct((levels // g...  12.9 us
    pallas_call x1, Pallas kernels, pack(): pl.pallas_call(functools.partial(pack_kernel, tiles, levels, plane, capac...  12.1 us
    ppermute x6, starting transfers between devices, owned_sum(): lax.ppermute(parts[d], 'mem', [(i, (i + d) % count) for i in range(count)])  11.8 us
    ppermute x10, starting transfers between devices, shifted(): return lax.ppermute(value, ('tx', 'ty'), pairs)  11.4 us
  transfers between devices with their start and end apart: 24, of which 9 were waited for; matrix products, arithmetic and copies ran while one was open for 1% of the time, Pallas kernels for 10%

profile of v1, /device:TPU:0, one launch (start us, length us, event | category | flops | bytes accessed | tf_op | source)
XLA Modules:
  0.0 152.4 jit_solution(5431012018437421412)
XLA Ops:
  1.6 2.4 %collective-permute-start.2 = (f32[32,640]{1,0:T(8,128)S(1)}, f32[32,640]{1,0:T(8,128)S(1)}, u32[]{:S(2)}, u32[]{:S(2)}) collective-permute-start(f32[32,640]{1,0:T(8,128)S(1)} %reshape.36), channel_id=1, source_target_pairs={{0,20},{4,24},{8,28},{12,16},{16,4},{20,8},{24,12},{28,0},{1,21},{... | collective-permute-start | bytes 245768 | tf_op jit(solution)/shard_map/ppermute | solution.py:603
  4.0 1.6 %collective-permute-start.1 = (f32[32,640]{1,0:T(8,128)S(1)}, f32[32,640]{1,0:T(8,128)S(1)}, u32[]{:S(2)}, u32[]{:S(2)}) collective-permute-start(f32[32,640]{1,0:T(8,128)S(1)} %reshape.36), channel_id=1, source_target_pairs={{0,4},{4,8},{8,12},{12,0},{16,20},{20,24},{24,28},{28,16},{1,5},{5... | collective-permute-start | bytes 245768 | tf_op jit(solution)/shard_map/ppermute | solution.py:603
  6.9 2.0 %collective-permute-start = (f32[8,32,640]{2,1,0:T(8,128)}, f32[8,32,640]{2,1,0:T(8,128)S(1)}, u32[]{:S(2)}, u32[]{:S(2)}) collective-permute-start(f32[8,32,640]{2,1,0:T(8,128)} %alpha_ref.1), channel_id=1, source_target_pairs={{0,16},{4,20},{8,24},{12,28},{16,0},{20,4},{24,8},{28,12},{1,17},{... | collective-permute-start | bytes 1966088 | tf_op jit(solution)/shard_map/ppermute | solution.py:603
  14.3 12.1 %pack.1 = (f32[8,48,256]{2,1,0:T(8,128)}, s32[64,128]{1,0:T(8,128)S(1)}) custom-call(s32[1]{0:T(128)S(6)} %copy.15.count_ref, s32[64,128]{1,0:T(8,128)S(1)} %bitcast.9, s32[64,128]{1,0:T(8,128)S(1)} %bitcast.10, s32[64,128]{1,0:T(8,128)S(1)} %bitcast.11, f32[3,8192]{1,0:T(4,128)S(1)} %copy-done.3, f32[64,128]{1,0:T(8,128)S(1)} %bitcast.12, ...), custom_call_target="tpu_custom_call" | custom-call | flops 8589934592 | bytes 1048576 | tf_op jit(solution)/shard_map/pack/pallas_call | solution.py:144
  26.5 12.9 %ensemble.1 = (f32[8,32,128]{2,1,0:T(8,128)S(1)}, f32[8,32,128]{2,1,0:T(8,128)S(1)}, f32[8,32,128]{2,1,0:T(8,128)S(1)}, f32[8,32,128]{2,1,0:T(8,128)S(1)}) custom-call(s32[1]{0:T(128)} %bitcast.refs_0_, f32[8,32,640]{2,1,0:T(8,128)S(1)} %copy-done, f32[8,32,640]{2,1,0:T(8,128)S(1)} %collective-permute-done.refs_2_.refs_3_, ...), custom_call_target="tpu_custom_call" | custom-call | flops 8589934592 | bytes 8388608 | tf_op jit(solution)/shard_map/ensemble/pallas_call | solution.py:636
  41.0 2.6 %collective-permute-start.6 = (f32[8,32,128]{2,1,0:T(8,128)S(1)}, f32[8,32,128]{2,1,0:T(8,128)S(1)}, u32[]{:S(2)}, u32[]{:S(2)}) collective-permute-start(f32[8,32,128]{2,1,0:T(8,128)S(1)} %get-tuple-element.36), channel_id=1, source_target_pairs={{0,2},{1,3},{2,0},{3,1},{4,6},{5,7},{6,4},{7,5},{8,10},{9,11},{10,... | collective-permute-start | bytes 393224 | tf_op jit(solution)/shard_map/ppermute | solution.py:720
  45.0 2.8 %collective-permute-done.5 = f32[8,32,128]{2,1,0:T(8,128)S(1)} collective-permute-done((f32[8,32,128]{2,1,0:T(8,128)S(1)}, f32[8,32,128]{2,1,0:T(8,128)S(1)}, u32[]{:S(2)}, u32[]{:S(2)}) %collective-permute-start.5) | collective-permute-done | bytes 131104 | tf_op jit(solution)/shard_map/ppermute | solution.py:720
  47.8 4.3 %collective-permute-done.6 = f32[8,32,128]{2,1,0:T(8,128)S(1)} collective-permute-done((f32[8,32,128]{2,1,0:T(8,128)S(1)}, f32[8,32,128]{2,1,0:T(8,128)S(1)}, u32[]{:S(2)}, u32[]{:S(2)}) %collective-permute-start.6) | collective-permute-done | bytes 131104 | tf_op jit(solution)/shard_map/ppermute | solution.py:720
  52.1 3.5 %all-to-all-start = ((f32[8,48,256]{2,1,0:T(8,128)}), f32[8,48,256]{2,1,0:T(8,128)S(1)}, u32[]{:S(2)}, u32[]{:S(2)}) async-start(f32[8,48,256]{2,1,0:T(8,128)} %get-tuple-element.40), calls=%async_computation | async-start | bytes 786432 | tf_op jit(solution)/shard_map/all_to_all | solution.py:753
  55.6 4.4 %collective-permute-start.10 = (f32[8,32,128]{2,1,0:T(8,128)S(1)}, f32[8,32,128]{2,1,0:T(8,128)S(1)}, u32[]{:S(2)}, u32[]{:S(2)}) collective-permute-start(f32[8,32,128]{2,1,0:T(8,128)S(1)} %add_add_fusion.1.refs_1_), channel_id=1, source_target_pairs={{0,3},{1,0},{2,1},{3,2},{4,7},{5,4},{6,5},{7,6},{8,11},{9,8},{10,9... | collective-permute-start | bytes 393224 | tf_op jit(solution)/shard_map/ppermute | solution.py:726
  60.6 3.3 %collective-permute-done.10.refs_4_ = f32[8,32,128]{2,1,0:T(8,128)S(1)} collective-permute-done((f32[8,32,128]{2,1,0:T(8,128)S(1)}, f32[8,32,128]{2,1,0:T(8,128)S(1)}, u32[]{:S(2)}, u32[]{:S(2)}) %collective-permute-start.10) | collective-permute-done | bytes 131104 | tf_op jit(solution)/shard_map/ppermute | solution.py:726
  63.9 8.7 %collective-permute-done.9.refs_3_ = f32[8,32,128]{2,1,0:T(8,128)S(1)} collective-permute-done((f32[8,32,128]{2,1,0:T(8,128)S(1)}, f32[8,32,128]{2,1,0:T(8,128)S(1)}, u32[]{:S(2)}, u32[]{:S(2)}) %collective-permute-start.9) | collective-permute-done | bytes 131104 | tf_op jit(solution)/shard_map/ppermute | solution.py:726
  72.6 14.4 %stencil.1 = (f32[8,8,256]{2,1,0:T(8,128)}, f32[8,32,128]{2,1,0:T(8,128)S(1)}, f32[8,32,128]{2,1,0:T(8,128)S(1)}, f32[8,32,128]{2,1,0:T(8,128)S(1)}, f32[8,32,128]{2,1,0:T(8,128)S(1)}) custom-call(s32[1]{0:T(128)} %bitcast.refs_0_, f32[8,32,128]{2,1,0:T(8,128)S(1)} %add_add_fusion.1.refs_1_, f32[8,32,128]{2,1,0:T(8,128)S(1)} %collective-permute-done.8.refs_2_, ...), custom_call_target="tpu_custom_call" | custom-call | flops 17179869184 | bytes 1048576 | tf_op jit(solution)/shard_map/stencil/pallas_call | solution.py:330
  88.1 2.2 %collective-permute-start.12 = (f32[8,32,128]{2,1,0:T(8,128)S(1)}, f32[8,32,128]{2,1,0:T(8,128)S(1)}, u32[]{:S(2)}, u32[]{:S(2)}) collective-permute-start(f32[8,32,128]{2,1,0:T(8,128)S(1)} %get-tuple-element.43), channel_id=1, source_target_pairs={{0,2},{1,3},{2,0},{3,1},{4,6},{5,7},{6,4},{7,5},{8,10},{9,11},{10,... | collective-permute-start | bytes 393224 | tf_op jit(solution)/shard_map/ppermute | solution.py:720
  90.3 2.8 %collective-permute-start.13 = (f32[8,32,128]{2,1,0:T(8,128)S(1)}, f32[8,32,128]{2,1,0:T(8,128)S(1)}, u32[]{:S(2)}, u32[]{:S(2)}) collective-permute-start(f32[8,32,128]{2,1,0:T(8,128)S(1)} %get-tuple-element.44), channel_id=1, source_target_pairs={{0,3},{1,0},{2,1},{3,2},{4,7},{5,4},{6,5},{7,6},{8,11},{9,8},{10,9... | collective-permute-start | bytes 393224 | tf_op jit(solution)/shard_map/ppermute | solution.py:720
  93.2 1.9 %collective-permute-done.11 = f32[8,32,128]{2,1,0:T(8,128)S(1)} collective-permute-done((f32[8,32,128]{2,1,0:T(8,128)S(1)}, f32[8,32,128]{2,1,0:T(8,128)S(1)}, u32[]{:S(2)}, u32[]{:S(2)}) %collective-permute-start.11) | collective-permute-done | bytes 131104 | tf_op jit(solution)/shard_map/ppermute | solution.py:720
  95.1 5.8 %collective-permute-done.12 = f32[8,32,128]{2,1,0:T(8,128)S(1)} collective-permute-done((f32[8,32,128]{2,1,0:T(8,128)S(1)}, f32[8,32,128]{2,1,0:T(8,128)S(1)}, u32[]{:S(2)}, u32[]{:S(2)}) %collective-permute-start.12) | collective-permute-done | bytes 131104 | tf_op jit(solution)/shard_map/ppermute | solution.py:720
  101.0 4.2 %all-to-all-start.1 = ((f32[8,8,256]{2,1,0:T(8,128)}), f32[8,8,256]{2,1,0:T(8,128)S(1)}, u32[]{:S(2)}, u32[]{:S(2)}) async-start(f32[8,8,256]{2,1,0:T(8,128)} %get-tuple-element.48), calls=%async_computation.1 | async-start | bytes 131072 | tf_op jit(solution)/shard_map/all_to_all | solution.py:756
  105.1 3.3 %collective-permute-start.16 = (f32[8,32,128]{2,1,0:T(8,128)S(1)}, f32[8,32,128]{2,1,0:T(8,128)S(1)}, u32[]{:S(2)}, u32[]{:S(2)}) collective-permute-start(f32[8,32,128]{2,1,0:T(8,128)S(1)} %add_add_fusion.refs_1_), channel_id=1, source_target_pairs={{0,3},{1,0},{2,1},{3,2},{4,7},{5,4},{6,5},{7,6},{8,11},{9,8},{10,9... | collective-permute-start | bytes 393224 | tf_op jit(solution)/shard_map/ppermute | solution.py:726
  110.0 3.1 %unpack.1 = f32[64,128]{1,0:T(8,128)} custom-call(s32[64,128]{1,0:T(8,128)S(1)} %get-tuple-element.47.target_ref, f32[64,256]{1,0:T(8,128)S(1)} %bitcast.8), custom_call_target="tpu_custom_call" | custom-call | flops 2147483648 | bytes 262144 | tf_op jit(solution)/shard_map/unpack/pallas_call | solution.py:374
  113.1 9.1 %collective-permute-done.15.refs_3_ = f32[8,32,128]{2,1,0:T(8,128)S(1)} collective-permute-done((f32[8,32,128]{2,1,0:T(8,128)S(1)}, f32[8,32,128]{2,1,0:T(8,128)S(1)}, u32[]{:S(2)}, u32[]{:S(2)}) %collective-permute-start.15) | collective-permute-done | bytes 131104 | tf_op jit(solution)/shard_map/ppermute | solution.py:726
  122.2 9.9 %backward.1 = (f32[32,32,128]{2,1,0:T(8,128)}, f32[8,32,640]{2,1,0:T(8,128)S(1)}, f32[8,32,640]{2,1,0:T(8,128)S(1)}, f32[32,640]{1,0:T(8,128)S(1)}, f32[32,640]{...) custom-call(s32[1]{0:T(128)} %bitcast.refs_0_, f32[8,32,128]{2,1,0:T(8,128)S(1)} %add_add_fusion.refs_1_, ...), custom_call_target="tpu_custom_call" | custom-call | flops 8589934592 | bytes 8388608 | tf_op jit(solution)/shard_map/backward/pallas_call | solution.py:678
  132.1 1.7 %collective-permute-start.17 = (f32[8,32,640]{2,1,0:T(8,128)S(1)}, f32[8,32,640]{2,1,0:T(8,128)S(1)}, u32[]{:S(2)}, u32[]{:S(2)}) collective-permute-start(f32[8,32,640]{2,1,0:T(8,128)S(1)} %get-tuple-element.54), channel_id=1, source_target_pairs={{0,16},{4,20},{8,24},{12,28},{16,0},{20,4},{24,8},{28,12},{1,17},{... | collective-permute-start | bytes 1966088 | tf_op jit(solution)/shard_map/ppermute | solution.py:603
  137.1 14.1 %collective-permute-done.18.refs_1_ = f32[32,640]{1,0:T(8,128)S(1)} collective-permute-done((f32[32,640]{1,0:T(8,128)S(1)}, f32[32,640]{1,0:T(8,128)S(1)}, u32[]{:S(2)}, u32[]{:S(2)}) %collective-permute-start.18) | collective-permute-done | bytes 81952 | tf_op jit(solution)/shard_map/ppermute | solution.py:603
  (56 shorter events, 17.7 us)
Async XLA Ops:
  1.6 24.8 %collective-permute-start.2 = (f32[32,640]{1,0:T(8,128)S(1)}, f32[32,640]{1,0:T(8,128)S(1)}, u32[]{:S(2)}, u32[]{:S(2)}) collective-permute-start(f32[32,640]{1,0:T(8,128)S(1)} %reshape.36), channel_id=1, source_target_pairs={{0,20},{4,24},{8,28},{12,16},{16,4},{20,8},{24,12},{28,0},{1,21},{... | collective-permute-start | bytes 245768 | tf_op jit(solution)/shard_map/ppermute | solution.py:603
  4.0 22.3 %collective-permute-start.1 = (f32[32,640]{1,0:T(8,128)S(1)}, f32[32,640]{1,0:T(8,128)S(1)}, u32[]{:S(2)}, u32[]{:S(2)}) collective-permute-start(f32[32,640]{1,0:T(8,128)S(1)} %reshape.36), channel_id=1, source_target_pairs={{0,4},{4,8},{8,12},{12,0},{16,20},{20,24},{24,28},{28,16},{1,5},{5... | collective-permute-start | bytes 245768 | tf_op jit(solution)/shard_map/ppermute | solution.py:603
  6.6 19.8 %collective-permute-start.4 = (f32[40,640]{1,0:T(8,128)S(1)}, f32[40,640]{1,0:T(8,128)S(1)}, u32[]{:S(2)}, u32[]{:S(2)}) collective-permute-start(f32[40,640]{1,0:T(8,128)S(1)} %reshape.41), channel_id=1, source_target_pairs={{0,28},{4,16},{8,20},{12,24},{16,12},{20,0},{24,4},{28,8},{1,29},{... | collective-permute-start | bytes 307208 | tf_op jit(solution)/shard_map/ppermute | solution.py:603
  6.9 19.6 %collective-permute-start.3 = (f32[40,640]{1,0:T(8,128)S(1)}, f32[40,640]{1,0:T(8,128)S(1)}, u32[]{:S(2)}, u32[]{:S(2)}) collective-permute-start(f32[40,640]{1,0:T(8,128)S(1)} %reshape.41), channel_id=1, source_target_pairs={{0,12},{4,0},{8,4},{12,8},{16,28},{20,16},{24,20},{28,24},{1,13},{... | collective-permute-start | bytes 307208 | tf_op jit(solution)/shard_map/ppermute | solution.py:603
  6.9 19.5 %collective-permute-start = (f32[8,32,640]{2,1,0:T(8,128)}, f32[8,32,640]{2,1,0:T(8,128)S(1)}, u32[]{:S(2)}, u32[]{:S(2)}) collective-permute-start(f32[8,32,640]{2,1,0:T(8,128)} %alpha_ref.1), channel_id=1, source_target_pairs={{0,16},{4,20},{8,24},{12,28},{16,0},{20,4},{24,8},{28,12},{1,17},{... | collective-permute-start | bytes 1966088 | tf_op jit(solution)/shard_map/ppermute | solution.py:603
  39.4 8.4 %collective-permute-start.5 = (f32[8,32,128]{2,1,0:T(8,128)S(1)}, f32[8,32,128]{2,1,0:T(8,128)S(1)}, u32[]{:S(2)}, u32[]{:S(2)}) collective-permute-start(f32[8,32,128]{2,1,0:T(8,128)S(1)} %get-tuple-element.35), channel_id=1, source_target_pairs={{0,1},{1,2},{2,3},{3,0},{4,5},{5,6},{6,7},{7,4},{8,9},{9,10},{10,1... | collective-permute-start | bytes 393224 | tf_op jit(solution)/shard_map/ppermute | solution.py:720
  41.0 11.0 %collective-permute-start.6 = (f32[8,32,128]{2,1,0:T(8,128)S(1)}, f32[8,32,128]{2,1,0:T(8,128)S(1)}, u32[]{:S(2)}, u32[]{:S(2)}) collective-permute-start(f32[8,32,128]{2,1,0:T(8,128)S(1)} %get-tuple-element.36), channel_id=1, source_target_pairs={{0,2},{1,3},{2,0},{3,1},{4,6},{5,7},{6,4},{7,5},{8,10},{9,11},{10,... | collective-permute-start | bytes 393224 | tf_op jit(solution)/shard_map/ppermute | solution.py:720
  43.6 8.4 %collective-permute-start.7 = (f32[8,32,128]{2,1,0:T(8,128)S(1)}, f32[8,32,128]{2,1,0:T(8,128)S(1)}, u32[]{:S(2)}, u32[]{:S(2)}) collective-permute-start(f32[8,32,128]{2,1,0:T(8,128)S(1)} %get-tuple-element.37), channel_id=1, source_target_pairs={{0,3},{1,0},{2,1},{3,2},{4,7},{5,4},{6,5},{7,6},{8,11},{9,8},{10,9... | collective-permute-start | bytes 393224 | tf_op jit(solution)/shard_map/ppermute | solution.py:720
  52.1 20.4 %all-to-all-start = ((f32[8,48,256]{2,1,0:T(8,128)}), f32[8,48,256]{2,1,0:T(8,128)S(1)}, u32[]{:S(2)}, u32[]{:S(2)}) async-start(f32[8,48,256]{2,1,0:T(8,128)} %get-tuple-element.40), calls=%async_computation | async-start | bytes 786432 | tf_op jit(solution)/shard_map/all_to_all | solution.py:753
  55.6 8.3 %collective-permute-start.10 = (f32[8,32,128]{2,1,0:T(8,128)S(1)}, f32[8,32,128]{2,1,0:T(8,128)S(1)}, u32[]{:S(2)}, u32[]{:S(2)}) collective-permute-start(f32[8,32,128]{2,1,0:T(8,128)S(1)} %add_add_fusion.1.refs_1_), channel_id=1, source_target_pairs={{0,3},{1,0},{2,1},{3,2},{4,7},{5,4},{6,5},{7,6},{8,11},{9,8},{10,9... | collective-permute-start | bytes 393224 | tf_op jit(solution)/shard_map/ppermute | solution.py:726
  60.0 12.6 %collective-permute-start.9 = (f32[8,32,128]{2,1,0:T(8,128)S(1)}, f32[8,32,128]{2,1,0:T(8,128)S(1)}, u32[]{:S(2)}, u32[]{:S(2)}) collective-permute-start(f32[8,32,128]{2,1,0:T(8,128)S(1)} %add_add_fusion.1.refs_1_), channel_id=1, source_target_pairs={{0,2},{1,3},{2,0},{3,1},{4,6},{5,7},{6,4},{7,5},{8,10},{9,11},{10,... | collective-permute-start | bytes 393224 | tf_op jit(solution)/shard_map/ppermute | solution.py:726
  60.4 12.2 %collective-permute-start.8 = (f32[8,32,128]{2,1,0:T(8,128)S(1)}, f32[8,32,128]{2,1,0:T(8,128)S(1)}, u32[]{:S(2)}, u32[]{:S(2)}) collective-permute-start(f32[8,32,128]{2,1,0:T(8,128)S(1)} %add_add_fusion.1.refs_1_), channel_id=1, source_target_pairs={{0,1},{1,2},{2,3},{3,0},{4,5},{5,6},{6,7},{7,4},{8,9},{9,10},{10,1... | collective-permute-start | bytes 393224 | tf_op jit(solution)/shard_map/ppermute | solution.py:726
  87.0 8.1 %collective-permute-start.11 = (f32[8,32,128]{2,1,0:T(8,128)S(1)}, f32[8,32,128]{2,1,0:T(8,128)S(1)}, u32[]{:S(2)}, u32[]{:S(2)}) collective-permute-start(f32[8,32,128]{2,1,0:T(8,128)S(1)} %get-tuple-element.42), channel_id=1, source_target_pairs={{0,1},{1,2},{2,3},{3,0},{4,5},{5,6},{6,7},{7,4},{8,9},{9,10},{10,1... | collective-permute-start | bytes 393224 | tf_op jit(solution)/shard_map/ppermute | solution.py:720
  88.1 12.8 %collective-permute-start.12 = (f32[8,32,128]{2,1,0:T(8,128)S(1)}, f32[8,32,128]{2,1,0:T(8,128)S(1)}, u32[]{:S(2)}, u32[]{:S(2)}) collective-permute-start(f32[8,32,128]{2,1,0:T(8,128)S(1)} %get-tuple-element.43), channel_id=1, source_target_pairs={{0,2},{1,3},{2,0},{3,1},{4,6},{5,7},{6,4},{7,5},{8,10},{9,11},{10,... | collective-permute-start | bytes 393224 | tf_op jit(solution)/shard_map/ppermute | solution.py:720
  90.3 10.6 %collective-permute-start.13 = (f32[8,32,128]{2,1,0:T(8,128)S(1)}, f32[8,32,128]{2,1,0:T(8,128)S(1)}, u32[]{:S(2)}, u32[]{:S(2)}) collective-permute-start(f32[8,32,128]{2,1,0:T(8,128)S(1)} %get-tuple-element.44), channel_id=1, source_target_pairs={{0,3},{1,0},{2,1},{3,2},{4,7},{5,4},{6,5},{7,6},{8,11},{9,8},{10,9... | collective-permute-start | bytes 393224 | tf_op jit(solution)/shard_map/ppermute | solution.py:720
  101.0 9.0 %all-to-all-start.1 = ((f32[8,8,256]{2,1,0:T(8,128)}), f32[8,8,256]{2,1,0:T(8,128)S(1)}, u32[]{:S(2)}, u32[]{:S(2)}) async-start(f32[8,8,256]{2,1,0:T(8,128)} %get-tuple-element.48), calls=%async_computation.1 | async-start | bytes 131072 | tf_op jit(solution)/shard_map/all_to_all | solution.py:756
  105.1 8.0 %collective-permute-start.16 = (f32[8,32,128]{2,1,0:T(8,128)S(1)}, f32[8,32,128]{2,1,0:T(8,128)S(1)}, u32[]{:S(2)}, u32[]{:S(2)}) collective-permute-start(f32[8,32,128]{2,1,0:T(8,128)S(1)} %add_add_fusion.refs_1_), channel_id=1, source_target_pairs={{0,3},{1,0},{2,1},{3,2},{4,7},{5,4},{6,5},{7,6},{8,11},{9,8},{10,9... | collective-permute-start | bytes 393224 | tf_op jit(solution)/shard_map/ppermute | solution.py:726
  108.5 13.7 %collective-permute-start.15 = (f32[8,32,128]{2,1,0:T(8,128)S(1)}, f32[8,32,128]{2,1,0:T(8,128)S(1)}, u32[]{:S(2)}, u32[]{:S(2)}) collective-permute-start(f32[8,32,128]{2,1,0:T(8,128)S(1)} %add_add_fusion.refs_1_), channel_id=1, source_target_pairs={{0,2},{1,3},{2,0},{3,1},{4,6},{5,7},{6,4},{7,5},{8,10},{9,11},{10,... | collective-permute-start | bytes 393224 | tf_op jit(solution)/shard_map/ppermute | solution.py:726
  109.9 12.3 %collective-permute-start.14 = (f32[8,32,128]{2,1,0:T(8,128)S(1)}, f32[8,32,128]{2,1,0:T(8,128)S(1)}, u32[]{:S(2)}, u32[]{:S(2)}) collective-permute-start(f32[8,32,128]{2,1,0:T(8,128)S(1)} %add_add_fusion.refs_1_), channel_id=1, source_target_pairs={{0,1},{1,2},{2,3},{3,0},{4,5},{5,6},{6,7},{7,4},{8,9},{9,10},{10,1... | collective-permute-start | bytes 393224 | tf_op jit(solution)/shard_map/ppermute | solution.py:726
  132.1 19.2 %collective-permute-start.17 = (f32[8,32,640]{2,1,0:T(8,128)S(1)}, f32[8,32,640]{2,1,0:T(8,128)S(1)}, u32[]{:S(2)}, u32[]{:S(2)}) collective-permute-start(f32[8,32,640]{2,1,0:T(8,128)S(1)} %get-tuple-element.54), channel_id=1, source_target_pairs={{0,16},{4,20},{8,24},{12,28},{16,0},{20,4},{24,8},{28,12},{1,17},{... | collective-permute-start | bytes 1966088 | tf_op jit(solution)/shard_map/ppermute | solution.py:603
  133.8 17.4 %collective-permute-start.19 = (f32[40,640]{1,0:T(8,128)S(1)}, f32[40,640]{1,0:T(8,128)S(1)}, u32[]{:S(2)}, u32[]{:S(2)}) collective-permute-start(f32[40,640]{1,0:T(8,128)S(1)} %get-tuple-element.56), channel_id=1, source_target_pairs={{0,20},{4,24},{8,28},{12,16},{16,4},{20,8},{24,12},{28,0},{1,21},{... | collective-permute-start | bytes 307208 | tf_op jit(solution)/shard_map/ppermute | solution.py:603
  133.8 17.4 %collective-permute-start.21 = (f32[40,640]{1,0:T(8,128)S(1)}, f32[40,640]{1,0:T(8,128)S(1)}, u32[]{:S(2)}, u32[]{:S(2)}) collective-permute-start(f32[40,640]{1,0:T(8,128)S(1)} %get-tuple-element.58), channel_id=1, source_target_pairs={{0,4},{4,8},{8,12},{12,0},{16,20},{20,24},{24,28},{28,16},{1,5},{5... | collective-permute-start | bytes 307208 | tf_op jit(solution)/shard_map/ppermute | solution.py:603
  135.4 15.8 %collective-permute-start.18 = (f32[32,640]{1,0:T(8,128)S(1)}, f32[32,640]{1,0:T(8,128)S(1)}, u32[]{:S(2)}, u32[]{:S(2)}) collective-permute-start(f32[32,640]{1,0:T(8,128)S(1)} %get-tuple-element.55), channel_id=1, source_target_pairs={{0,28},{4,16},{8,20},{12,24},{16,12},{20,0},{24,4},{28,8},{1,29},{... | collective-permute-start | bytes 245768 | tf_op jit(solution)/shard_map/ppermute | solution.py:603
  136.5 14.8 %collective-permute-start.20 = (f32[32,640]{1,0:T(8,128)S(1)}, f32[32,640]{1,0:T(8,128)S(1)}, u32[]{:S(2)}, u32[]{:S(2)}) collective-permute-start(f32[32,640]{1,0:T(8,128)S(1)} %get-tuple-element.57), channel_id=1, source_target_pairs={{0,12},{4,0},{8,4},{12,8},{16,28},{20,16},{24,20},{28,24},{1,13},{... | collective-permute-start | bytes 245768 | tf_op jit(solution)/shard_map/ppermute | solution.py:603
  (10 other events, 121.2 us)

commit v2 on v1

--- a/solution.py
+++ b/solution.py
@@ -47,11 +47,14 @@
     tiles, levels, plane, capacity,
     count_ref, *refs,
 ):
-    sources, (out_ref, target_ref, carry, total, gathered, *held), sems = refs[:6], refs[6:-1], refs[-1]
+    sources, (out_ref, target_ref, carry, total, gathered, *held), sems = refs[:3], refs[3:-1], refs[-1]
     copies = [pltpu.make_async_copy(source, here, sems.at[i]) for i, (source, here) in enumerate(zip(sources, held))]
     for copy in copies:
         copy.start()
-    owner_ref, level_ref, column_ref, frac_ref, innov_ref, rinv_ref = held
+    ints_ref, floats_ref, frac_ref = held
+    size = target_ref.shape[0]
+    owner_ref, level_ref, column_ref = [ints_ref.at[pl.ds(i * size, size)] for i in range(3)]
+    innov_ref, rinv_ref = [floats_ref.at[pl.ds(i * size, size)] for i in range(2)]
     blocks = target_ref.shape[0] * LANES // BLOCK
     keys = tiles * levels
     deep = capacity // BLOCK
@@ -70,7 +73,7 @@
 
     ones = jnp.ones((BLOCK, LANES), HALF)
     total[...] = jnp.zeros_like(total)
-    for copy in copies[:2]:
+    for copy in copies[:1]:
         copy.wait()
 
     def count_group(g, unused):
@@ -80,7 +83,7 @@
         return unused
 
     lax.fori_loop(0, blocks // group, count_group, 0)
-    for copy in copies[2:]:
+    for copy in copies[1:]:
         copy.wait()
     high = jnp.floor(total[...] * (1.0 / LANES))
     low = total[...] - high * LANES
@@ -138,8 +141,7 @@
     slots = owner.shape[0]
     rows = slots // LANES
     deep = capacity // BLOCK
-    values = [value.reshape(rows, LANES) for value in (owner, level, column)]
-    values += [frac, innov.reshape(rows, LANES), rinv.reshape(rows, LANES)]
+    values = [jnp.concatenate(some).reshape(-1, LANES) for some in ((owner, level, column), (innov, rinv))] + [frac]
     vmem = pl.BlockSpec(memory_space=pltpu.VMEM)
     return pl.pallas_call(
         functools.partial(pack_kernel, tiles, levels, plane, capacity),
@@ -147,7 +149,7 @@
             jax.ShapeDtypeStruct((tiles, 6 * deep, BLOCK), jnp.float32),
             jax.ShapeDtypeStruct((rows, LANES), jnp.int32),
         ),
-        in_specs=[SMEM] + [HBM] * 6,
+        in_specs=[SMEM] + [HBM] * 3,
         out_specs=(vmem, vmem),
         scratch_shapes=[
             pltpu.VMEM((tiles * levels, LANES), jnp.float32),
@@ -450,8 +452,8 @@
             ext[begin + i, EDGE + coarse_y:EDGE + coarse_y + REACH + 1, :] = right[
                 at * (REACH + 1):(at + 1) * (REACH + 1), :
             ]
-    spread_y = interpolation((fine_y, coarse_y + PAD), 0, 1, EDGE)
-    spread_y = jnp.concatenate([spread_y.astype(jnp.float32)] * 2, 1).astype(HALF)
+    spread_y = interpolation((coarse_y + PAD, fine_y), 1, 0, EDGE)
+    spread_y = jnp.concatenate([spread_y, spread_y], 0)
     high, low = mixing(mix_ref)
     mix = jnp.concatenate([high, high, low], 1)
 
@@ -462,10 +464,10 @@
             inner = field[1:-1]
             field = inner + field[2:] + field[:-2] + neighbours(inner)
         high, low = split_two(field * SCALE)
+        both = jnp.concatenate([high.astype(jnp.float32), low.astype(jnp.float32)], 1)
         for c in range(coarse_x + 1):
-            wide = dot_nn(spread_y, jnp.concatenate([high[c], low[c]], 0))
-            wide_high, wide_low = split_two(wide)
-            coarse[c, lanes, :] = dot_nt(mix, jnp.concatenate([wide_high, wide_low, wide_high], 1))
+            wide_high, wide_low = split_two(dot_nn(both[c].T.astype(HALF), spread_y))
+            coarse[c, lanes, :] = dot_nn(mix, jnp.concatenate([wide_high, wide_low, wide_high], 0))
         return unused
 
     lax.fori_loop(0, channels // LANES, one_group, 0)
@@ -502,9 +504,9 @@
 
 
 def backward_kernel(
-    coarse_x, coarse_y, joined,
+    coarse_x, coarse_y, joined, base,
     me_ref, parts_refs, mix_ref, sigma_ref, static_ref, pert_hbm,
-    grad_ref, center_ref, middle_refs, left_refs, right_refs,
+    earlier_refs, grad_ref, center_ref, middle_refs, left_refs, right_refs,
     adjoint, coarse, pert_ref, sems,
 ):
     members, levels, fine_x, fine_y = pert_ref.shape
@@ -513,13 +515,19 @@
     copies = []
     for p in range(sems.shape[0]):
         some = pl.ds(p * unroll, unroll)
-        copies.append(pltpu.make_async_copy(pert_hbm.at[some], pert_ref.at[some], sems.at[p]))
+        there = pert_hbm.at[pl.ds(base + p * unroll, unroll)]
+        copies.append(pltpu.make_async_copy(there, pert_ref.at[some], sems.at[p]))
         copies[p].start()
     share = levels // len(parts_refs)
     for slot, part in enumerate(parts_refs):
         first = lax.rem(me_ref[0] + len(parts_refs) - slot, len(parts_refs)) * share
         adjoint[pl.ds(first, share)] = part[...]
-    grad_ref[...] = static_ref[...] + sigma_ref[...] * adjoint[...]
+    shift = 0
+    for earlier, strip in zip(earlier_refs, left_refs + right_refs):
+        shift = earlier.shape[1]
+        strip[:, :shift] = earlier[...]
+    if grad_ref is not None:
+        grad_ref[...] = static_ref[...] + sigma_ref[...] * adjoint[...]
     depth = coarse_x + 2
     fold_x = interpolation_rows(fine_x, depth, 1, True)
 
@@ -561,6 +569,7 @@
             field = jnp.concatenate([field, empty, empty], 0) + jnp.concatenate([empty, own, empty], 0) + jnp.concatenate(
                 [empty, empty, field], 0
             )
+        shifted_lanes = pl.ds(pl.multiple_of(shift + g * LANES, LANES), LANES)
         inside = field[REACH:REACH + coarse_x]
         up, down = field[:REACH], field[REACH + coarse_x:]
         if joined:
@@ -573,8 +582,8 @@
             ref[:, :, lanes] = value[:, EDGE:EDGE + coarse_y]
         for left, right, value in zip(left_refs, right_refs, [inside] + outside):
             for i in range(value.shape[0]):
-                left[i * REACH:(i + 1) * REACH, lanes] = value[i, EDGE - REACH:EDGE]
-                right[i * (REACH + 1):(i + 1) * (REACH + 1), lanes] = value[
+                left[i * REACH:(i + 1) * REACH, shifted_lanes] = value[i, EDGE - REACH:EDGE]
+                right[i * (REACH + 1):(i + 1) * (REACH + 1), shifted_lanes] = value[
                     i, EDGE + coarse_y:EDGE + coarse_y + REACH + 1
                 ]
         return unused
@@ -582,15 +591,16 @@
     lax.fori_loop(0, channels // LANES, one_group, 0)
 
 
-def fold_kernel(places, alpha_ref, center_ref, *refs):
+def fold_kernel(places, alpha_ref, *refs):
     part_refs, out_ref = refs[:-1], refs[-1]
-    out_ref[...] = alpha_ref[...] + center_ref[...]
-    for (row, count, column, width), ref in zip(places, part_refs):
+    out_ref[...] = alpha_ref[...]
+    for (row, count, column, width, begin), ref in zip(places, part_refs):
+        lanes = slice(begin, begin + ref.shape[-1])
         if width == out_ref.shape[1]:
-            out_ref[row:row + count] += ref[...]
+            out_ref[row:row + count, :, lanes] += ref[...]
         else:
             for i in range(count):
-                out_ref[row + i, column:column + width, :] += ref[i * width:(i + 1) * width, :]
+                out_ref[row + i, column:column + width, lanes] += ref[i * width:(i + 1) * width, :]
 
 
 def shifted(value, by_x, by_y):
@@ -651,65 +661,85 @@
     return parts, beside
 
 
-def backward(alpha, adjoint_parts, mix, bg_sigma, static_ctrl, ens_pert, me):
-    coarse_x, coarse_y, channels = alpha.shape
-    members, levels, fine_x, fine_y = ens_pert.shape
+def backward_chunk(alpha, adjoint_parts, mix, bg_sigma, static_ctrl, ens_pert, me, begin, end, earlier, before):
+    coarse_x, coarse_y = alpha.shape[:2]
+    levels, fine_x, fine_y = ens_pert.shape[1:]
+    members = end - begin
+    channels = members * levels
     joined = lax.axis_size("tx") == 2
     groups = len(adjoint_parts)
     outside = [coarse_x] if joined else [REACH, REACH + 1]
     strips = [coarse_x] + outside
-    shapes = [bg_sigma.shape, alpha.shape]
+    shapes = [(coarse_x, coarse_y, channels)]
     shapes += [(rows, coarse_y, channels) for rows in outside]
-    shapes += [(rows * REACH, channels) for rows in strips]
-    shapes += [(rows * (REACH + 1), channels) for rows in strips]
-    n_in, n_mid, n_strip = 5 + groups, len(outside), len(strips)
+    shapes += [(rows * REACH, end * levels) for rows in strips]
+    shapes += [(rows * (REACH + 1), end * levels) for rows in strips]
+    last = end == ens_pert.shape[0]
+    if last:
+        shapes += [bg_sigma.shape]
+    n_in, n_mid, n_strip = 5 + groups + len(earlier), len(outside), len(strips)
 
     def kernel(*refs):
-        me_ref, parts, rest = refs[0], refs[1:1 + groups], refs[1 + groups:n_in]
+        me_ref, parts, rest = refs[0], refs[1:1 + groups], refs[1 + groups:5 + groups]
         outs = refs[n_in:n_in + len(shapes)]
-        middle = outs[2:2 + n_mid]
-        left = outs[2 + n_mid:2 + n_mid + n_strip]
-        right = outs[2 + n_mid + n_strip:]
+        middle = outs[1:1 + n_mid]
+        left = outs[1 + n_mid:1 + n_mid + n_strip]
+        right = outs[1 + n_mid + n_strip:1 + n_mid + 2 * n_strip]
         backward_kernel(
-            coarse_x, coarse_y, joined, me_ref, parts, *rest,
-            outs[0], outs[1], middle, left, right, *refs[n_in + len(shapes):]
+            coarse_x, coarse_y, joined, begin, me_ref, parts, *rest, refs[5 + groups:n_in],
+            outs[-1] if last else None, outs[0], middle, left, right, *refs[n_in + len(shapes):]
         )
 
     results = pl.pallas_call(
         kernel,
         out_shape=tuple(jax.ShapeDtypeStruct(shape, jnp.float32) for shape in shapes),
-        in_specs=[SMEM] + [VMEM] * (groups + 3) + [HBM],
+        in_specs=[SMEM] + [VMEM] * (groups + 3) + [HBM] + [VMEM] * len(earlier),
         out_specs=(VMEM,) * len(shapes),
         scratch_shapes=[
             pltpu.VMEM(bg_sigma.shape, jnp.float32),
             pltpu.VMEM((coarse_x + 1, channels, fine_y), jnp.float32),
-            pltpu.VMEM(ens_pert.shape, ens_pert.dtype),
-            pltpu.SemaphoreType.DMA((members // math.gcd(members, 5),)),
+            pltpu.VMEM((members,) + ens_pert.shape[1:], ens_pert.dtype),
+            pltpu.SemaphoreType.DMA((members // 4,)),
         ],
         compiler_params=room(50),
-        cost_estimate=pl.CostEstimate(flops=8 << 30, bytes_accessed=8 << 20, transcendentals=0),
+        cost_estimate=pl.CostEstimate(flops=4 << 30, bytes_accessed=4 << 20, transcendentals=0),
         name="backward",
-    )(me, *adjoint_parts, mix, bg_sigma, static_ctrl, ens_pert)
-    grad_static, center = results[:2]
-    middle = results[2:2 + n_mid]
-    left, right = results[2 + n_mid:2 + n_mid + n_strip], results[2 + n_mid + n_strip:]
-    last, wide = coarse_y - REACH, REACH + 1
+    )(me, *adjoint_parts, mix, bg_sigma, static_ctrl, ens_pert, *earlier)
+    edges = results[1 + n_mid:1 + n_mid + 2 * n_strip]
     moves = [(1, 0, coarse_x)] if joined else [(-1, coarse_x - REACH, REACH), (1, 0, REACH + 1)]
-    places, parts = [], []
-    for (by, row, count), value, to_left, to_right in zip(moves, middle, left[1:], right[1:]):
-        parts += [shifted(value, by, 0), shifted(to_left, by, -1), shifted(to_right, by, 1)]
-        places += [(row, count, 0, coarse_y), (row, count, last, REACH), (row, count, 0, wide)]
-    parts += [shifted(left[0], 0, -1), shifted(right[0], 0, 1)]
-    places += [(0, coarse_x, last, REACH), (0, coarse_x, 0, wide)]
+    places, parts = [(0, coarse_x, 0, coarse_y, begin * levels)], [results[0]]
+    for (by, row, count), value in zip(moves, results[1:1 + n_mid]):
+        parts.append(shifted(value, by, 0))
+        places.append((row, count, 0, coarse_y, begin * levels))
+    if joined and not last:
+        places, parts = places[:1], [parts[0] + parts[1]]
+    if last:
+        edges, before = lax.optimization_barrier((edges, before))
+        for (by, row, count), to_left, to_right in zip([(0, 0, coarse_x)] + moves, edges[:n_strip], edges[n_strip:]):
+            parts += [shifted(to_left, by, -1), shifted(to_right, by, 1)]
+            places += [(row, count, coarse_y - REACH, REACH, 0), (row, count, 0, REACH + 1, 0)]
+    return before + parts, places, edges, results[-1]
+
+
+def backward(alpha, adjoint_parts, mix, bg_sigma, static_ctrl, ens_pert, me):
+    members, levels = ens_pert.shape[:2]
+    copies = LANES // levels
+    cut = max(members * 2 // 5 // copies, 1) * copies
+    parts, places, edges = [], [], []
+    for begin, end in ((0, cut), (cut, members)):
+        parts, at, edges, grad_static = backward_chunk(
+            alpha, adjoint_parts, mix, bg_sigma, static_ctrl, ens_pert, me, begin, end, edges, parts
+        )
+        places += at
     grad_alpha = pl.pallas_call(
         functools.partial(fold_kernel, places),
         out_shape=jax.ShapeDtypeStruct(alpha.shape, jnp.float32),
-        in_specs=[VMEM] * (2 + len(parts)),
+        in_specs=[VMEM] * (1 + len(parts)),
         out_specs=VMEM,
-        compiler_params=room(8),
+        compiler_params=room(12),
         cost_estimate=pl.CostEstimate(flops=1 << 20, bytes_accessed=2 << 20, transcendentals=0),
         name="fold",
-    )(alpha, center, *parts)
+    )(alpha, *parts)
     return grad_alpha, grad_static
 
 
@@ -749,13 +779,15 @@
         obs_count, obs_owner[:, 0], obs_column, obs_level, obs_frac, innovation, obs_rinv,
     )
     partial, outgoing = ensemble(alpha, lv_sqrt, ens_pert, me, outgoing)
-    increment, outgoing = lax.optimization_barrier((owned_sum(partial), outgoing))
+    increment = gathered(owned_sum(partial))
+    increment[-1], outgoing = lax.optimization_barrier((increment[-1], outgoing))
     incoming = lax.all_to_all(outgoing, ("tx", "ty"), split_axis=0, concat_axis=0, tiled=True)
-    departure, adjoint = stencil(gathered(increment), incoming, bg_sigma, static_ctrl, me)
-    total, departure = lax.optimization_barrier((owned_sum(adjoint), departure))
+    departure, adjoint = stencil(increment, incoming, bg_sigma, static_ctrl, me)
+    parts = gathered(owned_sum(adjoint))
+    parts[-1], departure = lax.optimization_barrier((parts[-1], departure))
     returned = lax.all_to_all(departure, ("tx", "ty"), split_axis=0, concat_axis=0, tiled=True)
     departures = unpack(target, returned.reshape(-1, BLOCK))
-    parts, departures = lax.optimization_barrier((gathered(total), departures))
+    parts, departures = lax.optimization_barrier((parts, departures))
     grad_alpha, grad_static = backward(alpha, parts, lv_sqrt, bg_sigma, static_ctrl, ens_pert, me)
     return (grad_alpha, grad_static, departures)
 

time: 153 us -> 164 us (1.072)
  starting transfers between devices: 40.5 us -> 49 us
  Pallas kernels: 53.5 us -> 58.6 us
  local copies, waits for them, and re-layouts: 6.62 us -> 2.83 us
    ppermute x6, starting transfers between devices: 9.75 us -> 17 us  [gathered(): lax.ppermute(own, 'mem', [(i, (i + d) % count) for i in range(count)])]
    ppermute x10 -> x11, waiting for transfers between devices: 14.1 us -> 19.9 us  [shifted(): return lax.ppermute(value, ('tx', 'ty'), pairs)]
    ppermute x6, waiting for transfers between devices: 21 us -> 17.1 us  [gathered(): lax.ppermute(own, 'mem', [(i, (i + d) % count) for i in range(count)])]
    unnamed x20 -> x10, local copies, waits for them, and re-layouts: 4.71 us -> 0.92 us
    pallas_call x1, Pallas kernels: 14.4 us -> 18.2 us  [stencil(): pl.pallas_call(kernel, out_shape=(jax.ShapeDtypeStruct((sources, deep, bl...]
    all_to_all x1, starting transfers between devices: 4.15 us -> 7 us  [per_device(): lax.all_to_all(departure, ('tx', 'ty'), split_axis=0, concat_axis=0, tile...]
    pallas_call x1 -> x2, Pallas kernels: 9.89 us -> 11.9 us  [backward_chunk(): pl.pallas_call(kernel, out_shape=tuple((jax.ShapeDtypeStruct(shape, jnp.f...]
    ppermute x6, starting transfers between devices: 11.8 us -> 9.79 us  [owned_sum(): lax.ppermute(parts[d], 'mem', [(i, (i + d) % count) for i in range(count)])]
  transfers between devices with their start and end apart: 24 -> 25, of which waited for: 9 -> 13; matrix products, arithmetic and copies ran while one was open for 1% -> 2% of each run, Pallas kernels for 10% -> 9%
where the time goes in v2:
time: 164 us
  Pallas kernels  58.6 us (36%)
  waiting for transfers between devices  50.5 us (31%)
  starting transfers between devices  49 us (30%)
  local copies, waits for them, and re-layouts  2.83 us (2%)
  other arithmetic  1.7 us (1%)
    ppermute x11, waiting for transfers between devices, shifted(): return lax.ppermute(value, ('tx', 'ty'), pairs)  19.9 us
    pallas_call x1, Pallas kernels, stencil(): pl.pallas_call(kernel, out_shape=(jax.ShapeDtypeStruct((sources, deep, bl...  18.2 us
    ppermute x6, waiting for transfers between devices, gathered(): lax.ppermute(own, 'mem', [(i, (i + d) % count) for i in range(count)])  17.1 us
    ppermute x6, starting transfers between devices, gathered(): lax.ppermute(own, 'mem', [(i, (i + d) % count) for i in range(count)])  17 us
    ppermute x6, waiting for transfers between devices, owned_sum(): lax.ppermute(parts[d], 'mem', [(i, (i + d) % count) for i in range(count)])  13.5 us
    pallas_call x1, Pallas kernels, ensemble(): pl.pallas_call(kernel, out_shape=tuple((jax.ShapeDtypeStruct((levels // g...  12.3 us
    pallas_call x1, Pallas kernels, pack(): pl.pallas_call(functools.partial(pack_kernel, tiles, levels, plane, capac...  12 us
    pallas_call x2, Pallas kernels, backward_chunk(): pl.pallas_call(kernel, out_shape=tuple((jax.ShapeDtypeStruct(shape, jnp.f...  11.9 us
  transfers between devices with their start and end apart: 25, of which 13 were waited for; matrix products, arithmetic and copies ran while one was open for 2% of the time, Pallas kernels for 9%

profile of v2, /device:TPU:0, one launch (start us, length us, event | category | flops | bytes accessed | tf_op | source)
XLA Modules:
  0.0 164.1 jit_solution(13159174757902645004)
XLA Ops:
  1.6 2.4 %collective-permute-start.2 = (f32[32,640]{1,0:T(8,128)S(1)}, f32[32,640]{1,0:T(8,128)S(1)}, u32[]{:S(2)}, u32[]{:S(2)}) collective-permute-start(f32[32,640]{1,0:T(8,128)S(1)} %reshape.32), channel_id=1, source_target_pairs={{0,20},{4,24},{8,28},{12,16},{16,4},{20,8},{24,12},{28,0},{1,21},{... | collective-permute-start | bytes 245768 | tf_op jit(solution)/shard_map/ppermute | solution.py:613
  12.1 12.0 %pack.1 = (f32[8,48,256]{2,1,0:T(8,128)}, s32[64,128]{1,0:T(8,128)S(1)}) custom-call(s32[1]{0:T(128)S(6)} %copy.15.count_ref, s32[192,128]{1,0:T(8,128)S(1)} %pad_add_fusion.refs_0_, f32[128,128]{1,0:T(8,128)S(1)} %pad_maximum_fusion.refs_1_, f32[3,8192]{1,0:T(4,128)S(1)} %copy-done.3), custom_call_target="tpu_custom_call" | custom-call | flops 8589934592 | bytes 1048576 | tf_op jit(solution)/shard_map/pack/pallas_call | solution.py:146
  25.9 12.3 %ensemble.1 = (f32[8,32,128]{2,1,0:T(8,128)S(1)}, f32[8,32,128]{2,1,0:T(8,128)S(1)}, f32[8,32,128]{2,1,0:T(8,128)S(1)}, f32[8,32,128]{2,1,0:T(8,128)S(1)}) custom-call(s32[1]{0:T(128)} %bitcast.refs_0_, f32[8,32,640]{2,1,0:T(8,128)S(1)} %copy-done, f32[8,32,640]{2,1,0:T(8,128)S(1)} %collective-permute-done.refs_2_.refs_3_, ...), custom_call_target="tpu_custom_call" | custom-call | flops 8589934592 | bytes 8388608 | tf_op jit(solution)/shard_map/ensemble/pallas_call | solution.py:646
  39.9 2.6 %collective-permute-start.6 = (f32[8,32,128]{2,1,0:T(8,128)S(1)}, f32[8,32,128]{2,1,0:T(8,128)S(1)}, u32[]{:S(2)}, u32[]{:S(2)}) collective-permute-start(f32[8,32,128]{2,1,0:T(8,128)S(1)} %get-tuple-element.47), channel_id=1, source_target_pairs={{0,2},{1,3},{2,0},{3,1},{4,6},{5,7},{6,4},{7,5},{8,10},{9,11},{10,... | collective-permute-start | bytes 393224 | tf_op jit(solution)/shard_map/ppermute | solution.py:750
  43.8 2.7 %collective-permute-done.5 = f32[8,32,128]{2,1,0:T(8,128)S(1)} collective-permute-done((f32[8,32,128]{2,1,0:T(8,128)S(1)}, f32[8,32,128]{2,1,0:T(8,128)S(1)}, u32[]{:S(2)}, u32[]{:S(2)}) %collective-permute-start.5) | collective-permute-done | bytes 131104 | tf_op jit(solution)/shard_map/ppermute | solution.py:750
  46.5 4.7 %collective-permute-done.6 = f32[8,32,128]{2,1,0:T(8,128)S(1)} collective-permute-done((f32[8,32,128]{2,1,0:T(8,128)S(1)}, f32[8,32,128]{2,1,0:T(8,128)S(1)}, u32[]{:S(2)}, u32[]{:S(2)}) %collective-permute-start.6) | collective-permute-done | bytes 131104 | tf_op jit(solution)/shard_map/ppermute | solution.py:750
  51.3 4.4 %collective-permute-start.10 = (f32[8,32,128]{2,1,0:T(8,128)S(1)}, f32[8,32,128]{2,1,0:T(8,128)S(1)}, u32[]{:S(2)}, u32[]{:S(2)}) collective-permute-start(f32[8,32,128]{2,1,0:T(8,128)S(1)} %add_add_fusion.1.refs_1_), channel_id=1, source_target_pairs={{0,3},{1,0},{2,1},{3,2},{4,7},{5,4},{6,5},{7,6},{8,11},{9,8},{10,9... | collective-permute-start | bytes 393224 | tf_op jit(solution)/shard_map/ppermute | solution.py:756
  55.7 2.6 %collective-permute-done.10.refs_4_ = f32[8,32,128]{2,1,0:T(8,128)S(1)} collective-permute-done((f32[8,32,128]{2,1,0:T(8,128)S(1)}, f32[8,32,128]{2,1,0:T(8,128)S(1)}, u32[]{:S(2)}, u32[]{:S(2)}) %collective-permute-start.10) | collective-permute-done | bytes 131104 | tf_op jit(solution)/shard_map/ppermute | solution.py:756
  58.3 3.5 %all-to-all-start = ((f32[8,48,256]{2,1,0:T(8,128)}), f32[8,48,256]{2,1,0:T(8,128)S(1)}, u32[]{:S(2)}, u32[]{:S(2)}) async-start(f32[8,48,256]{2,1,0:T(8,128)} %get-tuple-element.51), calls=%async_computation | async-start | bytes 786432 | tf_op jit(solution)/shard_map/all_to_all | solution.py:784
  62.7 3.8 %collective-permute-start.8 = (f32[8,32,128]{2,1,0:T(8,128)S(1)}, f32[8,32,128]{2,1,0:T(8,128)S(1)}, u32[]{:S(2)}, u32[]{:S(2)}) collective-permute-start(f32[8,32,128]{2,1,0:T(8,128)S(1)} %add_add_fusion.1.refs_1_), channel_id=1, source_target_pairs={{0,1},{1,2},{2,3},{3,0},{4,5},{5,6},{6,7},{7,4},{8,9},{9,10},{10,1... | collective-permute-start | bytes 393224 | tf_op jit(solution)/shard_map/ppermute | solution.py:756
  66.6 7.5 %collective-permute-done.9.refs_3_ = f32[8,32,128]{2,1,0:T(8,128)S(1)} collective-permute-done((f32[8,32,128]{2,1,0:T(8,128)S(1)}, f32[8,32,128]{2,1,0:T(8,128)S(1)}, u32[]{:S(2)}, u32[]{:S(2)}) %collective-permute-start.9) | collective-permute-done | bytes 131104 | tf_op jit(solution)/shard_map/ppermute | solution.py:756
  74.1 18.2 %stencil.1 = (f32[8,8,256]{2,1,0:T(8,128)}, f32[8,32,128]{2,1,0:T(8,128)S(1)}, f32[8,32,128]{2,1,0:T(8,128)S(1)}, f32[8,32,128]{2,1,0:T(8,128)S(1)}, f32[8,32,128]{2,1,0:T(8,128)S(1)}) custom-call(s32[1]{0:T(128)} %bitcast.refs_0_, f32[8,32,128]{2,1,0:T(8,128)S(1)} %add_add_fusion.1.refs_1_, f32[8,32,128]{2,1,0:T(8,128)S(1)} %collective-permute-done.8.refs_2_, ...), custom_call_target="tpu_custom_call" | custom-call | flops 17179869184 | bytes 1048576 | tf_op jit(solution)/shard_map/stencil/pallas_call | solution.py:332
  93.6 2.8 %collective-permute-start.13 = (f32[8,32,128]{2,1,0:T(8,128)S(1)}, f32[8,32,128]{2,1,0:T(8,128)S(1)}, u32[]{:S(2)}, u32[]{:S(2)}) collective-permute-start(f32[8,32,128]{2,1,0:T(8,128)S(1)} %get-tuple-element.55), channel_id=1, source_target_pairs={{0,3},{1,0},{2,1},{3,2},{4,7},{5,4},{6,5},{7,6},{8,11},{9,8},{10,9... | collective-permute-start | bytes 393224 | tf_op jit(solution)/shard_map/ppermute | solution.py:750
  96.5 2.8 %collective-permute-done.11 = f32[8,32,128]{2,1,0:T(8,128)S(1)} collective-permute-done((f32[8,32,128]{2,1,0:T(8,128)S(1)}, f32[8,32,128]{2,1,0:T(8,128)S(1)}, u32[]{:S(2)}, u32[]{:S(2)}) %collective-permute-start.11) | collective-permute-done | bytes 131104 | tf_op jit(solution)/shard_map/ppermute | solution.py:750
  102.6 2.9 %collective-permute-start.16 = (f32[8,32,128]{2,1,0:T(8,128)S(1)}, f32[8,32,128]{2,1,0:T(8,128)S(1)}, u32[]{:S(2)}, u32[]{:S(2)}) collective-permute-start(f32[8,32,128]{2,1,0:T(8,128)S(1)} %add_add_fusion.refs_1_), channel_id=1, source_target_pairs={{0,3},{1,0},{2,1},{3,2},{4,7},{5,4},{6,5},{7,6},{8,11},{9,8},{10,9... | collective-permute-start | bytes 393224 | tf_op jit(solution)/shard_map/ppermute | solution.py:756
  105.5 2.5 %collective-permute-done.16.refs_4_ = f32[8,32,128]{2,1,0:T(8,128)S(1)} collective-permute-done((f32[8,32,128]{2,1,0:T(8,128)S(1)}, f32[8,32,128]{2,1,0:T(8,128)S(1)}, u32[]{:S(2)}, u32[]{:S(2)}) %collective-permute-start.16) | collective-permute-done | bytes 131104 | tf_op jit(solution)/shard_map/ppermute | solution.py:756
  108.0 7.0 %all-to-all-start.1 = ((f32[8,8,256]{2,1,0:T(8,128)}), f32[8,8,256]{2,1,0:T(8,128)S(1)}, u32[]{:S(2)}, u32[]{:S(2)}) async-start(f32[8,8,256]{2,1,0:T(8,128)} %get-tuple-element.59), calls=%async_computation.1 | async-start | bytes 131072 | tf_op jit(solution)/shard_map/all_to_all | solution.py:788
  116.3 3.5 %collective-permute-start.14 = (f32[8,32,128]{2,1,0:T(8,128)S(1)}, f32[8,32,128]{2,1,0:T(8,128)S(1)}, u32[]{:S(2)}, u32[]{:S(2)}) collective-permute-start(f32[8,32,128]{2,1,0:T(8,128)S(1)} %add_add_fusion.refs_1_), channel_id=1, source_target_pairs={{0,1},{1,2},{2,3},{3,0},{4,5},{5,6},{6,7},{7,4},{8,9},{9,10},{10,1... | collective-permute-start | bytes 393224 | tf_op jit(solution)/shard_map/ppermute | solution.py:756
  119.9 3.1 %unpack.1 = f32[64,128]{1,0:T(8,128)} custom-call(s32[64,128]{1,0:T(8,128)S(1)} %get-tuple-element.58.target_ref, f32[64,256]{1,0:T(8,128)S(1)} %bitcast.8), custom_call_target="tpu_custom_call" | custom-call | flops 2147483648 | bytes 262144 | tf_op jit(solution)/shard_map/unpack/pallas_call | solution.py:376
  123.0 4.5 %collective-permute-done.15.refs_3_ = f32[8,32,128]{2,1,0:T(8,128)S(1)} collective-permute-done((f32[8,32,128]{2,1,0:T(8,128)S(1)}, f32[8,32,128]{2,1,0:T(8,128)S(1)}, u32[]{:S(2)}, u32[]{:S(2)}) %collective-permute-start.15) | collective-permute-done | bytes 131104 | tf_op jit(solution)/shard_map/ppermute | solution.py:756
  127.4 4.9 %backward.2 = (f32[8,32,256]{2,1,0:T(8,128)S(1)}, f32[8,32,256]{2,1,0:T(8,128)S(1)}, f32[32,256]{1,0:T(8,128)S(1)}, f32[32,256]{1,0:T(8,128)S(1)}, f32[40,256]{1,0:T(8,128)S(1)}, /*index=5*/f32[40,256]{1,0:T(8,128)S(1)}) custom-call(s32[1]{0:T(128)} %bitcast.refs_0_, f32[8,32,128]{2,1,0:T(8,128)S(1)} %add_add_fusion.refs_1_, ...), custom_call_target="tpu_custom_call" | custom-call | flops 4294967296 | bytes 4194304 | tf_op jit(solution)/shard_map/backward/pallas_call | solution.py:693
  132.4 7.0 %backward.3 = (f32[8,32,384]{2,1,0:T(8,128)S(1)}, f32[8,32,384]{2,1,0:T(8,128)S(1)}, f32[32,640]{1,0:T(8,128)S(1)}, f32[32,640]{1,0:T(8,128)S(1)}, f32[40,640]{1...) custom-call(s32[1]{0:T(128)} %bitcast.refs_0_, f32[8,32,128]{2,1,0:T(8,128)S(1)} %add_add_fusion.refs_1_, ...), custom_call_target="tpu_custom_call" | custom-call | flops 4294967296 | bytes 4194304 | tf_op jit(solution)/shard_map/backward/pallas_call | solution.py:693
  141.5 14.3 %collective-permute-done.17 = f32[8,32,256]{2,1,0:T(8,128)S(1)} collective-permute-done((f32[8,32,256]{2,1,0:T(8,128)S(1)}, f32[8,32,256]{2,1,0:T(8,128)S(1)}, u32[]{:S(2)}, u32[]{:S(2)}) %collective-permute-start.17) | collective-permute-done | bytes 262176 | tf_op jit(solution)/shard_map/ppermute | solution.py:613
  155.9 2.4 %collective-permute-start.22 = (f32[40,640]{1,0:T(8,128)S(1)}, f32[40,640]{1,0:T(8,128)S(1)}, u32[]{:S(2)}, u32[]{:S(2)}) collective-permute-start(f32[40,640]{1,0:T(8,128)S(1)} %get-tuple-element.80), channel_id=1, source_target_pairs={{0,20},{4,24},{8,28},{12,16},{16,4},{20,8},{24,12},{28,0},{1,21},{... | collective-permute-start | bytes 307208 | tf_op jit(solution)/shard_map/ppermute | solution.py:613
  (52 shorter events, 28.0 us)
Async XLA Ops:
  1.6 22.5 %collective-permute-start.2 = (f32[32,640]{1,0:T(8,128)S(1)}, f32[32,640]{1,0:T(8,128)S(1)}, u32[]{:S(2)}, u32[]{:S(2)}) collective-permute-start(f32[32,640]{1,0:T(8,128)S(1)} %reshape.32), channel_id=1, source_target_pairs={{0,20},{4,24},{8,28},{12,16},{16,4},{20,8},{24,12},{28,0},{1,21},{... | collective-permute-start | bytes 245768 | tf_op jit(solution)/shard_map/ppermute | solution.py:613
  4.0 20.1 %collective-permute-start.1 = (f32[32,640]{1,0:T(8,128)S(1)}, f32[32,640]{1,0:T(8,128)S(1)}, u32[]{:S(2)}, u32[]{:S(2)}) collective-permute-start(f32[32,640]{1,0:T(8,128)S(1)} %reshape.32), channel_id=1, source_target_pairs={{0,4},{4,8},{8,12},{12,0},{16,20},{20,24},{24,28},{28,16},{1,5},{5... | collective-permute-start | bytes 245768 | tf_op jit(solution)/shard_map/ppermute | solution.py:613
  6.6 17.5 %collective-permute-start.4 = (f32[40,640]{1,0:T(8,128)S(1)}, f32[40,640]{1,0:T(8,128)S(1)}, u32[]{:S(2)}, u32[]{:S(2)}) collective-permute-start(f32[40,640]{1,0:T(8,128)S(1)} %reshape.33), channel_id=1, source_target_pairs={{0,28},{4,16},{8,20},{12,24},{16,12},{20,0},{24,4},{28,8},{1,29},{... | collective-permute-start | bytes 307208 | tf_op jit(solution)/shard_map/ppermute | solution.py:613
  6.9 17.3 %collective-permute-start.3 = (f32[40,640]{1,0:T(8,128)S(1)}, f32[40,640]{1,0:T(8,128)S(1)}, u32[]{:S(2)}, u32[]{:S(2)}) collective-permute-start(f32[40,640]{1,0:T(8,128)S(1)} %reshape.33), channel_id=1, source_target_pairs={{0,12},{4,0},{8,4},{12,8},{16,28},{20,16},{24,20},{28,24},{1,13},{... | collective-permute-start | bytes 307208 | tf_op jit(solution)/shard_map/ppermute | solution.py:613
  6.9 19.0 %collective-permute-start = (f32[8,32,640]{2,1,0:T(8,128)}, f32[8,32,640]{2,1,0:T(8,128)S(1)}, u32[]{:S(2)}, u32[]{:S(2)}) collective-permute-start(f32[8,32,640]{2,1,0:T(8,128)} %alpha_ref.1), channel_id=1, source_target_pairs={{0,16},{4,20},{8,24},{12,28},{16,0},{20,4},{24,8},{28,12},{1,17},{... | collective-permute-start | bytes 1966088 | tf_op jit(solution)/shard_map/ppermute | solution.py:613
  38.2 8.3 %collective-permute-start.5 = (f32[8,32,128]{2,1,0:T(8,128)S(1)}, f32[8,32,128]{2,1,0:T(8,128)S(1)}, u32[]{:S(2)}, u32[]{:S(2)}) collective-permute-start(f32[8,32,128]{2,1,0:T(8,128)S(1)} %get-tuple-element.46), channel_id=1, source_target_pairs={{0,1},{1,2},{2,3},{3,0},{4,5},{5,6},{6,7},{7,4},{8,9},{9,10},{10,1... | collective-permute-start | bytes 393224 | tf_op jit(solution)/shard_map/ppermute | solution.py:750
  39.9 11.4 %collective-permute-start.6 = (f32[8,32,128]{2,1,0:T(8,128)S(1)}, f32[8,32,128]{2,1,0:T(8,128)S(1)}, u32[]{:S(2)}, u32[]{:S(2)}) collective-permute-start(f32[8,32,128]{2,1,0:T(8,128)S(1)} %get-tuple-element.47), channel_id=1, source_target_pairs={{0,2},{1,3},{2,0},{3,1},{4,6},{5,7},{6,4},{7,5},{8,10},{9,11},{10,... | collective-permute-start | bytes 393224 | tf_op jit(solution)/shard_map/ppermute | solution.py:750
  42.5 8.8 %collective-permute-start.7 = (f32[8,32,128]{2,1,0:T(8,128)S(1)}, f32[8,32,128]{2,1,0:T(8,128)S(1)}, u32[]{:S(2)}, u32[]{:S(2)}) collective-permute-start(f32[8,32,128]{2,1,0:T(8,128)S(1)} %get-tuple-element.48), channel_id=1, source_target_pairs={{0,3},{1,0},{2,1},{3,2},{4,7},{5,4},{6,5},{7,6},{8,11},{9,8},{10,9... | collective-permute-start | bytes 393224 | tf_op jit(solution)/shard_map/ppermute | solution.py:750
  51.3 7.0 %collective-permute-start.10 = (f32[8,32,128]{2,1,0:T(8,128)S(1)}, f32[8,32,128]{2,1,0:T(8,128)S(1)}, u32[]{:S(2)}, u32[]{:S(2)}) collective-permute-start(f32[8,32,128]{2,1,0:T(8,128)S(1)} %add_add_fusion.1.refs_1_), channel_id=1, source_target_pairs={{0,3},{1,0},{2,1},{3,2},{4,7},{5,4},{6,5},{7,6},{8,11},{9,8},{10,9... | collective-permute-start | bytes 393224 | tf_op jit(solution)/shard_map/ppermute | solution.py:756
  58.3 15.8 %all-to-all-start = ((f32[8,48,256]{2,1,0:T(8,128)}), f32[8,48,256]{2,1,0:T(8,128)S(1)}, u32[]{:S(2)}, u32[]{:S(2)}) async-start(f32[8,48,256]{2,1,0:T(8,128)} %get-tuple-element.51), calls=%async_computation | async-start | bytes 786432 | tf_op jit(solution)/shard_map/all_to_all | solution.py:784
  61.8 12.3 %collective-permute-start.9 = (f32[8,32,128]{2,1,0:T(8,128)S(1)}, f32[8,32,128]{2,1,0:T(8,128)S(1)}, u32[]{:S(2)}, u32[]{:S(2)}) collective-permute-start(f32[8,32,128]{2,1,0:T(8,128)S(1)} %add_add_fusion.1.refs_1_), channel_id=1, source_target_pairs={{0,2},{1,3},{2,0},{3,1},{4,6},{5,7},{6,4},{7,5},{8,10},{9,11},{10,... | collective-permute-start | bytes 393224 | tf_op jit(solution)/shard_map/ppermute | solution.py:756
  62.7 11.3 %collective-permute-start.8 = (f32[8,32,128]{2,1,0:T(8,128)S(1)}, f32[8,32,128]{2,1,0:T(8,128)S(1)}, u32[]{:S(2)}, u32[]{:S(2)}) collective-permute-start(f32[8,32,128]{2,1,0:T(8,128)S(1)} %add_add_fusion.1.refs_1_), channel_id=1, source_target_pairs={{0,1},{1,2},{2,3},{3,0},{4,5},{5,6},{6,7},{7,4},{8,9},{9,10},{10,1... | collective-permute-start | bytes 393224 | tf_op jit(solution)/shard_map/ppermute | solution.py:756
  92.3 7.0 %collective-permute-start.11 = (f32[8,32,128]{2,1,0:T(8,128)S(1)}, f32[8,32,128]{2,1,0:T(8,128)S(1)}, u32[]{:S(2)}, u32[]{:S(2)}) collective-permute-start(f32[8,32,128]{2,1,0:T(8,128)S(1)} %get-tuple-element.53), channel_id=1, source_target_pairs={{0,1},{1,2},{2,3},{3,0},{4,5},{5,6},{6,7},{7,4},{8,9},{9,10},{10,1... | collective-permute-start | bytes 393224 | tf_op jit(solution)/shard_map/ppermute | solution.py:750
  92.4 9.0 %collective-permute-start.12 = (f32[8,32,128]{2,1,0:T(8,128)S(1)}, f32[8,32,128]{2,1,0:T(8,128)S(1)}, u32[]{:S(2)}, u32[]{:S(2)}) collective-permute-start(f32[8,32,128]{2,1,0:T(8,128)S(1)} %get-tuple-element.54), channel_id=1, source_target_pairs={{0,2},{1,3},{2,0},{3,1},{4,6},{5,7},{6,4},{7,5},{8,10},{9,11},{10,... | collective-permute-start | bytes 393224 | tf_op jit(solution)/shard_map/ppermute | solution.py:750
  93.6 8.9 %collective-permute-start.13 = (f32[8,32,128]{2,1,0:T(8,128)S(1)}, f32[8,32,128]{2,1,0:T(8,128)S(1)}, u32[]{:S(2)}, u32[]{:S(2)}) collective-permute-start(f32[8,32,128]{2,1,0:T(8,128)S(1)} %get-tuple-element.55), channel_id=1, source_target_pairs={{0,3},{1,0},{2,1},{3,2},{4,7},{5,4},{6,5},{7,6},{8,11},{9,8},{10,9... | collective-permute-start | bytes 393224 | tf_op jit(solution)/shard_map/ppermute | solution.py:750
  102.6 5.4 %collective-permute-start.16 = (f32[8,32,128]{2,1,0:T(8,128)S(1)}, f32[8,32,128]{2,1,0:T(8,128)S(1)}, u32[]{:S(2)}, u32[]{:S(2)}) collective-permute-start(f32[8,32,128]{2,1,0:T(8,128)S(1)} %add_add_fusion.refs_1_), channel_id=1, source_target_pairs={{0,3},{1,0},{2,1},{3,2},{4,7},{5,4},{6,5},{7,6},{8,11},{9,8},{10,9... | collective-permute-start | bytes 393224 | tf_op jit(solution)/shard_map/ppermute | solution.py:756
  108.0 11.8 %all-to-all-start.1 = ((f32[8,8,256]{2,1,0:T(8,128)}), f32[8,8,256]{2,1,0:T(8,128)S(1)}, u32[]{:S(2)}, u32[]{:S(2)}) async-start(f32[8,8,256]{2,1,0:T(8,128)} %get-tuple-element.59), calls=%async_computation.1 | async-start | bytes 131072 | tf_op jit(solution)/shard_map/all_to_all | solution.py:788
  115.0 12.4 %collective-permute-start.15 = (f32[8,32,128]{2,1,0:T(8,128)S(1)}, f32[8,32,128]{2,1,0:T(8,128)S(1)}, u32[]{:S(2)}, u32[]{:S(2)}) collective-permute-start(f32[8,32,128]{2,1,0:T(8,128)S(1)} %add_add_fusion.refs_1_), channel_id=1, source_target_pairs={{0,2},{1,3},{2,0},{3,1},{4,6},{5,7},{6,4},{7,5},{8,10},{9,11},{10,... | collective-permute-start | bytes 393224 | tf_op jit(solution)/shard_map/ppermute | solution.py:756
  116.3 11.1 %collective-permute-start.14 = (f32[8,32,128]{2,1,0:T(8,128)S(1)}, f32[8,32,128]{2,1,0:T(8,128)S(1)}, u32[]{:S(2)}, u32[]{:S(2)}) collective-permute-start(f32[8,32,128]{2,1,0:T(8,128)S(1)} %add_add_fusion.refs_1_), channel_id=1, source_target_pairs={{0,1},{1,2},{2,3},{3,0},{4,5},{5,6},{6,7},{7,4},{8,9},{9,10},{10,1... | collective-permute-start | bytes 393224 | tf_op jit(solution)/shard_map/ppermute | solution.py:756
  139.4 23.7 %collective-permute-start.18 = (f32[8,32,384]{2,1,0:T(8,128)S(1)}, f32[8,32,384]{2,1,0:T(8,128)S(1)}, u32[]{:S(2)}, u32[]{:S(2)}) collective-permute-start(f32[8,32,384]{2,1,0:T(8,128)S(1)} %get-tuple-element.76), channel_id=1, source_target_pairs={{0,16},{4,20},{8,24},{12,28},{16,0},{20,4},{24,8},{28,12},{1,17},{... | collective-permute-start | bytes 1179656 | tf_op jit(solution)/shard_map/ppermute | solution.py:613
  141.1 14.7 %collective-permute-start.17 = (f32[8,32,256]{2,1,0:T(8,128)S(1)}, f32[8,32,256]{2,1,0:T(8,128)S(1)}, u32[]{:S(2)}, u32[]{:S(2)}) collective-permute-start(f32[8,32,256]{2,1,0:T(8,128)S(1)} %get-tuple-element.73), channel_id=1, source_target_pairs={{0,16},{4,20},{8,24},{12,28},{16,0},{20,4},{24,8},{28,12},{1,17},{... | collective-permute-start | bytes 786440 | tf_op jit(solution)/shard_map/ppermute | solution.py:613
  155.8 7.2 %collective-permute-start.20 = (f32[40,640]{1,0:T(8,128)S(1)}, f32[40,640]{1,0:T(8,128)S(1)}, u32[]{:S(2)}, u32[]{:S(2)}) collective-permute-start(f32[40,640]{1,0:T(8,128)S(1)} %get-tuple-element.78), channel_id=1, source_target_pairs={{0,4},{4,8},{8,12},{12,0},{16,20},{20,24},{24,28},{28,16},{1,5},{5... | collective-permute-start | bytes 307208 | tf_op jit(solution)/shard_map/ppermute | solution.py:613
  155.9 7.2 %collective-permute-start.22 = (f32[40,640]{1,0:T(8,128)S(1)}, f32[40,640]{1,0:T(8,128)S(1)}, u32[]{:S(2)}, u32[]{:S(2)}) collective-permute-start(f32[40,640]{1,0:T(8,128)S(1)} %get-tuple-element.80), channel_id=1, source_target_pairs={{0,20},{4,24},{8,28},{12,16},{16,4},{20,8},{24,12},{28,0},{1,21},{... | collective-permute-start | bytes 307208 | tf_op jit(solution)/shard_map/ppermute | solution.py:613
  158.3 4.7 %collective-permute-start.21 = (f32[32,640]{1,0:T(8,128)S(1)}, f32[32,640]{1,0:T(8,128)S(1)}, u32[]{:S(2)}, u32[]{:S(2)}) collective-permute-start(f32[32,640]{1,0:T(8,128)S(1)} %get-tuple-element.79), channel_id=1, source_target_pairs={{0,28},{4,16},{8,20},{12,24},{16,12},{20,0},{24,4},{28,8},{1,29},{... | collective-permute-start | bytes 245768 | tf_op jit(solution)/shard_map/ppermute | solution.py:613
  (6 other events, 127.3 us)

commit v3 on v1

--- a/solution.py
+++ b/solution.py
@@ -21,8 +21,8 @@
 
 BLOCK = 256
 LANES = 128
-NARROW = 8
-WIDE = 16
+STEPS = (8, 12, 16)
+WIDE = STEPS[-1]
 HALF = jnp.bfloat16
 
 
@@ -47,11 +47,14 @@
     tiles, levels, plane, capacity,
     count_ref, *refs,
 ):
-    sources, (out_ref, target_ref, carry, total, gathered, *held), sems = refs[:6], refs[6:-1], refs[-1]
+    sources, (out_ref, target_ref, carry, total, gathered, *held), sems = refs[:3], refs[3:-1], refs[-1]
     copies = [pltpu.make_async_copy(source, here, sems.at[i]) for i, (source, here) in enumerate(zip(sources, held))]
     for copy in copies:
         copy.start()
-    owner_ref, level_ref, column_ref, frac_ref, innov_ref, rinv_ref = held
+    ints_ref, floats_ref, frac_ref = held
+    size = target_ref.shape[0]
+    owner_ref, level_ref, column_ref = [ints_ref.at[pl.ds(i * size, size)] for i in range(3)]
+    innov_ref, rinv_ref = [floats_ref.at[pl.ds(i * size, size)] for i in range(2)]
     blocks = target_ref.shape[0] * LANES // BLOCK
     keys = tiles * levels
     deep = capacity // BLOCK
@@ -70,18 +73,18 @@
 
     ones = jnp.ones((BLOCK, LANES), HALF)
     total[...] = jnp.zeros_like(total)
-    for copy in copies[:2]:
+    for copy in copies[:1]:
         copy.wait()
 
+    many = math.gcd(blocks, 8)
+
     def count_group(g, unused):
-        masks = [onehot(g * group + i)[1] for i in range(group)]
+        masks = [onehot(g * many + i)[1] for i in range(many)]
         counted = jnp.concatenate([jnp.where(mask, 1.0, 0.0).astype(HALF) for mask in masks], 1)
-        total[...] += dot_nn(counted, jnp.concatenate([ones] * group, 0))
+        total[...] += dot_nn(counted, jnp.concatenate([ones] * many, 0))
         return unused
 
-    lax.fori_loop(0, blocks // group, count_group, 0)
-    for copy in copies[2:]:
-        copy.wait()
+    lax.fori_loop(0, blocks // many, count_group, 0)
     high = jnp.floor(total[...] * (1.0 / LANES))
     low = total[...] - high * LANES
     row_key, col_key = iota((keys, keys), 0), iota((keys, keys), 1)
@@ -93,15 +96,25 @@
     prefix = jnp.concatenate([earlier, ones], 1)
     gathered[...] = jnp.zeros_like(gathered)
 
+    def rank_group(g, unused):
+        now = carry[...]
+        seen = [onehot(g * many + i) for i in range(many)]
+        ranks = [dot_nn(jnp.where(mask, 1.0, 0.0).astype(HALF), prefix) for live, mask in seen]
+        for i, ((live, mask), rank) in enumerate(zip(seen, ranks)):
+            here = rank[:, :BLOCK] + jnp.concatenate([now] * (BLOCK // LANES), 1)
+            now = now + rank[:, BLOCK:]
+            slot = jnp.sum(jnp.where(mask, here, 0.0), 0, keepdims=True)
+            target = jnp.where(live, slot.astype(jnp.int32), -1)
+            target_ref[pl.ds(2 * (g * many + i), 2), :] = jnp.concatenate([target[:, :LANES], target[:, LANES:]], 0)
+        carry[...] = now
+        return unused
+
+    lax.fori_loop(0, blocks // many, rank_group, 0)
+    for copy in copies[1:]:
+        copy.wait()
+
     def place(j):
-        live, mask = onehot(j)
-        ranks = dot_nn(jnp.where(mask, 1.0, 0.0).astype(HALF), prefix)
-        now = carry[...]
-        here = ranks[:, :BLOCK] + jnp.concatenate([now] * (BLOCK // LANES), 1)
-        carry[...] = now + ranks[:, BLOCK:]
-        slot = jnp.sum(jnp.where(mask, here, 0.0), 0, keepdims=True)
-        target = jnp.where(live, slot.astype(jnp.int32), -1)
-        target_ref[pl.ds(2 * j, 2), :] = jnp.concatenate([target[:, :LANES], target[:, LANES:]], 0)
+        target = row_of(target_ref, j)
         rows = jnp.where(iota((slot_rows, BLOCK), 0) == (target >> 8), 1.0, 0.0).astype(HALF)
         lanes = jnp.where(iota((BLOCK, BLOCK), 0) == (target & (BLOCK - 1)), 1.0, 0.0).astype(HALF)
         column = row_of(column_ref, j)
@@ -138,8 +151,7 @@
     slots = owner.shape[0]
     rows = slots // LANES
     deep = capacity // BLOCK
-    values = [value.reshape(rows, LANES) for value in (owner, level, column)]
-    values += [frac, innov.reshape(rows, LANES), rinv.reshape(rows, LANES)]
+    values = [jnp.concatenate(some).reshape(-1, LANES) for some in ((owner, level, column), (innov, rinv))] + [frac]
     vmem = pl.BlockSpec(memory_space=pltpu.VMEM)
     return pl.pallas_call(
         functools.partial(pack_kernel, tiles, levels, plane, capacity),
@@ -147,7 +159,7 @@
             jax.ShapeDtypeStruct((tiles, 6 * deep, BLOCK), jnp.float32),
             jax.ShapeDtypeStruct((rows, LANES), jnp.int32),
         ),
-        in_specs=[SMEM] + [HBM] * 6,
+        in_specs=[SMEM] + [HBM] * 3,
         out_specs=(vmem, vmem),
         scratch_shapes=[
             pltpu.VMEM((tiles * levels, LANES), jnp.float32),
@@ -157,7 +169,7 @@
         + [pltpu.VMEM(value.shape, value.dtype) for value in values]
         + [pltpu.SemaphoreType.DMA((len(values),))],
         compiler_params=room(16),
-        cost_estimate=pl.CostEstimate(flops=8 << 30, bytes_accessed=1 << 20, transcendentals=0),
+        cost_estimate=pl.CostEstimate(flops=1 << 20, bytes_accessed=1 << 20, transcendentals=0),
         name="pack",
     )(count, *values)
 
@@ -293,13 +305,10 @@
         needs = [spans_ref[row, 2 * half + 1] for row, half in numbers]
         most = functools.reduce(jnp.maximum, needs)
 
-        @pl.when((most > 0) & (most <= NARROW))
-        def _():
-            together(blocks, bottoms, NARROW)
-
-        @pl.when((most > NARROW) & (most <= WIDE))
-        def _():
-            together(blocks, bottoms, WIDE)
+        for below, reach in zip((0,) + STEPS, STEPS):
+            @pl.when((most > below) & (most <= reach))
+            def _():
+                together(blocks, bottoms, reach)
 
         @pl.when(most > WIDE)
         def _():
@@ -450,8 +459,8 @@
             ext[begin + i, EDGE + coarse_y:EDGE + coarse_y + REACH + 1, :] = right[
                 at * (REACH + 1):(at + 1) * (REACH + 1), :
             ]
-    spread_y = interpolation((fine_y, coarse_y + PAD), 0, 1, EDGE)
-    spread_y = jnp.concatenate([spread_y.astype(jnp.float32)] * 2, 1).astype(HALF)
+    spread_y = interpolation((coarse_y + PAD, fine_y), 1, 0, EDGE)
+    spread_y = jnp.concatenate([spread_y, spread_y], 0)
     high, low = mixing(mix_ref)
     mix = jnp.concatenate([high, high, low], 1)
 
@@ -462,13 +471,13 @@
             inner = field[1:-1]
             field = inner + field[2:] + field[:-2] + neighbours(inner)
         high, low = split_two(field * SCALE)
+        both = jnp.concatenate([high.astype(jnp.float32), low.astype(jnp.float32)], 1)
         for c in range(coarse_x + 1):
-            wide = dot_nn(spread_y, jnp.concatenate([high[c], low[c]], 0))
-            wide_high, wide_low = split_two(wide)
-            coarse[c, lanes, :] = dot_nt(mix, jnp.concatenate([wide_high, wide_low, wide_high], 1))
+            wide_high, wide_low = split_two(dot_nn(both[c].T.astype(HALF), spread_y))
+            coarse[c, lanes, :] = dot_nn(mix, jnp.concatenate([wide_high, wide_low, wide_high], 0))
         return unused
 
-    lax.fori_loop(0, channels // LANES, one_group, 0)
+    lax.fori_loop(0, channels // LANES, one_group, 0, unroll=True)
     fetch.wait()
     depth = coarse_x + 2
     spread_x = interpolation_rows(fine_x, depth, 2, False)
@@ -579,7 +588,7 @@
                 ]
         return unused
 
-    lax.fori_loop(0, channels // LANES, one_group, 0)
+    lax.fori_loop(0, channels // LANES, one_group, 0, unroll=True)
 
 
 def fold_kernel(places, alpha_ref, center_ref, *refs):
@@ -749,8 +758,9 @@
         obs_count, obs_owner[:, 0], obs_column, obs_level, obs_frac, innovation, obs_rinv,
     )
     partial, outgoing = ensemble(alpha, lv_sqrt, ens_pert, me, outgoing)
-    increment, outgoing = lax.optimization_barrier((owned_sum(partial), outgoing))
     incoming = lax.all_to_all(outgoing, ("tx", "ty"), split_axis=0, concat_axis=0, tiled=True)
+    partial, incoming = lax.optimization_barrier((partial, incoming))
+    increment = owned_sum(partial)
     departure, adjoint = stencil(gathered(increment), incoming, bg_sigma, static_ctrl, me)
     total, departure = lax.optimization_barrier((owned_sum(adjoint), departure))
     returned = lax.all_to_all(departure, ("tx", "ty"), split_axis=0, concat_axis=0, tiled=True)

time: 153 us -> 150 us (0.980)
  starting transfers between devices: 40.5 us -> 36.3 us
  Pallas kernels: 53.5 us -> 55.7 us
  waiting for transfers between devices: 50.1 us -> 48 us
  local copies, waits for them, and re-layouts: 6.62 us -> 4.66 us
  other arithmetic: 0.07 us -> 1.66 us
    pallas_call x1, Pallas kernels: 14.4 us -> 19.1 us  [stencil(): pl.pallas_call(kernel, out_shape=(jax.ShapeDtypeStruct((sources, deep, bl...]
    ppermute x6, starting transfers between devices: 11.8 us -> 9.45 us  [owned_sum(): lax.ppermute(parts[d], 'mem', [(i, (i + d) % count) for i in range(count)])]
    ppermute x6, waiting for transfers between devices: 14.8 us -> 12.8 us  [owned_sum(): lax.ppermute(parts[d], 'mem', [(i, (i + d) % count) for i in range(count)])]
    unnamed x20 -> x14, local copies, waits for them, and re-layouts: 4.71 us -> 2.72 us
    ppermute x6, waiting for transfers between devices: 21 us -> 19.4 us  [gathered(): lax.ppermute(own, 'mem', [(i, (i + d) % count) for i in range(count)])]
    concatenate x0 -> x2, other arithmetic: none -> 1.58 us  [pack(): jnp.concatenate(some).reshape(-1, LANES)]
  transfers between devices with their start and end apart: 24 -> 24, of which waited for: 9 -> 9; matrix products, arithmetic and copies ran while one was open for 1% -> 2% of each run, Pallas kernels for 10% -> 18%
where the time goes in v3:
time: 150 us; the launch traced here: 148 us
  Pallas kernels  55.7 us (37%)
  waiting for transfers between devices  48 us (32%)
  starting transfers between devices  36.3 us (24%)
  local copies, waits for them, and re-layouts  4.66 us (3%)
  other arithmetic  1.66 us (1%)
  between operations  1.5 us (1%)
    ppermute x6, waiting for transfers between devices, gathered(): lax.ppermute(own, 'mem', [(i, (i + d) % count) for i in range(count)])  19.4 us
    pallas_call x1, Pallas kernels, stencil(): pl.pallas_call(kernel, out_shape=(jax.ShapeDtypeStruct((sources, deep, bl...  19.1 us
    ppermute x10, waiting for transfers between devices, shifted(): return lax.ppermute(value, ('tx', 'ty'), pairs)  14.7 us
    ppermute x6, waiting for transfers between devices, owned_sum(): lax.ppermute(parts[d], 'mem', [(i, (i + d) % count) for i in range(count)])  12.8 us
    pallas_call x1, Pallas kernels, ensemble(): pl.pallas_call(kernel, out_shape=tuple((jax.ShapeDtypeStruct((levels // g...  12 us
    pallas_call x1, Pallas kernels, pack(): pl.pallas_call(functools.partial(pack_kernel, tiles, levels, plane, capac...  11.6 us
    ppermute x10, starting transfers between devices, shifted(): return lax.ppermute(value, ('tx', 'ty'), pairs)  11.5 us
    ppermute x6, starting transfers between devices, owned_sum(): lax.ppermute(parts[d], 'mem', [(i, (i + d) % count) for i in range(count)])  9.45 us
  transfers between devices with their start and end apart: 24, of which 9 were waited for; matrix products, arithmetic and copies ran while one was open for 2% of the time, Pallas kernels for 18%

profile of v3, /device:TPU:0, one launch (start us, length us, event | category | flops | bytes accessed | tf_op | source)
XLA Modules:
  0.0 147.9 jit_solution(13795149505117682377)
XLA Ops:
  0.6 3.0 %collective-permute-start = (f32[8,32,640]{2,1,0:T(8,128)}, f32[8,32,640]{2,1,0:T(8,128)S(1)}, u32[]{:S(2)}, u32[]{:S(2)}) collective-permute-start(f32[8,32,640]{2,1,0:T(8,128)} %alpha_ref.1), channel_id=1, source_target_pairs={{0,16},{4,20},{8,24},{12,28},{16,0},{20,4},{24,8},{28,12},{1,17},{... | collective-permute-start | bytes 1966088 | tf_op jit(solution)/shard_map/ppermute | solution.py:612
  4.7 1.6 %collective-permute-start.1 = (f32[32,640]{1,0:T(8,128)S(1)}, f32[32,640]{1,0:T(8,128)S(1)}, u32[]{:S(2)}, u32[]{:S(2)}) collective-permute-start(f32[32,640]{1,0:T(8,128)S(1)} %reshape.32), channel_id=1, source_target_pairs={{0,4},{4,8},{8,12},{12,0},{16,20},{20,24},{24,28},{28,16},{1,5},{5... | collective-permute-start | bytes 245768 | tf_op jit(solution)/shard_map/ppermute | solution.py:612
  12.2 11.6 %pack.1 = (f32[8,48,256]{2,1,0:T(8,128)}, s32[64,128]{1,0:T(8,128)S(1)}) custom-call(s32[1]{0:T(128)S(6)} %copy.15.count_ref, s32[192,128]{1,0:T(8,128)S(1)} %pad_add_fusion.refs_0_, f32[128,128]{1,0:T(8,128)S(1)} %pad_maximum_fusion.refs_1_, f32[3,8192]{1,0:T(4,128)S(1)} %copy-done.2), custom_call_target="tpu_custom_call" | custom-call | flops 1048576 | bytes 1048576 | tf_op jit(solution)/shard_map/pack/pallas_call | solution.py:156
  23.7 3.5 %all-to-all-start = ((f32[8,48,256]{2,1,0:T(8,128)}), f32[8,48,256]{2,1,0:T(8,128)S(1)}, u32[]{:S(2)}, u32[]{:S(2)}) async-start(f32[8,48,256]{2,1,0:T(8,128)} %get-tuple-element.41), calls=%async_computation | async-start | bytes 786432 | tf_op jit(solution)/shard_map/all_to_all | solution.py:761
  29.1 12.0 %ensemble.1 = (f32[8,32,128]{2,1,0:T(8,128)S(1)}, f32[8,32,128]{2,1,0:T(8,128)S(1)}, f32[8,32,128]{2,1,0:T(8,128)S(1)}, f32[8,32,128]{2,1,0:T(8,128)S(1)}) custom-call(s32[1]{0:T(128)} %bitcast.refs_0_, f32[8,32,640]{2,1,0:T(8,128)S(1)} %copy-done, f32[8,32,640]{2,1,0:T(8,128)S(1)} %collective-permute-done.refs_2_.refs_3_, ...), custom_call_target="tpu_custom_call" | custom-call | flops 8589934592 | bytes 8388608 | tf_op jit(solution)/shard_map/ensemble/pallas_call | solution.py:645
  41.1 1.7 %collective-permute-start.5 = (f32[8,32,128]{2,1,0:T(8,128)S(1)}, f32[8,32,128]{2,1,0:T(8,128)S(1)}, u32[]{:S(2)}, u32[]{:S(2)}) collective-permute-start(f32[8,32,128]{2,1,0:T(8,128)S(1)} %get-tuple-element.43), channel_id=1, source_target_pairs={{0,1},{1,2},{2,3},{3,0},{4,5},{5,6},{6,7},{7,4},{8,9},{9,10},{10,1... | collective-permute-start | bytes 393224 | tf_op jit(solution)/shard_map/ppermute | solution.py:729
  42.8 2.6 %collective-permute-start.6 = (f32[8,32,128]{2,1,0:T(8,128)S(1)}, f32[8,32,128]{2,1,0:T(8,128)S(1)}, u32[]{:S(2)}, u32[]{:S(2)}) collective-permute-start(f32[8,32,128]{2,1,0:T(8,128)S(1)} %get-tuple-element.44), channel_id=1, source_target_pairs={{0,2},{1,3},{2,0},{3,1},{4,6},{5,7},{6,4},{7,5},{8,10},{9,11},{10,... | collective-permute-start | bytes 393224 | tf_op jit(solution)/shard_map/ppermute | solution.py:729
  46.7 2.7 %collective-permute-done.5 = f32[8,32,128]{2,1,0:T(8,128)S(1)} collective-permute-done((f32[8,32,128]{2,1,0:T(8,128)S(1)}, f32[8,32,128]{2,1,0:T(8,128)S(1)}, u32[]{:S(2)}, u32[]{:S(2)}) %collective-permute-start.5) | collective-permute-done | bytes 131104 | tf_op jit(solution)/shard_map/ppermute | solution.py:729
  49.4 5.1 %collective-permute-done.6 = f32[8,32,128]{2,1,0:T(8,128)S(1)} collective-permute-done((f32[8,32,128]{2,1,0:T(8,128)S(1)}, f32[8,32,128]{2,1,0:T(8,128)S(1)}, u32[]{:S(2)}, u32[]{:S(2)}) %collective-permute-start.6) | collective-permute-done | bytes 131104 | tf_op jit(solution)/shard_map/ppermute | solution.py:729
  54.6 4.4 %collective-permute-start.10 = (f32[8,32,128]{2,1,0:T(8,128)S(1)}, f32[8,32,128]{2,1,0:T(8,128)S(1)}, u32[]{:S(2)}, u32[]{:S(2)}) collective-permute-start(f32[8,32,128]{2,1,0:T(8,128)S(1)} %add_add_fusion.1.refs_1_), channel_id=1, source_target_pairs={{0,3},{1,0},{2,1},{3,2},{4,7},{5,4},{6,5},{7,6},{8,11},{9,8},{10,9... | collective-permute-start | bytes 393224 | tf_op jit(solution)/shard_map/ppermute | solution.py:735
  59.6 3.3 %collective-permute-done.10.refs_4_ = f32[8,32,128]{2,1,0:T(8,128)S(1)} collective-permute-done((f32[8,32,128]{2,1,0:T(8,128)S(1)}, f32[8,32,128]{2,1,0:T(8,128)S(1)}, u32[]{:S(2)}, u32[]{:S(2)}) %collective-permute-start.10) | collective-permute-done | bytes 131104 | tf_op jit(solution)/shard_map/ppermute | solution.py:735
  62.9 8.3 %collective-permute-done.9.refs_3_ = f32[8,32,128]{2,1,0:T(8,128)S(1)} collective-permute-done((f32[8,32,128]{2,1,0:T(8,128)S(1)}, f32[8,32,128]{2,1,0:T(8,128)S(1)}, u32[]{:S(2)}, u32[]{:S(2)}) %collective-permute-start.9) | collective-permute-done | bytes 131104 | tf_op jit(solution)/shard_map/ppermute | solution.py:735
  71.2 19.1 %stencil.1 = (f32[8,8,256]{2,1,0:T(8,128)}, f32[8,32,128]{2,1,0:T(8,128)S(1)}, f32[8,32,128]{2,1,0:T(8,128)S(1)}, f32[8,32,128]{2,1,0:T(8,128)S(1)}, f32[8,32,128]{2,1,0:T(8,128)S(1)}) custom-call(s32[1]{0:T(128)} %bitcast.refs_0_, f32[8,32,128]{2,1,0:T(8,128)S(1)} %add_add_fusion.1.refs_1_, f32[8,32,128]{2,1,0:T(8,128)S(1)} %collective-permute-done.8.refs_2_, ...), custom_call_target="tpu_custom_call" | custom-call | flops 17179869184 | bytes 1048576 | tf_op jit(solution)/shard_map/stencil/pallas_call | solution.py:339
  90.5 3.7 %collective-permute-start.13 = (f32[8,32,128]{2,1,0:T(8,128)S(1)}, f32[8,32,128]{2,1,0:T(8,128)S(1)}, u32[]{:S(2)}, u32[]{:S(2)}) collective-permute-start(f32[8,32,128]{2,1,0:T(8,128)S(1)} %get-tuple-element.50), channel_id=1, source_target_pairs={{0,3},{1,0},{2,1},{3,2},{4,7},{5,4},{6,5},{7,6},{8,11},{9,8},{10,9... | collective-permute-start | bytes 393224 | tf_op jit(solution)/shard_map/ppermute | solution.py:729
  94.2 3.1 %collective-permute-done.11 = f32[8,32,128]{2,1,0:T(8,128)S(1)} collective-permute-done((f32[8,32,128]{2,1,0:T(8,128)S(1)}, f32[8,32,128]{2,1,0:T(8,128)S(1)}, u32[]{:S(2)}, u32[]{:S(2)}) %collective-permute-start.11) | collective-permute-done | bytes 131104 | tf_op jit(solution)/shard_map/ppermute | solution.py:729
  97.3 1.8 %collective-permute-done.12 = f32[8,32,128]{2,1,0:T(8,128)S(1)} collective-permute-done((f32[8,32,128]{2,1,0:T(8,128)S(1)}, f32[8,32,128]{2,1,0:T(8,128)S(1)}, u32[]{:S(2)}, u32[]{:S(2)}) %collective-permute-start.12) | collective-permute-done | bytes 131104 | tf_op jit(solution)/shard_map/ppermute | solution.py:729
  99.2 3.4 %all-to-all-start.1 = ((f32[8,8,256]{2,1,0:T(8,128)}), f32[8,8,256]{2,1,0:T(8,128)S(1)}, u32[]{:S(2)}, u32[]{:S(2)}) async-start(f32[8,8,256]{2,1,0:T(8,128)} %get-tuple-element.54), calls=%async_computation.1 | async-start | bytes 131072 | tf_op jit(solution)/shard_map/all_to_all | solution.py:766
  102.5 2.9 %collective-permute-start.16 = (f32[8,32,128]{2,1,0:T(8,128)S(1)}, f32[8,32,128]{2,1,0:T(8,128)S(1)}, u32[]{:S(2)}, u32[]{:S(2)}) collective-permute-start(f32[8,32,128]{2,1,0:T(8,128)S(1)} %add_add_fusion.refs_1_), channel_id=1, source_target_pairs={{0,3},{1,0},{2,1},{3,2},{4,7},{5,4},{6,5},{7,6},{8,11},{9,8},{10,9... | collective-permute-start | bytes 393224 | tf_op jit(solution)/shard_map/ppermute | solution.py:735
  107.3 3.1 %unpack.1 = f32[64,128]{1,0:T(8,128)} custom-call(s32[64,128]{1,0:T(8,128)S(1)} %get-tuple-element.53.target_ref, f32[64,256]{1,0:T(8,128)S(1)} %bitcast.8), custom_call_target="tpu_custom_call" | custom-call | flops 2147483648 | bytes 262144 | tf_op jit(solution)/shard_map/unpack/pallas_call | solution.py:383
  110.4 7.7 %collective-permute-done.15.refs_3_ = f32[8,32,128]{2,1,0:T(8,128)S(1)} collective-permute-done((f32[8,32,128]{2,1,0:T(8,128)S(1)}, f32[8,32,128]{2,1,0:T(8,128)S(1)}, u32[]{:S(2)}, u32[]{:S(2)}) %collective-permute-start.15) | collective-permute-done | bytes 131104 | tf_op jit(solution)/shard_map/ppermute | solution.py:735
  118.2 8.8 %backward.1 = (f32[32,32,128]{2,1,0:T(8,128)}, f32[8,32,640]{2,1,0:T(8,128)S(1)}, f32[8,32,640]{2,1,0:T(8,128)S(1)}, f32[32,640]{1,0:T(8,128)S(1)}, f32[32,640]{...) custom-call(s32[1]{0:T(128)} %bitcast.refs_0_, f32[8,32,128]{2,1,0:T(8,128)S(1)} %add_add_fusion.refs_1_, ...), custom_call_target="tpu_custom_call" | custom-call | flops 8589934592 | bytes 8388608 | tf_op jit(solution)/shard_map/backward/pallas_call | solution.py:687
  127.0 1.7 %collective-permute-start.17 = (f32[8,32,640]{2,1,0:T(8,128)S(1)}, f32[8,32,640]{2,1,0:T(8,128)S(1)}, u32[]{:S(2)}, u32[]{:S(2)}) collective-permute-start(f32[8,32,640]{2,1,0:T(8,128)S(1)} %get-tuple-element.60), channel_id=1, source_target_pairs={{0,16},{4,20},{8,24},{12,28},{16,0},{20,4},{24,8},{28,12},{1,17},{... | collective-permute-start | bytes 1966088 | tf_op jit(solution)/shard_map/ppermute | solution.py:612
  128.7 1.6 %collective-permute-start.21 = (f32[40,640]{1,0:T(8,128)S(1)}, f32[40,640]{1,0:T(8,128)S(1)}, u32[]{:S(2)}, u32[]{:S(2)}) collective-permute-start(f32[40,640]{1,0:T(8,128)S(1)} %get-tuple-element.64), channel_id=1, source_target_pairs={{0,4},{4,8},{8,12},{12,0},{16,20},{20,24},{24,28},{28,16},{1,5},{5... | collective-permute-start | bytes 307208 | tf_op jit(solution)/shard_map/ppermute | solution.py:612
  132.1 14.6 %collective-permute-done.18.refs_1_ = f32[32,640]{1,0:T(8,128)S(1)} collective-permute-done((f32[32,640]{1,0:T(8,128)S(1)}, f32[32,640]{1,0:T(8,128)S(1)}, u32[]{:S(2)}, u32[]{:S(2)}) %collective-permute-start.18) | collective-permute-done | bytes 81952 | tf_op jit(solution)/shard_map/ppermute | solution.py:612
  (52 shorter events, 15.0 us)
Async XLA Ops:
  0.6 26.6 %collective-permute-start = (f32[8,32,640]{2,1,0:T(8,128)}, f32[8,32,640]{2,1,0:T(8,128)S(1)}, u32[]{:S(2)}, u32[]{:S(2)}) collective-permute-start(f32[8,32,640]{2,1,0:T(8,128)} %alpha_ref.1), channel_id=1, source_target_pairs={{0,16},{4,20},{8,24},{12,28},{16,0},{20,4},{24,8},{28,12},{1,17},{... | collective-permute-start | bytes 1966088 | tf_op jit(solution)/shard_map/ppermute | solution.py:612
  4.6 22.6 %collective-permute-start.2 = (f32[32,640]{1,0:T(8,128)S(1)}, f32[32,640]{1,0:T(8,128)S(1)}, u32[]{:S(2)}, u32[]{:S(2)}) collective-permute-start(f32[32,640]{1,0:T(8,128)S(1)} %reshape.32), channel_id=1, source_target_pairs={{0,20},{4,24},{8,28},{12,16},{16,4},{20,8},{24,12},{28,0},{1,21},{... | collective-permute-start | bytes 245768 | tf_op jit(solution)/shard_map/ppermute | solution.py:612
  4.7 19.0 %collective-permute-start.1 = (f32[32,640]{1,0:T(8,128)S(1)}, f32[32,640]{1,0:T(8,128)S(1)}, u32[]{:S(2)}, u32[]{:S(2)}) collective-permute-start(f32[32,640]{1,0:T(8,128)S(1)} %reshape.32), channel_id=1, source_target_pairs={{0,4},{4,8},{8,12},{12,0},{16,20},{20,24},{24,28},{28,16},{1,5},{5... | collective-permute-start | bytes 245768 | tf_op jit(solution)/shard_map/ppermute | solution.py:612
  7.3 20.0 %collective-permute-start.4 = (f32[40,640]{1,0:T(8,128)S(1)}, f32[40,640]{1,0:T(8,128)S(1)}, u32[]{:S(2)}, u32[]{:S(2)}) collective-permute-start(f32[40,640]{1,0:T(8,128)S(1)} %reshape.33), channel_id=1, source_target_pairs={{0,28},{4,16},{8,20},{12,24},{16,12},{20,0},{24,4},{28,8},{1,29},{... | collective-permute-start | bytes 307208 | tf_op jit(solution)/shard_map/ppermute | solution.py:612
  8.4 18.9 %collective-permute-start.3 = (f32[40,640]{1,0:T(8,128)S(1)}, f32[40,640]{1,0:T(8,128)S(1)}, u32[]{:S(2)}, u32[]{:S(2)}) collective-permute-start(f32[40,640]{1,0:T(8,128)S(1)} %reshape.33), channel_id=1, source_target_pairs={{0,12},{4,0},{8,4},{12,8},{16,28},{20,16},{24,20},{28,24},{1,13},{... | collective-permute-start | bytes 307208 | tf_op jit(solution)/shard_map/ppermute | solution.py:612
  23.7 17.4 %all-to-all-start = ((f32[8,48,256]{2,1,0:T(8,128)}), f32[8,48,256]{2,1,0:T(8,128)S(1)}, u32[]{:S(2)}, u32[]{:S(2)}) async-start(f32[8,48,256]{2,1,0:T(8,128)} %get-tuple-element.41), calls=%async_computation | async-start | bytes 786432 | tf_op jit(solution)/shard_map/all_to_all | solution.py:761
  41.1 8.3 %collective-permute-start.5 = (f32[8,32,128]{2,1,0:T(8,128)S(1)}, f32[8,32,128]{2,1,0:T(8,128)S(1)}, u32[]{:S(2)}, u32[]{:S(2)}) collective-permute-start(f32[8,32,128]{2,1,0:T(8,128)S(1)} %get-tuple-element.43), channel_id=1, source_target_pairs={{0,1},{1,2},{2,3},{3,0},{4,5},{5,6},{6,7},{7,4},{8,9},{9,10},{10,1... | collective-permute-start | bytes 393224 | tf_op jit(solution)/shard_map/ppermute | solution.py:729
  42.8 11.7 %collective-permute-start.6 = (f32[8,32,128]{2,1,0:T(8,128)S(1)}, f32[8,32,128]{2,1,0:T(8,128)S(1)}, u32[]{:S(2)}, u32[]{:S(2)}) collective-permute-start(f32[8,32,128]{2,1,0:T(8,128)S(1)} %get-tuple-element.44), channel_id=1, source_target_pairs={{0,2},{1,3},{2,0},{3,1},{4,6},{5,7},{6,4},{7,5},{8,10},{9,11},{10,... | collective-permute-start | bytes 393224 | tf_op jit(solution)/shard_map/ppermute | solution.py:729
  45.4 9.2 %collective-permute-start.7 = (f32[8,32,128]{2,1,0:T(8,128)S(1)}, f32[8,32,128]{2,1,0:T(8,128)S(1)}, u32[]{:S(2)}, u32[]{:S(2)}) collective-permute-start(f32[8,32,128]{2,1,0:T(8,128)S(1)} %get-tuple-element.45), channel_id=1, source_target_pairs={{0,3},{1,0},{2,1},{3,2},{4,7},{5,4},{6,5},{7,6},{8,11},{9,8},{10,9... | collective-permute-start | bytes 393224 | tf_op jit(solution)/shard_map/ppermute | solution.py:729
  54.6 8.3 %collective-permute-start.10 = (f32[8,32,128]{2,1,0:T(8,128)S(1)}, f32[8,32,128]{2,1,0:T(8,128)S(1)}, u32[]{:S(2)}, u32[]{:S(2)}) collective-permute-start(f32[8,32,128]{2,1,0:T(8,128)S(1)} %add_add_fusion.1.refs_1_), channel_id=1, source_target_pairs={{0,3},{1,0},{2,1},{3,2},{4,7},{5,4},{6,5},{7,6},{8,11},{9,8},{10,9... | collective-permute-start | bytes 393224 | tf_op jit(solution)/shard_map/ppermute | solution.py:735
  59.0 12.2 %collective-permute-start.9 = (f32[8,32,128]{2,1,0:T(8,128)S(1)}, f32[8,32,128]{2,1,0:T(8,128)S(1)}, u32[]{:S(2)}, u32[]{:S(2)}) collective-permute-start(f32[8,32,128]{2,1,0:T(8,128)S(1)} %add_add_fusion.1.refs_1_), channel_id=1, source_target_pairs={{0,2},{1,3},{2,0},{3,1},{4,6},{5,7},{6,4},{7,5},{8,10},{9,11},{10,... | collective-permute-start | bytes 393224 | tf_op jit(solution)/shard_map/ppermute | solution.py:735
  59.4 11.8 %collective-permute-start.8 = (f32[8,32,128]{2,1,0:T(8,128)S(1)}, f32[8,32,128]{2,1,0:T(8,128)S(1)}, u32[]{:S(2)}, u32[]{:S(2)}) collective-permute-start(f32[8,32,128]{2,1,0:T(8,128)S(1)} %add_add_fusion.1.refs_1_), channel_id=1, source_target_pairs={{0,1},{1,2},{2,3},{3,0},{4,5},{5,6},{6,7},{7,4},{8,9},{9,10},{10,1... | collective-permute-start | bytes 393224 | tf_op jit(solution)/shard_map/ppermute | solution.py:735
  90.3 7.0 %collective-permute-start.11 = (f32[8,32,128]{2,1,0:T(8,128)S(1)}, f32[8,32,128]{2,1,0:T(8,128)S(1)}, u32[]{:S(2)}, u32[]{:S(2)}) collective-permute-start(f32[8,32,128]{2,1,0:T(8,128)S(1)} %get-tuple-element.48), channel_id=1, source_target_pairs={{0,1},{1,2},{2,3},{3,0},{4,5},{5,6},{6,7},{7,4},{8,9},{9,10},{10,1... | collective-permute-start | bytes 393224 | tf_op jit(solution)/shard_map/ppermute | solution.py:729
  90.4 8.7 %collective-permute-start.12 = (f32[8,32,128]{2,1,0:T(8,128)S(1)}, f32[8,32,128]{2,1,0:T(8,128)S(1)}, u32[]{:S(2)}, u32[]{:S(2)}) collective-permute-start(f32[8,32,128]{2,1,0:T(8,128)S(1)} %get-tuple-element.49), channel_id=1, source_target_pairs={{0,2},{1,3},{2,0},{3,1},{4,6},{5,7},{6,4},{7,5},{8,10},{9,11},{10,... | collective-permute-start | bytes 393224 | tf_op jit(solution)/shard_map/ppermute | solution.py:729
  90.5 8.7 %collective-permute-start.13 = (f32[8,32,128]{2,1,0:T(8,128)S(1)}, f32[8,32,128]{2,1,0:T(8,128)S(1)}, u32[]{:S(2)}, u32[]{:S(2)}) collective-permute-start(f32[8,32,128]{2,1,0:T(8,128)S(1)} %get-tuple-element.50), channel_id=1, source_target_pairs={{0,3},{1,0},{2,1},{3,2},{4,7},{5,4},{6,5},{7,6},{8,11},{9,8},{10,9... | collective-permute-start | bytes 393224 | tf_op jit(solution)/shard_map/ppermute | solution.py:729
  99.2 8.1 %all-to-all-start.1 = ((f32[8,8,256]{2,1,0:T(8,128)}), f32[8,8,256]{2,1,0:T(8,128)S(1)}, u32[]{:S(2)}, u32[]{:S(2)}) async-start(f32[8,8,256]{2,1,0:T(8,128)} %get-tuple-element.54), calls=%async_computation.1 | async-start | bytes 131072 | tf_op jit(solution)/shard_map/all_to_all | solution.py:766
  102.5 7.9 %collective-permute-start.16 = (f32[8,32,128]{2,1,0:T(8,128)S(1)}, f32[8,32,128]{2,1,0:T(8,128)S(1)}, u32[]{:S(2)}, u32[]{:S(2)}) collective-permute-start(f32[8,32,128]{2,1,0:T(8,128)S(1)} %add_add_fusion.refs_1_), channel_id=1, source_target_pairs={{0,3},{1,0},{2,1},{3,2},{4,7},{5,4},{6,5},{7,6},{8,11},{9,8},{10,9... | collective-permute-start | bytes 393224 | tf_op jit(solution)/shard_map/ppermute | solution.py:735
  105.4 12.7 %collective-permute-start.15 = (f32[8,32,128]{2,1,0:T(8,128)S(1)}, f32[8,32,128]{2,1,0:T(8,128)S(1)}, u32[]{:S(2)}, u32[]{:S(2)}) collective-permute-start(f32[8,32,128]{2,1,0:T(8,128)S(1)} %add_add_fusion.refs_1_), channel_id=1, source_target_pairs={{0,2},{1,3},{2,0},{3,1},{4,6},{5,7},{6,4},{7,5},{8,10},{9,11},{10,... | collective-permute-start | bytes 393224 | tf_op jit(solution)/shard_map/ppermute | solution.py:735
  106.0 12.2 %collective-permute-start.14 = (f32[8,32,128]{2,1,0:T(8,128)S(1)}, f32[8,32,128]{2,1,0:T(8,128)S(1)}, u32[]{:S(2)}, u32[]{:S(2)}) collective-permute-start(f32[8,32,128]{2,1,0:T(8,128)S(1)} %add_add_fusion.refs_1_), channel_id=1, source_target_pairs={{0,1},{1,2},{2,3},{3,0},{4,5},{5,6},{6,7},{7,4},{8,9},{9,10},{10,1... | collective-permute-start | bytes 393224 | tf_op jit(solution)/shard_map/ppermute | solution.py:735
  127.0 19.7 %collective-permute-start.17 = (f32[8,32,640]{2,1,0:T(8,128)S(1)}, f32[8,32,640]{2,1,0:T(8,128)S(1)}, u32[]{:S(2)}, u32[]{:S(2)}) collective-permute-start(f32[8,32,640]{2,1,0:T(8,128)S(1)} %get-tuple-element.60), channel_id=1, source_target_pairs={{0,16},{4,20},{8,24},{12,28},{16,0},{20,4},{24,8},{28,12},{1,17},{... | collective-permute-start | bytes 1966088 | tf_op jit(solution)/shard_map/ppermute | solution.py:612
  128.7 18.0 %collective-permute-start.19 = (f32[40,640]{1,0:T(8,128)S(1)}, f32[40,640]{1,0:T(8,128)S(1)}, u32[]{:S(2)}, u32[]{:S(2)}) collective-permute-start(f32[40,640]{1,0:T(8,128)S(1)} %get-tuple-element.62), channel_id=1, source_target_pairs={{0,20},{4,24},{8,28},{12,16},{16,4},{20,8},{24,12},{28,0},{1,21},{... | collective-permute-start | bytes 307208 | tf_op jit(solution)/shard_map/ppermute | solution.py:612
  128.7 18.0 %collective-permute-start.21 = (f32[40,640]{1,0:T(8,128)S(1)}, f32[40,640]{1,0:T(8,128)S(1)}, u32[]{:S(2)}, u32[]{:S(2)}) collective-permute-start(f32[40,640]{1,0:T(8,128)S(1)} %get-tuple-element.64), channel_id=1, source_target_pairs={{0,4},{4,8},{8,12},{12,0},{16,20},{20,24},{24,28},{28,16},{1,5},{5... | collective-permute-start | bytes 307208 | tf_op jit(solution)/shard_map/ppermute | solution.py:612
  130.3 16.4 %collective-permute-start.18 = (f32[32,640]{1,0:T(8,128)S(1)}, f32[32,640]{1,0:T(8,128)S(1)}, u32[]{:S(2)}, u32[]{:S(2)}) collective-permute-start(f32[32,640]{1,0:T(8,128)S(1)} %get-tuple-element.61), channel_id=1, source_target_pairs={{0,28},{4,16},{8,20},{12,24},{16,12},{20,0},{24,4},{28,8},{1,29},{... | collective-permute-start | bytes 245768 | tf_op jit(solution)/shard_map/ppermute | solution.py:612
  131.4 15.3 %collective-permute-start.20 = (f32[32,640]{1,0:T(8,128)S(1)}, f32[32,640]{1,0:T(8,128)S(1)}, u32[]{:S(2)}, u32[]{:S(2)}) collective-permute-start(f32[32,640]{1,0:T(8,128)S(1)} %get-tuple-element.63), channel_id=1, source_target_pairs={{0,12},{4,0},{8,4},{12,8},{16,28},{20,16},{24,20},{28,24},{1,13},{... | collective-permute-start | bytes 245768 | tf_op jit(solution)/shard_map/ppermute | solution.py:612
  (7 other events, 143.5 us)

commit v4 on v3

--- a/solution.py
+++ b/solution.py
@@ -47,7 +47,7 @@
     tiles, levels, plane, capacity,
     count_ref, *refs,
 ):
-    sources, (out_ref, target_ref, carry, total, gathered, *held), sems = refs[:3], refs[3:-1], refs[-1]
+    sources, (out_ref, target_ref, carry, total, gathered, left_a, right_a, left_b, right_b, *held), sems = refs[:3], refs[3:-1], refs[-1]
     copies = [pltpu.make_async_copy(source, here, sems.at[i]) for i, (source, here) in enumerate(zip(sources, held))]
     for copy in copies:
         copy.start()
@@ -127,14 +127,23 @@
         spread = [rows * jnp.concatenate([term] * (slot_rows // 16), 0) for term in terms]
         return jnp.concatenate(spread, 0), lanes
 
-    def scatter_group(g, unused):
-        placed = [place(g * group + i) for i in range(group)]
-        left = jnp.concatenate([a for a, b in placed], 1)
-        right = jnp.concatenate([b for a, b in placed], 1)
-        gathered[...] += dot_nt(left, right)
+    def build(g, left, right):
+        for i in range(group):
+            lanes = slice(i * BLOCK, (i + 1) * BLOCK)
+            left[:, lanes], right[:, lanes] = place(g * group + i)
+
+    def multiply(left, right):
+        gathered[...] += dot_nt(left[...], right[...])
+
+    def scatter_pair(g, unused):
+        build(2 * g + 1, left_b, right_b)
+        multiply(left_a, right_a)
+        build(jnp.minimum(2 * g + 2, blocks // group - 1), left_a, right_a)
+        multiply(left_b, right_b)
         return unused
 
-    lax.fori_loop(0, blocks // group, scatter_group, 0)
+    build(0, left_a, right_a)
+    lax.fori_loop(0, blocks // (2 * group), scatter_pair, 0)
 
     def part(index, tile):
         begin = index * slot_rows + tile * deep
@@ -166,6 +175,7 @@
             pltpu.VMEM((tiles * levels, LANES), jnp.float32),
             pltpu.VMEM((13 * tiles * deep, BLOCK), jnp.float32),
         ]
+        + [pltpu.VMEM((count_rows, 4 * BLOCK), HALF) for count_rows in (13 * tiles * deep, BLOCK) * 2]
         + [pltpu.VMEM(value.shape, value.dtype) for value in values]
         + [pltpu.SemaphoreType.DMA((len(values),))],
         compiler_params=room(16),
@@ -237,10 +247,9 @@
 
         def weights(bottom, reach):
             offset = level - bottom.astype(jnp.float32)
-            picks = []
-            for g in range(reach):
-                pick_l = jnp.where(offset == float(g), 1.0 - frac_l, 0.0) + jnp.where(offset == float(g - 1), frac_l, 0.0)
-                picks.append(pick_x * pick_l)
+            rows_l = iota((reach, LANES), 0).astype(jnp.float32)
+            pick_l = jnp.where(rows_l == offset, 1.0 - frac_l, 0.0) + jnp.where(rows_l == offset + 1.0, frac_l, 0.0)
+            picks = [pick_x * pick_l[g:g + 1] for g in range(reach)]
             return jnp.concatenate(split_two(jnp.concatenate(picks, 0)), 1)
 
         def finish(picked):
@@ -426,6 +435,16 @@
         tiled = dot_nt(dot_nn(tile, term).astype(HALF), tile)
         terms.append(jnp.where(same, tiled, 0.0).astype(HALF))
     return terms
+
+
+def corner_counts(coarse_x, joined):
+    above = [[j, j + 1] for j in range(REACH)]
+    below = [[REACH - i, REACH + 1 - i] for i in range(REACH + 1)]
+    if not joined:
+        return [above, below]
+    gap = [[0, 0]] * (coarse_x - REACH)
+    high, low = gap + above, below + gap[1:]
+    return [[[max(a, b) for a, b in zip(*pair)] for pair in zip(high, low)]]
 
 
 def neighbours(field):
@@ -511,7 +530,7 @@
 
 
 def backward_kernel(
-    coarse_x, coarse_y, joined,
+    coarse_x, coarse_y, joined, strips,
     me_ref, parts_refs, mix_ref, sigma_ref, static_ref, pert_hbm,
     grad_ref, center_ref, middle_refs, left_refs, right_refs,
     adjoint, coarse, pert_ref, sems,
@@ -580,12 +599,14 @@
         center_ref[:, :, lanes] = inside[:, EDGE:EDGE + coarse_y]
         for ref, value in zip(middle_refs, outside):
             ref[:, :, lanes] = value[:, EDGE:EDGE + coarse_y]
-        for left, right, value in zip(left_refs, right_refs, [inside] + outside):
-            for i in range(value.shape[0]):
-                left[i * REACH:(i + 1) * REACH, lanes] = value[i, EDGE - REACH:EDGE]
-                right[i * (REACH + 1):(i + 1) * (REACH + 1), lanes] = value[
-                    i, EDGE + coarse_y:EDGE + coarse_y + REACH + 1
-                ]
+        for left, right, value, counts in zip(left_refs, right_refs, [inside] + outside, strips):
+            at_left, at_right = 0, 0
+            for i, (to_left, to_right) in enumerate(counts):
+                if to_left:
+                    left[at_left:at_left + to_left, lanes] = value[i, EDGE - to_left:EDGE]
+                if to_right:
+                    right[at_right:at_right + to_right, lanes] = value[i, EDGE + coarse_y:EDGE + coarse_y + to_right]
+                at_left, at_right = at_left + to_left, at_right + to_right
         return unused
 
     lax.fori_loop(0, channels // LANES, one_group, 0, unroll=True)
@@ -593,13 +614,18 @@
 
 def fold_kernel(places, alpha_ref, center_ref, *refs):
     part_refs, out_ref = refs[:-1], refs[-1]
+    coarse_y = out_ref.shape[1]
     out_ref[...] = alpha_ref[...] + center_ref[...]
-    for (row, count, column, width), ref in zip(places, part_refs):
-        if width == out_ref.shape[1]:
-            out_ref[row:row + count] += ref[...]
-        else:
-            for i in range(count):
-                out_ref[row + i, column:column + width, :] += ref[i * width:(i + 1) * width, :]
+    for (row, counts, at_end), ref in zip(places, part_refs):
+        if at_end is None:
+            out_ref[row:row + counts] += ref[...]
+            continue
+        at = 0
+        for i, count in enumerate(counts):
+            if count:
+                begin = coarse_y - count if at_end else 0
+                out_ref[row + i, begin:begin + count, :] += ref[at:at + count, :]
+            at += count
 
 
 def shifted(value, by_x, by_y):
@@ -660,17 +686,16 @@
     return parts, beside
 
 
-def backward(alpha, adjoint_parts, mix, bg_sigma, static_ctrl, ens_pert, me):
+def backward(alpha, adjoint_parts, mix, bg_sigma, static_ctrl, ens_pert, me, beside):
     coarse_x, coarse_y, channels = alpha.shape
     members, levels, fine_x, fine_y = ens_pert.shape
     joined = lax.axis_size("tx") == 2
     groups = len(adjoint_parts)
     outside = [coarse_x] if joined else [REACH, REACH + 1]
-    strips = [coarse_x] + outside
+    strips = [[[REACH, REACH + 1]] * coarse_x] + corner_counts(coarse_x, joined)
     shapes = [bg_sigma.shape, alpha.shape]
     shapes += [(rows, coarse_y, channels) for rows in outside]
-    shapes += [(rows * REACH, channels) for rows in strips]
-    shapes += [(rows * (REACH + 1), channels) for rows in strips]
+    shapes += [(sum(count[side] for count in counts), channels) for side in range(2) for counts in strips]
     n_in, n_mid, n_strip = 5 + groups, len(outside), len(strips)
 
     def kernel(*refs):
@@ -680,7 +705,7 @@
         left = outs[2 + n_mid:2 + n_mid + n_strip]
         right = outs[2 + n_mid + n_strip:]
         backward_kernel(
-            coarse_x, coarse_y, joined, me_ref, parts, *rest,
+            coarse_x, coarse_y, joined, strips, me_ref, parts, *rest,
             outs[0], outs[1], middle, left, right, *refs[n_in + len(shapes):]
         )
 
@@ -699,17 +724,18 @@
         cost_estimate=pl.CostEstimate(flops=8 << 30, bytes_accessed=8 << 20, transcendentals=0),
         name="backward",
     )(me, *adjoint_parts, mix, bg_sigma, static_ctrl, ens_pert)
+    results, beside = lax.optimization_barrier((results, beside))
     grad_static, center = results[:2]
     middle = results[2:2 + n_mid]
     left, right = results[2 + n_mid:2 + n_mid + n_strip], results[2 + n_mid + n_strip:]
-    last, wide = coarse_y - REACH, REACH + 1
-    moves = [(1, 0, coarse_x)] if joined else [(-1, coarse_x - REACH, REACH), (1, 0, REACH + 1)]
+    moves = [(1, 0)] if joined else [(-1, coarse_x - REACH), (1, 0)]
     places, parts = [], []
-    for (by, row, count), value, to_left, to_right in zip(moves, middle, left[1:], right[1:]):
-        parts += [shifted(value, by, 0), shifted(to_left, by, -1), shifted(to_right, by, 1)]
-        places += [(row, count, 0, coarse_y), (row, count, last, REACH), (row, count, 0, wide)]
-    parts += [shifted(left[0], 0, -1), shifted(right[0], 0, 1)]
-    places += [(0, coarse_x, last, REACH), (0, coarse_x, 0, wide)]
+    for (by, row), value in zip(moves, middle):
+        parts.append(shifted(value, by, 0))
+        places.append((row, value.shape[0], None))
+    for (by, row), counts, to_left, to_right in zip([(0, 0)] + moves, strips, left, right):
+        parts += [shifted(to_left, by, -1), shifted(to_right, by, 1)]
+        places += [(row, [count[0] for count in counts], True), (row, [count[1] for count in counts], False)]
     grad_alpha = pl.pallas_call(
         functools.partial(fold_kernel, places),
         out_shape=jax.ShapeDtypeStruct(alpha.shape, jnp.float32),
@@ -719,7 +745,7 @@
         cost_estimate=pl.CostEstimate(flops=1 << 20, bytes_accessed=2 << 20, transcendentals=0),
         name="fold",
     )(alpha, center, *parts)
-    return grad_alpha, grad_static
+    return grad_alpha, grad_static, beside
 
 
 def owned_sum(parts):
@@ -762,11 +788,12 @@
     partial, incoming = lax.optimization_barrier((partial, incoming))
     increment = owned_sum(partial)
     departure, adjoint = stencil(gathered(increment), incoming, bg_sigma, static_ctrl, me)
-    total, departure = lax.optimization_barrier((owned_sum(adjoint), departure))
+    parts, departure = lax.optimization_barrier((gathered(owned_sum(adjoint)), departure))
     returned = lax.all_to_all(departure, ("tx", "ty"), split_axis=0, concat_axis=0, tiled=True)
+    grad_alpha, grad_static, returned = backward(
+        alpha, parts, lv_sqrt, bg_sigma, static_ctrl, ens_pert, me, returned
+    )
     departures = unpack(target, returned.reshape(-1, BLOCK))
-    parts, departures = lax.optimization_barrier((gathered(total), departures))
-    grad_alpha, grad_static = backward(alpha, parts, lv_sqrt, bg_sigma, static_ctrl, ens_pert, me)
     return (grad_alpha, grad_static, departures)
 
 

time: 150 us -> 149 us (level)
  starting transfers between devices: 36.3 us -> 45.7 us
  waiting for transfers between devices: 48 us -> 42.3 us
  Pallas kernels: 55.7 us -> 51.6 us
    ppermute x10, waiting for transfers between devices: 14.7 us -> 10.9 us  [shifted(): return lax.ppermute(value, ('tx', 'ty'), pairs)]
    all_to_all x1, starting transfers between devices: 3.36 us -> 7.07 us  [per_device(): lax.all_to_all(departure, ('tx', 'ty'), split_axis=0, concat_axis=0, tile...]
    pallas_call x1, Pallas kernels: 19.1 us -> 15.5 us  [stencil(): pl.pallas_call(kernel, out_shape=(jax.ShapeDtypeStruct((sources, deep, bl...]
    ppermute x6, starting transfers between devices: 9.45 us -> 12.7 us  [owned_sum(): lax.ppermute(parts[d], 'mem', [(i, (i + d) % count) for i in range(count)])]
    ppermute x6, starting transfers between devices: 8.56 us -> 10.4 us  [gathered(): lax.ppermute(own, 'mem', [(i, (i + d) % count) for i in range(count)])]
  transfers between devices with their start and end apart: 24 -> 24, of which waited for: 9 -> 10; matrix products, arithmetic and copies ran while one was open for 2% -> 2% of each run, Pallas kernels for 18% -> 24%
where the time goes in v4:
time: 149 us; the launch traced here: 148 us
  Pallas kernels  51.6 us (35%)
  starting transfers between devices  45.7 us (31%)
  waiting for transfers between devices  42.3 us (28%)
  local copies, waits for them, and re-layouts  4.67 us (3%)
  other arithmetic  1.65 us (1%)
    ppermute x6, waiting for transfers between devices, gathered(): lax.ppermute(own, 'mem', [(i, (i + d) % count) for i in range(count)])  19.4 us
    pallas_call x1, Pallas kernels, stencil(): pl.pallas_call(kernel, out_shape=(jax.ShapeDtypeStruct((sources, deep, bl...  15.5 us
    ppermute x6, starting transfers between devices, owned_sum(): lax.ppermute(parts[d], 'mem', [(i, (i + d) % count) for i in range(count)])  12.7 us
    ppermute x10, starting transfers between devices, shifted(): return lax.ppermute(value, ('tx', 'ty'), pairs)  12.1 us
    pallas_call x1, Pallas kernels, ensemble(): pl.pallas_call(kernel, out_shape=tuple((jax.ShapeDtypeStruct((levels // g...  12 us
    ppermute x6, waiting for transfers between devices, owned_sum(): lax.ppermute(parts[d], 'mem', [(i, (i + d) % count) for i in range(count)])  12 us
    pallas_call x1, Pallas kernels, pack(): pl.pallas_call(functools.partial(pack_kernel, tiles, levels, plane, capac...  11.2 us
    ppermute x10, waiting for transfers between devices, shifted(): return lax.ppermute(value, ('tx', 'ty'), pairs)  10.9 us
  transfers between devices with their start and end apart: 24, of which 10 were waited for; matrix products, arithmetic and copies ran while one was open for 2% of the time, Pallas kernels for 24%

profile of v4, /device:TPU:0, one launch (start us, length us, event | category | flops | bytes accessed | tf_op | source)
XLA Modules:
  0.0 147.5 jit_solution(13586798468781548001)
XLA Ops:
  0.6 3.0 %collective-permute-start = (f32[8,32,640]{2,1,0:T(8,128)}, f32[8,32,640]{2,1,0:T(8,128)S(1)}, u32[]{:S(2)}, u32[]{:S(2)}) collective-permute-start(f32[8,32,640]{2,1,0:T(8,128)} %alpha_ref.1), channel_id=1, source_target_pairs={{0,16},{4,20},{8,24},{12,28},{16,0},{20,4},{24,8},{28,12},{1,17},{... | collective-permute-start | bytes 1966088 | tf_op jit(solution)/shard_map/ppermute | solution.py:638
  12.2 11.2 %pack.1 = (f32[8,48,256]{2,1,0:T(8,128)}, s32[64,128]{1,0:T(8,128)S(1)}) custom-call(s32[1]{0:T(128)S(6)} %copy.15.count_ref, s32[192,128]{1,0:T(8,128)S(1)} %pad_add_fusion.refs_0_, f32[128,128]{1,0:T(8,128)S(1)} %pad_maximum_fusion.refs_1_, f32[3,8192]{1,0:T(4,128)S(1)} %copy-done.2), custom_call_target="tpu_custom_call" | custom-call | flops 1048576 | bytes 1048576 | tf_op jit(solution)/shard_map/pack/pallas_call | solution.py:165
  23.4 3.5 %all-to-all-start = ((f32[8,48,256]{2,1,0:T(8,128)}), f32[8,48,256]{2,1,0:T(8,128)S(1)}, u32[]{:S(2)}, u32[]{:S(2)}) async-start(f32[8,48,256]{2,1,0:T(8,128)} %get-tuple-element.47), calls=%async_computation | async-start | bytes 786432 | tf_op jit(solution)/shard_map/all_to_all | solution.py:787
  28.7 12.0 %ensemble.1 = (f32[8,32,128]{2,1,0:T(8,128)S(1)}, f32[8,32,128]{2,1,0:T(8,128)S(1)}, f32[8,32,128]{2,1,0:T(8,128)S(1)}, f32[8,32,128]{2,1,0:T(8,128)S(1)}) custom-call(s32[1]{0:T(128)} %bitcast.refs_0_, f32[8,32,640]{2,1,0:T(8,128)S(1)} %copy-done, f32[8,32,640]{2,1,0:T(8,128)S(1)} %collective-permute-done.refs_2_.refs_3_, ...), custom_call_target="tpu_custom_call" | custom-call | flops 8589934592 | bytes 8388608 | tf_op jit(solution)/shard_map/ensemble/pallas_call | solution.py:671
  42.4 2.6 %collective-permute-start.6 = (f32[8,32,128]{2,1,0:T(8,128)S(1)}, f32[8,32,128]{2,1,0:T(8,128)S(1)}, u32[]{:S(2)}, u32[]{:S(2)}) collective-permute-start(f32[8,32,128]{2,1,0:T(8,128)S(1)} %get-tuple-element.50), channel_id=1, source_target_pairs={{0,2},{1,3},{2,0},{3,1},{4,6},{5,7},{6,4},{7,5},{8,10},{9,11},{10,... | collective-permute-start | bytes 393224 | tf_op jit(solution)/shard_map/ppermute | solution.py:755
  46.4 2.7 %collective-permute-done.5 = f32[8,32,128]{2,1,0:T(8,128)S(1)} collective-permute-done((f32[8,32,128]{2,1,0:T(8,128)S(1)}, f32[8,32,128]{2,1,0:T(8,128)S(1)}, u32[]{:S(2)}, u32[]{:S(2)}) %collective-permute-start.5) | collective-permute-done | bytes 131104 | tf_op jit(solution)/shard_map/ppermute | solution.py:755
  49.1 5.1 %collective-permute-done.6 = f32[8,32,128]{2,1,0:T(8,128)S(1)} collective-permute-done((f32[8,32,128]{2,1,0:T(8,128)S(1)}, f32[8,32,128]{2,1,0:T(8,128)S(1)}, u32[]{:S(2)}, u32[]{:S(2)}) %collective-permute-start.6) | collective-permute-done | bytes 131104 | tf_op jit(solution)/shard_map/ppermute | solution.py:755
  54.2 4.4 %collective-permute-start.10 = (f32[8,32,128]{2,1,0:T(8,128)S(1)}, f32[8,32,128]{2,1,0:T(8,128)S(1)}, u32[]{:S(2)}, u32[]{:S(2)}) collective-permute-start(f32[8,32,128]{2,1,0:T(8,128)S(1)} %add_add_fusion.1.refs_1_), channel_id=1, source_target_pairs={{0,3},{1,0},{2,1},{3,2},{4,7},{5,4},{6,5},{7,6},{8,11},{9,8},{10,9... | collective-permute-start | bytes 393224 | tf_op jit(solution)/shard_map/ppermute | solution.py:761
  59.3 3.3 %collective-permute-done.10.refs_4_ = f32[8,32,128]{2,1,0:T(8,128)S(1)} collective-permute-done((f32[8,32,128]{2,1,0:T(8,128)S(1)}, f32[8,32,128]{2,1,0:T(8,128)S(1)}, u32[]{:S(2)}, u32[]{:S(2)}) %collective-permute-start.10) | collective-permute-done | bytes 131104 | tf_op jit(solution)/shard_map/ppermute | solution.py:761
  62.6 8.3 %collective-permute-done.9.refs_3_ = f32[8,32,128]{2,1,0:T(8,128)S(1)} collective-permute-done((f32[8,32,128]{2,1,0:T(8,128)S(1)}, f32[8,32,128]{2,1,0:T(8,128)S(1)}, u32[]{:S(2)}, u32[]{:S(2)}) %collective-permute-start.9) | collective-permute-done | bytes 131104 | tf_op jit(solution)/shard_map/ppermute | solution.py:761
  70.9 15.5 %stencil.1 = (f32[8,8,256]{2,1,0:T(8,128)}, f32[8,32,128]{2,1,0:T(8,128)S(1)}, f32[8,32,128]{2,1,0:T(8,128)S(1)}, f32[8,32,128]{2,1,0:T(8,128)S(1)}, f32[8,32,128]{2,1,0:T(8,128)S(1)}) custom-call(s32[1]{0:T(128)} %bitcast.refs_0_, f32[8,32,128]{2,1,0:T(8,128)S(1)} %add_add_fusion.1.refs_1_, f32[8,32,128]{2,1,0:T(8,128)S(1)} %collective-permute-done.8.refs_2_, ...), custom_call_target="tpu_custom_call" | custom-call | flops 17179869184 | bytes 1048576 | tf_op jit(solution)/shard_map/stencil/pallas_call | solution.py:348
  86.4 2.3 %collective-permute-start.11 = (f32[8,32,128]{2,1,0:T(8,128)S(1)}, f32[8,32,128]{2,1,0:T(8,128)S(1)}, u32[]{:S(2)}, u32[]{:S(2)}) collective-permute-start(f32[8,32,128]{2,1,0:T(8,128)S(1)} %get-tuple-element.54), channel_id=1, source_target_pairs={{0,1},{1,2},{2,3},{3,0},{4,5},{5,6},{6,7},{7,4},{8,9},{9,10},{10,1... | collective-permute-start | bytes 393224 | tf_op jit(solution)/shard_map/ppermute | solution.py:755
  88.7 2.0 %collective-permute-start.12 = (f32[8,32,128]{2,1,0:T(8,128)S(1)}, f32[8,32,128]{2,1,0:T(8,128)S(1)}, u32[]{:S(2)}, u32[]{:S(2)}) collective-permute-start(f32[8,32,128]{2,1,0:T(8,128)S(1)} %get-tuple-element.55), channel_id=1, source_target_pairs={{0,2},{1,3},{2,0},{3,1},{4,6},{5,7},{6,4},{7,5},{8,10},{9,11},{10,... | collective-permute-start | bytes 393224 | tf_op jit(solution)/shard_map/ppermute | solution.py:755
  90.7 2.8 %collective-permute-start.13 = (f32[8,32,128]{2,1,0:T(8,128)S(1)}, f32[8,32,128]{2,1,0:T(8,128)S(1)}, u32[]{:S(2)}, u32[]{:S(2)}) collective-permute-start(f32[8,32,128]{2,1,0:T(8,128)S(1)} %get-tuple-element.56), channel_id=1, source_target_pairs={{0,3},{1,0},{2,1},{3,2},{4,7},{5,4},{6,5},{7,6},{8,11},{9,8},{10,9... | collective-permute-start | bytes 393224 | tf_op jit(solution)/shard_map/ppermute | solution.py:755
  94.3 3.3 %collective-permute-done.12 = f32[8,32,128]{2,1,0:T(8,128)S(1)} collective-permute-done((f32[8,32,128]{2,1,0:T(8,128)S(1)}, f32[8,32,128]{2,1,0:T(8,128)S(1)}, u32[]{:S(2)}, u32[]{:S(2)}) %collective-permute-start.12) | collective-permute-done | bytes 131104 | tf_op jit(solution)/shard_map/ppermute | solution.py:755
  97.7 4.7 %collective-permute-start.16 = (f32[8,32,128]{2,1,0:T(8,128)S(1)}, f32[8,32,128]{2,1,0:T(8,128)S(1)}, u32[]{:S(2)}, u32[]{:S(2)}) collective-permute-start(f32[8,32,128]{2,1,0:T(8,128)S(1)} %add_add_fusion.refs_1_), channel_id=1, source_target_pairs={{0,3},{1,0},{2,1},{3,2},{4,7},{5,4},{6,5},{7,6},{8,11},{9,8},{10,9... | collective-permute-start | bytes 393224 | tf_op jit(solution)/shard_map/ppermute | solution.py:761
  103.1 1.9 %collective-permute-done.16.refs_4_ = f32[8,32,128]{2,1,0:T(8,128)S(1)} collective-permute-done((f32[8,32,128]{2,1,0:T(8,128)S(1)}, f32[8,32,128]{2,1,0:T(8,128)S(1)}, u32[]{:S(2)}, u32[]{:S(2)}) %collective-permute-start.16) | collective-permute-done | bytes 131104 | tf_op jit(solution)/shard_map/ppermute | solution.py:761
  105.0 5.9 %collective-permute-done.15.refs_3_ = f32[8,32,128]{2,1,0:T(8,128)S(1)} collective-permute-done((f32[8,32,128]{2,1,0:T(8,128)S(1)}, f32[8,32,128]{2,1,0:T(8,128)S(1)}, u32[]{:S(2)}, u32[]{:S(2)}) %collective-permute-start.15) | collective-permute-done | bytes 131104 | tf_op jit(solution)/shard_map/ppermute | solution.py:761
  110.9 7.1 %all-to-all-start.1 = ((f32[8,8,256]{2,1,0:T(8,128)}), f32[8,8,256]{2,1,0:T(8,128)S(1)}, u32[]{:S(2)}, u32[]{:S(2)}) async-start(f32[8,8,256]{2,1,0:T(8,128)} %get-tuple-element.69), calls=%async_computation.1 | async-start | bytes 131072 | tf_op jit(solution)/shard_map/all_to_all | solution.py:792
  118.0 8.7 %backward.1 = (f32[32,32,128]{2,1,0:T(8,128)}, f32[8,32,640]{2,1,0:T(8,128)S(1)}, f32[8,32,640]{2,1,0:T(8,128)S(1)}, f32[32,640]{1,0:T(8,128)S(1)}, f32[16,640]{...) custom-call(s32[1]{0:T(128)} %bitcast.refs_0_, f32[8,32,128]{2,1,0:T(8,128)S(1)} %add_add_fusion.refs_1_, ...), custom_call_target="tpu_custom_call" | custom-call | flops 8589934592 | bytes 8388608 | tf_op jit(solution)/shard_map/backward/pallas_call | solution.py:712
  126.7 2.1 %collective-permute-start.17 = (f32[8,32,640]{2,1,0:T(8,128)S(1)}, f32[8,32,640]{2,1,0:T(8,128)S(1)}, u32[]{:S(2)}, u32[]{:S(2)}) collective-permute-start(f32[8,32,640]{2,1,0:T(8,128)S(1)} %get-tuple-element.71), channel_id=1, source_target_pairs={{0,16},{4,20},{8,24},{12,28},{16,0},{20,4},{24,8},{28,12},{1,17},{... | collective-permute-start | bytes 1966088 | tf_op jit(solution)/shard_map/ppermute | solution.py:638
  130.6 1.8 %collective-permute-start.18 = (f32[32,640]{1,0:T(8,128)S(1)}, f32[32,640]{1,0:T(8,128)S(1)}, u32[]{:S(2)}, u32[]{:S(2)}) collective-permute-start(f32[32,640]{1,0:T(8,128)S(1)} %get-tuple-element.72), channel_id=1, source_target_pairs={{0,12},{4,0},{8,4},{12,8},{16,28},{20,16},{24,20},{28,24},{1,13},{... | collective-permute-start | bytes 245768 | tf_op jit(solution)/shard_map/ppermute | solution.py:638
  132.4 3.1 %unpack.1 = f32[64,128]{1,0:T(8,128)} custom-call(s32[64,128]{1,0:T(8,128)S(1)} %get-tuple-element.77.target_ref, f32[64,256]{1,0:T(8,128)S(1)} %bitcast.8), custom_call_target="tpu_custom_call" | custom-call | flops 2147483648 | bytes 262144 | tf_op jit(solution)/shard_map/unpack/pallas_call | solution.py:392
  135.5 9.1 %collective-permute-done.20.refs_3_ = f32[16,640]{1,0:T(8,128)S(1)} collective-permute-done((f32[16,640]{1,0:T(8,128)S(1)}, f32[16,640]{1,0:T(8,128)S(1)}, u32[]{:S(2)}, u32[]{:S(2)}) %collective-permute-start.20) | collective-permute-done | bytes 40992 | tf_op jit(solution)/shard_map/ppermute | solution.py:638
  (52 shorter events, 19.4 us)
Async XLA Ops:
  0.6 26.3 %collective-permute-start = (f32[8,32,640]{2,1,0:T(8,128)}, f32[8,32,640]{2,1,0:T(8,128)S(1)}, u32[]{:S(2)}, u32[]{:S(2)}) collective-permute-start(f32[8,32,640]{2,1,0:T(8,128)} %alpha_ref.1), channel_id=1, source_target_pairs={{0,16},{4,20},{8,24},{12,28},{16,0},{20,4},{24,8},{28,12},{1,17},{... | collective-permute-start | bytes 1966088 | tf_op jit(solution)/shard_map/ppermute | solution.py:638
  4.6 22.2 %collective-permute-start.2 = (f32[32,640]{1,0:T(8,128)S(1)}, f32[32,640]{1,0:T(8,128)S(1)}, u32[]{:S(2)}, u32[]{:S(2)}) collective-permute-start(f32[32,640]{1,0:T(8,128)S(1)} %reshape.32), channel_id=1, source_target_pairs={{0,20},{4,24},{8,28},{12,16},{16,4},{20,8},{24,12},{28,0},{1,21},{... | collective-permute-start | bytes 245768 | tf_op jit(solution)/shard_map/ppermute | solution.py:638
  4.7 18.7 %collective-permute-start.1 = (f32[32,640]{1,0:T(8,128)S(1)}, f32[32,640]{1,0:T(8,128)S(1)}, u32[]{:S(2)}, u32[]{:S(2)}) collective-permute-start(f32[32,640]{1,0:T(8,128)S(1)} %reshape.32), channel_id=1, source_target_pairs={{0,4},{4,8},{8,12},{12,0},{16,20},{20,24},{24,28},{28,16},{1,5},{5... | collective-permute-start | bytes 245768 | tf_op jit(solution)/shard_map/ppermute | solution.py:638
  7.3 19.6 %collective-permute-start.4 = (f32[40,640]{1,0:T(8,128)S(1)}, f32[40,640]{1,0:T(8,128)S(1)}, u32[]{:S(2)}, u32[]{:S(2)}) collective-permute-start(f32[40,640]{1,0:T(8,128)S(1)} %reshape.33), channel_id=1, source_target_pairs={{0,28},{4,16},{8,20},{12,24},{16,12},{20,0},{24,4},{28,8},{1,29},{... | collective-permute-start | bytes 307208 | tf_op jit(solution)/shard_map/ppermute | solution.py:638
  8.4 18.5 %collective-permute-start.3 = (f32[40,640]{1,0:T(8,128)S(1)}, f32[40,640]{1,0:T(8,128)S(1)}, u32[]{:S(2)}, u32[]{:S(2)}) collective-permute-start(f32[40,640]{1,0:T(8,128)S(1)} %reshape.33), channel_id=1, source_target_pairs={{0,12},{4,0},{8,4},{12,8},{16,28},{20,16},{24,20},{28,24},{1,13},{... | collective-permute-start | bytes 307208 | tf_op jit(solution)/shard_map/ppermute | solution.py:638
  23.4 17.4 %all-to-all-start = ((f32[8,48,256]{2,1,0:T(8,128)}), f32[8,48,256]{2,1,0:T(8,128)S(1)}, u32[]{:S(2)}, u32[]{:S(2)}) async-start(f32[8,48,256]{2,1,0:T(8,128)} %get-tuple-element.47), calls=%async_computation | async-start | bytes 786432 | tf_op jit(solution)/shard_map/all_to_all | solution.py:787
  40.8 8.3 %collective-permute-start.5 = (f32[8,32,128]{2,1,0:T(8,128)S(1)}, f32[8,32,128]{2,1,0:T(8,128)S(1)}, u32[]{:S(2)}, u32[]{:S(2)}) collective-permute-start(f32[8,32,128]{2,1,0:T(8,128)S(1)} %get-tuple-element.49), channel_id=1, source_target_pairs={{0,1},{1,2},{2,3},{3,0},{4,5},{5,6},{6,7},{7,4},{8,9},{9,10},{10,1... | collective-permute-start | bytes 393224 | tf_op jit(solution)/shard_map/ppermute | solution.py:755
  42.4 11.7 %collective-permute-start.6 = (f32[8,32,128]{2,1,0:T(8,128)S(1)}, f32[8,32,128]{2,1,0:T(8,128)S(1)}, u32[]{:S(2)}, u32[]{:S(2)}) collective-permute-start(f32[8,32,128]{2,1,0:T(8,128)S(1)} %get-tuple-element.50), channel_id=1, source_target_pairs={{0,2},{1,3},{2,0},{3,1},{4,6},{5,7},{6,4},{7,5},{8,10},{9,11},{10,... | collective-permute-start | bytes 393224 | tf_op jit(solution)/shard_map/ppermute | solution.py:755
  45.0 9.2 %collective-permute-start.7 = (f32[8,32,128]{2,1,0:T(8,128)S(1)}, f32[8,32,128]{2,1,0:T(8,128)S(1)}, u32[]{:S(2)}, u32[]{:S(2)}) collective-permute-start(f32[8,32,128]{2,1,0:T(8,128)S(1)} %get-tuple-element.51), channel_id=1, source_target_pairs={{0,3},{1,0},{2,1},{3,2},{4,7},{5,4},{6,5},{7,6},{8,11},{9,8},{10,9... | collective-permute-start | bytes 393224 | tf_op jit(solution)/shard_map/ppermute | solution.py:755
  54.2 8.3 %collective-permute-start.10 = (f32[8,32,128]{2,1,0:T(8,128)S(1)}, f32[8,32,128]{2,1,0:T(8,128)S(1)}, u32[]{:S(2)}, u32[]{:S(2)}) collective-permute-start(f32[8,32,128]{2,1,0:T(8,128)S(1)} %add_add_fusion.1.refs_1_), channel_id=1, source_target_pairs={{0,3},{1,0},{2,1},{3,2},{4,7},{5,4},{6,5},{7,6},{8,11},{9,8},{10,9... | collective-permute-start | bytes 393224 | tf_op jit(solution)/shard_map/ppermute | solution.py:761
  58.6 12.2 %collective-permute-start.9 = (f32[8,32,128]{2,1,0:T(8,128)S(1)}, f32[8,32,128]{2,1,0:T(8,128)S(1)}, u32[]{:S(2)}, u32[]{:S(2)}) collective-permute-start(f32[8,32,128]{2,1,0:T(8,128)S(1)} %add_add_fusion.1.refs_1_), channel_id=1, source_target_pairs={{0,2},{1,3},{2,0},{3,1},{4,6},{5,7},{6,4},{7,5},{8,10},{9,11},{10,... | collective-permute-start | bytes 393224 | tf_op jit(solution)/shard_map/ppermute | solution.py:761
  59.0 11.8 %collective-permute-start.8 = (f32[8,32,128]{2,1,0:T(8,128)S(1)}, f32[8,32,128]{2,1,0:T(8,128)S(1)}, u32[]{:S(2)}, u32[]{:S(2)}) collective-permute-start(f32[8,32,128]{2,1,0:T(8,128)S(1)} %add_add_fusion.1.refs_1_), channel_id=1, source_target_pairs={{0,1},{1,2},{2,3},{3,0},{4,5},{5,6},{6,7},{7,4},{8,9},{9,10},{10,1... | collective-permute-start | bytes 393224 | tf_op jit(solution)/shard_map/ppermute | solution.py:761
  86.4 7.9 %collective-permute-start.11 = (f32[8,32,128]{2,1,0:T(8,128)S(1)}, f32[8,32,128]{2,1,0:T(8,128)S(1)}, u32[]{:S(2)}, u32[]{:S(2)}) collective-permute-start(f32[8,32,128]{2,1,0:T(8,128)S(1)} %get-tuple-element.54), channel_id=1, source_target_pairs={{0,1},{1,2},{2,3},{3,0},{4,5},{5,6},{6,7},{7,4},{8,9},{9,10},{10,1... | collective-permute-start | bytes 393224 | tf_op jit(solution)/shard_map/ppermute | solution.py:755
  88.7 9.0 %collective-permute-start.12 = (f32[8,32,128]{2,1,0:T(8,128)S(1)}, f32[8,32,128]{2,1,0:T(8,128)S(1)}, u32[]{:S(2)}, u32[]{:S(2)}) collective-permute-start(f32[8,32,128]{2,1,0:T(8,128)S(1)} %get-tuple-element.55), channel_id=1, source_target_pairs={{0,2},{1,3},{2,0},{3,1},{4,6},{5,7},{6,4},{7,5},{8,10},{9,11},{10,... | collective-permute-start | bytes 393224 | tf_op jit(solution)/shard_map/ppermute | solution.py:755
  90.7 7.0 %collective-permute-start.13 = (f32[8,32,128]{2,1,0:T(8,128)S(1)}, f32[8,32,128]{2,1,0:T(8,128)S(1)}, u32[]{:S(2)}, u32[]{:S(2)}) collective-permute-start(f32[8,32,128]{2,1,0:T(8,128)S(1)} %get-tuple-element.56), channel_id=1, source_target_pairs={{0,3},{1,0},{2,1},{3,2},{4,7},{5,4},{6,5},{7,6},{8,11},{9,8},{10,9... | collective-permute-start | bytes 393224 | tf_op jit(solution)/shard_map/ppermute | solution.py:755
  97.7 7.2 %collective-permute-start.16 = (f32[8,32,128]{2,1,0:T(8,128)S(1)}, f32[8,32,128]{2,1,0:T(8,128)S(1)}, u32[]{:S(2)}, u32[]{:S(2)}) collective-permute-start(f32[8,32,128]{2,1,0:T(8,128)S(1)} %add_add_fusion.refs_1_), channel_id=1, source_target_pairs={{0,3},{1,0},{2,1},{3,2},{4,7},{5,4},{6,5},{7,6},{8,11},{9,8},{10,9... | collective-permute-start | bytes 393224 | tf_op jit(solution)/shard_map/ppermute | solution.py:761
  102.4 8.5 %collective-permute-start.15 = (f32[8,32,128]{2,1,0:T(8,128)S(1)}, f32[8,32,128]{2,1,0:T(8,128)S(1)}, u32[]{:S(2)}, u32[]{:S(2)}) collective-permute-start(f32[8,32,128]{2,1,0:T(8,128)S(1)} %add_add_fusion.refs_1_), channel_id=1, source_target_pairs={{0,2},{1,3},{2,0},{3,1},{4,6},{5,7},{6,4},{7,5},{8,10},{9,11},{10,... | collective-permute-start | bytes 393224 | tf_op jit(solution)/shard_map/ppermute | solution.py:761
  102.4 8.5 %collective-permute-start.14 = (f32[8,32,128]{2,1,0:T(8,128)S(1)}, f32[8,32,128]{2,1,0:T(8,128)S(1)}, u32[]{:S(2)}, u32[]{:S(2)}) collective-permute-start(f32[8,32,128]{2,1,0:T(8,128)S(1)} %add_add_fusion.refs_1_), channel_id=1, source_target_pairs={{0,1},{1,2},{2,3},{3,0},{4,5},{5,6},{6,7},{7,4},{8,9},{9,10},{10,1... | collective-permute-start | bytes 393224 | tf_op jit(solution)/shard_map/ppermute | solution.py:761
  110.9 15.8 %all-to-all-start.1 = ((f32[8,8,256]{2,1,0:T(8,128)}), f32[8,8,256]{2,1,0:T(8,128)S(1)}, u32[]{:S(2)}, u32[]{:S(2)}) async-start(f32[8,8,256]{2,1,0:T(8,128)} %get-tuple-element.69), calls=%async_computation.1 | async-start | bytes 131072 | tf_op jit(solution)/shard_map/all_to_all | solution.py:792
  126.7 19.7 %collective-permute-start.17 = (f32[8,32,640]{2,1,0:T(8,128)S(1)}, f32[8,32,640]{2,1,0:T(8,128)S(1)}, u32[]{:S(2)}, u32[]{:S(2)}) collective-permute-start(f32[8,32,640]{2,1,0:T(8,128)S(1)} %get-tuple-element.71), channel_id=1, source_target_pairs={{0,16},{4,20},{8,24},{12,28},{16,0},{20,4},{24,8},{28,12},{1,17},{... | collective-permute-start | bytes 1966088 | tf_op jit(solution)/shard_map/ppermute | solution.py:638
  128.8 15.8 %collective-permute-start.20 = (f32[16,640]{1,0:T(8,128)S(1)}, f32[16,640]{1,0:T(8,128)S(1)}, u32[]{:S(2)}, u32[]{:S(2)}) collective-permute-start(f32[16,640]{1,0:T(8,128)S(1)} %get-tuple-element.74), channel_id=1, source_target_pairs={{0,28},{4,16},{8,20},{12,24},{16,12},{20,0},{24,4},{28,8},{1,29},{... | collective-permute-start | bytes 122888 | tf_op jit(solution)/shard_map/ppermute | solution.py:638
  129.8 16.7 %collective-permute-start.21 = (f32[24,640]{1,0:T(8,128)S(1)}, f32[24,640]{1,0:T(8,128)S(1)}, u32[]{:S(2)}, u32[]{:S(2)}) collective-permute-start(f32[24,640]{1,0:T(8,128)S(1)} %get-tuple-element.75), channel_id=1, source_target_pairs={{0,20},{4,24},{8,28},{12,16},{16,4},{20,8},{24,12},{28,0},{1,21},{... | collective-permute-start | bytes 184328 | tf_op jit(solution)/shard_map/ppermute | solution.py:638
  130.6 15.9 %collective-permute-start.18 = (f32[32,640]{1,0:T(8,128)S(1)}, f32[32,640]{1,0:T(8,128)S(1)}, u32[]{:S(2)}, u32[]{:S(2)}) collective-permute-start(f32[32,640]{1,0:T(8,128)S(1)} %get-tuple-element.72), channel_id=1, source_target_pairs={{0,12},{4,0},{8,4},{12,8},{16,28},{20,16},{24,20},{28,24},{1,13},{... | collective-permute-start | bytes 245768 | tf_op jit(solution)/shard_map/ppermute | solution.py:638
  132.4 14.0 %collective-permute-start.19 = (f32[40,640]{1,0:T(8,128)S(1)}, f32[40,640]{1,0:T(8,128)S(1)}, u32[]{:S(2)}, u32[]{:S(2)}) collective-permute-start(f32[40,640]{1,0:T(8,128)S(1)} %get-tuple-element.73), channel_id=1, source_target_pairs={{0,4},{4,8},{8,12},{12,0},{16,20},{20,24},{24,28},{28,16},{1,5},{5... | collective-permute-start | bytes 307208 | tf_op jit(solution)/shard_map/ppermute | solution.py:638
  (7 other events, 170.5 us)

commit v5 on v4

--- a/solution.py
+++ b/solution.py
@@ -21,8 +21,7 @@
 
 BLOCK = 256
 LANES = 128
-STEPS = (8, 12, 16)
-WIDE = STEPS[-1]
+STEPS = (8, 12, 16, 32)
 HALF = jnp.bfloat16
 
 
@@ -43,28 +42,17 @@
     return lax.broadcasted_iota(jnp.int32, shape, dim)
 
 
-def pack_kernel(
-    tiles, levels, plane, capacity,
-    count_ref, *refs,
-):
-    sources, (out_ref, target_ref, carry, total, gathered, left_a, right_a, left_b, right_b, *held), sems = refs[:3], refs[3:-1], refs[-1]
-    copies = [pltpu.make_async_copy(source, here, sems.at[i]) for i, (source, here) in enumerate(zip(sources, held))]
-    for copy in copies:
-        copy.start()
-    ints_ref, floats_ref, frac_ref = held
+def row_of(ref, j):
+    pair = ref[pl.ds(2 * j, 2), :]
+    return jnp.concatenate([pair[0:1], pair[1:2]], 1)
+
+
+def rank_kernel(tiles, levels, capacity, count_ref, ints_ref, target_ref, carry, total):
     size = target_ref.shape[0]
-    owner_ref, level_ref, column_ref = [ints_ref.at[pl.ds(i * size, size)] for i in range(3)]
-    innov_ref, rinv_ref = [floats_ref.at[pl.ds(i * size, size)] for i in range(2)]
-    blocks = target_ref.shape[0] * LANES // BLOCK
+    owner_ref, level_ref = [ints_ref.at[pl.ds(i * size, size)] for i in range(2)]
+    blocks = size * LANES // BLOCK
     keys = tiles * levels
-    deep = capacity // BLOCK
-    slot_rows = tiles * deep
-    group = 4
     count = count_ref[0]
-
-    def row_of(ref, j):
-        pair = ref[pl.ds(2 * j, 2), :]
-        return jnp.concatenate([pair[0:1], pair[1:2]], 1)
 
     def onehot(j):
         live = iota((1, BLOCK), 1) + j * BLOCK < count
@@ -73,8 +61,6 @@
 
     ones = jnp.ones((BLOCK, LANES), HALF)
     total[...] = jnp.zeros_like(total)
-    for copy in copies[:1]:
-        copy.wait()
 
     many = math.gcd(blocks, 8)
 
@@ -94,7 +80,6 @@
 
     earlier = jnp.where(iota((BLOCK, BLOCK), 0) < iota((BLOCK, BLOCK), 1), 1.0, 0.0).astype(HALF)
     prefix = jnp.concatenate([earlier, ones], 1)
-    gathered[...] = jnp.zeros_like(gathered)
 
     def rank_group(g, unused):
         now = carry[...]
@@ -110,8 +95,34 @@
         return unused
 
     lax.fori_loop(0, blocks // many, rank_group, 0)
-    for copy in copies[1:]:
-        copy.wait()
+
+
+def ranked(tiles, levels, capacity, count, ints):
+    return pl.pallas_call(
+        functools.partial(rank_kernel, tiles, levels, capacity),
+        out_shape=jax.ShapeDtypeStruct((ints.shape[0] // 3, LANES), jnp.int32),
+        in_specs=[SMEM, VMEM],
+        out_specs=VMEM,
+        scratch_shapes=[
+            pltpu.VMEM((tiles * levels, LANES), jnp.float32),
+            pltpu.VMEM((tiles * levels, LANES), jnp.float32),
+        ],
+        compiler_params=room(16),
+        cost_estimate=pl.CostEstimate(flops=1 << 20, bytes_accessed=1 << 17, transcendentals=0),
+        name="rank",
+    )(count, ints)
+
+
+def pack_kernel(tiles, plane, capacity, target_ref, ints_ref, floats_ref, frac_ref, out_ref, *scratch):
+    gathered, left_a, right_a, left_b, right_b = scratch
+    size = target_ref.shape[0]
+    level_ref, column_ref = [ints_ref.at[pl.ds(i * size, size)] for i in (1, 2)]
+    innov_ref, rinv_ref = [floats_ref.at[pl.ds(i * size, size)] for i in range(2)]
+    blocks = size * LANES // BLOCK
+    deep = capacity // BLOCK
+    slot_rows = tiles * deep
+    group = 4
+    gathered[...] = jnp.zeros_like(gathered)
 
     def place(j):
         target = row_of(target_ref, j)
@@ -156,32 +167,20 @@
         out_ref[tile, 5 * deep:6 * deep, :] = base
 
 
-def pack(tiles, levels, plane, capacity, count, owner, column, level, frac, innov, rinv):
-    slots = owner.shape[0]
-    rows = slots // LANES
+def pack(tiles, plane, capacity, target, ints, floats, frac):
     deep = capacity // BLOCK
-    values = [jnp.concatenate(some).reshape(-1, LANES) for some in ((owner, level, column), (innov, rinv))] + [frac]
-    vmem = pl.BlockSpec(memory_space=pltpu.VMEM)
+    rows = 13 * tiles * deep
     return pl.pallas_call(
-        functools.partial(pack_kernel, tiles, levels, plane, capacity),
-        out_shape=(
-            jax.ShapeDtypeStruct((tiles, 6 * deep, BLOCK), jnp.float32),
-            jax.ShapeDtypeStruct((rows, LANES), jnp.int32),
-        ),
-        in_specs=[SMEM] + [HBM] * 3,
-        out_specs=(vmem, vmem),
-        scratch_shapes=[
-            pltpu.VMEM((tiles * levels, LANES), jnp.float32),
-            pltpu.VMEM((tiles * levels, LANES), jnp.float32),
-            pltpu.VMEM((13 * tiles * deep, BLOCK), jnp.float32),
-        ]
-        + [pltpu.VMEM((count_rows, 4 * BLOCK), HALF) for count_rows in (13 * tiles * deep, BLOCK) * 2]
-        + [pltpu.VMEM(value.shape, value.dtype) for value in values]
-        + [pltpu.SemaphoreType.DMA((len(values),))],
+        functools.partial(pack_kernel, tiles, plane, capacity),
+        out_shape=jax.ShapeDtypeStruct((tiles, 6 * deep, BLOCK), jnp.float32),
+        in_specs=[VMEM] * 4,
+        out_specs=VMEM,
+        scratch_shapes=[pltpu.VMEM((rows, BLOCK), jnp.float32)]
+        + [pltpu.VMEM((count, 4 * BLOCK), HALF) for count in (rows, BLOCK) * 2],
         compiler_params=room(16),
-        cost_estimate=pl.CostEstimate(flops=1 << 20, bytes_accessed=1 << 20, transcendentals=0),
+        cost_estimate=pl.CostEstimate(flops=8 << 30, bytes_accessed=1 << 20, transcendentals=0),
         name="pack",
-    )(count, *values)
+    )(target, ints, floats, frac)
 
 
 def stencil_kernel(
@@ -246,7 +245,7 @@
         pick_y = jnp.where(rows_y == along, 1.0 - frac_y, 0.0) + jnp.where(rows_y == along + 1.0, frac_y, 0.0)
 
         def weights(bottom, reach):
-            offset = level - bottom.astype(jnp.float32)
+            offset = level - jnp.asarray(bottom, jnp.int32).astype(jnp.float32)
             rows_l = iota((reach, LANES), 0).astype(jnp.float32)
             pick_l = jnp.where(rows_l == offset, 1.0 - frac_l, 0.0) + jnp.where(rows_l == offset + 1.0, frac_l, 0.0)
             picks = [pick_x * pick_l[g:g + 1] for g in range(reach)]
@@ -260,8 +259,11 @@
         return weights, finish
 
     def look(bottom, pick):
-        lanes = pl.ds(pl.multiple_of((bottom // chunk) * LANES, LANES), pick.shape[0])
-        seen = dot_nn(field_t[lax.rem(bottom, chunk), :, lanes], pick)
+        if isinstance(bottom, int):
+            seen = dot_nn(field_t[0, :, :pick.shape[0]], pick)
+        else:
+            lanes = pl.ds(pl.multiple_of((bottom // chunk) * LANES, LANES), pick.shape[0])
+            seen = dot_nn(field_t[lax.rem(bottom, chunk), :, lanes], pick)
         return seen[:fine_y, :LANES] + (seen[:fine_y, LANES:] + seen[fine_y:, :LANES])
 
     def spread(pick, term):
@@ -286,24 +288,6 @@
             source, at, half = blocks[i]
             dep_ref[source, pl.ds(at, 1), :] = jnp.concatenate(departures[i:i + halves], 1)
 
-    def alone(block, first, needed):
-        weights, finish = block_of(*block)
-        windows = (needed + WIDE - 1) // WIDE
-
-        def forward(w, total):
-            bottom = first + w * WIDE
-            return total + look(bottom, weights(bottom, WIDE))
-
-        departure, term = finish(lax.fori_loop(0, windows, forward, jnp.zeros((fine_y, LANES), jnp.float32)))
-
-        def backward(w, unused):
-            bottom = first + w * WIDE
-            adjoint[rows_at(bottom, WIDE), :] += spread(weights(bottom, WIDE), term)
-            return unused
-
-        lax.fori_loop(0, windows, backward, 0)
-        return departure
-
     step = 2 if deep % 2 == 0 else 1
 
     def one_step(i, unused):
@@ -317,11 +301,7 @@
         for below, reach in zip((0,) + STEPS, STEPS):
             @pl.when((most > below) & (most <= reach))
             def _():
-                together(blocks, bottoms, reach)
-
-        @pl.when(most > WIDE)
-        def _():
-            keep(blocks, [alone(*each) for each in zip(blocks, bottoms, needs)])
+                together(blocks, [0] * len(blocks) if reach == levels else bottoms, reach)
 
         return unused
 
@@ -336,7 +316,7 @@
     sources, packed_rows, block = incoming.shape
     deep, groups = packed_rows // 6, len(parts)
     rows = levels * fine_x
-    padded = rows + WIDE * fine_x
+    padded = rows + STEPS[-2] * fine_x
 
     def kernel(*refs):
         parts_end = 1 + groups
@@ -359,7 +339,7 @@
             pltpu.SMEM((sources * deep, LANES), jnp.int32),
             pltpu.SemaphoreType.DMA,
         ],
-        compiler_params=room(20),
+        compiler_params=room(32),
         cost_estimate=pl.CostEstimate(flops=16 << 30, bytes_accessed=1 << 20, transcendentals=0),
         name="stencil",
     )(me, *parts, bg_sigma, static_ctrl, incoming)
@@ -779,13 +759,14 @@
     tiles = lax.axis_size("tx") * lax.axis_size("ty")
     capacity = 2 * obs_owner.shape[0] // tiles
     me = lax.axis_index("mem").astype(jnp.int32).reshape(1)
-    outgoing, target = pack(
-        tiles, levels, fine_x * fine_y, capacity,
-        obs_count, obs_owner[:, 0], obs_column, obs_level, obs_frac, innovation, obs_rinv,
-    )
-    partial, outgoing = ensemble(alpha, lv_sqrt, ens_pert, me, outgoing)
+    rows = obs_owner.shape[0] // LANES
+    ints = jnp.concatenate([obs_owner[:, 0], obs_level, obs_column]).reshape(3 * rows, LANES)
+    floats = jnp.concatenate([innovation, obs_rinv]).reshape(2 * rows, LANES)
+    target = ranked(tiles, levels, capacity, obs_count, ints)
+    partial, target = ensemble(alpha, lv_sqrt, ens_pert, me, target)
+    partial, target = lax.optimization_barrier((partial, target))
+    outgoing = pack(tiles, fine_x * fine_y, capacity, target, ints, floats, obs_frac)
     incoming = lax.all_to_all(outgoing, ("tx", "ty"), split_axis=0, concat_axis=0, tiled=True)
-    partial, incoming = lax.optimization_barrier((partial, incoming))
     increment = owned_sum(partial)
     departure, adjoint = stencil(gathered(increment), incoming, bg_sigma, static_ctrl, me)
     parts, departure = lax.optimization_barrier((gathered(owned_sum(adjoint)), departure))

time: 149 us -> 145 us (0.973)
  starting transfers between devices: 45.7 us -> 39.4 us
  waiting for transfers between devices: 42.3 us -> 46.7 us
  Pallas kernels: 51.6 us -> 49.6 us
    ppermute x10, waiting for transfers between devices: 10.9 us -> 16.3 us  [shifted(): return lax.ppermute(value, ('tx', 'ty'), pairs)]
    ppermute x6, waiting for transfers between devices: 12 us -> 7.39 us  [owned_sum(): lax.ppermute(parts[d], 'mem', [(i, (i + d) % count) for i in range(count)])]
    ppermute x6, waiting for transfers between devices: 19.4 us -> 23 us  [gathered(): lax.ppermute(own, 'mem', [(i, (i + d) % count) for i in range(count)])]
    ppermute x6, starting transfers between devices: 12.7 us -> 9.52 us  [owned_sum(): lax.ppermute(parts[d], 'mem', [(i, (i + d) % count) for i in range(count)])]
    all_to_all x1, starting transfers between devices: 7.07 us -> 5.16 us  [per_device(): lax.all_to_all(departure, ('tx', 'ty'), split_axis=0, concat_axis=0, tile...]
    pallas_call x1, Pallas kernels: 15.5 us -> 13.9 us  [stencil(): pl.pallas_call(kernel, out_shape=(jax.ShapeDtypeStruct((sources, deep, bl...]
    pallas_call x1 -> x2, Pallas kernels: 11.2 us -> 10.8 us  [the longest x1 5.61 us: pack(): pl.pallas_call(functools.partial(pack_kernel, tiles, plane, capacity), ou...]
  transfers between devices with their start and end apart: 24 -> 24, of which waited for: 10 -> 10; matrix products, arithmetic and copies ran while one was open for 2% -> 2% of each run, Pallas kernels for 24% -> 16%
where the time goes in v5:
time: 145 us; the launch traced here: 143 us
  Pallas kernels  49.6 us (34%)
  waiting for transfers between devices  46.7 us (32%)
  starting transfers between devices  39.4 us (27%)
  local copies, waits for them, and re-layouts  3.78 us (3%)
  other arithmetic  1.66 us (1%)
  between operations  1.47 us (1%)
    ppermute x6, waiting for transfers between devices, gathered(): lax.ppermute(own, 'mem', [(i, (i + d) % count) for i in range(count)])  23 us
    ppermute x10, waiting for transfers between devices, shifted(): return lax.ppermute(value, ('tx', 'ty'), pairs)  16.3 us
    pallas_call x1, Pallas kernels, stencil(): pl.pallas_call(kernel, out_shape=(jax.ShapeDtypeStruct((sources, deep, bl...  13.9 us
    ppermute x10, starting transfers between devices, shifted(): return lax.ppermute(value, ('tx', 'ty'), pairs)  12.1 us
    pallas_call x1, Pallas kernels, ensemble(): pl.pallas_call(kernel, out_shape=tuple((jax.ShapeDtypeStruct((levels // g...  12 us
    ppermute x6, starting transfers between devices, owned_sum(): lax.ppermute(parts[d], 'mem', [(i, (i + d) % count) for i in range(count)])  9.52 us
    ppermute x6, starting transfers between devices, gathered(): lax.ppermute(own, 'mem', [(i, (i + d) % count) for i in range(count)])  9.11 us
    pallas_call x1, Pallas kernels, backward(): pl.pallas_call(kernel, out_shape=tuple((jax.ShapeDtypeStruct(shape, jnp.f...  8.74 us
  transfers between devices with their start and end apart: 24, of which 10 were waited for; matrix products, arithmetic and copies ran while one was open for 2% of the time, Pallas kernels for 16%

profile of v5, /device:TPU:0, one launch (start us, length us, event | category | flops | bytes accessed | tf_op | source)
XLA Modules:
  0.0 142.6 jit_solution(5004344298585929170)
XLA Ops:
  0.6 3.0 %collective-permute-start = (f32[8,32,640]{2,1,0:T(8,128)}, f32[8,32,640]{2,1,0:T(8,128)S(1)}, u32[]{:S(2)}, u32[]{:S(2)}) collective-permute-start(f32[8,32,640]{2,1,0:T(8,128)} %alpha_ref.1), channel_id=1, source_target_pairs={{0,16},{4,20},{8,24},{12,28},{16,0},{20,4},{24,8},{28,12},{1,17},{... | collective-permute-start | bytes 1966088 | tf_op jit(solution)/shard_map/ppermute | solution.py:618
  10.5 5.2 %rank.1.target_ref = s32[64,128]{1,0:T(8,128)S(1)} custom-call(s32[1]{0:T(128)S(6)} %copy.15.count_ref, s32[192,128]{1,0:T(8,128)S(1)} %pad_add_fusion.ints_ref), custom_call_target="tpu_custom_call" | custom-call | flops 1048576 | bytes 131072 | tf_op jit(solution)/shard_map/rank/pallas_call | solution.py:101
  16.5 4.3 %collective-permute-done.2.refs_5_.refs_6_ = f32[32,640]{1,0:T(8,128)S(1)} collective-permute-done((f32[32,640]{1,0:T(8,128)S(1)}, f32[32,640]{1,0:T(8,128)S(1)}, u32[]{:S(2)}, u32[]{:S(2)}) %collective-permute-start.2) | collective-permute-done | bytes 81952 | tf_op jit(solution)/shard_map/ppermute | solution.py:618
  23.6 12.0 %ensemble.1 = (f32[8,32,128]{2,1,0:T(8,128)S(1)}, f32[8,32,128]{2,1,0:T(8,128)S(1)}, f32[8,32,128]{2,1,0:T(8,128)S(1)}, f32[8,32,128]{2,1,0:T(8,128)S(1)}) custom-call(s32[1]{0:T(128)} %bitcast.refs_0_, f32[8,32,640]{2,1,0:T(8,128)S(1)} %copy-done, f32[8,32,640]{2,1,0:T(8,128)S(1)} %collective-permute-done.refs_2_.refs_3_, ...), custom_call_target="tpu_custom_call" | custom-call | flops 8589934592 | bytes 8388608 | tf_op jit(solution)/shard_map/ensemble/pallas_call | solution.py:651
  37.3 2.6 %collective-permute-start.6 = (f32[8,32,128]{2,1,0:T(8,128)S(1)}, f32[8,32,128]{2,1,0:T(8,128)S(1)}, u32[]{:S(2)}, u32[]{:S(2)}) collective-permute-start(f32[8,32,128]{2,1,0:T(8,128)S(1)} %get-tuple-element.47), channel_id=1, source_target_pairs={{0,2},{1,3},{2,0},{3,1},{4,6},{5,7},{6,4},{7,5},{8,10},{9,11},{10,... | collective-permute-start | bytes 393224 | tf_op jit(solution)/shard_map/ppermute | solution.py:735
  41.2 5.6 %pack.1 = f32[8,48,256]{2,1,0:T(8,128)} custom-call(s32[64,128]{1,0:T(8,128)S(1)} %rank.1.target_ref, s32[192,128]{1,0:T(8,128)S(1)} %pad_add_fusion.ints_ref, f32[128,128]{1,0:T(8,128)S(1)} %pad_maximum_fusion.floats_ref, f32[3,8192]{1,0:T(4,128)S(1)} %copy-done.4), custom_call_target="tpu_custom_call" | custom-call | flops 8589934592 | bytes 1048576 | tf_op jit(solution)/shard_map/pack/pallas_call | solution.py:173
  46.8 3.6 %all-to-all-start = ((f32[8,48,256]{2,1,0:T(8,128)}), f32[8,48,256]{2,1,0:T(8,128)S(1)}, u32[]{:S(2)}, u32[]{:S(2)}) async-start(f32[8,48,256]{2,1,0:T(8,128)} %pack.1), calls=%async_computation | async-start | bytes 786432 | tf_op jit(solution)/shard_map/all_to_all | solution.py:769
  50.5 2.9 %collective-permute-start.10 = (f32[8,32,128]{2,1,0:T(8,128)S(1)}, f32[8,32,128]{2,1,0:T(8,128)S(1)}, u32[]{:S(2)}, u32[]{:S(2)}) collective-permute-start(f32[8,32,128]{2,1,0:T(8,128)S(1)} %add_add_fusion.1.refs_1_), channel_id=1, source_target_pairs={{0,3},{1,0},{2,1},{3,2},{4,7},{5,4},{6,5},{7,6},{8,11},{9,8},{10,9... | collective-permute-start | bytes 393224 | tf_op jit(solution)/shard_map/ppermute | solution.py:741
  54.4 2.8 %collective-permute-done.10.refs_4_ = f32[8,32,128]{2,1,0:T(8,128)S(1)} collective-permute-done((f32[8,32,128]{2,1,0:T(8,128)S(1)}, f32[8,32,128]{2,1,0:T(8,128)S(1)}, u32[]{:S(2)}, u32[]{:S(2)}) %collective-permute-start.10) | collective-permute-done | bytes 131104 | tf_op jit(solution)/shard_map/ppermute | solution.py:741
  57.2 9.1 %collective-permute-done.9.refs_3_ = f32[8,32,128]{2,1,0:T(8,128)S(1)} collective-permute-done((f32[8,32,128]{2,1,0:T(8,128)S(1)}, f32[8,32,128]{2,1,0:T(8,128)S(1)}, u32[]{:S(2)}, u32[]{:S(2)}) %collective-permute-start.9) | collective-permute-done | bytes 131104 | tf_op jit(solution)/shard_map/ppermute | solution.py:741
  66.4 13.9 %stencil.1 = (f32[8,8,256]{2,1,0:T(8,128)}, f32[8,32,128]{2,1,0:T(8,128)S(1)}, f32[8,32,128]{2,1,0:T(8,128)S(1)}, f32[8,32,128]{2,1,0:T(8,128)S(1)}, f32[8,32,128]{2,1,0:T(8,128)S(1)}) custom-call(s32[1]{0:T(128)} %bitcast.refs_0_, f32[8,32,128]{2,1,0:T(8,128)S(1)} %add_add_fusion.1.refs_1_, f32[8,32,128]{2,1,0:T(8,128)S(1)} %collective-permute-done.8.refs_2_, ...), custom_call_target="tpu_custom_call" | custom-call | flops 17179869184 | bytes 1048576 | tf_op jit(solution)/shard_map/stencil/pallas_call | solution.py:328
  81.4 2.8 %collective-permute-start.13 = (f32[8,32,128]{2,1,0:T(8,128)S(1)}, f32[8,32,128]{2,1,0:T(8,128)S(1)}, u32[]{:S(2)}, u32[]{:S(2)}) collective-permute-start(f32[8,32,128]{2,1,0:T(8,128)S(1)} %get-tuple-element.53), channel_id=1, source_target_pairs={{0,3},{1,0},{2,1},{3,2},{4,7},{5,4},{6,5},{7,6},{8,11},{9,8},{10,9... | collective-permute-start | bytes 393224 | tf_op jit(solution)/shard_map/ppermute | solution.py:735
  84.2 4.3 %collective-permute-done.11 = f32[8,32,128]{2,1,0:T(8,128)S(1)} collective-permute-done((f32[8,32,128]{2,1,0:T(8,128)S(1)}, f32[8,32,128]{2,1,0:T(8,128)S(1)}, u32[]{:S(2)}, u32[]{:S(2)}) %collective-permute-start.11) | collective-permute-done | bytes 131104 | tf_op jit(solution)/shard_map/ppermute | solution.py:735
  88.6 3.1 %collective-permute-done.12 = f32[8,32,128]{2,1,0:T(8,128)S(1)} collective-permute-done((f32[8,32,128]{2,1,0:T(8,128)S(1)}, f32[8,32,128]{2,1,0:T(8,128)S(1)}, u32[]{:S(2)}, u32[]{:S(2)}) %collective-permute-start.12) | collective-permute-done | bytes 131104 | tf_op jit(solution)/shard_map/ppermute | solution.py:735
  91.7 4.5 %collective-permute-start.16 = (f32[8,32,128]{2,1,0:T(8,128)S(1)}, f32[8,32,128]{2,1,0:T(8,128)S(1)}, u32[]{:S(2)}, u32[]{:S(2)}) collective-permute-start(f32[8,32,128]{2,1,0:T(8,128)S(1)} %add_add_fusion.refs_1_), channel_id=1, source_target_pairs={{0,3},{1,0},{2,1},{3,2},{4,7},{5,4},{6,5},{7,6},{8,11},{9,8},{10,9... | collective-permute-start | bytes 393224 | tf_op jit(solution)/shard_map/ppermute | solution.py:741
  96.8 3.3 %collective-permute-done.16.refs_4_ = f32[8,32,128]{2,1,0:T(8,128)S(1)} collective-permute-done((f32[8,32,128]{2,1,0:T(8,128)S(1)}, f32[8,32,128]{2,1,0:T(8,128)S(1)}, u32[]{:S(2)}, u32[]{:S(2)}) %collective-permute-start.16) | collective-permute-done | bytes 131104 | tf_op jit(solution)/shard_map/ppermute | solution.py:741
  100.1 7.8 %collective-permute-done.15.refs_3_ = f32[8,32,128]{2,1,0:T(8,128)S(1)} collective-permute-done((f32[8,32,128]{2,1,0:T(8,128)S(1)}, f32[8,32,128]{2,1,0:T(8,128)S(1)}, u32[]{:S(2)}, u32[]{:S(2)}) %collective-permute-start.15) | collective-permute-done | bytes 131104 | tf_op jit(solution)/shard_map/ppermute | solution.py:741
  107.9 5.2 %all-to-all-start.1 = ((f32[8,8,256]{2,1,0:T(8,128)}), f32[8,8,256]{2,1,0:T(8,128)S(1)}, u32[]{:S(2)}, u32[]{:S(2)}) async-start(f32[8,8,256]{2,1,0:T(8,128)} %get-tuple-element.66), calls=%async_computation.1 | async-start | bytes 131072 | tf_op jit(solution)/shard_map/all_to_all | solution.py:773
  113.1 8.7 %backward.1 = (f32[32,32,128]{2,1,0:T(8,128)}, f32[8,32,640]{2,1,0:T(8,128)S(1)}, f32[8,32,640]{2,1,0:T(8,128)S(1)}, f32[32,640]{1,0:T(8,128)S(1)}, f32[16,640]{...) custom-call(s32[1]{0:T(128)} %bitcast.refs_0_, f32[8,32,128]{2,1,0:T(8,128)S(1)} %add_add_fusion.refs_1_, ...), custom_call_target="tpu_custom_call" | custom-call | flops 8589934592 | bytes 8388608 | tf_op jit(solution)/shard_map/backward/pallas_call | solution.py:692
  121.9 2.1 %collective-permute-start.17 = (f32[8,32,640]{2,1,0:T(8,128)S(1)}, f32[8,32,640]{2,1,0:T(8,128)S(1)}, u32[]{:S(2)}, u32[]{:S(2)}) collective-permute-start(f32[8,32,640]{2,1,0:T(8,128)S(1)} %get-tuple-element.68), channel_id=1, source_target_pairs={{0,16},{4,20},{8,24},{12,28},{16,0},{20,4},{24,8},{28,12},{1,17},{... | collective-permute-start | bytes 1966088 | tf_op jit(solution)/shard_map/ppermute | solution.py:618
  125.7 1.8 %collective-permute-start.18 = (f32[32,640]{1,0:T(8,128)S(1)}, f32[32,640]{1,0:T(8,128)S(1)}, u32[]{:S(2)}, u32[]{:S(2)}) collective-permute-start(f32[32,640]{1,0:T(8,128)S(1)} %get-tuple-element.69), channel_id=1, source_target_pairs={{0,12},{4,0},{8,4},{12,8},{16,28},{20,16},{24,20},{28,24},{1,13},{... | collective-permute-start | bytes 245768 | tf_op jit(solution)/shard_map/ppermute | solution.py:618
  127.5 3.1 %unpack.1 = f32[64,128]{1,0:T(8,128)} custom-call(s32[64,128]{1,0:T(8,128)S(1)} %rank.1.target_ref, f32[64,256]{1,0:T(8,128)S(1)} %bitcast.8), custom_call_target="tpu_custom_call" | custom-call | flops 2147483648 | bytes 262144 | tf_op jit(solution)/shard_map/unpack/pallas_call | solution.py:372
  130.6 9.1 %collective-permute-done.20.refs_3_ = f32[16,640]{1,0:T(8,128)S(1)} collective-permute-done((f32[16,640]{1,0:T(8,128)S(1)}, f32[16,640]{1,0:T(8,128)S(1)}, u32[]{:S(2)}, u32[]{:S(2)}) %collective-permute-start.20) | collective-permute-done | bytes 40992 | tf_op jit(solution)/shard_map/ppermute | solution.py:618
  139.8 1.8 %collective-permute-done.21.refs_4_ = f32[24,640]{1,0:T(8,128)S(1)} collective-permute-done((f32[24,640]{1,0:T(8,128)S(1)}, f32[24,640]{1,0:T(8,128)S(1)}, u32[]{:S(2)}, u32[]{:S(2)}) %collective-permute-start.21) | collective-permute-done | bytes 61472 | tf_op jit(solution)/shard_map/ppermute | solution.py:618
  (53 shorter events, 18.6 us)
Async XLA Ops:
  0.6 21.2 %collective-permute-start = (f32[8,32,640]{2,1,0:T(8,128)}, f32[8,32,640]{2,1,0:T(8,128)S(1)}, u32[]{:S(2)}, u32[]{:S(2)}) collective-permute-start(f32[8,32,640]{2,1,0:T(8,128)} %alpha_ref.1), channel_id=1, source_target_pairs={{0,16},{4,20},{8,24},{12,28},{16,0},{20,4},{24,8},{28,12},{1,17},{... | collective-permute-start | bytes 1966088 | tf_op jit(solution)/shard_map/ppermute | solution.py:618
  4.6 16.1 %collective-permute-start.2 = (f32[32,640]{1,0:T(8,128)S(1)}, f32[32,640]{1,0:T(8,128)S(1)}, u32[]{:S(2)}, u32[]{:S(2)}) collective-permute-start(f32[32,640]{1,0:T(8,128)S(1)} %reshape.32), channel_id=1, source_target_pairs={{0,20},{4,24},{8,28},{12,16},{16,4},{20,8},{24,12},{28,0},{1,21},{... | collective-permute-start | bytes 245768 | tf_op jit(solution)/shard_map/ppermute | solution.py:618
  4.7 11.8 %collective-permute-start.1 = (f32[32,640]{1,0:T(8,128)S(1)}, f32[32,640]{1,0:T(8,128)S(1)}, u32[]{:S(2)}, u32[]{:S(2)}) collective-permute-start(f32[32,640]{1,0:T(8,128)S(1)} %reshape.32), channel_id=1, source_target_pairs={{0,4},{4,8},{8,12},{12,0},{16,20},{20,24},{24,28},{28,16},{1,5},{5... | collective-permute-start | bytes 245768 | tf_op jit(solution)/shard_map/ppermute | solution.py:618
  7.3 14.5 %collective-permute-start.4 = (f32[40,640]{1,0:T(8,128)S(1)}, f32[40,640]{1,0:T(8,128)S(1)}, u32[]{:S(2)}, u32[]{:S(2)}) collective-permute-start(f32[40,640]{1,0:T(8,128)S(1)} %reshape.33), channel_id=1, source_target_pairs={{0,28},{4,16},{8,20},{12,24},{16,12},{20,0},{24,4},{28,8},{1,29},{... | collective-permute-start | bytes 307208 | tf_op jit(solution)/shard_map/ppermute | solution.py:618
  8.4 13.4 %collective-permute-start.3 = (f32[40,640]{1,0:T(8,128)S(1)}, f32[40,640]{1,0:T(8,128)S(1)}, u32[]{:S(2)}, u32[]{:S(2)}) collective-permute-start(f32[40,640]{1,0:T(8,128)S(1)} %reshape.33), channel_id=1, source_target_pairs={{0,12},{4,0},{8,4},{12,8},{16,28},{20,16},{24,20},{28,24},{1,13},{... | collective-permute-start | bytes 307208 | tf_op jit(solution)/shard_map/ppermute | solution.py:618
  35.7 14.7 %collective-permute-start.5 = (f32[8,32,128]{2,1,0:T(8,128)S(1)}, f32[8,32,128]{2,1,0:T(8,128)S(1)}, u32[]{:S(2)}, u32[]{:S(2)}) collective-permute-start(f32[8,32,128]{2,1,0:T(8,128)S(1)} %get-tuple-element.46), channel_id=1, source_target_pairs={{0,1},{1,2},{2,3},{3,0},{4,5},{5,6},{6,7},{7,4},{8,9},{9,10},{10,1... | collective-permute-start | bytes 393224 | tf_op jit(solution)/shard_map/ppermute | solution.py:735
  37.3 13.1 %collective-permute-start.6 = (f32[8,32,128]{2,1,0:T(8,128)S(1)}, f32[8,32,128]{2,1,0:T(8,128)S(1)}, u32[]{:S(2)}, u32[]{:S(2)}) collective-permute-start(f32[8,32,128]{2,1,0:T(8,128)S(1)} %get-tuple-element.47), channel_id=1, source_target_pairs={{0,2},{1,3},{2,0},{3,1},{4,6},{5,7},{6,4},{7,5},{8,10},{9,11},{10,... | collective-permute-start | bytes 393224 | tf_op jit(solution)/shard_map/ppermute | solution.py:735
  39.9 10.5 %collective-permute-start.7 = (f32[8,32,128]{2,1,0:T(8,128)S(1)}, f32[8,32,128]{2,1,0:T(8,128)S(1)}, u32[]{:S(2)}, u32[]{:S(2)}) collective-permute-start(f32[8,32,128]{2,1,0:T(8,128)S(1)} %get-tuple-element.48), channel_id=1, source_target_pairs={{0,3},{1,0},{2,1},{3,2},{4,7},{5,4},{6,5},{7,6},{8,11},{9,8},{10,9... | collective-permute-start | bytes 393224 | tf_op jit(solution)/shard_map/ppermute | solution.py:735
  46.8 19.5 %all-to-all-start = ((f32[8,48,256]{2,1,0:T(8,128)}), f32[8,48,256]{2,1,0:T(8,128)S(1)}, u32[]{:S(2)}, u32[]{:S(2)}) async-start(f32[8,48,256]{2,1,0:T(8,128)} %pack.1), calls=%async_computation | async-start | bytes 786432 | tf_op jit(solution)/shard_map/all_to_all | solution.py:769
  50.5 6.7 %collective-permute-start.10 = (f32[8,32,128]{2,1,0:T(8,128)S(1)}, f32[8,32,128]{2,1,0:T(8,128)S(1)}, u32[]{:S(2)}, u32[]{:S(2)}) collective-permute-start(f32[8,32,128]{2,1,0:T(8,128)S(1)} %add_add_fusion.1.refs_1_), channel_id=1, source_target_pairs={{0,3},{1,0},{2,1},{3,2},{4,7},{5,4},{6,5},{7,6},{8,11},{9,8},{10,9... | collective-permute-start | bytes 393224 | tf_op jit(solution)/shard_map/ppermute | solution.py:741
  53.3 13.0 %collective-permute-start.9 = (f32[8,32,128]{2,1,0:T(8,128)S(1)}, f32[8,32,128]{2,1,0:T(8,128)S(1)}, u32[]{:S(2)}, u32[]{:S(2)}) collective-permute-start(f32[8,32,128]{2,1,0:T(8,128)S(1)} %add_add_fusion.1.refs_1_), channel_id=1, source_target_pairs={{0,2},{1,3},{2,0},{3,1},{4,6},{5,7},{6,4},{7,5},{8,10},{9,11},{10,... | collective-permute-start | bytes 393224 | tf_op jit(solution)/shard_map/ppermute | solution.py:741
  54.4 11.9 %collective-permute-start.8 = (f32[8,32,128]{2,1,0:T(8,128)S(1)}, f32[8,32,128]{2,1,0:T(8,128)S(1)}, u32[]{:S(2)}, u32[]{:S(2)}) collective-permute-start(f32[8,32,128]{2,1,0:T(8,128)S(1)} %add_add_fusion.1.refs_1_), channel_id=1, source_target_pairs={{0,1},{1,2},{2,3},{3,0},{4,5},{5,6},{6,7},{7,4},{8,9},{9,10},{10,1... | collective-permute-start | bytes 393224 | tf_op jit(solution)/shard_map/ppermute | solution.py:741
  80.3 8.3 %collective-permute-start.11 = (f32[8,32,128]{2,1,0:T(8,128)S(1)}, f32[8,32,128]{2,1,0:T(8,128)S(1)}, u32[]{:S(2)}, u32[]{:S(2)}) collective-permute-start(f32[8,32,128]{2,1,0:T(8,128)S(1)} %get-tuple-element.51), channel_id=1, source_target_pairs={{0,1},{1,2},{2,3},{3,0},{4,5},{5,6},{6,7},{7,4},{8,9},{9,10},{10,1... | collective-permute-start | bytes 393224 | tf_op jit(solution)/shard_map/ppermute | solution.py:735
  80.3 11.3 %collective-permute-start.12 = (f32[8,32,128]{2,1,0:T(8,128)S(1)}, f32[8,32,128]{2,1,0:T(8,128)S(1)}, u32[]{:S(2)}, u32[]{:S(2)}) collective-permute-start(f32[8,32,128]{2,1,0:T(8,128)S(1)} %get-tuple-element.52), channel_id=1, source_target_pairs={{0,2},{1,3},{2,0},{3,1},{4,6},{5,7},{6,4},{7,5},{8,10},{9,11},{10,... | collective-permute-start | bytes 393224 | tf_op jit(solution)/shard_map/ppermute | solution.py:735
  81.4 10.2 %collective-permute-start.13 = (f32[8,32,128]{2,1,0:T(8,128)S(1)}, f32[8,32,128]{2,1,0:T(8,128)S(1)}, u32[]{:S(2)}, u32[]{:S(2)}) collective-permute-start(f32[8,32,128]{2,1,0:T(8,128)S(1)} %get-tuple-element.53), channel_id=1, source_target_pairs={{0,3},{1,0},{2,1},{3,2},{4,7},{5,4},{6,5},{7,6},{8,11},{9,8},{10,9... | collective-permute-start | bytes 393224 | tf_op jit(solution)/shard_map/ppermute | solution.py:735
  91.7 8.5 %collective-permute-start.16 = (f32[8,32,128]{2,1,0:T(8,128)S(1)}, f32[8,32,128]{2,1,0:T(8,128)S(1)}, u32[]{:S(2)}, u32[]{:S(2)}) collective-permute-start(f32[8,32,128]{2,1,0:T(8,128)S(1)} %add_add_fusion.refs_1_), channel_id=1, source_target_pairs={{0,3},{1,0},{2,1},{3,2},{4,7},{5,4},{6,5},{7,6},{8,11},{9,8},{10,9... | collective-permute-start | bytes 393224 | tf_op jit(solution)/shard_map/ppermute | solution.py:741
  96.2 11.7 %collective-permute-start.15 = (f32[8,32,128]{2,1,0:T(8,128)S(1)}, f32[8,32,128]{2,1,0:T(8,128)S(1)}, u32[]{:S(2)}, u32[]{:S(2)}) collective-permute-start(f32[8,32,128]{2,1,0:T(8,128)S(1)} %add_add_fusion.refs_1_), channel_id=1, source_target_pairs={{0,2},{1,3},{2,0},{3,1},{4,6},{5,7},{6,4},{7,5},{8,10},{9,11},{10,... | collective-permute-start | bytes 393224 | tf_op jit(solution)/shard_map/ppermute | solution.py:741
  96.3 11.6 %collective-permute-start.14 = (f32[8,32,128]{2,1,0:T(8,128)S(1)}, f32[8,32,128]{2,1,0:T(8,128)S(1)}, u32[]{:S(2)}, u32[]{:S(2)}) collective-permute-start(f32[8,32,128]{2,1,0:T(8,128)S(1)} %add_add_fusion.refs_1_), channel_id=1, source_target_pairs={{0,1},{1,2},{2,3},{3,0},{4,5},{5,6},{6,7},{7,4},{8,9},{9,10},{10,1... | collective-permute-start | bytes 393224 | tf_op jit(solution)/shard_map/ppermute | solution.py:741
  107.9 13.9 %all-to-all-start.1 = ((f32[8,8,256]{2,1,0:T(8,128)}), f32[8,8,256]{2,1,0:T(8,128)S(1)}, u32[]{:S(2)}, u32[]{:S(2)}) async-start(f32[8,8,256]{2,1,0:T(8,128)} %get-tuple-element.66), calls=%async_computation.1 | async-start | bytes 131072 | tf_op jit(solution)/shard_map/all_to_all | solution.py:773
  121.9 19.7 %collective-permute-start.17 = (f32[8,32,640]{2,1,0:T(8,128)S(1)}, f32[8,32,640]{2,1,0:T(8,128)S(1)}, u32[]{:S(2)}, u32[]{:S(2)}) collective-permute-start(f32[8,32,640]{2,1,0:T(8,128)S(1)} %get-tuple-element.68), channel_id=1, source_target_pairs={{0,16},{4,20},{8,24},{12,28},{16,0},{20,4},{24,8},{28,12},{1,17},{... | collective-permute-start | bytes 1966088 | tf_op jit(solution)/shard_map/ppermute | solution.py:618
  123.9 15.8 %collective-permute-start.20 = (f32[16,640]{1,0:T(8,128)S(1)}, f32[16,640]{1,0:T(8,128)S(1)}, u32[]{:S(2)}, u32[]{:S(2)}) collective-permute-start(f32[16,640]{1,0:T(8,128)S(1)} %get-tuple-element.71), channel_id=1, source_target_pairs={{0,28},{4,16},{8,20},{12,24},{16,12},{20,0},{24,4},{28,8},{1,29},{... | collective-permute-start | bytes 122888 | tf_op jit(solution)/shard_map/ppermute | solution.py:618
  124.9 16.7 %collective-permute-start.21 = (f32[24,640]{1,0:T(8,128)S(1)}, f32[24,640]{1,0:T(8,128)S(1)}, u32[]{:S(2)}, u32[]{:S(2)}) collective-permute-start(f32[24,640]{1,0:T(8,128)S(1)} %get-tuple-element.72), channel_id=1, source_target_pairs={{0,20},{4,24},{8,28},{12,16},{16,4},{20,8},{24,12},{28,0},{1,21},{... | collective-permute-start | bytes 184328 | tf_op jit(solution)/shard_map/ppermute | solution.py:618
  125.7 15.9 %collective-permute-start.18 = (f32[32,640]{1,0:T(8,128)S(1)}, f32[32,640]{1,0:T(8,128)S(1)}, u32[]{:S(2)}, u32[]{:S(2)}) collective-permute-start(f32[32,640]{1,0:T(8,128)S(1)} %get-tuple-element.69), channel_id=1, source_target_pairs={{0,12},{4,0},{8,4},{12,8},{16,28},{20,16},{24,20},{28,24},{1,13},{... | collective-permute-start | bytes 245768 | tf_op jit(solution)/shard_map/ppermute | solution.py:618
  127.5 14.0 %collective-permute-start.19 = (f32[40,640]{1,0:T(8,128)S(1)}, f32[40,640]{1,0:T(8,128)S(1)}, u32[]{:S(2)}, u32[]{:S(2)}) collective-permute-start(f32[40,640]{1,0:T(8,128)S(1)} %get-tuple-element.70), channel_id=1, source_target_pairs={{0,4},{4,8},{8,12},{12,0},{16,20},{20,24},{24,28},{28,16},{1,5},{5... | collective-permute-start | bytes 307208 | tf_op jit(solution)/shard_map/ppermute | solution.py:618
  (7 other events, 163.2 us)

commit v6 on v5

--- a/solution.py
+++ b/solution.py
@@ -221,11 +221,18 @@
         field[where, :] = (part[...] + static).reshape(share * fine_x, fine_y)
     for shift in range(chunk):
         field_t[shift, :, rows:] = jnp.zeros((2 * fine_y, field_t.shape[2] - rows), HALF)
-        for g in range(rows // LANES):
-            begin = shift * fine_x + g * LANES
-            high, low = split_two(field[begin:begin + LANES, :].T)
+    after = jnp.zeros((fine_y, LANES), jnp.float32)
+    lane = iota((fine_y, LANES), 1)
+    for g in reversed(range(rows // LANES)):
+        now = field[g * LANES:(g + 1) * LANES, :].T
+        for shift in range(chunk):
+            value, move = now, LANES - shift * fine_x
+            if shift:
+                value = jnp.where(lane < move, pltpu.roll(now, move, 1), pltpu.roll(after, move, 1))
+            high, low = split_two(value)
             field_t[shift, :fine_y, g * LANES:(g + 1) * LANES] = high
             field_t[shift, fine_y:, g * LANES:(g + 1) * LANES] = low
+        after = now
 
     fetch.wait()
 
@@ -432,8 +439,22 @@
     return pltpu.roll(field, 1, 1) + pltpu.roll(field, width - 1, 1)
 
 
+def edges_kernel(strips, rows, alpha_ref, mix_ref, alpha_out, mix_out, *outs):
+    coarse_y = alpha_ref.shape[1]
+    alpha_out[...] = alpha_ref[...]
+    mix_out[...] = mix_ref[...]
+    for (begin, counts), left, right in zip(zip(rows, strips), outs[:len(strips)], outs[len(strips):]):
+        at_left, at_right = 0, 0
+        for i, (to_left, to_right) in enumerate(counts):
+            if to_left:
+                left[at_left:at_left + to_left, :] = alpha_ref[begin + i, coarse_y - to_left:, :]
+            if to_right:
+                right[at_right:at_right + to_right, :] = alpha_ref[begin + i, :to_right, :]
+            at_left, at_right = at_left + to_left, at_right + to_right
+
+
 def ensemble_kernel(
-    coarse_x, coarse_y, offsets,
+    coarse_x, coarse_y, offsets, strips,
     me_ref, alpha_ref, above_ref, below_ref,
     left_ref, left_above_ref, left_below_ref, right_ref, right_above_ref, right_below_ref,
     mix_ref, pert_hbm, out_refs, pert_ref, sem, ext, coarse,
@@ -446,18 +467,19 @@
     ext[:, EDGE + coarse_y:, :] = jnp.zeros((ext.shape[0], EDGE, channels), jnp.float32)
     above, below = offsets
     groups = (
-        (0, REACH, above, above_ref, left_above_ref, right_above_ref),
-        (REACH, coarse_x, 0, alpha_ref, left_ref, right_ref),
-        (REACH + coarse_x, REACH + 1, below, below_ref, left_below_ref, right_below_ref),
+        (0, REACH, above, strips[1], above_ref, left_above_ref, right_above_ref),
+        (REACH, coarse_x, 0, strips[0], alpha_ref, left_ref, right_ref),
+        (REACH + coarse_x, REACH + 1, below, strips[-1], below_ref, left_below_ref, right_below_ref),
     )
-    for begin, count, offset, middle, left, right in groups:
+    for begin, count, offset, counts, middle, left, right in groups:
         ext[begin:begin + count, EDGE:EDGE + coarse_y, :] = middle[offset:offset + count]
         for i in range(count):
-            at = offset + i
-            ext[begin + i, EDGE - REACH:EDGE, :] = left[at * REACH:(at + 1) * REACH, :]
-            ext[begin + i, EDGE + coarse_y:EDGE + coarse_y + REACH + 1, :] = right[
-                at * (REACH + 1):(at + 1) * (REACH + 1), :
-            ]
+            at_left, at_right = [sum(row[side] for row in counts[:offset + i]) for side in range(2)]
+            n_left, n_right = counts[offset + i]
+            if n_left:
+                ext[begin + i, EDGE - n_left:EDGE, :] = left[at_left:at_left + n_left, :]
+            if n_right:
+                ext[begin + i, EDGE + coarse_y:EDGE + coarse_y + n_right, :] = right[at_right:at_right + n_right, :]
     spread_y = interpolation((coarse_y + PAD, fine_y), 1, 0, EDGE)
     spread_y = jnp.concatenate([spread_y, spread_y], 0)
     high, low = mixing(mix_ref)
@@ -622,31 +644,36 @@
     coarse_x, coarse_y, channels = alpha.shape
     members, levels, fine_x, fine_y = ens_pert.shape
     joined = lax.axis_size("tx") == 2
-    ends = alpha[:, coarse_y - REACH:]
-    starts = alpha[:, :REACH + 1]
-
-    def flat(strip):
-        return strip.reshape(-1, channels)
-
+    strips = [[[REACH, REACH + 1]] * coarse_x] + corner_counts(coarse_x, joined)
+    rows = [0, 0] if joined else [0, coarse_x - REACH, 0]
+    shapes = [alpha.shape, mix.shape]
+    shapes += [(sum(count[side] for count in counts), channels) for side in range(2) for counts in strips]
+    held, mix, *sides = pl.pallas_call(
+        functools.partial(edges_kernel, strips, rows),
+        out_shape=tuple(jax.ShapeDtypeStruct(shape, jnp.float32) for shape in shapes),
+        in_specs=[VMEM] * 2,
+        out_specs=(VMEM,) * len(shapes),
+        compiler_params=room(8),
+        cost_estimate=pl.CostEstimate(flops=1 << 10, bytes_accessed=1 << 10, transcendentals=0),
+        name="edges",
+    )(alpha, mix)
+    ends, starts = sides[:len(strips)], sides[len(strips):]
     if joined:
-        other = shifted(alpha, 1, 0)
-        above = below = other
-        left_above = left_below = shifted(flat(ends), 1, 1)
-        right_above = right_below = shifted(flat(starts), 1, -1)
+        above = below = shifted(alpha, 1, 0)
+        left_above = left_below = shifted(ends[1], 1, 1)
+        right_above = right_below = shifted(starts[1], 1, -1)
         offsets = (coarse_x - REACH, 0)
     else:
-        last = slice(coarse_x - REACH, coarse_x)
-        first = slice(0, REACH + 1)
-        above, below = shifted(alpha[last], 1, 0), shifted(alpha[first], -1, 0)
-        left_above, left_below = shifted(flat(ends[last]), 1, 1), shifted(flat(ends[first]), -1, 1)
-        right_above, right_below = shifted(flat(starts[last]), 1, -1), shifted(flat(starts[first]), -1, -1)
+        above, below = shifted(alpha[coarse_x - REACH:], 1, 0), shifted(alpha[:REACH + 1], -1, 0)
+        left_above, left_below = shifted(ends[1], 1, 1), shifted(ends[2], -1, 1)
+        right_above, right_below = shifted(starts[1], 1, -1), shifted(starts[2], -1, -1)
         offsets = (0, 0)
-    left, right = shifted(flat(ends), 0, 1), shifted(flat(starts), 0, -1)
+    left, right = shifted(ends[0], 0, 1), shifted(starts[0], 0, -1)
     left, beside = lax.optimization_barrier((left, beside))
     groups = lax.axis_size("mem")
 
     def kernel(*refs):
-        ensemble_kernel(coarse_x, coarse_y, offsets, *refs[:12], refs[12:12 + groups], *refs[12 + groups:])
+        ensemble_kernel(coarse_x, coarse_y, offsets, strips, *refs[:12], refs[12:12 + groups], *refs[12 + groups:])
 
     parts = pl.pallas_call(
         kernel,
@@ -662,7 +689,7 @@
         compiler_params=room(50),
         cost_estimate=pl.CostEstimate(flops=8 << 30, bytes_accessed=8 << 20, transcendentals=0),
         name="ensemble",
-    )(me, alpha, above, below, left, left_above, left_below, right, right_above, right_below, mix, ens_pert)
+    )(me, held, above, below, left, left_above, left_below, right, right_above, right_below, mix, ens_pert)
     return parts, beside
 
 

time: 145 us -> 141 us (0.972)
  waiting for transfers between devices: 46.7 us -> 40.5 us
  starting transfers between devices: 39.4 us -> 44.5 us
  local copies, waits for them, and re-layouts: 3.78 us -> 1.87 us
    ppermute x10, waiting for transfers between devices: 16.3 us -> 13.5 us  [shifted(): return lax.ppermute(value, ('tx', 'ty'), pairs)]
    ppermute x6, starting transfers between devices: 9.52 us -> 11.5 us  [owned_sum(): lax.ppermute(parts[d], 'mem', [(i, (i + d) % count) for i in range(count)])]
    slice x2 -> x0, local copies, waits for them, and re-layouts: 1.89 us -> none  [the longest x1 0.97 us: ensemble(): ends = alpha[:, coarse_y - REACH:]]
    ppermute x6, waiting for transfers between devices: 23 us -> 21.3 us  [gathered(): lax.ppermute(own, 'mem', [(i, (i + d) % count) for i in range(count)])]
    ppermute x6, waiting for transfers between devices: 7.39 us -> 5.76 us  [owned_sum(): lax.ppermute(parts[d], 'mem', [(i, (i + d) % count) for i in range(count)])]
  transfers between devices with their start and end apart: 24 -> 24, of which waited for: 10 -> 10; matrix products, arithmetic and copies ran while one was open for 2% -> 1% of each run, Pallas kernels for 16% -> 16%
where the time goes in v6:
time: 141 us; the launch traced here: 139 us
  Pallas kernels  49.4 us (35%)
  starting transfers between devices  44.5 us (32%)
  waiting for transfers between devices  40.5 us (29%)
  local copies, waits for them, and re-layouts  1.87 us (1%)
  other arithmetic  1.65 us (1%)
  between operations  1.46 us (1%)
    ppermute x6, waiting for transfers between devices, gathered(): lax.ppermute(own, 'mem', [(i, (i + d) % count) for i in range(count)])  21.3 us
    ppermute x10, waiting for transfers between devices, shifted(): return lax.ppermute(value, ('tx', 'ty'), pairs)  13.5 us
    pallas_call x1, Pallas kernels, stencil(): pl.pallas_call(kernel, out_shape=(jax.ShapeDtypeStruct((sources, deep, bl...  13.3 us
    ppermute x10, starting transfers between devices, shifted(): return lax.ppermute(value, ('tx', 'ty'), pairs)  13.1 us
    pallas_call x1, Pallas kernels, ensemble(): pl.pallas_call(kernel, out_shape=tuple((jax.ShapeDtypeStruct((levels // g...  12.3 us
    ppermute x6, starting transfers between devices, owned_sum(): lax.ppermute(parts[d], 'mem', [(i, (i + d) % count) for i in range(count)])  11.5 us
    ppermute x6, starting transfers between devices, gathered(): lax.ppermute(own, 'mem', [(i, (i + d) % count) for i in range(count)])  10.1 us
    pallas_call x1, Pallas kernels, backward(): pl.pallas_call(kernel, out_shape=tuple((jax.ShapeDtypeStruct(shape, jnp.f...  8.74 us
  transfers between devices with their start and end apart: 24, of which 10 were waited for; matrix products, arithmetic and copies ran while one was open for 1% of the time, Pallas kernels for 16%

profile of v6, /device:TPU:0, one launch (start us, length us, event | category | flops | bytes accessed | tf_op | source)
XLA Modules:
  0.0 139.4 jit_solution(8490004784336526987)
XLA Ops:
  0.6 3.0 %collective-permute-start = (f32[8,32,640]{2,1,0:T(8,128)}, f32[8,32,640]{2,1,0:T(8,128)S(1)}, u32[]{:S(2)}, u32[]{:S(2)}) collective-permute-start(f32[8,32,640]{2,1,0:T(8,128)} %alpha_ref.3), channel_id=1, source_target_pairs={{0,16},{4,20},{8,24},{12,28},{16,0},{20,4},{24,8},{28,12},{1,17},{... | collective-permute-start | bytes 1966088 | tf_op jit(solution)/shard_map/ppermute | solution.py:640
  5.7 2.6 %collective-permute-start.4 = (f32[24,640]{1,0:T(8,128)S(1)}, f32[24,640]{1,0:T(8,128)S(1)}, u32[]{:S(2)}, u32[]{:S(2)}) collective-permute-start(f32[24,640]{1,0:T(8,128)S(1)} %get-tuple-element.50), channel_id=1, source_target_pairs={{0,28},{4,16},{8,20},{12,24},{16,12},{20,0},{24,4},{28,8},{1,29},{... | collective-permute-start | bytes 184328 | tf_op jit(solution)/shard_map/ppermute | solution.py:640
  12.3 5.2 %rank.1.target_ref = s32[64,128]{1,0:T(8,128)S(1)} custom-call(s32[1]{0:T(128)S(6)} %copy.15.count_ref, s32[192,128]{1,0:T(8,128)S(1)} %pad_add_fusion.ints_ref), custom_call_target="tpu_custom_call" | custom-call | flops 1048576 | bytes 131072 | tf_op jit(solution)/shard_map/rank/pallas_call | solution.py:101
  17.5 2.0 %collective-permute-done.2.refs_5_.refs_6_ = f32[16,640]{1,0:T(8,128)S(1)} collective-permute-done((f32[16,640]{1,0:T(8,128)S(1)}, f32[16,640]{1,0:T(8,128)S(1)}, u32[]{:S(2)}, u32[]{:S(2)}) %collective-permute-start.2) | collective-permute-done | bytes 40992 | tf_op jit(solution)/shard_map/ppermute | solution.py:640
  20.0 12.3 %ensemble.1 = (f32[8,32,128]{2,1,0:T(8,128)S(1)}, f32[8,32,128]{2,1,0:T(8,128)S(1)}, f32[8,32,128]{2,1,0:T(8,128)S(1)}, f32[8,32,128]{2,1,0:T(8,128)S(1)}) custom-call(s32[1]{0:T(128)} %bitcast.refs_0_, f32[8,32,640]{2,1,0:T(8,128)S(1)} %get-tuple-element.45.refs_1_, f32[8,32,640]{2,1,0:T(8,128)S(1)} %collective-permute-done.refs_2_.refs_3_, ...), custom_call_target="tpu_custom_call" | custom-call | flops 8589934592 | bytes 8388608 | tf_op jit(solution)/shard_map/ensemble/pallas_call | solution.py:678
  34.0 2.6 %collective-permute-start.6 = (f32[8,32,128]{2,1,0:T(8,128)S(1)}, f32[8,32,128]{2,1,0:T(8,128)S(1)}, u32[]{:S(2)}, u32[]{:S(2)}) collective-permute-start(f32[8,32,128]{2,1,0:T(8,128)S(1)} %get-tuple-element.59), channel_id=1, source_target_pairs={{0,2},{1,3},{2,0},{3,1},{4,6},{5,7},{6,4},{7,5},{8,10},{9,11},{10,... | collective-permute-start | bytes 393224 | tf_op jit(solution)/shard_map/ppermute | solution.py:762
  38.0 5.6 %pack.1 = f32[8,48,256]{2,1,0:T(8,128)} custom-call(s32[64,128]{1,0:T(8,128)S(1)} %rank.1.target_ref, s32[192,128]{1,0:T(8,128)S(1)} %pad_add_fusion.ints_ref, f32[128,128]{1,0:T(8,128)S(1)} %pad_maximum_fusion.floats_ref, f32[3,8192]{1,0:T(4,128)S(1)} %copy-done.6), custom_call_target="tpu_custom_call" | custom-call | flops 8589934592 | bytes 1048576 | tf_op jit(solution)/shard_map/pack/pallas_call | solution.py:173
  43.6 3.6 %all-to-all-start = ((f32[8,48,256]{2,1,0:T(8,128)}), f32[8,48,256]{2,1,0:T(8,128)S(1)}, u32[]{:S(2)}, u32[]{:S(2)}) async-start(f32[8,48,256]{2,1,0:T(8,128)} %pack.1), calls=%async_computation | async-start | bytes 786432 | tf_op jit(solution)/shard_map/all_to_all | solution.py:796
  47.2 2.8 %collective-permute-start.10 = (f32[8,32,128]{2,1,0:T(8,128)S(1)}, f32[8,32,128]{2,1,0:T(8,128)S(1)}, u32[]{:S(2)}, u32[]{:S(2)}) collective-permute-start(f32[8,32,128]{2,1,0:T(8,128)S(1)} %add_add_fusion.1.refs_1_), channel_id=1, source_target_pairs={{0,3},{1,0},{2,1},{3,2},{4,7},{5,4},{6,5},{7,6},{8,11},{9,8},{10,9... | collective-permute-start | bytes 393224 | tf_op jit(solution)/shard_map/ppermute | solution.py:768
  51.2 2.7 %collective-permute-done.10.refs_4_ = f32[8,32,128]{2,1,0:T(8,128)S(1)} collective-permute-done((f32[8,32,128]{2,1,0:T(8,128)S(1)}, f32[8,32,128]{2,1,0:T(8,128)S(1)}, u32[]{:S(2)}, u32[]{:S(2)}) %collective-permute-start.10) | collective-permute-done | bytes 131104 | tf_op jit(solution)/shard_map/ppermute | solution.py:768
  54.0 9.2 %collective-permute-done.9.refs_3_ = f32[8,32,128]{2,1,0:T(8,128)S(1)} collective-permute-done((f32[8,32,128]{2,1,0:T(8,128)S(1)}, f32[8,32,128]{2,1,0:T(8,128)S(1)}, u32[]{:S(2)}, u32[]{:S(2)}) %collective-permute-start.9) | collective-permute-done | bytes 131104 | tf_op jit(solution)/shard_map/ppermute | solution.py:768
  63.1 13.3 %stencil.1 = (f32[8,8,256]{2,1,0:T(8,128)}, f32[8,32,128]{2,1,0:T(8,128)S(1)}, f32[8,32,128]{2,1,0:T(8,128)S(1)}, f32[8,32,128]{2,1,0:T(8,128)S(1)}, f32[8,32,128]{2,1,0:T(8,128)S(1)}) custom-call(s32[1]{0:T(128)} %bitcast.refs_0_, f32[8,32,128]{2,1,0:T(8,128)S(1)} %add_add_fusion.1.refs_1_, f32[8,32,128]{2,1,0:T(8,128)S(1)} %collective-permute-done.8.refs_2_, ...), custom_call_target="tpu_custom_call" | custom-call | flops 17179869184 | bytes 1048576 | tf_op jit(solution)/shard_map/stencil/pallas_call | solution.py:335
  76.5 3.1 %collective-permute-start.12 = (f32[8,32,128]{2,1,0:T(8,128)S(1)}, f32[8,32,128]{2,1,0:T(8,128)S(1)}, u32[]{:S(2)}, u32[]{:S(2)}) collective-permute-start(f32[8,32,128]{2,1,0:T(8,128)S(1)} %get-tuple-element.64), channel_id=1, source_target_pairs={{0,2},{1,3},{2,0},{3,1},{4,6},{5,7},{6,4},{7,5},{8,10},{9,11},{10,... | collective-permute-start | bytes 393224 | tf_op jit(solution)/shard_map/ppermute | solution.py:762
  79.6 2.8 %collective-permute-start.13 = (f32[8,32,128]{2,1,0:T(8,128)S(1)}, f32[8,32,128]{2,1,0:T(8,128)S(1)}, u32[]{:S(2)}, u32[]{:S(2)}) collective-permute-start(f32[8,32,128]{2,1,0:T(8,128)S(1)} %get-tuple-element.65), channel_id=1, source_target_pairs={{0,3},{1,0},{2,1},{3,2},{4,7},{5,4},{6,5},{7,6},{8,11},{9,8},{10,9... | collective-permute-start | bytes 393224 | tf_op jit(solution)/shard_map/ppermute | solution.py:762
  82.4 2.0 %collective-permute-done.11 = f32[8,32,128]{2,1,0:T(8,128)S(1)} collective-permute-done((f32[8,32,128]{2,1,0:T(8,128)S(1)}, f32[8,32,128]{2,1,0:T(8,128)S(1)}, u32[]{:S(2)}, u32[]{:S(2)}) %collective-permute-start.11) | collective-permute-done | bytes 131104 | tf_op jit(solution)/shard_map/ppermute | solution.py:762
  84.4 3.8 %collective-permute-done.12 = f32[8,32,128]{2,1,0:T(8,128)S(1)} collective-permute-done((f32[8,32,128]{2,1,0:T(8,128)S(1)}, f32[8,32,128]{2,1,0:T(8,128)S(1)}, u32[]{:S(2)}, u32[]{:S(2)}) %collective-permute-start.12) | collective-permute-done | bytes 131104 | tf_op jit(solution)/shard_map/ppermute | solution.py:762
  88.2 5.5 %collective-permute-start.16 = (f32[8,32,128]{2,1,0:T(8,128)S(1)}, f32[8,32,128]{2,1,0:T(8,128)S(1)}, u32[]{:S(2)}, u32[]{:S(2)}) collective-permute-start(f32[8,32,128]{2,1,0:T(8,128)S(1)} %add_add_fusion.refs_1_), channel_id=1, source_target_pairs={{0,3},{1,0},{2,1},{3,2},{4,7},{5,4},{6,5},{7,6},{8,11},{9,8},{10,9... | collective-permute-start | bytes 393224 | tf_op jit(solution)/shard_map/ppermute | solution.py:768
  94.4 3.3 %collective-permute-done.16.refs_4_ = f32[8,32,128]{2,1,0:T(8,128)S(1)} collective-permute-done((f32[8,32,128]{2,1,0:T(8,128)S(1)}, f32[8,32,128]{2,1,0:T(8,128)S(1)}, u32[]{:S(2)}, u32[]{:S(2)}) %collective-permute-start.16) | collective-permute-done | bytes 131104 | tf_op jit(solution)/shard_map/ppermute | solution.py:768
  97.7 6.1 %collective-permute-done.15.refs_3_ = f32[8,32,128]{2,1,0:T(8,128)S(1)} collective-permute-done((f32[8,32,128]{2,1,0:T(8,128)S(1)}, f32[8,32,128]{2,1,0:T(8,128)S(1)}, u32[]{:S(2)}, u32[]{:S(2)}) %collective-permute-start.15) | collective-permute-done | bytes 131104 | tf_op jit(solution)/shard_map/ppermute | solution.py:768
  103.8 6.1 %all-to-all-start.1 = ((f32[8,8,256]{2,1,0:T(8,128)}), f32[8,8,256]{2,1,0:T(8,128)S(1)}, u32[]{:S(2)}, u32[]{:S(2)}) async-start(f32[8,8,256]{2,1,0:T(8,128)} %get-tuple-element.78), calls=%async_computation.1 | async-start | bytes 131072 | tf_op jit(solution)/shard_map/all_to_all | solution.py:800
  109.9 8.7 %backward.1 = (f32[32,32,128]{2,1,0:T(8,128)}, f32[8,32,640]{2,1,0:T(8,128)S(1)}, f32[8,32,640]{2,1,0:T(8,128)S(1)}, f32[32,640]{1,0:T(8,128)S(1)}, f32[16,640]{...) custom-call(s32[1]{0:T(128)} %bitcast.refs_0_, f32[8,32,128]{2,1,0:T(8,128)S(1)} %add_add_fusion.refs_1_, ...), custom_call_target="tpu_custom_call" | custom-call | flops 8589934592 | bytes 8388608 | tf_op jit(solution)/shard_map/backward/pallas_call | solution.py:719
  118.6 2.1 %collective-permute-start.17 = (f32[8,32,640]{2,1,0:T(8,128)S(1)}, f32[8,32,640]{2,1,0:T(8,128)S(1)}, u32[]{:S(2)}, u32[]{:S(2)}) collective-permute-start(f32[8,32,640]{2,1,0:T(8,128)S(1)} %get-tuple-element.80), channel_id=1, source_target_pairs={{0,16},{4,20},{8,24},{12,28},{16,0},{20,4},{24,8},{28,12},{1,17},{... | collective-permute-start | bytes 1966088 | tf_op jit(solution)/shard_map/ppermute | solution.py:640
  124.3 3.1 %unpack.1 = f32[64,128]{1,0:T(8,128)} custom-call(s32[64,128]{1,0:T(8,128)S(1)} %rank.1.target_ref, f32[64,256]{1,0:T(8,128)S(1)} %bitcast.8), custom_call_target="tpu_custom_call" | custom-call | flops 2147483648 | bytes 262144 | tf_op jit(solution)/shard_map/unpack/pallas_call | solution.py:379
  127.4 9.1 %collective-permute-done.20.refs_3_ = f32[16,640]{1,0:T(8,128)S(1)} collective-permute-done((f32[16,640]{1,0:T(8,128)S(1)}, f32[16,640]{1,0:T(8,128)S(1)}, u32[]{:S(2)}, u32[]{:S(2)}) %collective-permute-start.20) | collective-permute-done | bytes 40992 | tf_op jit(solution)/shard_map/ppermute | solution.py:640
  (50 shorter events, 17.2 us)
Async XLA Ops:
  0.6 19.4 %collective-permute-start = (f32[8,32,640]{2,1,0:T(8,128)}, f32[8,32,640]{2,1,0:T(8,128)S(1)}, u32[]{:S(2)}, u32[]{:S(2)}) collective-permute-start(f32[8,32,640]{2,1,0:T(8,128)} %alpha_ref.3), channel_id=1, source_target_pairs={{0,16},{4,20},{8,24},{12,28},{16,0},{20,4},{24,8},{28,12},{1,17},{... | collective-permute-start | bytes 1966088 | tf_op jit(solution)/shard_map/ppermute | solution.py:640
  5.6 13.9 %collective-permute-start.2 = (f32[16,640]{1,0:T(8,128)S(1)}, f32[16,640]{1,0:T(8,128)S(1)}, u32[]{:S(2)}, u32[]{:S(2)}) collective-permute-start(f32[16,640]{1,0:T(8,128)S(1)} %get-tuple-element.48), channel_id=1, source_target_pairs={{0,20},{4,24},{8,28},{12,16},{16,4},{20,8},{24,12},{28,0},{1,21},{... | collective-permute-start | bytes 122888 | tf_op jit(solution)/shard_map/ppermute | solution.py:640
  5.7 14.4 %collective-permute-start.4 = (f32[24,640]{1,0:T(8,128)S(1)}, f32[24,640]{1,0:T(8,128)S(1)}, u32[]{:S(2)}, u32[]{:S(2)}) collective-permute-start(f32[24,640]{1,0:T(8,128)S(1)} %get-tuple-element.50), channel_id=1, source_target_pairs={{0,28},{4,16},{8,20},{12,24},{16,12},{20,0},{24,4},{28,8},{1,29},{... | collective-permute-start | bytes 184328 | tf_op jit(solution)/shard_map/ppermute | solution.py:640
  8.3 9.2 %collective-permute-start.1 = (f32[32,640]{1,0:T(8,128)S(1)}, f32[32,640]{1,0:T(8,128)S(1)}, u32[]{:S(2)}, u32[]{:S(2)}) collective-permute-start(f32[32,640]{1,0:T(8,128)S(1)} %get-tuple-element.46), channel_id=1, source_target_pairs={{0,4},{4,8},{8,12},{12,0},{16,20},{20,24},{24,28},{28,16},{1,5},{5... | collective-permute-start | bytes 245768 | tf_op jit(solution)/shard_map/ppermute | solution.py:640
  8.3 11.7 %collective-permute-start.3 = (f32[40,640]{1,0:T(8,128)S(1)}, f32[40,640]{1,0:T(8,128)S(1)}, u32[]{:S(2)}, u32[]{:S(2)}) collective-permute-start(f32[40,640]{1,0:T(8,128)S(1)} %get-tuple-element.49), channel_id=1, source_target_pairs={{0,12},{4,0},{8,4},{12,8},{16,28},{20,16},{24,20},{28,24},{1,13},{... | collective-permute-start | bytes 307208 | tf_op jit(solution)/shard_map/ppermute | solution.py:640
  32.4 14.7 %collective-permute-start.5 = (f32[8,32,128]{2,1,0:T(8,128)S(1)}, f32[8,32,128]{2,1,0:T(8,128)S(1)}, u32[]{:S(2)}, u32[]{:S(2)}) collective-permute-start(f32[8,32,128]{2,1,0:T(8,128)S(1)} %get-tuple-element.58), channel_id=1, source_target_pairs={{0,1},{1,2},{2,3},{3,0},{4,5},{5,6},{6,7},{7,4},{8,9},{9,10},{10,1... | collective-permute-start | bytes 393224 | tf_op jit(solution)/shard_map/ppermute | solution.py:762
  34.0 13.1 %collective-permute-start.6 = (f32[8,32,128]{2,1,0:T(8,128)S(1)}, f32[8,32,128]{2,1,0:T(8,128)S(1)}, u32[]{:S(2)}, u32[]{:S(2)}) collective-permute-start(f32[8,32,128]{2,1,0:T(8,128)S(1)} %get-tuple-element.59), channel_id=1, source_target_pairs={{0,2},{1,3},{2,0},{3,1},{4,6},{5,7},{6,4},{7,5},{8,10},{9,11},{10,... | collective-permute-start | bytes 393224 | tf_op jit(solution)/shard_map/ppermute | solution.py:762
  36.6 10.5 %collective-permute-start.7 = (f32[8,32,128]{2,1,0:T(8,128)S(1)}, f32[8,32,128]{2,1,0:T(8,128)S(1)}, u32[]{:S(2)}, u32[]{:S(2)}) collective-permute-start(f32[8,32,128]{2,1,0:T(8,128)S(1)} %get-tuple-element.60), channel_id=1, source_target_pairs={{0,3},{1,0},{2,1},{3,2},{4,7},{5,4},{6,5},{7,6},{8,11},{9,8},{10,9... | collective-permute-start | bytes 393224 | tf_op jit(solution)/shard_map/ppermute | solution.py:762
  43.6 19.6 %all-to-all-start = ((f32[8,48,256]{2,1,0:T(8,128)}), f32[8,48,256]{2,1,0:T(8,128)S(1)}, u32[]{:S(2)}, u32[]{:S(2)}) async-start(f32[8,48,256]{2,1,0:T(8,128)} %pack.1), calls=%async_computation | async-start | bytes 786432 | tf_op jit(solution)/shard_map/all_to_all | solution.py:796
  47.2 6.7 %collective-permute-start.10 = (f32[8,32,128]{2,1,0:T(8,128)S(1)}, f32[8,32,128]{2,1,0:T(8,128)S(1)}, u32[]{:S(2)}, u32[]{:S(2)}) collective-permute-start(f32[8,32,128]{2,1,0:T(8,128)S(1)} %add_add_fusion.1.refs_1_), channel_id=1, source_target_pairs={{0,3},{1,0},{2,1},{3,2},{4,7},{5,4},{6,5},{7,6},{8,11},{9,8},{10,9... | collective-permute-start | bytes 393224 | tf_op jit(solution)/shard_map/ppermute | solution.py:768
  50.1 13.1 %collective-permute-start.9 = (f32[8,32,128]{2,1,0:T(8,128)S(1)}, f32[8,32,128]{2,1,0:T(8,128)S(1)}, u32[]{:S(2)}, u32[]{:S(2)}) collective-permute-start(f32[8,32,128]{2,1,0:T(8,128)S(1)} %add_add_fusion.1.refs_1_), channel_id=1, source_target_pairs={{0,2},{1,3},{2,0},{3,1},{4,6},{5,7},{6,4},{7,5},{8,10},{9,11},{10,... | collective-permute-start | bytes 393224 | tf_op jit(solution)/shard_map/ppermute | solution.py:768
  51.2 11.9 %collective-permute-start.8 = (f32[8,32,128]{2,1,0:T(8,128)S(1)}, f32[8,32,128]{2,1,0:T(8,128)S(1)}, u32[]{:S(2)}, u32[]{:S(2)}) collective-permute-start(f32[8,32,128]{2,1,0:T(8,128)S(1)} %add_add_fusion.1.refs_1_), channel_id=1, source_target_pairs={{0,1},{1,2},{2,3},{3,0},{4,5},{5,6},{6,7},{7,4},{8,9},{9,10},{10,1... | collective-permute-start | bytes 393224 | tf_op jit(solution)/shard_map/ppermute | solution.py:768
  76.4 8.0 %collective-permute-start.11 = (f32[8,32,128]{2,1,0:T(8,128)S(1)}, f32[8,32,128]{2,1,0:T(8,128)S(1)}, u32[]{:S(2)}, u32[]{:S(2)}) collective-permute-start(f32[8,32,128]{2,1,0:T(8,128)S(1)} %get-tuple-element.63), channel_id=1, source_target_pairs={{0,1},{1,2},{2,3},{3,0},{4,5},{5,6},{6,7},{7,4},{8,9},{9,10},{10,1... | collective-permute-start | bytes 393224 | tf_op jit(solution)/shard_map/ppermute | solution.py:762
  76.5 11.7 %collective-permute-start.12 = (f32[8,32,128]{2,1,0:T(8,128)S(1)}, f32[8,32,128]{2,1,0:T(8,128)S(1)}, u32[]{:S(2)}, u32[]{:S(2)}) collective-permute-start(f32[8,32,128]{2,1,0:T(8,128)S(1)} %get-tuple-element.64), channel_id=1, source_target_pairs={{0,2},{1,3},{2,0},{3,1},{4,6},{5,7},{6,4},{7,5},{8,10},{9,11},{10,... | collective-permute-start | bytes 393224 | tf_op jit(solution)/shard_map/ppermute | solution.py:762
  79.6 8.6 %collective-permute-start.13 = (f32[8,32,128]{2,1,0:T(8,128)S(1)}, f32[8,32,128]{2,1,0:T(8,128)S(1)}, u32[]{:S(2)}, u32[]{:S(2)}) collective-permute-start(f32[8,32,128]{2,1,0:T(8,128)S(1)} %get-tuple-element.65), channel_id=1, source_target_pairs={{0,3},{1,0},{2,1},{3,2},{4,7},{5,4},{6,5},{7,6},{8,11},{9,8},{10,9... | collective-permute-start | bytes 393224 | tf_op jit(solution)/shard_map/ppermute | solution.py:762
  88.2 9.5 %collective-permute-start.16 = (f32[8,32,128]{2,1,0:T(8,128)S(1)}, f32[8,32,128]{2,1,0:T(8,128)S(1)}, u32[]{:S(2)}, u32[]{:S(2)}) collective-permute-start(f32[8,32,128]{2,1,0:T(8,128)S(1)} %add_add_fusion.refs_1_), channel_id=1, source_target_pairs={{0,3},{1,0},{2,1},{3,2},{4,7},{5,4},{6,5},{7,6},{8,11},{9,8},{10,9... | collective-permute-start | bytes 393224 | tf_op jit(solution)/shard_map/ppermute | solution.py:768
  93.8 10.0 %collective-permute-start.15 = (f32[8,32,128]{2,1,0:T(8,128)S(1)}, f32[8,32,128]{2,1,0:T(8,128)S(1)}, u32[]{:S(2)}, u32[]{:S(2)}) collective-permute-start(f32[8,32,128]{2,1,0:T(8,128)S(1)} %add_add_fusion.refs_1_), channel_id=1, source_target_pairs={{0,2},{1,3},{2,0},{3,1},{4,6},{5,7},{6,4},{7,5},{8,10},{9,11},{10,... | collective-permute-start | bytes 393224 | tf_op jit(solution)/shard_map/ppermute | solution.py:768
  93.8 10.0 %collective-permute-start.14 = (f32[8,32,128]{2,1,0:T(8,128)S(1)}, f32[8,32,128]{2,1,0:T(8,128)S(1)}, u32[]{:S(2)}, u32[]{:S(2)}) collective-permute-start(f32[8,32,128]{2,1,0:T(8,128)S(1)} %add_add_fusion.refs_1_), channel_id=1, source_target_pairs={{0,1},{1,2},{2,3},{3,0},{4,5},{5,6},{6,7},{7,4},{8,9},{9,10},{10,1... | collective-permute-start | bytes 393224 | tf_op jit(solution)/shard_map/ppermute | solution.py:768
  103.8 14.9 %all-to-all-start.1 = ((f32[8,8,256]{2,1,0:T(8,128)}), f32[8,8,256]{2,1,0:T(8,128)S(1)}, u32[]{:S(2)}, u32[]{:S(2)}) async-start(f32[8,8,256]{2,1,0:T(8,128)} %get-tuple-element.78), calls=%async_computation.1 | async-start | bytes 131072 | tf_op jit(solution)/shard_map/all_to_all | solution.py:800
  118.6 19.7 %collective-permute-start.17 = (f32[8,32,640]{2,1,0:T(8,128)S(1)}, f32[8,32,640]{2,1,0:T(8,128)S(1)}, u32[]{:S(2)}, u32[]{:S(2)}) collective-permute-start(f32[8,32,640]{2,1,0:T(8,128)S(1)} %get-tuple-element.80), channel_id=1, source_target_pairs={{0,16},{4,20},{8,24},{12,28},{16,0},{20,4},{24,8},{28,12},{1,17},{... | collective-permute-start | bytes 1966088 | tf_op jit(solution)/shard_map/ppermute | solution.py:640
  120.7 15.8 %collective-permute-start.20 = (f32[16,640]{1,0:T(8,128)S(1)}, f32[16,640]{1,0:T(8,128)S(1)}, u32[]{:S(2)}, u32[]{:S(2)}) collective-permute-start(f32[16,640]{1,0:T(8,128)S(1)} %get-tuple-element.83), channel_id=1, source_target_pairs={{0,28},{4,16},{8,20},{12,24},{16,12},{20,0},{24,4},{28,8},{1,29},{... | collective-permute-start | bytes 122888 | tf_op jit(solution)/shard_map/ppermute | solution.py:640
  121.7 16.7 %collective-permute-start.21 = (f32[24,640]{1,0:T(8,128)S(1)}, f32[24,640]{1,0:T(8,128)S(1)}, u32[]{:S(2)}, u32[]{:S(2)}) collective-permute-start(f32[24,640]{1,0:T(8,128)S(1)} %get-tuple-element.84), channel_id=1, source_target_pairs={{0,20},{4,24},{8,28},{12,16},{16,4},{20,8},{24,12},{28,0},{1,21},{... | collective-permute-start | bytes 184328 | tf_op jit(solution)/shard_map/ppermute | solution.py:640
  122.5 15.9 %collective-permute-start.18 = (f32[32,640]{1,0:T(8,128)S(1)}, f32[32,640]{1,0:T(8,128)S(1)}, u32[]{:S(2)}, u32[]{:S(2)}) collective-permute-start(f32[32,640]{1,0:T(8,128)S(1)} %get-tuple-element.81), channel_id=1, source_target_pairs={{0,12},{4,0},{8,4},{12,8},{16,28},{20,16},{24,20},{28,24},{1,13},{... | collective-permute-start | bytes 245768 | tf_op jit(solution)/shard_map/ppermute | solution.py:640
  124.3 14.0 %collective-permute-start.19 = (f32[40,640]{1,0:T(8,128)S(1)}, f32[40,640]{1,0:T(8,128)S(1)}, u32[]{:S(2)}, u32[]{:S(2)}) collective-permute-start(f32[40,640]{1,0:T(8,128)S(1)} %get-tuple-element.82), channel_id=1, source_target_pairs={{0,4},{4,8},{8,12},{12,0},{16,20},{20,24},{24,28},{28,16},{1,5},{5... | collective-permute-start | bytes 307208 | tf_op jit(solution)/shard_map/ppermute | solution.py:640
  (7 other events, 163.6 us)

commit v7 on v6

--- a/solution.py
+++ b/solution.py
@@ -297,22 +297,35 @@
 
     step = 2 if deep % 2 == 0 else 1
 
-    def one_step(i, unused):
-        source, at = i // (deep // step), lax.rem(i, deep // step) * step
+    def group_of(source, at):
         blocks = [(source, at + r, half) for r in range(step) for half in range(halves)]
         numbers = [(source * deep + at + r, half) for r in range(step) for half in range(halves)]
         bottoms = [spans_ref[row, 2 * half] for row, half in numbers]
         needs = [spans_ref[row, 2 * half + 1] for row, half in numbers]
-        most = functools.reduce(jnp.maximum, needs)
-
-        for below, reach in zip((0,) + STEPS, STEPS):
-            @pl.when((most > below) & (most <= reach))
-            def _():
-                together(blocks, [0] * len(blocks) if reach == levels else bottoms, reach)
+        return blocks, bottoms, functools.reduce(jnp.maximum, needs)
+
+    def one_step(i, unused):
+        at = lax.rem(i, deep // step) * step
+        groups = [group_of(2 * (i // (deep // step)) + k, at) for k in range(2)]
+        most = [group[2] for group in groups]
+        low, high = jnp.minimum(*most), jnp.maximum(*most)
+        both = (low > 0) & (high <= STEPS[0])
+
+        @pl.when(both)
+        def _():
+            together(groups[0][0] + groups[1][0], groups[0][1] + groups[1][1], STEPS[0])
+
+        @pl.when((high > 0) & jnp.logical_not(both))
+        def _():
+            for blocks, bottoms, needed in groups:
+                for below, reach in zip((0,) + STEPS, STEPS):
+                    @pl.when((needed > below) & (needed <= reach))
+                    def _():
+                        together(blocks, [0] * len(blocks) if reach == levels else bottoms, reach)
 
         return unused
 
-    lax.fori_loop(0, sources * deep // step, one_step, 0)
+    lax.fori_loop(0, sources * deep // (2 * step), one_step, 0)
     for slot, adj_ref in enumerate(adj_refs):
         start = lax.rem(me + slot, groups) * share * fine_x
         adj_ref[...] = adjoint[pl.ds(pl.multiple_of(start, LANES), share * fine_x), :].reshape(share, fine_x, fine_y)
@@ -503,7 +516,7 @@
     depth = coarse_x + 2
     spread_x = interpolation_rows(fine_x, depth, 2, False)
     share = levels // len(out_refs)
-    unroll = math.gcd(members // 2, 5)
+    unroll = math.gcd(members // 2, 10)
 
     for slot, out_ref in enumerate(out_refs):
         for sub in range(share // EDGE):

time: 141 us -> 138 us (0.979); the launches traced: 139 us -> 138 us
  starting transfers between devices: 44.5 us -> 39.7 us
  waiting for transfers between devices: 40.5 us -> 45.1 us
    ppermute x6, waiting for transfers between devices: 5.76 us -> 8.38 us  [owned_sum(): lax.ppermute(parts[d], 'mem', [(i, (i + d) % count) for i in range(count)])]
    ppermute x6, starting transfers between devices: 10.1 us -> 7.96 us  [gathered(): lax.ppermute(own, 'mem', [(i, (i + d) % count) for i in range(count)])]
    ppermute x6, waiting for transfers between devices: 21.3 us -> 23.2 us  [gathered(): lax.ppermute(own, 'mem', [(i, (i + d) % count) for i in range(count)])]
where the time goes in v7:
time: 138 us
  Pallas kernels  48.2 us (35%)
  waiting for transfers between devices  45.1 us (33%)
  starting transfers between devices  39.7 us (29%)
  local copies, waits for them, and re-layouts  1.87 us (1%)
  other arithmetic  1.65 us (1%)
  between operations  1.46 us (1%)
    ppermute x6, waiting for transfers between devices, gathered(): lax.ppermute(own, 'mem', [(i, (i + d) % count) for i in range(count)])  23.2 us
    ppermute x10, waiting for transfers between devices, shifted(): return lax.ppermute(value, ('tx', 'ty'), pairs)  13.5 us
    ppermute x10, starting transfers between devices, shifted(): return lax.ppermute(value, ('tx', 'ty'), pairs)  13.1 us
    pallas_call x1, Pallas kernels, stencil(): pl.pallas_call(kernel, out_shape=(jax.ShapeDtypeStruct((sources, deep, bl...  12.8 us
    pallas_call x1, Pallas kernels, ensemble(): pl.pallas_call(kernel, out_shape=tuple((jax.ShapeDtypeStruct((levels // g...  11.6 us
    ppermute x6, starting transfers between devices, owned_sum(): lax.ppermute(parts[d], 'mem', [(i, (i + d) % count) for i in range(count)])  10.3 us
    pallas_call x1, Pallas kernels, backward(): pl.pallas_call(kernel, out_shape=tuple((jax.ShapeDtypeStruct(shape, jnp.f...  8.74 us
    ppermute x6, waiting for transfers between devices, owned_sum(): lax.ppermute(parts[d], 'mem', [(i, (i + d) % count) for i in range(count)])  8.38 us
  transfers between devices with their start and end apart: 24, of which 10 were waited for; matrix products, arithmetic and copies ran while one was open for 1% of the time, Pallas kernels for 16%

profile of v7, /device:TPU:0, one launch (start us, length us, event | category | flops | bytes accessed | tf_op | source)
XLA Modules:
  0.0 138.0 jit_solution(13263816296870620694)
XLA Ops:
  0.6 3.0 %collective-permute-start = (f32[8,32,640]{2,1,0:T(8,128)}, f32[8,32,640]{2,1,0:T(8,128)S(1)}, u32[]{:S(2)}, u32[]{:S(2)}) collective-permute-start(f32[8,32,640]{2,1,0:T(8,128)} %alpha_ref.3), channel_id=1, source_target_pairs={{0,16},{4,20},{8,24},{12,28},{16,0},{20,4},{24,8},{28,12},{1,17},{... | collective-permute-start | bytes 1966088 | tf_op jit(solution)/shard_map/ppermute | solution.py:653
  5.7 2.6 %collective-permute-start.4 = (f32[24,640]{1,0:T(8,128)S(1)}, f32[24,640]{1,0:T(8,128)S(1)}, u32[]{:S(2)}, u32[]{:S(2)}) collective-permute-start(f32[24,640]{1,0:T(8,128)S(1)} %get-tuple-element.50), channel_id=1, source_target_pairs={{0,28},{4,16},{8,20},{12,24},{16,12},{20,0},{24,4},{28,8},{1,29},{... | collective-permute-start | bytes 184328 | tf_op jit(solution)/shard_map/ppermute | solution.py:653
  12.3 5.2 %rank.1.target_ref = s32[64,128]{1,0:T(8,128)S(1)} custom-call(s32[1]{0:T(128)S(6)} %copy.15.count_ref, s32[192,128]{1,0:T(8,128)S(1)} %pad_add_fusion.ints_ref), custom_call_target="tpu_custom_call" | custom-call | flops 1048576 | bytes 131072 | tf_op jit(solution)/shard_map/rank/pallas_call | solution.py:101
  17.5 2.0 %collective-permute-done.2.refs_5_.refs_6_ = f32[16,640]{1,0:T(8,128)S(1)} collective-permute-done((f32[16,640]{1,0:T(8,128)S(1)}, f32[16,640]{1,0:T(8,128)S(1)}, u32[]{:S(2)}, u32[]{:S(2)}) %collective-permute-start.2) | collective-permute-done | bytes 40992 | tf_op jit(solution)/shard_map/ppermute | solution.py:653
  20.0 11.6 %ensemble.1 = (f32[8,32,128]{2,1,0:T(8,128)S(1)}, f32[8,32,128]{2,1,0:T(8,128)S(1)}, f32[8,32,128]{2,1,0:T(8,128)S(1)}, f32[8,32,128]{2,1,0:T(8,128)S(1)}) custom-call(s32[1]{0:T(128)} %bitcast.refs_0_, f32[8,32,640]{2,1,0:T(8,128)S(1)} %get-tuple-element.45.refs_1_, f32[8,32,640]{2,1,0:T(8,128)S(1)} %collective-permute-done.refs_2_.refs_3_, ...), custom_call_target="tpu_custom_call" | custom-call | flops 8589934592 | bytes 8388608 | tf_op jit(solution)/shard_map/ensemble/pallas_call | solution.py:691
  33.3 2.6 %collective-permute-start.6 = (f32[8,32,128]{2,1,0:T(8,128)S(1)}, f32[8,32,128]{2,1,0:T(8,128)S(1)}, u32[]{:S(2)}, u32[]{:S(2)}) collective-permute-start(f32[8,32,128]{2,1,0:T(8,128)S(1)} %get-tuple-element.59), channel_id=1, source_target_pairs={{0,2},{1,3},{2,0},{3,1},{4,6},{5,7},{6,4},{7,5},{8,10},{9,11},{10,... | collective-permute-start | bytes 393224 | tf_op jit(solution)/shard_map/ppermute | solution.py:775
  37.3 5.6 %pack.1 = f32[8,48,256]{2,1,0:T(8,128)} custom-call(s32[64,128]{1,0:T(8,128)S(1)} %rank.1.target_ref, s32[192,128]{1,0:T(8,128)S(1)} %pad_add_fusion.ints_ref, f32[128,128]{1,0:T(8,128)S(1)} %pad_maximum_fusion.floats_ref, f32[3,8192]{1,0:T(4,128)S(1)} %copy-done.6), custom_call_target="tpu_custom_call" | custom-call | flops 8589934592 | bytes 1048576 | tf_op jit(solution)/shard_map/pack/pallas_call | solution.py:173
  42.9 3.6 %all-to-all-start = ((f32[8,48,256]{2,1,0:T(8,128)}), f32[8,48,256]{2,1,0:T(8,128)S(1)}, u32[]{:S(2)}, u32[]{:S(2)}) async-start(f32[8,48,256]{2,1,0:T(8,128)} %pack.1), calls=%async_computation | async-start | bytes 786432 | tf_op jit(solution)/shard_map/all_to_all | solution.py:809
  46.6 2.8 %collective-permute-start.10 = (f32[8,32,128]{2,1,0:T(8,128)S(1)}, f32[8,32,128]{2,1,0:T(8,128)S(1)}, u32[]{:S(2)}, u32[]{:S(2)}) collective-permute-start(f32[8,32,128]{2,1,0:T(8,128)S(1)} %add_add_fusion.1.refs_1_), channel_id=1, source_target_pairs={{0,3},{1,0},{2,1},{3,2},{4,7},{5,4},{6,5},{7,6},{8,11},{9,8},{10,9... | collective-permute-start | bytes 393224 | tf_op jit(solution)/shard_map/ppermute | solution.py:781
  50.4 2.9 %collective-permute-done.10.refs_4_ = f32[8,32,128]{2,1,0:T(8,128)S(1)} collective-permute-done((f32[8,32,128]{2,1,0:T(8,128)S(1)}, f32[8,32,128]{2,1,0:T(8,128)S(1)}, u32[]{:S(2)}, u32[]{:S(2)}) %collective-permute-start.10) | collective-permute-done | bytes 131104 | tf_op jit(solution)/shard_map/ppermute | solution.py:781
  53.3 9.1 %collective-permute-done.9.refs_3_ = f32[8,32,128]{2,1,0:T(8,128)S(1)} collective-permute-done((f32[8,32,128]{2,1,0:T(8,128)S(1)}, f32[8,32,128]{2,1,0:T(8,128)S(1)}, u32[]{:S(2)}, u32[]{:S(2)}) %collective-permute-start.9) | collective-permute-done | bytes 131104 | tf_op jit(solution)/shard_map/ppermute | solution.py:781
  62.4 12.8 %stencil.1 = (f32[8,8,256]{2,1,0:T(8,128)}, f32[8,32,128]{2,1,0:T(8,128)S(1)}, f32[8,32,128]{2,1,0:T(8,128)S(1)}, f32[8,32,128]{2,1,0:T(8,128)S(1)}, f32[8,32,128]{2,1,0:T(8,128)S(1)}) custom-call(s32[1]{0:T(128)} %bitcast.refs_0_, f32[8,32,128]{2,1,0:T(8,128)S(1)} %add_add_fusion.1.refs_1_, f32[8,32,128]{2,1,0:T(8,128)S(1)} %collective-permute-done.8.refs_2_, ...), custom_call_target="tpu_custom_call" | custom-call | flops 17179869184 | bytes 1048576 | tf_op jit(solution)/shard_map/stencil/pallas_call | solution.py:348
  77.0 2.8 %collective-permute-start.13 = (f32[8,32,128]{2,1,0:T(8,128)S(1)}, f32[8,32,128]{2,1,0:T(8,128)S(1)}, u32[]{:S(2)}, u32[]{:S(2)}) collective-permute-start(f32[8,32,128]{2,1,0:T(8,128)S(1)} %get-tuple-element.65), channel_id=1, source_target_pairs={{0,3},{1,0},{2,1},{3,2},{4,7},{5,4},{6,5},{7,6},{8,11},{9,8},{10,9... | collective-permute-start | bytes 393224 | tf_op jit(solution)/shard_map/ppermute | solution.py:775
  79.8 3.7 %collective-permute-done.11 = f32[8,32,128]{2,1,0:T(8,128)S(1)} collective-permute-done((f32[8,32,128]{2,1,0:T(8,128)S(1)}, f32[8,32,128]{2,1,0:T(8,128)S(1)}, u32[]{:S(2)}, u32[]{:S(2)}) %collective-permute-start.11) | collective-permute-done | bytes 131104 | tf_op jit(solution)/shard_map/ppermute | solution.py:775
  83.5 4.7 %collective-permute-done.12 = f32[8,32,128]{2,1,0:T(8,128)S(1)} collective-permute-done((f32[8,32,128]{2,1,0:T(8,128)S(1)}, f32[8,32,128]{2,1,0:T(8,128)S(1)}, u32[]{:S(2)}, u32[]{:S(2)}) %collective-permute-start.12) | collective-permute-done | bytes 131104 | tf_op jit(solution)/shard_map/ppermute | solution.py:775
  88.3 3.1 %collective-permute-start.16 = (f32[8,32,128]{2,1,0:T(8,128)S(1)}, f32[8,32,128]{2,1,0:T(8,128)S(1)}, u32[]{:S(2)}, u32[]{:S(2)}) collective-permute-start(f32[8,32,128]{2,1,0:T(8,128)S(1)} %add_add_fusion.refs_1_), channel_id=1, source_target_pairs={{0,3},{1,0},{2,1},{3,2},{4,7},{5,4},{6,5},{7,6},{8,11},{9,8},{10,9... | collective-permute-start | bytes 393224 | tf_op jit(solution)/shard_map/ppermute | solution.py:781
  92.4 2.9 %collective-permute-done.16.refs_4_ = f32[8,32,128]{2,1,0:T(8,128)S(1)} collective-permute-done((f32[8,32,128]{2,1,0:T(8,128)S(1)}, f32[8,32,128]{2,1,0:T(8,128)S(1)}, u32[]{:S(2)}, u32[]{:S(2)}) %collective-permute-start.16) | collective-permute-done | bytes 131104 | tf_op jit(solution)/shard_map/ppermute | solution.py:781
  95.2 8.4 %collective-permute-done.15.refs_3_ = f32[8,32,128]{2,1,0:T(8,128)S(1)} collective-permute-done((f32[8,32,128]{2,1,0:T(8,128)S(1)}, f32[8,32,128]{2,1,0:T(8,128)S(1)}, u32[]{:S(2)}, u32[]{:S(2)}) %collective-permute-start.15) | collective-permute-done | bytes 131104 | tf_op jit(solution)/shard_map/ppermute | solution.py:781
  103.7 4.8 %all-to-all-start.1 = ((f32[8,8,256]{2,1,0:T(8,128)}), f32[8,8,256]{2,1,0:T(8,128)S(1)}, u32[]{:S(2)}, u32[]{:S(2)}) async-start(f32[8,8,256]{2,1,0:T(8,128)} %get-tuple-element.78), calls=%async_computation.1 | async-start | bytes 131072 | tf_op jit(solution)/shard_map/all_to_all | solution.py:813
  108.4 8.7 %backward.1 = (f32[32,32,128]{2,1,0:T(8,128)}, f32[8,32,640]{2,1,0:T(8,128)S(1)}, f32[8,32,640]{2,1,0:T(8,128)S(1)}, f32[32,640]{1,0:T(8,128)S(1)}, f32[16,640]{...) custom-call(s32[1]{0:T(128)} %bitcast.refs_0_, f32[8,32,128]{2,1,0:T(8,128)S(1)} %add_add_fusion.refs_1_, ...), custom_call_target="tpu_custom_call" | custom-call | flops 8589934592 | bytes 8388608 | tf_op jit(solution)/shard_map/backward/pallas_call | solution.py:732
  117.2 2.1 %collective-permute-start.17 = (f32[8,32,640]{2,1,0:T(8,128)S(1)}, f32[8,32,640]{2,1,0:T(8,128)S(1)}, u32[]{:S(2)}, u32[]{:S(2)}) collective-permute-start(f32[8,32,640]{2,1,0:T(8,128)S(1)} %get-tuple-element.80), channel_id=1, source_target_pairs={{0,16},{4,20},{8,24},{12,28},{16,0},{20,4},{24,8},{28,12},{1,17},{... | collective-permute-start | bytes 1966088 | tf_op jit(solution)/shard_map/ppermute | solution.py:653
  121.0 1.8 %collective-permute-start.18 = (f32[32,640]{1,0:T(8,128)S(1)}, f32[32,640]{1,0:T(8,128)S(1)}, u32[]{:S(2)}, u32[]{:S(2)}) collective-permute-start(f32[32,640]{1,0:T(8,128)S(1)} %get-tuple-element.81), channel_id=1, source_target_pairs={{0,12},{4,0},{8,4},{12,8},{16,28},{20,16},{24,20},{28,24},{1,13},{... | collective-permute-start | bytes 245768 | tf_op jit(solution)/shard_map/ppermute | solution.py:653
  122.9 3.1 %unpack.1 = f32[64,128]{1,0:T(8,128)} custom-call(s32[64,128]{1,0:T(8,128)S(1)} %rank.1.target_ref, f32[64,256]{1,0:T(8,128)S(1)} %bitcast.8), custom_call_target="tpu_custom_call" | custom-call | flops 2147483648 | bytes 262144 | tf_op jit(solution)/shard_map/unpack/pallas_call | solution.py:392
  126.0 9.1 %collective-permute-done.20.refs_3_ = f32[16,640]{1,0:T(8,128)S(1)} collective-permute-done((f32[16,640]{1,0:T(8,128)S(1)}, f32[16,640]{1,0:T(8,128)S(1)}, u32[]{:S(2)}, u32[]{:S(2)}) %collective-permute-start.20) | collective-permute-done | bytes 40992 | tf_op jit(solution)/shard_map/ppermute | solution.py:653
  (50 shorter events, 17.5 us)
Async XLA Ops:
  0.6 19.4 %collective-permute-start = (f32[8,32,640]{2,1,0:T(8,128)}, f32[8,32,640]{2,1,0:T(8,128)S(1)}, u32[]{:S(2)}, u32[]{:S(2)}) collective-permute-start(f32[8,32,640]{2,1,0:T(8,128)} %alpha_ref.3), channel_id=1, source_target_pairs={{0,16},{4,20},{8,24},{12,28},{16,0},{20,4},{24,8},{28,12},{1,17},{... | collective-permute-start | bytes 1966088 | tf_op jit(solution)/shard_map/ppermute | solution.py:653
  5.6 13.9 %collective-permute-start.2 = (f32[16,640]{1,0:T(8,128)S(1)}, f32[16,640]{1,0:T(8,128)S(1)}, u32[]{:S(2)}, u32[]{:S(2)}) collective-permute-start(f32[16,640]{1,0:T(8,128)S(1)} %get-tuple-element.48), channel_id=1, source_target_pairs={{0,20},{4,24},{8,28},{12,16},{16,4},{20,8},{24,12},{28,0},{1,21},{... | collective-permute-start | bytes 122888 | tf_op jit(solution)/shard_map/ppermute | solution.py:653
  5.7 14.4 %collective-permute-start.4 = (f32[24,640]{1,0:T(8,128)S(1)}, f32[24,640]{1,0:T(8,128)S(1)}, u32[]{:S(2)}, u32[]{:S(2)}) collective-permute-start(f32[24,640]{1,0:T(8,128)S(1)} %get-tuple-element.50), channel_id=1, source_target_pairs={{0,28},{4,16},{8,20},{12,24},{16,12},{20,0},{24,4},{28,8},{1,29},{... | collective-permute-start | bytes 184328 | tf_op jit(solution)/shard_map/ppermute | solution.py:653
  8.3 9.2 %collective-permute-start.1 = (f32[32,640]{1,0:T(8,128)S(1)}, f32[32,640]{1,0:T(8,128)S(1)}, u32[]{:S(2)}, u32[]{:S(2)}) collective-permute-start(f32[32,640]{1,0:T(8,128)S(1)} %get-tuple-element.46), channel_id=1, source_target_pairs={{0,4},{4,8},{8,12},{12,0},{16,20},{20,24},{24,28},{28,16},{1,5},{5... | collective-permute-start | bytes 245768 | tf_op jit(solution)/shard_map/ppermute | solution.py:653
  8.3 11.7 %collective-permute-start.3 = (f32[40,640]{1,0:T(8,128)S(1)}, f32[40,640]{1,0:T(8,128)S(1)}, u32[]{:S(2)}, u32[]{:S(2)}) collective-permute-start(f32[40,640]{1,0:T(8,128)S(1)} %get-tuple-element.49), channel_id=1, source_target_pairs={{0,12},{4,0},{8,4},{12,8},{16,28},{20,16},{24,20},{28,24},{1,13},{... | collective-permute-start | bytes 307208 | tf_op jit(solution)/shard_map/ppermute | solution.py:653
  31.7 14.8 %collective-permute-start.5 = (f32[8,32,128]{2,1,0:T(8,128)S(1)}, f32[8,32,128]{2,1,0:T(8,128)S(1)}, u32[]{:S(2)}, u32[]{:S(2)}) collective-permute-start(f32[8,32,128]{2,1,0:T(8,128)S(1)} %get-tuple-element.58), channel_id=1, source_target_pairs={{0,1},{1,2},{2,3},{3,0},{4,5},{5,6},{6,7},{7,4},{8,9},{9,10},{10,1... | collective-permute-start | bytes 393224 | tf_op jit(solution)/shard_map/ppermute | solution.py:775
  33.3 13.2 %collective-permute-start.6 = (f32[8,32,128]{2,1,0:T(8,128)S(1)}, f32[8,32,128]{2,1,0:T(8,128)S(1)}, u32[]{:S(2)}, u32[]{:S(2)}) collective-permute-start(f32[8,32,128]{2,1,0:T(8,128)S(1)} %get-tuple-element.59), channel_id=1, source_target_pairs={{0,2},{1,3},{2,0},{3,1},{4,6},{5,7},{6,4},{7,5},{8,10},{9,11},{10,... | collective-permute-start | bytes 393224 | tf_op jit(solution)/shard_map/ppermute | solution.py:775
  35.9 10.6 %collective-permute-start.7 = (f32[8,32,128]{2,1,0:T(8,128)S(1)}, f32[8,32,128]{2,1,0:T(8,128)S(1)}, u32[]{:S(2)}, u32[]{:S(2)}) collective-permute-start(f32[8,32,128]{2,1,0:T(8,128)S(1)} %get-tuple-element.60), channel_id=1, source_target_pairs={{0,3},{1,0},{2,1},{3,2},{4,7},{5,4},{6,5},{7,6},{8,11},{9,8},{10,9... | collective-permute-start | bytes 393224 | tf_op jit(solution)/shard_map/ppermute | solution.py:775
  42.9 19.5 %all-to-all-start = ((f32[8,48,256]{2,1,0:T(8,128)}), f32[8,48,256]{2,1,0:T(8,128)S(1)}, u32[]{:S(2)}, u32[]{:S(2)}) async-start(f32[8,48,256]{2,1,0:T(8,128)} %pack.1), calls=%async_computation | async-start | bytes 786432 | tf_op jit(solution)/shard_map/all_to_all | solution.py:809
  46.6 6.7 %collective-permute-start.10 = (f32[8,32,128]{2,1,0:T(8,128)S(1)}, f32[8,32,128]{2,1,0:T(8,128)S(1)}, u32[]{:S(2)}, u32[]{:S(2)}) collective-permute-start(f32[8,32,128]{2,1,0:T(8,128)S(1)} %add_add_fusion.1.refs_1_), channel_id=1, source_target_pairs={{0,3},{1,0},{2,1},{3,2},{4,7},{5,4},{6,5},{7,6},{8,11},{9,8},{10,9... | collective-permute-start | bytes 393224 | tf_op jit(solution)/shard_map/ppermute | solution.py:781
  49.4 13.0 %collective-permute-start.9 = (f32[8,32,128]{2,1,0:T(8,128)S(1)}, f32[8,32,128]{2,1,0:T(8,128)S(1)}, u32[]{:S(2)}, u32[]{:S(2)}) collective-permute-start(f32[8,32,128]{2,1,0:T(8,128)S(1)} %add_add_fusion.1.refs_1_), channel_id=1, source_target_pairs={{0,2},{1,3},{2,0},{3,1},{4,6},{5,7},{6,4},{7,5},{8,10},{9,11},{10,... | collective-permute-start | bytes 393224 | tf_op jit(solution)/shard_map/ppermute | solution.py:781
  50.4 11.9 %collective-permute-start.8 = (f32[8,32,128]{2,1,0:T(8,128)S(1)}, f32[8,32,128]{2,1,0:T(8,128)S(1)}, u32[]{:S(2)}, u32[]{:S(2)}) collective-permute-start(f32[8,32,128]{2,1,0:T(8,128)S(1)} %add_add_fusion.1.refs_1_), channel_id=1, source_target_pairs={{0,1},{1,2},{2,3},{3,0},{4,5},{5,6},{6,7},{7,4},{8,9},{9,10},{10,1... | collective-permute-start | bytes 393224 | tf_op jit(solution)/shard_map/ppermute | solution.py:781
  75.2 8.3 %collective-permute-start.11 = (f32[8,32,128]{2,1,0:T(8,128)S(1)}, f32[8,32,128]{2,1,0:T(8,128)S(1)}, u32[]{:S(2)}, u32[]{:S(2)}) collective-permute-start(f32[8,32,128]{2,1,0:T(8,128)S(1)} %get-tuple-element.63), channel_id=1, source_target_pairs={{0,1},{1,2},{2,3},{3,0},{4,5},{5,6},{6,7},{7,4},{8,9},{9,10},{10,1... | collective-permute-start | bytes 393224 | tf_op jit(solution)/shard_map/ppermute | solution.py:775
  75.2 13.0 %collective-permute-start.12 = (f32[8,32,128]{2,1,0:T(8,128)S(1)}, f32[8,32,128]{2,1,0:T(8,128)S(1)}, u32[]{:S(2)}, u32[]{:S(2)}) collective-permute-start(f32[8,32,128]{2,1,0:T(8,128)S(1)} %get-tuple-element.64), channel_id=1, source_target_pairs={{0,2},{1,3},{2,0},{3,1},{4,6},{5,7},{6,4},{7,5},{8,10},{9,11},{10,... | collective-permute-start | bytes 393224 | tf_op jit(solution)/shard_map/ppermute | solution.py:775
  77.0 11.2 %collective-permute-start.13 = (f32[8,32,128]{2,1,0:T(8,128)S(1)}, f32[8,32,128]{2,1,0:T(8,128)S(1)}, u32[]{:S(2)}, u32[]{:S(2)}) collective-permute-start(f32[8,32,128]{2,1,0:T(8,128)S(1)} %get-tuple-element.65), channel_id=1, source_target_pairs={{0,3},{1,0},{2,1},{3,2},{4,7},{5,4},{6,5},{7,6},{8,11},{9,8},{10,9... | collective-permute-start | bytes 393224 | tf_op jit(solution)/shard_map/ppermute | solution.py:775
  88.3 7.0 %collective-permute-start.16 = (f32[8,32,128]{2,1,0:T(8,128)S(1)}, f32[8,32,128]{2,1,0:T(8,128)S(1)}, u32[]{:S(2)}, u32[]{:S(2)}) collective-permute-start(f32[8,32,128]{2,1,0:T(8,128)S(1)} %add_add_fusion.refs_1_), channel_id=1, source_target_pairs={{0,3},{1,0},{2,1},{3,2},{4,7},{5,4},{6,5},{7,6},{8,11},{9,8},{10,9... | collective-permute-start | bytes 393224 | tf_op jit(solution)/shard_map/ppermute | solution.py:781
  91.3 12.3 %collective-permute-start.15 = (f32[8,32,128]{2,1,0:T(8,128)S(1)}, f32[8,32,128]{2,1,0:T(8,128)S(1)}, u32[]{:S(2)}, u32[]{:S(2)}) collective-permute-start(f32[8,32,128]{2,1,0:T(8,128)S(1)} %add_add_fusion.refs_1_), channel_id=1, source_target_pairs={{0,2},{1,3},{2,0},{3,1},{4,6},{5,7},{6,4},{7,5},{8,10},{9,11},{10,... | collective-permute-start | bytes 393224 | tf_op jit(solution)/shard_map/ppermute | solution.py:781
  92.4 11.3 %collective-permute-start.14 = (f32[8,32,128]{2,1,0:T(8,128)S(1)}, f32[8,32,128]{2,1,0:T(8,128)S(1)}, u32[]{:S(2)}, u32[]{:S(2)}) collective-permute-start(f32[8,32,128]{2,1,0:T(8,128)S(1)} %add_add_fusion.refs_1_), channel_id=1, source_target_pairs={{0,1},{1,2},{2,3},{3,0},{4,5},{5,6},{6,7},{7,4},{8,9},{9,10},{10,1... | collective-permute-start | bytes 393224 | tf_op jit(solution)/shard_map/ppermute | solution.py:781
  103.7 13.5 %all-to-all-start.1 = ((f32[8,8,256]{2,1,0:T(8,128)}), f32[8,8,256]{2,1,0:T(8,128)S(1)}, u32[]{:S(2)}, u32[]{:S(2)}) async-start(f32[8,8,256]{2,1,0:T(8,128)} %get-tuple-element.78), calls=%async_computation.1 | async-start | bytes 131072 | tf_op jit(solution)/shard_map/all_to_all | solution.py:813
  117.2 19.7 %collective-permute-start.17 = (f32[8,32,640]{2,1,0:T(8,128)S(1)}, f32[8,32,640]{2,1,0:T(8,128)S(1)}, u32[]{:S(2)}, u32[]{:S(2)}) collective-permute-start(f32[8,32,640]{2,1,0:T(8,128)S(1)} %get-tuple-element.80), channel_id=1, source_target_pairs={{0,16},{4,20},{8,24},{12,28},{16,0},{20,4},{24,8},{28,12},{1,17},{... | collective-permute-start | bytes 1966088 | tf_op jit(solution)/shard_map/ppermute | solution.py:653
  119.3 15.8 %collective-permute-start.20 = (f32[16,640]{1,0:T(8,128)S(1)}, f32[16,640]{1,0:T(8,128)S(1)}, u32[]{:S(2)}, u32[]{:S(2)}) collective-permute-start(f32[16,640]{1,0:T(8,128)S(1)} %get-tuple-element.83), channel_id=1, source_target_pairs={{0,28},{4,16},{8,20},{12,24},{16,12},{20,0},{24,4},{28,8},{1,29},{... | collective-permute-start | bytes 122888 | tf_op jit(solution)/shard_map/ppermute | solution.py:653
  120.2 16.7 %collective-permute-start.21 = (f32[24,640]{1,0:T(8,128)S(1)}, f32[24,640]{1,0:T(8,128)S(1)}, u32[]{:S(2)}, u32[]{:S(2)}) collective-permute-start(f32[24,640]{1,0:T(8,128)S(1)} %get-tuple-element.84), channel_id=1, source_target_pairs={{0,20},{4,24},{8,28},{12,16},{16,4},{20,8},{24,12},{28,0},{1,21},{... | collective-permute-start | bytes 184328 | tf_op jit(solution)/shard_map/ppermute | solution.py:653
  121.0 15.9 %collective-permute-start.18 = (f32[32,640]{1,0:T(8,128)S(1)}, f32[32,640]{1,0:T(8,128)S(1)}, u32[]{:S(2)}, u32[]{:S(2)}) collective-permute-start(f32[32,640]{1,0:T(8,128)S(1)} %get-tuple-element.81), channel_id=1, source_target_pairs={{0,12},{4,0},{8,4},{12,8},{16,28},{20,16},{24,20},{28,24},{1,13},{... | collective-permute-start | bytes 245768 | tf_op jit(solution)/shard_map/ppermute | solution.py:653
  122.9 14.0 %collective-permute-start.19 = (f32[40,640]{1,0:T(8,128)S(1)}, f32[40,640]{1,0:T(8,128)S(1)}, u32[]{:S(2)}, u32[]{:S(2)}) collective-permute-start(f32[40,640]{1,0:T(8,128)S(1)} %get-tuple-element.82), channel_id=1, source_target_pairs={{0,4},{4,8},{8,12},{12,0},{16,20},{20,24},{24,28},{28,16},{1,5},{5... | collective-permute-start | bytes 307208 | tf_op jit(solution)/shard_map/ppermute | solution.py:653
  (7 other events, 162.1 us)

commit v8 on v7

--- a/solution.py
+++ b/solution.py
@@ -309,11 +309,11 @@
         groups = [group_of(2 * (i // (deep // step)) + k, at) for k in range(2)]
         most = [group[2] for group in groups]
         low, high = jnp.minimum(*most), jnp.maximum(*most)
-        both = (low > 0) & (high <= STEPS[0])
-
-        @pl.when(both)
-        def _():
-            together(groups[0][0] + groups[1][0], groups[0][1] + groups[1][1], STEPS[0])
+        both = (low > 0) & (high <= STEPS[1])
+        for below, reach in zip((0, STEPS[0]), STEPS[:2]):
+            @pl.when(both & (high > below) & (high <= reach))
+            def _():
+                together(groups[0][0] + groups[1][0], groups[0][1] + groups[1][1], reach)
 
         @pl.when((high > 0) & jnp.logical_not(both))
         def _():
@@ -569,7 +569,7 @@
     for p, copy in enumerate(copies):
         copy.wait()
 
-        def one_level_group(group, unused):
+        def one_level_group(group):
             some = pl.ds(group * EDGE, EDGE)
             field = adjoint[some].reshape(EDGE * fine_x, fine_y)
             for k in range(p * unroll, (p + 1) * unroll):
@@ -580,9 +580,13 @@
                 for c in range(coarse_x + 1):
                     piece = both[c * EDGE:(c + 1) * EDGE]
                     coarse[c, rows, :] = piece[:, :fine_y] + piece[:, fine_y:]
+
+        def two_level_groups(i, unused):
+            one_level_group(2 * i)
+            one_level_group(2 * i + 1)
             return unused
 
-        lax.fori_loop(0, levels // EDGE, one_level_group, 0)
+        lax.fori_loop(0, levels // (2 * EDGE), two_level_groups, 0)
 
     fold_y = interpolation((coarse_y + PAD, fine_y), 1, 0, EDGE)
     fold_y = jnp.concatenate([fold_y, fold_y], 1)

time: 138 us -> 136 us (0.986)
  Pallas kernels: 48.2 us -> 45.8 us
where the time goes in v8:
time: 136 us; the launch traced here: 137 us
  Pallas kernels  45.8 us (34%)
  waiting for transfers between devices  45.3 us (33%)
  starting transfers between devices  40.5 us (30%)
  local copies, waits for them, and re-layouts  1.87 us (1%)
  other arithmetic  1.65 us (1%)
  between operations  1.45 us (1%)
    ppermute x6, waiting for transfers between devices, gathered(): lax.ppermute(own, 'mem', [(i, (i + d) % count) for i in range(count)])  22.9 us
    ppermute x10, waiting for transfers between devices, shifted(): return lax.ppermute(value, ('tx', 'ty'), pairs)  13.5 us
    ppermute x10, starting transfers between devices, shifted(): return lax.ppermute(value, ('tx', 'ty'), pairs)  13.1 us
    pallas_call x1, Pallas kernels, ensemble(): pl.pallas_call(kernel, out_shape=tuple((jax.ShapeDtypeStruct((levels // g...  11.6 us
    pallas_call x1, Pallas kernels, stencil(): pl.pallas_call(kernel, out_shape=(jax.ShapeDtypeStruct((sources, deep, bl...  11.5 us
    ppermute x6, starting transfers between devices, owned_sum(): lax.ppermute(parts[d], 'mem', [(i, (i + d) % count) for i in range(count)])  10.3 us
    ppermute x6, waiting for transfers between devices, owned_sum(): lax.ppermute(parts[d], 'mem', [(i, (i + d) % count) for i in range(count)])  8.85 us
    ppermute x6, starting transfers between devices, gathered(): lax.ppermute(own, 'mem', [(i, (i + d) % count) for i in range(count)])  7.78 us
  transfers between devices with their start and end apart: 24, of which 10 were waited for; matrix products, arithmetic and copies ran while one was open for 1% of the time, Pallas kernels for 16%

profile of v8, /device:TPU:0, one launch (start us, length us, event | category | flops | bytes accessed | tf_op | source)
XLA Modules:
  0.0 136.5 jit_solution(18331535945729064653)
XLA Ops:
  0.6 3.0 %collective-permute-start = (f32[8,32,640]{2,1,0:T(8,128)}, f32[8,32,640]{2,1,0:T(8,128)S(1)}, u32[]{:S(2)}, u32[]{:S(2)}) collective-permute-start(f32[8,32,640]{2,1,0:T(8,128)} %alpha_ref.3), channel_id=1, source_target_pairs={{0,16},{4,20},{8,24},{12,28},{16,0},{20,4},{24,8},{28,12},{1,17},{... | collective-permute-start | bytes 1966088 | tf_op jit(solution)/shard_map/ppermute | solution.py:657
  5.7 2.6 %collective-permute-start.4 = (f32[24,640]{1,0:T(8,128)S(1)}, f32[24,640]{1,0:T(8,128)S(1)}, u32[]{:S(2)}, u32[]{:S(2)}) collective-permute-start(f32[24,640]{1,0:T(8,128)S(1)} %get-tuple-element.50), channel_id=1, source_target_pairs={{0,28},{4,16},{8,20},{12,24},{16,12},{20,0},{24,4},{28,8},{1,29},{... | collective-permute-start | bytes 184328 | tf_op jit(solution)/shard_map/ppermute | solution.py:657
  12.3 5.2 %rank.1.target_ref = s32[64,128]{1,0:T(8,128)S(1)} custom-call(s32[1]{0:T(128)S(6)} %copy.15.count_ref, s32[192,128]{1,0:T(8,128)S(1)} %pad_add_fusion.ints_ref), custom_call_target="tpu_custom_call" | custom-call | flops 1048576 | bytes 131072 | tf_op jit(solution)/shard_map/rank/pallas_call | solution.py:101
  17.5 2.0 %collective-permute-done.2.refs_5_.refs_6_ = f32[16,640]{1,0:T(8,128)S(1)} collective-permute-done((f32[16,640]{1,0:T(8,128)S(1)}, f32[16,640]{1,0:T(8,128)S(1)}, u32[]{:S(2)}, u32[]{:S(2)}) %collective-permute-start.2) | collective-permute-done | bytes 40992 | tf_op jit(solution)/shard_map/ppermute | solution.py:657
  20.0 11.6 %ensemble.1 = (f32[8,32,128]{2,1,0:T(8,128)S(1)}, f32[8,32,128]{2,1,0:T(8,128)S(1)}, f32[8,32,128]{2,1,0:T(8,128)S(1)}, f32[8,32,128]{2,1,0:T(8,128)S(1)}) custom-call(s32[1]{0:T(128)} %bitcast.refs_0_, f32[8,32,640]{2,1,0:T(8,128)S(1)} %get-tuple-element.45.refs_1_, f32[8,32,640]{2,1,0:T(8,128)S(1)} %collective-permute-done.refs_2_.refs_3_, ...), custom_call_target="tpu_custom_call" | custom-call | flops 8589934592 | bytes 8388608 | tf_op jit(solution)/shard_map/ensemble/pallas_call | solution.py:695
  33.3 2.6 %collective-permute-start.6 = (f32[8,32,128]{2,1,0:T(8,128)S(1)}, f32[8,32,128]{2,1,0:T(8,128)S(1)}, u32[]{:S(2)}, u32[]{:S(2)}) collective-permute-start(f32[8,32,128]{2,1,0:T(8,128)S(1)} %get-tuple-element.59), channel_id=1, source_target_pairs={{0,2},{1,3},{2,0},{3,1},{4,6},{5,7},{6,4},{7,5},{8,10},{9,11},{10,... | collective-permute-start | bytes 393224 | tf_op jit(solution)/shard_map/ppermute | solution.py:779
  37.3 5.6 %pack.1 = f32[8,48,256]{2,1,0:T(8,128)} custom-call(s32[64,128]{1,0:T(8,128)S(1)} %rank.1.target_ref, s32[192,128]{1,0:T(8,128)S(1)} %pad_add_fusion.ints_ref, f32[128,128]{1,0:T(8,128)S(1)} %pad_maximum_fusion.floats_ref, f32[3,8192]{1,0:T(4,128)S(1)} %copy-done.6), custom_call_target="tpu_custom_call" | custom-call | flops 8589934592 | bytes 1048576 | tf_op jit(solution)/shard_map/pack/pallas_call | solution.py:173
  42.9 3.6 %all-to-all-start = ((f32[8,48,256]{2,1,0:T(8,128)}), f32[8,48,256]{2,1,0:T(8,128)S(1)}, u32[]{:S(2)}, u32[]{:S(2)}) async-start(f32[8,48,256]{2,1,0:T(8,128)} %pack.1), calls=%async_computation | async-start | bytes 786432 | tf_op jit(solution)/shard_map/all_to_all | solution.py:813
  46.6 2.8 %collective-permute-start.10 = (f32[8,32,128]{2,1,0:T(8,128)S(1)}, f32[8,32,128]{2,1,0:T(8,128)S(1)}, u32[]{:S(2)}, u32[]{:S(2)}) collective-permute-start(f32[8,32,128]{2,1,0:T(8,128)S(1)} %add_add_fusion.1.refs_1_), channel_id=1, source_target_pairs={{0,3},{1,0},{2,1},{3,2},{4,7},{5,4},{6,5},{7,6},{8,11},{9,8},{10,9... | collective-permute-start | bytes 393224 | tf_op jit(solution)/shard_map/ppermute | solution.py:785
  50.4 2.9 %collective-permute-done.10.refs_4_ = f32[8,32,128]{2,1,0:T(8,128)S(1)} collective-permute-done((f32[8,32,128]{2,1,0:T(8,128)S(1)}, f32[8,32,128]{2,1,0:T(8,128)S(1)}, u32[]{:S(2)}, u32[]{:S(2)}) %collective-permute-start.10) | collective-permute-done | bytes 131104 | tf_op jit(solution)/shard_map/ppermute | solution.py:785
  53.3 9.1 %collective-permute-done.9.refs_3_ = f32[8,32,128]{2,1,0:T(8,128)S(1)} collective-permute-done((f32[8,32,128]{2,1,0:T(8,128)S(1)}, f32[8,32,128]{2,1,0:T(8,128)S(1)}, u32[]{:S(2)}, u32[]{:S(2)}) %collective-permute-start.9) | collective-permute-done | bytes 131104 | tf_op jit(solution)/shard_map/ppermute | solution.py:785
  62.4 11.5 %stencil.1 = (f32[8,8,256]{2,1,0:T(8,128)}, f32[8,32,128]{2,1,0:T(8,128)S(1)}, f32[8,32,128]{2,1,0:T(8,128)S(1)}, f32[8,32,128]{2,1,0:T(8,128)S(1)}, f32[8,32,128]{2,1,0:T(8,128)S(1)}) custom-call(s32[1]{0:T(128)} %bitcast.refs_0_, f32[8,32,128]{2,1,0:T(8,128)S(1)} %add_add_fusion.1.refs_1_, f32[8,32,128]{2,1,0:T(8,128)S(1)} %collective-permute-done.8.refs_2_, ...), custom_call_target="tpu_custom_call" | custom-call | flops 17179869184 | bytes 1048576 | tf_op jit(solution)/shard_map/stencil/pallas_call | solution.py:348
  75.7 2.8 %collective-permute-start.13 = (f32[8,32,128]{2,1,0:T(8,128)S(1)}, f32[8,32,128]{2,1,0:T(8,128)S(1)}, u32[]{:S(2)}, u32[]{:S(2)}) collective-permute-start(f32[8,32,128]{2,1,0:T(8,128)S(1)} %get-tuple-element.65), channel_id=1, source_target_pairs={{0,3},{1,0},{2,1},{3,2},{4,7},{5,4},{6,5},{7,6},{8,11},{9,8},{10,9... | collective-permute-start | bytes 393224 | tf_op jit(solution)/shard_map/ppermute | solution.py:779
  78.5 3.6 %collective-permute-done.11 = f32[8,32,128]{2,1,0:T(8,128)S(1)} collective-permute-done((f32[8,32,128]{2,1,0:T(8,128)S(1)}, f32[8,32,128]{2,1,0:T(8,128)S(1)}, u32[]{:S(2)}, u32[]{:S(2)}) %collective-permute-start.11) | collective-permute-done | bytes 131104 | tf_op jit(solution)/shard_map/ppermute | solution.py:779
  82.2 5.2 %collective-permute-done.12 = f32[8,32,128]{2,1,0:T(8,128)S(1)} collective-permute-done((f32[8,32,128]{2,1,0:T(8,128)S(1)}, f32[8,32,128]{2,1,0:T(8,128)S(1)}, u32[]{:S(2)}, u32[]{:S(2)}) %collective-permute-start.12) | collective-permute-done | bytes 131104 | tf_op jit(solution)/shard_map/ppermute | solution.py:779
  87.4 2.6 %collective-permute-start.16 = (f32[8,32,128]{2,1,0:T(8,128)S(1)}, f32[8,32,128]{2,1,0:T(8,128)S(1)}, u32[]{:S(2)}, u32[]{:S(2)}) collective-permute-start(f32[8,32,128]{2,1,0:T(8,128)S(1)} %add_add_fusion.refs_1_), channel_id=1, source_target_pairs={{0,3},{1,0},{2,1},{3,2},{4,7},{5,4},{6,5},{7,6},{8,11},{9,8},{10,9... | collective-permute-start | bytes 393224 | tf_op jit(solution)/shard_map/ppermute | solution.py:785
  91.4 2.6 %collective-permute-done.16.refs_4_ = f32[8,32,128]{2,1,0:T(8,128)S(1)} collective-permute-done((f32[8,32,128]{2,1,0:T(8,128)S(1)}, f32[8,32,128]{2,1,0:T(8,128)S(1)}, u32[]{:S(2)}, u32[]{:S(2)}) %collective-permute-start.16) | collective-permute-done | bytes 131104 | tf_op jit(solution)/shard_map/ppermute | solution.py:785
  93.9 8.4 %collective-permute-done.15.refs_3_ = f32[8,32,128]{2,1,0:T(8,128)S(1)} collective-permute-done((f32[8,32,128]{2,1,0:T(8,128)S(1)}, f32[8,32,128]{2,1,0:T(8,128)S(1)}, u32[]{:S(2)}, u32[]{:S(2)}) %collective-permute-start.15) | collective-permute-done | bytes 131104 | tf_op jit(solution)/shard_map/ppermute | solution.py:785
  102.3 5.7 %all-to-all-start.1 = ((f32[8,8,256]{2,1,0:T(8,128)}), f32[8,8,256]{2,1,0:T(8,128)S(1)}, u32[]{:S(2)}, u32[]{:S(2)}) async-start(f32[8,8,256]{2,1,0:T(8,128)} %get-tuple-element.78), calls=%async_computation.1 | async-start | bytes 131072 | tf_op jit(solution)/shard_map/all_to_all | solution.py:817
  108.0 7.7 %backward.1 = (f32[32,32,128]{2,1,0:T(8,128)}, f32[8,32,640]{2,1,0:T(8,128)S(1)}, f32[8,32,640]{2,1,0:T(8,128)S(1)}, f32[32,640]{1,0:T(8,128)S(1)}, f32[16,640]{...) custom-call(s32[1]{0:T(128)} %bitcast.refs_0_, f32[8,32,128]{2,1,0:T(8,128)S(1)} %add_add_fusion.refs_1_, ...), custom_call_target="tpu_custom_call" | custom-call | flops 8589934592 | bytes 8388608 | tf_op jit(solution)/shard_map/backward/pallas_call | solution.py:736
  115.7 2.1 %collective-permute-start.17 = (f32[8,32,640]{2,1,0:T(8,128)S(1)}, f32[8,32,640]{2,1,0:T(8,128)S(1)}, u32[]{:S(2)}, u32[]{:S(2)}) collective-permute-start(f32[8,32,640]{2,1,0:T(8,128)S(1)} %get-tuple-element.80), channel_id=1, source_target_pairs={{0,16},{4,20},{8,24},{12,28},{16,0},{20,4},{24,8},{28,12},{1,17},{... | collective-permute-start | bytes 1966088 | tf_op jit(solution)/shard_map/ppermute | solution.py:657
  119.6 1.8 %collective-permute-start.18 = (f32[32,640]{1,0:T(8,128)S(1)}, f32[32,640]{1,0:T(8,128)S(1)}, u32[]{:S(2)}, u32[]{:S(2)}) collective-permute-start(f32[32,640]{1,0:T(8,128)S(1)} %get-tuple-element.81), channel_id=1, source_target_pairs={{0,12},{4,0},{8,4},{12,8},{16,28},{20,16},{24,20},{28,24},{1,13},{... | collective-permute-start | bytes 245768 | tf_op jit(solution)/shard_map/ppermute | solution.py:657
  121.4 3.1 %unpack.1 = f32[64,128]{1,0:T(8,128)} custom-call(s32[64,128]{1,0:T(8,128)S(1)} %rank.1.target_ref, f32[64,256]{1,0:T(8,128)S(1)} %bitcast.8), custom_call_target="tpu_custom_call" | custom-call | flops 2147483648 | bytes 262144 | tf_op jit(solution)/shard_map/unpack/pallas_call | solution.py:392
  124.5 9.1 %collective-permute-done.20.refs_3_ = f32[16,640]{1,0:T(8,128)S(1)} collective-permute-done((f32[16,640]{1,0:T(8,128)S(1)}, f32[16,640]{1,0:T(8,128)S(1)}, u32[]{:S(2)}, u32[]{:S(2)}) %collective-permute-start.20) | collective-permute-done | bytes 40992 | tf_op jit(solution)/shard_map/ppermute | solution.py:657
  (50 shorter events, 17.8 us)
Async XLA Ops:
  0.6 19.4 %collective-permute-start = (f32[8,32,640]{2,1,0:T(8,128)}, f32[8,32,640]{2,1,0:T(8,128)S(1)}, u32[]{:S(2)}, u32[]{:S(2)}) collective-permute-start(f32[8,32,640]{2,1,0:T(8,128)} %alpha_ref.3), channel_id=1, source_target_pairs={{0,16},{4,20},{8,24},{12,28},{16,0},{20,4},{24,8},{28,12},{1,17},{... | collective-permute-start | bytes 1966088 | tf_op jit(solution)/shard_map/ppermute | solution.py:657
  5.6 13.9 %collective-permute-start.2 = (f32[16,640]{1,0:T(8,128)S(1)}, f32[16,640]{1,0:T(8,128)S(1)}, u32[]{:S(2)}, u32[]{:S(2)}) collective-permute-start(f32[16,640]{1,0:T(8,128)S(1)} %get-tuple-element.48), channel_id=1, source_target_pairs={{0,20},{4,24},{8,28},{12,16},{16,4},{20,8},{24,12},{28,0},{1,21},{... | collective-permute-start | bytes 122888 | tf_op jit(solution)/shard_map/ppermute | solution.py:657
  5.7 14.4 %collective-permute-start.4 = (f32[24,640]{1,0:T(8,128)S(1)}, f32[24,640]{1,0:T(8,128)S(1)}, u32[]{:S(2)}, u32[]{:S(2)}) collective-permute-start(f32[24,640]{1,0:T(8,128)S(1)} %get-tuple-element.50), channel_id=1, source_target_pairs={{0,28},{4,16},{8,20},{12,24},{16,12},{20,0},{24,4},{28,8},{1,29},{... | collective-permute-start | bytes 184328 | tf_op jit(solution)/shard_map/ppermute | solution.py:657
  8.3 9.2 %collective-permute-start.1 = (f32[32,640]{1,0:T(8,128)S(1)}, f32[32,640]{1,0:T(8,128)S(1)}, u32[]{:S(2)}, u32[]{:S(2)}) collective-permute-start(f32[32,640]{1,0:T(8,128)S(1)} %get-tuple-element.46), channel_id=1, source_target_pairs={{0,4},{4,8},{8,12},{12,0},{16,20},{20,24},{24,28},{28,16},{1,5},{5... | collective-permute-start | bytes 245768 | tf_op jit(solution)/shard_map/ppermute | solution.py:657
  8.3 11.7 %collective-permute-start.3 = (f32[40,640]{1,0:T(8,128)S(1)}, f32[40,640]{1,0:T(8,128)S(1)}, u32[]{:S(2)}, u32[]{:S(2)}) collective-permute-start(f32[40,640]{1,0:T(8,128)S(1)} %get-tuple-element.49), channel_id=1, source_target_pairs={{0,12},{4,0},{8,4},{12,8},{16,28},{20,16},{24,20},{28,24},{1,13},{... | collective-permute-start | bytes 307208 | tf_op jit(solution)/shard_map/ppermute | solution.py:657
  31.7 14.8 %collective-permute-start.5 = (f32[8,32,128]{2,1,0:T(8,128)S(1)}, f32[8,32,128]{2,1,0:T(8,128)S(1)}, u32[]{:S(2)}, u32[]{:S(2)}) collective-permute-start(f32[8,32,128]{2,1,0:T(8,128)S(1)} %get-tuple-element.58), channel_id=1, source_target_pairs={{0,1},{1,2},{2,3},{3,0},{4,5},{5,6},{6,7},{7,4},{8,9},{9,10},{10,1... | collective-permute-start | bytes 393224 | tf_op jit(solution)/shard_map/ppermute | solution.py:779
  33.3 13.2 %collective-permute-start.6 = (f32[8,32,128]{2,1,0:T(8,128)S(1)}, f32[8,32,128]{2,1,0:T(8,128)S(1)}, u32[]{:S(2)}, u32[]{:S(2)}) collective-permute-start(f32[8,32,128]{2,1,0:T(8,128)S(1)} %get-tuple-element.59), channel_id=1, source_target_pairs={{0,2},{1,3},{2,0},{3,1},{4,6},{5,7},{6,4},{7,5},{8,10},{9,11},{10,... | collective-permute-start | bytes 393224 | tf_op jit(solution)/shard_map/ppermute | solution.py:779
  35.9 10.6 %collective-permute-start.7 = (f32[8,32,128]{2,1,0:T(8,128)S(1)}, f32[8,32,128]{2,1,0:T(8,128)S(1)}, u32[]{:S(2)}, u32[]{:S(2)}) collective-permute-start(f32[8,32,128]{2,1,0:T(8,128)S(1)} %get-tuple-element.60), channel_id=1, source_target_pairs={{0,3},{1,0},{2,1},{3,2},{4,7},{5,4},{6,5},{7,6},{8,11},{9,8},{10,9... | collective-permute-start | bytes 393224 | tf_op jit(solution)/shard_map/ppermute | solution.py:779
  42.9 19.5 %all-to-all-start = ((f32[8,48,256]{2,1,0:T(8,128)}), f32[8,48,256]{2,1,0:T(8,128)S(1)}, u32[]{:S(2)}, u32[]{:S(2)}) async-start(f32[8,48,256]{2,1,0:T(8,128)} %pack.1), calls=%async_computation | async-start | bytes 786432 | tf_op jit(solution)/shard_map/all_to_all | solution.py:813
  46.6 6.7 %collective-permute-start.10 = (f32[8,32,128]{2,1,0:T(8,128)S(1)}, f32[8,32,128]{2,1,0:T(8,128)S(1)}, u32[]{:S(2)}, u32[]{:S(2)}) collective-permute-start(f32[8,32,128]{2,1,0:T(8,128)S(1)} %add_add_fusion.1.refs_1_), channel_id=1, source_target_pairs={{0,3},{1,0},{2,1},{3,2},{4,7},{5,4},{6,5},{7,6},{8,11},{9,8},{10,9... | collective-permute-start | bytes 393224 | tf_op jit(solution)/shard_map/ppermute | solution.py:785
  49.4 13.0 %collective-permute-start.9 = (f32[8,32,128]{2,1,0:T(8,128)S(1)}, f32[8,32,128]{2,1,0:T(8,128)S(1)}, u32[]{:S(2)}, u32[]{:S(2)}) collective-permute-start(f32[8,32,128]{2,1,0:T(8,128)S(1)} %add_add_fusion.1.refs_1_), channel_id=1, source_target_pairs={{0,2},{1,3},{2,0},{3,1},{4,6},{5,7},{6,4},{7,5},{8,10},{9,11},{10,... | collective-permute-start | bytes 393224 | tf_op jit(solution)/shard_map/ppermute | solution.py:785
  50.4 11.9 %collective-permute-start.8 = (f32[8,32,128]{2,1,0:T(8,128)S(1)}, f32[8,32,128]{2,1,0:T(8,128)S(1)}, u32[]{:S(2)}, u32[]{:S(2)}) collective-permute-start(f32[8,32,128]{2,1,0:T(8,128)S(1)} %add_add_fusion.1.refs_1_), channel_id=1, source_target_pairs={{0,1},{1,2},{2,3},{3,0},{4,5},{5,6},{6,7},{7,4},{8,9},{9,10},{10,1... | collective-permute-start | bytes 393224 | tf_op jit(solution)/shard_map/ppermute | solution.py:785
  73.9 8.3 %collective-permute-start.11 = (f32[8,32,128]{2,1,0:T(8,128)S(1)}, f32[8,32,128]{2,1,0:T(8,128)S(1)}, u32[]{:S(2)}, u32[]{:S(2)}) collective-permute-start(f32[8,32,128]{2,1,0:T(8,128)S(1)} %get-tuple-element.63), channel_id=1, source_target_pairs={{0,1},{1,2},{2,3},{3,0},{4,5},{5,6},{6,7},{7,4},{8,9},{9,10},{10,1... | collective-permute-start | bytes 393224 | tf_op jit(solution)/shard_map/ppermute | solution.py:779
  74.8 12.6 %collective-permute-start.12 = (f32[8,32,128]{2,1,0:T(8,128)S(1)}, f32[8,32,128]{2,1,0:T(8,128)S(1)}, u32[]{:S(2)}, u32[]{:S(2)}) collective-permute-start(f32[8,32,128]{2,1,0:T(8,128)S(1)} %get-tuple-element.64), channel_id=1, source_target_pairs={{0,2},{1,3},{2,0},{3,1},{4,6},{5,7},{6,4},{7,5},{8,10},{9,11},{10,... | collective-permute-start | bytes 393224 | tf_op jit(solution)/shard_map/ppermute | solution.py:779
  75.7 11.7 %collective-permute-start.13 = (f32[8,32,128]{2,1,0:T(8,128)S(1)}, f32[8,32,128]{2,1,0:T(8,128)S(1)}, u32[]{:S(2)}, u32[]{:S(2)}) collective-permute-start(f32[8,32,128]{2,1,0:T(8,128)S(1)} %get-tuple-element.65), channel_id=1, source_target_pairs={{0,3},{1,0},{2,1},{3,2},{4,7},{5,4},{6,5},{7,6},{8,11},{9,8},{10,9... | collective-permute-start | bytes 393224 | tf_op jit(solution)/shard_map/ppermute | solution.py:779
  87.4 6.5 %collective-permute-start.16 = (f32[8,32,128]{2,1,0:T(8,128)S(1)}, f32[8,32,128]{2,1,0:T(8,128)S(1)}, u32[]{:S(2)}, u32[]{:S(2)}) collective-permute-start(f32[8,32,128]{2,1,0:T(8,128)S(1)} %add_add_fusion.refs_1_), channel_id=1, source_target_pairs={{0,3},{1,0},{2,1},{3,2},{4,7},{5,4},{6,5},{7,6},{8,11},{9,8},{10,9... | collective-permute-start | bytes 393224 | tf_op jit(solution)/shard_map/ppermute | solution.py:785
  90.0 12.3 %collective-permute-start.15 = (f32[8,32,128]{2,1,0:T(8,128)S(1)}, f32[8,32,128]{2,1,0:T(8,128)S(1)}, u32[]{:S(2)}, u32[]{:S(2)}) collective-permute-start(f32[8,32,128]{2,1,0:T(8,128)S(1)} %add_add_fusion.refs_1_), channel_id=1, source_target_pairs={{0,2},{1,3},{2,0},{3,1},{4,6},{5,7},{6,4},{7,5},{8,10},{9,11},{10,... | collective-permute-start | bytes 393224 | tf_op jit(solution)/shard_map/ppermute | solution.py:785
  91.3 11.0 %collective-permute-start.14 = (f32[8,32,128]{2,1,0:T(8,128)S(1)}, f32[8,32,128]{2,1,0:T(8,128)S(1)}, u32[]{:S(2)}, u32[]{:S(2)}) collective-permute-start(f32[8,32,128]{2,1,0:T(8,128)S(1)} %add_add_fusion.refs_1_), channel_id=1, source_target_pairs={{0,1},{1,2},{2,3},{3,0},{4,5},{5,6},{6,7},{7,4},{8,9},{9,10},{10,1... | collective-permute-start | bytes 393224 | tf_op jit(solution)/shard_map/ppermute | solution.py:785
  102.3 13.4 %all-to-all-start.1 = ((f32[8,8,256]{2,1,0:T(8,128)}), f32[8,8,256]{2,1,0:T(8,128)S(1)}, u32[]{:S(2)}, u32[]{:S(2)}) async-start(f32[8,8,256]{2,1,0:T(8,128)} %get-tuple-element.78), calls=%async_computation.1 | async-start | bytes 131072 | tf_op jit(solution)/shard_map/all_to_all | solution.py:817
  115.7 19.7 %collective-permute-start.17 = (f32[8,32,640]{2,1,0:T(8,128)S(1)}, f32[8,32,640]{2,1,0:T(8,128)S(1)}, u32[]{:S(2)}, u32[]{:S(2)}) collective-permute-start(f32[8,32,640]{2,1,0:T(8,128)S(1)} %get-tuple-element.80), channel_id=1, source_target_pairs={{0,16},{4,20},{8,24},{12,28},{16,0},{20,4},{24,8},{28,12},{1,17},{... | collective-permute-start | bytes 1966088 | tf_op jit(solution)/shard_map/ppermute | solution.py:657
  117.8 15.8 %collective-permute-start.20 = (f32[16,640]{1,0:T(8,128)S(1)}, f32[16,640]{1,0:T(8,128)S(1)}, u32[]{:S(2)}, u32[]{:S(2)}) collective-permute-start(f32[16,640]{1,0:T(8,128)S(1)} %get-tuple-element.83), channel_id=1, source_target_pairs={{0,28},{4,16},{8,20},{12,24},{16,12},{20,0},{24,4},{28,8},{1,29},{... | collective-permute-start | bytes 122888 | tf_op jit(solution)/shard_map/ppermute | solution.py:657
  118.7 16.7 %collective-permute-start.21 = (f32[24,640]{1,0:T(8,128)S(1)}, f32[24,640]{1,0:T(8,128)S(1)}, u32[]{:S(2)}, u32[]{:S(2)}) collective-permute-start(f32[24,640]{1,0:T(8,128)S(1)} %get-tuple-element.84), channel_id=1, source_target_pairs={{0,20},{4,24},{8,28},{12,16},{16,4},{20,8},{24,12},{28,0},{1,21},{... | collective-permute-start | bytes 184328 | tf_op jit(solution)/shard_map/ppermute | solution.py:657
  119.6 15.9 %collective-permute-start.18 = (f32[32,640]{1,0:T(8,128)S(1)}, f32[32,640]{1,0:T(8,128)S(1)}, u32[]{:S(2)}, u32[]{:S(2)}) collective-permute-start(f32[32,640]{1,0:T(8,128)S(1)} %get-tuple-element.81), channel_id=1, source_target_pairs={{0,12},{4,0},{8,4},{12,8},{16,28},{20,16},{24,20},{28,24},{1,13},{... | collective-permute-start | bytes 245768 | tf_op jit(solution)/shard_map/ppermute | solution.py:657
  121.4 14.0 %collective-permute-start.19 = (f32[40,640]{1,0:T(8,128)S(1)}, f32[40,640]{1,0:T(8,128)S(1)}, u32[]{:S(2)}, u32[]{:S(2)}) collective-permute-start(f32[40,640]{1,0:T(8,128)S(1)} %get-tuple-element.82), channel_id=1, source_target_pairs={{0,4},{4,8},{8,12},{12,0},{16,20},{20,24},{24,28},{28,16},{1,5},{5... | collective-permute-start | bytes 307208 | tf_op jit(solution)/shard_map/ppermute | solution.py:657
  (7 other events, 161.7 us)
